TPU v7x, 256 devices: a whole 4x4x8 slice. The times are simulated.
256 devices in a mesh: fsdp: 16 (over z, core), grp: 16 (over y, x).
Axes of the slice: x: 4, y: 4, z: 8, core: 2. Of those that a mesh axis runs over, the one named last changes fastest.
Arguments:
- grads: bfloat16 [16, 1536, 4096], P(None, 'fsdp', 'grp')
- owner: int32 [16], replicated, may hold values from 0 to 15, as said below
Outputs:
- update: bfloat16 [16, 1536, 4096], P(None, 'fsdp', 'grp')
- owned: bfloat16 [32, 1536, 4096], P('fsdp', None, 'grp')
Inputs may be any that keep to these rules, and one draw needn't show every extreme that they name: `owner`: no group owns more than 2 matrices, and some group owns exactly 2.
All inputs are finite; a program needn't handle non-finite values.
Results may differ from a plain program's by a relative error of at most 0.02.
Values may be sent and summed in bfloat16 or wider, within the bound.
No kernel may reach another device: no remote copies, remote signals or barrier semaphores. Data moves between devices by JAX's collectives and lax.ppermute only.
A program may use at most 64 MiB of HBM per device.

v0:
```python
import math

import jax
import jax.numpy as jnp
from jax import lax
from jax.sharding import PartitionSpec as P

MOST = 2


def scaled(block, totals, rows):
    inverse = 1.0 / jnp.sqrt(totals / rows + 1e-06)
    return (block.astype(jnp.float32) * inverse[:, None, None]).astype(jnp.bfloat16)


def finish(factor, normed_rows, left_rows, right_rows):
    mixed = (
        3.4445 * normed_rows.astype(jnp.float32)
        - 4.775 * left_rows.astype(jnp.float32)
        + 2.0315 * right_rows
    )
    return (factor * mixed).astype(jnp.bfloat16)


def newton(normed, factor):
    gram_panel = lax.psum_scatter(
        lax.dot_general(
            normed, normed, (((1,), (1,)), ((), ())), preferred_element_type=jnp.float32
        ).astype(jnp.bfloat16),
        "grp",
        scatter_dimension=0,
        tiled=True,
    )
    left = jnp.dot(
        lax.all_gather(gram_panel, "grp", axis=0, tiled=True),
        normed,
        preferred_element_type=jnp.float32,
    ).astype(jnp.bfloat16)
    product = jnp.dot(
        lax.all_gather(gram_panel, "grp", axis=0, tiled=True),
        left,
        preferred_element_type=jnp.float32,
    )
    return finish(factor, normed, left, product)


def orthogonal(block, factor):
    rows = block.shape[1]
    partial_sums = jnp.sum(jnp.square(block.astype(jnp.float32)), axis=(1, 2))
    totals = lax.psum(partial_sums, "grp")
    block = scaled(block, totals, rows)
    results = [newton(block[slot], factor) for slot in range(block.shape[0])]
    return jnp.stack(results, axis=0)


def on_device(grads, owner):
    count, rows_dev, cols_dev = grads.shape
    groups = lax.axis_size("fsdp")
    rows = rows_dev * groups
    cols = cols_dev * lax.axis_size("grp")
    factor = 0.2 * math.sqrt(max(rows, cols))
    index = jnp.arange(count, dtype=jnp.int32)
    same = (owner[:, None] == owner[None, :]) & (index[None, :] < index[:, None])
    rank = jnp.sum(same.astype(jnp.int32), axis=1)
    target = owner * MOST + rank
    slots_all = jnp.arange(groups * MOST, dtype=jnp.int32)
    selector = (target[:, None] == slots_all[None, :]).astype(jnp.bfloat16)
    packed = jnp.einsum("eq,erc->qrc", selector, grads, preferred_element_type=jnp.float32)
    packed = packed.astype(jnp.bfloat16).reshape(groups, MOST, rows_dev, cols_dev)
    arrived = lax.all_to_all(packed, "fsdp", split_axis=0, concat_axis=2, tiled=True).reshape(
        MOST, rows, cols_dev
    )
    owned = orthogonal(arrived, factor)
    returned = lax.all_to_all(
        owned.reshape(1, MOST, rows, cols_dev), "fsdp", split_axis=2, concat_axis=0, tiled=True
    )
    returned = returned.reshape(groups * MOST, rows_dev, cols_dev)
    update = jnp.einsum(
        "eq,qrc->erc", selector, returned, preferred_element_type=jnp.float32
    ).astype(jnp.bfloat16)
    return (update, owned)


def solution(mesh):
    placed = (P(None, "fsdp", "grp"), P())
    return jax.shard_map(
        on_device,
        mesh=mesh,
        in_specs=placed,
        out_specs=(P(None, "fsdp", "grp"), P("fsdp", None, "grp")),
        check_vma=False,
    )
```

profile of v0, /device:TPU:1, one launch (start us, length us, event | category | flops | bytes accessed | tf_op | source)
XLA Modules:
  0.0 474.6 jit_solution(4034923113577593995)
XLA Ops:
  7.2 0.9 convert_reduce_fusion
  8.1 0.7 multiply_add_fusion
  8.8 1.9 convolution_convert_fusion.4
  10.7 2.5 reshape.26
  13.2 1.4 copy.15
  14.6 49.6 %all_to_all.24 = bf16[16,2,96,256]{3,1,2,0:T(2,128)(2,1)S(1)} all-to-all(bf16[16,2,96,256]{3,1,2,0:T(2,128)(2,1)S(1)} %copy.15), channel_id=1, replica_groups=mesh['fsdp'=16,'grp'=16] {'fsdp'}, dimensions={0} | all-to-all | bytes 3145728 | tf_op jit(solution)/shard_map/all_to_all | solution.py:70
  64.2 3.3 fusion
  67.6 33.4 %psum.7 = f32[2]{0:T(128)S(1)} all-reduce(f32[2]{0:T(128)S(1)} %fusion), channel_id=1, replica_groups=mesh['fsdp'=16,'grp'=16] {'grp'}, use_global_device_ids=true, to_apply=%region_2.0 | all-reduce | flops 2 | bytes 16 | tf_op jit(solution)/shard_map/psum | solution.py:50
  101.0 1.3 convert_bitcast_fusion
  102.3 0.4 copy.16
  102.7 0.4 multiply_convert_fusion
  103.1 3.6 convolution_convert_fusion
  106.7 3.7 convolution_convert_fusion.1
  110.5 77.2 %reduce-scatter.5.cloned.1.call-done = bf16[96,1536]{1,0:T(8,128)(2,1)} async-done(((bf16[1536,1536]{1,0:T(8,128)(2,1)}), bf16[96,1536]{1,0:T(8,128)(2,1)}) %reduce-scatter.5.cloned.1.call-update) | async-done | bytes 294928 | tf_op jit(solution)/shard_map/reduce_scatter | solution.py:26
  187.7 0.2 all-gather.3.cloned.1.call-start
  187.9 86.4 %reduce-scatter.3.cloned.1.call-done = bf16[96,1536]{1,0:T(8,128)(2,1)} async-done(((bf16[1536,1536]{1,0:T(8,128)(2,1)}), bf16[96,1536]{1,0:T(8,128)(2,1)}) %reduce-scatter.3.cloned.1.call-update) | async-done | bytes 294928 | tf_op jit(solution)/shard_map/reduce_scatter | solution.py:26
  274.3 62.5 %all-gather.5.cloned.1.call-done = bf16[1536,1536]{1,0:T(8,128)(2,1)} async-done(((bf16[96,1536]{1,0:T(8,128)(2,1)}), bf16[1536,1536]{1,0:T(8,128)(2,1)}) %all-gather.5.cloned.1.call-update) | async-done | bytes 4718608 | tf_op jit(solution)/shard_map/all_gather | solution.py:35
  336.8 3.9 convolution_convert_fusion.2
  340.7 1.6 fusion.8
  342.3 55.6 %all-gather.3.cloned.1.call-done = bf16[1536,1536]{1,0:T(8,128)(2,1)} async-done(((bf16[96,1536]{1,0:T(8,128)(2,1)}), bf16[1536,1536]{1,0:T(8,128)(2,1)}) %all-gather.3.cloned.1.call-update) | async-done | bytes 4718608 | tf_op jit(solution)/shard_map/all_gather | solution.py:35
  397.9 3.9 convolution_convert_fusion.3
  401.8 1.6 fusion.7
  403.4 0.1 fusion.23
  403.6 0.7 copy-done.1
  404.3 10.7 %copy.17 = bf16[1,2,1536,256]{3,1,0,2:T(2,128)(2,1)} copy(bf16[1,2,1536,256]{3,2,1,0:T(8,128)(2,1)S(1)} %fusion.23) | data formatting | bytes 3145728 | tf_op jit(solution)/shard_map/reshape | solution.py:75
  415.0 7.7 %all-to-all-start.1 = ((bf16[1,2,1536,256]{3,1,0,2:T(2,128)(2,1)}), bf16[1,2,1536,256]{3,1,0,2:T(2,128)(2,1)S(1)}, u32[]{:S(2)}, u32[]{:S(2)}) async-start(bf16[1,2,1536,256]{3,1,0,2:T(2,128)(2,1)} %copy.17), calls=%async_computation.3 | async-start | bytes 3145728 | tf_op jit(solution)/shard_map/all_to_all | solution.py:74
  422.6 2.4 pad_maximum_fusion
  425.1 36.0 %all-to-all-done.1 = bf16[1,2,1536,256]{3,1,0,2:T(2,128)(2,1)S(1)} async-done(((bf16[1,2,1536,256]{3,1,0,2:T(2,128)(2,1)}), bf16[1,2,1536,256]{3,1,0,2:T(2,128)(2,1)S(1)}, u32[]{:S(2)}, u32[]{:S(2)}) %all-to-all-start.1) | async-done | bytes 1572896 | tf_op jit(solution)/shard_map/all_to_all | solution.py:74
  461.1 2.9 copy.23
  464.0 2.5 reshape.28
  466.5 0.4 convolution_convert_fusion.5
  466.9 1.1 copy.19
  (15 shorter events, 0.2 us)
Async XLA Ops:
  7.2 1.6 copy-start
  7.2 180.5 %reduce-scatter.5.cloned.1.call-start = ((), (), s32[]{:S(2)}) async-start(), calls=%async_computation.6 | async-start | bytes 5013504 | tf_op jit(solution)/shard_map/reduce_scatter | solution.py:26
  106.7 167.6 %reduce-scatter.3.cloned.1.call-start = ((), (), s32[]{:S(2)}) async-start(), calls=%async_computation.4 | async-start | bytes 5013504 | tf_op jit(solution)/shard_map/reduce_scatter | solution.py:26
  110.4 226.4 %all-gather.5.cloned.1.call-start = ((), (), s32[]{:S(2)}) async-start(), calls=%async_computation.7 | async-start | bytes 5013504 | tf_op jit(solution)/shard_map/all_gather | solution.py:35
  187.7 210.2 %all-gather.3.cloned.1.call-start = ((), (), s32[]{:S(2)}) async-start(), calls=%async_computation.5 | async-start | bytes 5013504 | tf_op jit(solution)/shard_map/all_gather | solution.py:35
  336.8 3.9 copy-start.2
  397.9 3.9 copy-start.3
  403.4 0.9 copy-start.1
  415.0 46.1 %all-to-all-start.1 = ((bf16[1,2,1536,256]{3,1,0,2:T(2,128)(2,1)}), bf16[1,2,1536,256]{3,1,0,2:T(2,128)(2,1)S(1)}, u32[]{:S(2)}, u32[]{:S(2)}) async-start(bf16[1,2,1536,256]{3,1,0,2:T(2,128)(2,1)} %copy.17), calls=%async_computation.3 | async-start | bytes 3145728 | tf_op jit(solution)/shard_map/all_to_all | solution.py:74
Sparse Core Ops, SparseCore 0:
  106.8 80.8 reduce-scatter.4
  191.3 82.9 reduce-scatter.2
  276.7 60.0 all-gather.4
  339.1 58.7 all-gather.2
where the time goes:
time: 475 us
  waiting for transfers between devices  318 us (67%)
  blocking collectives  83 us (17%)
  local copies, waits for them, and re-layouts  22.3 us (5%)
  matrix products  20.4 us (4%)
  between operations  13.9 us (3%)
  other arithmetic  9.17 us (2%)
  starting transfers between devices  8.04 us (2%)
    reduce_scatter x2, waiting for transfers between devices, newton(): lax.psum_scatter(lax.dot_general(normed, normed, (((1,), (1,)), ((), ()))...  164 us
    all_gather x2, waiting for transfers between devices, newton(): lax.all_gather(gram_panel, 'grp', axis=0, tiled=True)  118 us
    all_to_all x1, blocking collectives, on_device(): lax.all_to_all(packed, 'fsdp', split_axis=0, concat_axis=2, tiled=True)  49.6 us
    all_to_all x1, waiting for transfers between devices, on_device(): lax.all_to_all(owned.reshape(1, MOST, rows, cols_dev), 'fsdp', split_axis...  36 us
    psum x1, blocking collectives, orthogonal(): totals = lax.psum(partial_sums, 'grp')  33.4 us
    reshape x1, local copies, waits for them, and re-layouts, on_device(): owned.reshape(1, MOST, rows, cols_dev)  10.7 us
  transfers between devices with their start and end apart: 5, of which 5 were waited for; matrix products, arithmetic and copies ran while one was open for 2% of the time, Pallas kernels for 0%

commit v1 on v0

v1 whole, which is shorter than its diff:
```python
import functools
import math

import jax
import jax.numpy as jnp
from jax import lax
from jax.experimental import pallas as pl
from jax.experimental.pallas import tpu as pltpu
from jax.sharding import PartitionSpec as P

MOST = 2
SIDE = 4
BLOCK = 256
HALF = 128
PIECE = BLOCK // SIDE
SUB = PIECE // SIDE
VMEM_LIMIT = 56 * 1024 * 1024

VMEM = pl.BlockSpec(memory_space=pltpu.VMEM)
SMEM = pl.BlockSpec(memory_space=pltpu.SMEM)


def params():
    return pltpu.CompilerParams(vmem_limit_bytes=VMEM_LIMIT)


def shape_of(*dims, dtype=jnp.bfloat16):
    return jax.ShapeDtypeStruct(dims, dtype)


def pairs_of(rows):
    side = rows // BLOCK
    return [(i, j) for i in range(side) for j in range(i + 1)]


def plan_kernel(owner_ref, grads_ref, table_ref, packed_ref, empty_ref):
    count = owner_ref.shape[0]

    def clear(g, _):
        table_ref[2, g] = -1
        table_ref[3, g] = 0
        return 0

    lax.fori_loop(0, count, clear, 0)

    def first(e, _):
        g = owner_ref[e]
        seen = table_ref[3, g]
        table_ref[3, g] = seen + 1

        @pl.when(seen == 0)
        def _():
            table_ref[0, g] = e
            table_ref[1, e] = g

        @pl.when(seen > 0)
        def _():
            table_ref[2, g] = e

        return 0

    lax.fori_loop(0, count, first, 0)

    def empties(g, n):
        none = table_ref[3, g] == 0

        @pl.when(none)
        def _():
            empty_ref[n] = g

        return n + none.astype(jnp.int32)

    lax.fori_loop(0, count, empties, 0)

    def second(g, n):
        e = table_ref[2, g]
        two = e >= 0

        @pl.when(two)
        def _():
            h = empty_ref[n]
            table_ref[2, g] = h
            table_ref[0, h] = e
            table_ref[1, e] = h

        return n + two.astype(jnp.int32)

    lax.fori_loop(0, count, second, 0)

    def move(g, _):
        packed_ref[g] = grads_ref[table_ref[0, g]]
        return 0

    lax.fori_loop(0, count, move, 0)


def plan(owner, grads):
    count = grads.shape[0]
    return pl.pallas_call(
        plan_kernel,
        out_shape=(shape_of(4, count, dtype=jnp.int32), shape_of(*grads.shape)),
        in_specs=[SMEM, VMEM],
        out_specs=(SMEM, VMEM),
        scratch_shapes=[pltpu.SMEM((count,), jnp.int32)],
        compiler_params=params(),
        name="plan",
    )(owner, grads)


def gram_kernel(pairs, place_ref, x_ref, *refs):
    outs, square_ref, full = refs[: 2 * SIDE], refs[2 * SIDE], refs[2 * SIDE + 1]
    for t, (i, j) in enumerate(pairs):
        full[t] = lax.dot_general(
            x_ref[i * BLOCK : (i + 1) * BLOCK, :],
            x_ref[j * BLOCK : (j + 1) * BLOCK, :],
            (((1,), (1,)), ((), ())),
            preferred_element_type=jnp.float32,
        ).astype(jnp.bfloat16)
        for half in range(2):
            for s in range(SIDE):
                p = lax.rem(place_ref[half] + s, SIDE)
                rows = pl.ds(pl.multiple_of(p * PIECE, PIECE), PIECE)
                outs[half * SIDE + s][t] = full[t, rows, half * HALF : (half + 1) * HALF]
    total = jnp.zeros((1, x_ref.shape[1]), jnp.float32)
    for i in range(x_ref.shape[0] // BLOCK):
        values = x_ref[i * BLOCK : (i + 1) * BLOCK, :].astype(jnp.float32)
        total = total + jnp.sum(values * values, axis=0, keepdims=True)
    total = jnp.sum(total, axis=1, keepdims=True)
    square_ref[...] = jnp.broadcast_to(total, square_ref.shape)


def gram_terms(place, x):
    pairs = pairs_of(x.shape[0])
    piece = shape_of(len(pairs), PIECE, HALF)
    return pl.pallas_call(
        functools.partial(gram_kernel, pairs),
        out_shape=(piece,) * (2 * SIDE) + (shape_of(8, HALF, dtype=jnp.float32),),
        in_specs=[SMEM, VMEM],
        out_specs=(VMEM,) * (2 * SIDE + 1),
        scratch_shapes=[pltpu.VMEM((len(pairs), BLOCK, BLOCK), jnp.bfloat16)],
        compiler_params=params(),
        name="gram",
    )(place, x)


def add_kernel(place_ref, *refs):
    ins, outs = refs[: 2 * SIDE], refs[2 * SIDE : 4 * SIDE]
    for half in range(2):
        got = ins[half * SIDE : (half + 1) * SIDE]
        for s in range(SIDE):
            p = lax.rem(place_ref[1 - half] + s, SIDE)
            rows = pl.ds(pl.multiple_of(p * SUB, SUB), SUB)
            total = got[0][:, rows, :].astype(jnp.float32)
            for other in got[1:]:
                total = total + other[:, rows, :].astype(jnp.float32)
            outs[half * SIDE + s][...] = total.astype(jnp.bfloat16)


def add_first(place, pieces):
    blocks = pieces[0].shape[0]
    return pl.pallas_call(
        add_kernel,
        out_shape=(shape_of(blocks, SUB, HALF),) * (2 * SIDE),
        in_specs=[SMEM] + [VMEM] * (2 * SIDE),
        out_specs=(VMEM,) * (2 * SIDE),
        compiler_params=params(),
        name="add_first",
    )(place, *pieces)


def add_last_kernel(square_ref, *refs):
    ins, outs = refs[: 2 * SIDE], refs[2 * SIDE :]
    blocks = ins[0].shape[0]
    for half in range(2):
        got = ins[half * SIDE : (half + 1) * SIDE]
        total = got[0][...].astype(jnp.float32)
        for other in got[1:]:
            total = total + other[...].astype(jnp.float32)
        outs[half][:blocks] = total.astype(jnp.bfloat16)
    rest = jnp.broadcast_to(square_ref[0:1, :], (SUB, HALF))
    row = lax.broadcasted_iota(jnp.int32, (SUB, HALF), 0)
    parts = jnp.zeros((SUB, HALF), jnp.float32)
    for k in range(3):
        top = lax.reduce_precision(rest, 8, 7)
        parts = jnp.where(row == k, top, parts)
        rest = rest - top
    outs[0][blocks] = parts.astype(jnp.bfloat16)


def add_last(square, pieces):
    blocks = pieces[0].shape[0]
    return pl.pallas_call(
        add_last_kernel,
        out_shape=(shape_of(blocks + 1, SUB, HALF), shape_of(blocks, SUB, HALF)),
        in_specs=[VMEM] * (2 * SIDE + 1),
        out_specs=(VMEM,) * 2,
        compiler_params=params(),
        name="add_last",
    )(square, *pieces)


def join_kernel(place_ref, *refs):
    ins, outs = refs[: 2 * SIDE], refs[2 * SIDE :]
    for half in range(2):
        for s in range(SIDE):
            p = lax.rem(place_ref[1 - half] - s + SIDE, SIDE)
            rows = pl.ds(pl.multiple_of(p * SUB, SUB), SUB)
            outs[half][:, rows, :] = ins[half * SIDE + s][...]


def join(place, parts):
    return pl.pallas_call(
        join_kernel,
        out_shape=tuple(
            shape_of(parts[half * SIDE].shape[0], PIECE, HALF) for half in range(2)
        ),
        in_specs=[SMEM] + [VMEM] * (2 * SIDE),
        out_specs=(VMEM,) * 2,
        compiler_params=params(),
        name="join",
    )(place, *parts)


def step_kernel(pairs, rows_all, factor, place_ref, x_ref, *refs):
    ins = refs[: 2 * SIDE]
    out_ref, gram, normed, left = refs[2 * SIDE :]
    blocks = len(pairs)
    total = jnp.zeros((1, HALF), jnp.float32)
    for s in range(SIDE):
        total = total + jnp.sum(ins[s][blocks].astype(jnp.float32), axis=0, keepdims=True)
    inverse = 1.0 / jnp.sqrt(total / rows_all + 1e-06)
    scale = inverse * inverse
    side = rows_all // BLOCK
    for i in range(side):
        rows = slice(i * BLOCK, (i + 1) * BLOCK)
        for half in range(2):
            lanes = slice(half * HALF, (half + 1) * HALF)
            normed[rows, lanes] = (x_ref[rows, lanes].astype(jnp.float32) * inverse).astype(
                jnp.bfloat16
            )
    for t, (i, j) in enumerate(pairs):
        for half in range(2):
            start = j * BLOCK + half * HALF
            for s in range(SIDE):
                p = lax.rem(place_ref[half] - s + SIDE, SIDE)
                rows = pl.ds(pl.multiple_of(i * BLOCK + p * PIECE, PIECE), PIECE)
                values = ins[half * SIDE + s][t].astype(jnp.float32) * scale
                gram[rows, start : start + HALF] = jnp.where(scale > 0, values, 0.0).astype(
                    jnp.bfloat16
                )
    for i, j in pairs:
        if i != j:
            block = gram[i * BLOCK : (i + 1) * BLOCK, j * BLOCK : (j + 1) * BLOCK]
            gram[j * BLOCK : (j + 1) * BLOCK, i * BLOCK : (i + 1) * BLOCK] = block.T
    for i in range(side):
        rows = slice(i * BLOCK, (i + 1) * BLOCK)
        left[rows, :] = jnp.dot(
            gram[rows, :], normed[...], preferred_element_type=jnp.float32
        ).astype(jnp.bfloat16)
    for i in range(side):
        rows = slice(i * BLOCK, (i + 1) * BLOCK)
        right = jnp.dot(gram[rows, :], left[...], preferred_element_type=jnp.float32)
        mixed = (
            3.4445 * normed[rows, :].astype(jnp.float32)
            - 4.775 * left[rows, :].astype(jnp.float32)
            + 2.0315 * right
        )
        out_ref[rows, :] = (factor * mixed).astype(jnp.bfloat16)


def step(place, x, pieces, factor):
    rows, cols = x.shape
    pairs = pairs_of(rows)
    return pl.pallas_call(
        functools.partial(step_kernel, pairs, rows, factor),
        out_shape=shape_of(rows, cols),
        in_specs=[SMEM, VMEM] + [VMEM] * (2 * SIDE),
        out_specs=VMEM,
        scratch_shapes=[
            pltpu.VMEM((rows, rows), jnp.bfloat16),
            pltpu.VMEM((rows, cols), jnp.bfloat16),
            pltpu.VMEM((rows, cols), jnp.bfloat16),
        ],
        compiler_params=params(),
        name="step",
    )(place, x, *pieces)


def deal_kernel(table_ref, back_ref, update_ref, second_ref):
    count = back_ref.shape[0]

    def move(e, _):
        update_ref[e] = back_ref[table_ref[1, e]]
        helper = table_ref[2, e]
        block = back_ref[jnp.maximum(helper, 0)]
        second_ref[e] = jnp.where(helper >= 0, block, jnp.zeros_like(block))
        return 0

    lax.fori_loop(0, count, move, 0)


def deal(table, back):
    return pl.pallas_call(
        deal_kernel,
        out_shape=(shape_of(*back.shape),) * 2,
        in_specs=[SMEM, VMEM],
        out_specs=(VMEM,) * 2,
        compiler_params=params(),
        name="deal",
    )(table, back)


def shift(value, axis, amount):
    moves = []
    for at in range(SIDE * SIDE):
        y, x = divmod(at, SIDE)
        if axis == 0:
            x = (x + amount) % SIDE
        else:
            y = (y + amount) % SIDE
        moves.append((at, y * SIDE + x))
    return lax.ppermute(value, "grp", moves)


def spread(send, axes):
    got = {(half, 0): send[half][0] for half in range(2)}
    for s in (1, 3, 2):
        for half in range(2):
            got[half, s] = shift(send[half][s], axes[half], s)
    return [got[half, s] for half in range(2) for s in range(SIDE)]


def on_device(grads, owner):
    count, rows_dev, cols_dev = grads.shape
    groups = lax.axis_size("fsdp")
    rows = rows_dev * groups
    cols = cols_dev * lax.axis_size("grp")
    factor = 0.2 * math.sqrt(max(rows, cols))
    at = lax.axis_index("grp")
    me = lax.axis_index("fsdp")
    place = jnp.stack([lax.rem(at, SIDE), lax.div(at, SIDE)]).astype(jnp.int32)
    table, packed = plan(owner, grads)
    x = lax.all_to_all(packed, "fsdp", split_axis=0, concat_axis=0, tiled=True)
    x = x.reshape(rows, cols_dev)
    *terms, square = gram_terms(place, x)
    pieces = spread((terms[:SIDE], terms[SIDE:]), (0, 1))
    parts = add_first(place, pieces)
    parts = spread((parts[:SIDE], parts[SIDE:]), (1, 0))
    own = add_last(square, parts)
    parts = spread(([own[0]] * SIDE, [own[1]] * SIDE), (1, 0))
    own = join(place, parts)
    pieces = spread(([own[0]] * SIDE, [own[1]] * SIDE), (0, 1))
    done = step(place, x, pieces, factor)
    back = lax.all_to_all(
        done.reshape(count, rows_dev, cols_dev), "fsdp", split_axis=0, concat_axis=0, tiled=True
    )
    update, second = deal(table, back)
    second = lax.all_to_all(second, "fsdp", split_axis=0, concat_axis=0, tiled=True)
    first = jnp.where(table[3, me] > 0, done, jnp.zeros_like(done))
    owned = jnp.stack([first, second.reshape(rows, cols_dev)], axis=0)
    return (update, owned)


def solution(mesh):
    return jax.shard_map(
        on_device,
        mesh=mesh,
        in_specs=(P(None, "fsdp", "grp"), P()),
        out_specs=(P(None, "fsdp", "grp"), P("fsdp", None, "grp")),
        check_vma=False,
    )
```

time: 475 us -> 189 us (0.40)
  waiting for transfers between devices: 318 us -> 78.6 us
  blocking collectives: 83 us -> 35.4 us
  starting transfers between devices: 8.04 us -> 42.6 us
  Pallas kernels: 0 us -> 23.1 us
  matrix products: 20.4 us -> 0 us
  local copies, waits for them, and re-layouts: 22.3 us -> 4.4 us
  between operations: 13.9 us -> 0.83 us
  other arithmetic: 9.17 us -> 3.87 us
    reduce_scatter x2 -> x0, waiting for transfers between devices: 164 us -> none  [newton(): lax.psum_scatter(lax.dot_general(normed, normed, (((1,), (1,)), ((), ()))...]
    all_gather x2 -> x0, waiting for transfers between devices: 118 us -> none  [newton(): lax.all_gather(gram_panel, 'grp', axis=0, tiled=True)]
    ppermute x0 -> x24, waiting for transfers between devices: none -> 36.7 us  [shift(): return lax.ppermute(value, 'grp', moves)]
    psum x1 -> x0, blocking collectives: 33.4 us -> none  [orthogonal(): totals = lax.psum(partial_sums, 'grp')]
    ppermute x0 -> x24, starting transfers between devices: none -> 29.1 us  [shift(): return lax.ppermute(value, 'grp', moves)]
    pallas_call x0 -> x7, Pallas kernels: none -> 23.1 us  [the longest x1 6.38 us: step(): pl.pallas_call(functools.partial(step_kernel, pairs, rows, factor), out_s...]
    dot_general x8 -> x0, matrix products: 20.4 us -> none  [the longest x2 7.74 us: newton(): jnp.dot(lax.all_gather(gram_panel, 'grp', axis=0, tiled=True), normed, pr...]
    reshape x4 -> x0, local copies, waits for them, and re-layouts: 17.1 us -> none  [the longest x1 10.7 us: on_device(): owned.reshape(1, MOST, rows, cols_dev)]
  transfers between devices with their start and end apart: 5 -> 26, of which waited for: 5 -> 14; matrix products, arithmetic and copies ran while one was open for 2% -> 1% of each run, Pallas kernels for 0% -> 0%
where the time goes in v1:
time: 189 us
  waiting for transfers between devices  78.6 us (42%)
  starting transfers between devices  42.6 us (23%)
  blocking collectives  35.4 us (19%)
  Pallas kernels  23.1 us (12%)
  local copies, waits for them, and re-layouts  4.4 us (2%)
  other arithmetic  3.87 us (2%)
    ppermute x24, waiting for transfers between devices, shift(): return lax.ppermute(value, 'grp', moves)  36.7 us
    all_to_all x1, blocking collectives, on_device(): lax.all_to_all(done.reshape(count, rows_dev, cols_dev), 'fsdp', split_axi...  35.4 us
    ppermute x24, starting transfers between devices, shift(): return lax.ppermute(value, 'grp', moves)  29.1 us
    all_to_all x1, waiting for transfers between devices, on_device(): x = lax.all_to_all(packed, 'fsdp', split_axis=0, concat_axis=0, tiled=True)  22 us
    all_to_all x1, waiting for transfers between devices, on_device(): lax.all_to_all(second, 'fsdp', split_axis=0, concat_axis=0, tiled=True)  19.8 us
    all_to_all x1, starting transfers between devices, on_device(): x = lax.all_to_all(packed, 'fsdp', split_axis=0, concat_axis=0, tiled=True)  9.99 us
    pallas_call x1, Pallas kernels, step(): pl.pallas_call(functools.partial(step_kernel, pairs, rows, factor), out_s...  6.38 us
    unnamed x52, local copies, waits for them, and re-layouts  4.4 us
  transfers between devices with their start and end apart: 26, of which 14 were waited for; matrix products, arithmetic and copies ran while one was open for 1% of the time, Pallas kernels for 0%

profile of v1, /device:TPU:1, one launch (start us, length us, event | category | flops | bytes accessed | tf_op | source)
XLA Modules:
  0.0 188.9 jit_solution(11014052504873468022)
XLA Ops:
  0.6 3.0 %plan.1 = (s32[4,16]{1,0:T(4,128)}, bf16[16,96,256]{2,1,0:T(8,128)(2,1)}) custom-call(s32[16]{0:T(128)} %owner_ref.1, bf16[16,96,256]{2,1,0:T(8,128)(2,1)} %grads_ref.1), custom_call_target="tpu_custom_call" | custom-call | tf_op jit(solution)/shard_map/plan/pallas_call | solution.py:99
  3.6 10.0 %all-to-all-start = ((bf16[16,96,256]{2,1,0:T(8,128)(2,1)}), bf16[16,96,256]{2,1,0:T(8,128)(2,1)S(1)}, u32[]{:S(2)}, u32[]{:S(2)}) async-start(bf16[16,96,256]{2,1,0:T(8,128)(2,1)} %get-tuple-element.28), calls=%async_computation | async-start | bytes 1572864 | tf_op jit(solution)/shard_map/all_to_all | solution.py:343
  14.2 22.0 %all-to-all-done = bf16[16,96,256]{2,1,0:T(8,128)(2,1)S(1)} async-done(((bf16[16,96,256]{2,1,0:T(8,128)(2,1)}), bf16[16,96,256]{2,1,0:T(8,128)(2,1)S(1)}, u32[]{:S(2)}, u32[]{:S(2)}) %all-to-all-start) | async-done | bytes 786464 | tf_op jit(solution)/shard_map/all_to_all | solution.py:343
  37.1 4.1 %gram.1 = (bf16[21,64,128]{2,1,0:T(8,128)(2,1)}, bf16[21,64,128]{2,1,0:T(8,128)(2,1)}, bf16[21,64,128]{2,1,0:T(8,128)(2,1)}, bf16[21,64,128]{2,1,0:T(8,128)(2,1)...) custom-call(s32[2]{0:T(128)} %pad_add_fusion.place_ref, ...), custom_call_target="tpu_custom_call" | custom-call | tf_op jit(solution)/shard_map/gram/pallas_call | solution.py:135
  42.5 2.5 %collective-permute-start.1 = (bf16[21,64,128]{2,1,0:T(8,128)(2,1)}, bf16[21,64,128]{2,1,0:T(8,128)(2,1)S(1)}, u32[]{:S(2)}, u32[]{:S(2)}) collective-permute-start(bf16[21,64,128]{2,1,0:T(8,128)(2,1)} %get-tuple-element.32), channel_id=1, source_target_pairs={{0,2},{1,3},{2,0},{3,1},{4,6},{5,7},{6,4},{7,5},{8,10},{9,11},{10,... | collective-permute-start | bytes 1032200 | tf_op jit(solution)/shard_map/ppermute | solution.py:322
  46.1 1.3 collective-permute-start.3
  47.4 2.6 %collective-permute-start.4 = (bf16[21,64,128]{2,1,0:T(8,128)(2,1)}, bf16[21,64,128]{2,1,0:T(8,128)(2,1)S(1)}, u32[]{:S(2)}, u32[]{:S(2)}) collective-permute-start(bf16[21,64,128]{2,1,0:T(8,128)(2,1)} %get-tuple-element.36), channel_id=1, source_target_pairs={{0,8},{1,9},{2,10},{3,11},{4,12},{5,13},{6,14},{7,15},{8,0},{9,1},... | collective-permute-start | bytes 1032200 | tf_op jit(solution)/shard_map/ppermute | solution.py:322
  50.0 1.8 collective-permute-done.refs_1_
  51.8 2.7 %collective-permute-start.5 = (bf16[21,64,128]{2,1,0:T(8,128)(2,1)}, bf16[21,64,128]{2,1,0:T(8,128)(2,1)S(1)}, u32[]{:S(2)}, u32[]{:S(2)}) collective-permute-start(bf16[21,64,128]{2,1,0:T(8,128)(2,1)} %get-tuple-element.37), channel_id=1, source_target_pairs={{0,12},{1,13},{2,14},{3,15},{4,0},{5,1},{6,2},{7,3},{8,4},{9,5},{1... | collective-permute-start | bytes 1032200 | tf_op jit(solution)/shard_map/ppermute | solution.py:322
  54.6 5.1 %collective-permute-done.1.refs_2_ = bf16[21,64,128]{2,1,0:T(8,128)(2,1)S(1)} collective-permute-done((bf16[21,64,128]{2,1,0:T(8,128)(2,1)}, bf16[21,64,128]{2,1,0:T(8,128)(2,1)S(1)}, u32[]{:S(2)}, u32[]{:S(2)}) %collective-permute-start.1) | collective-permute-done | bytes 344096 | tf_op jit(solution)/shard_map/ppermute | solution.py:322
  59.8 5.6 %collective-permute-done.4.refs_6_ = bf16[21,64,128]{2,1,0:T(8,128)(2,1)S(1)} collective-permute-done((bf16[21,64,128]{2,1,0:T(8,128)(2,1)}, bf16[21,64,128]{2,1,0:T(8,128)(2,1)S(1)}, u32[]{:S(2)}, u32[]{:S(2)}) %collective-permute-start.4) | collective-permute-done | bytes 344096 | tf_op jit(solution)/shard_map/ppermute | solution.py:322
  66.2 2.9 %add_first.1 = (bf16[21,16,128]{2,1,0:T(8,128)(2,1)}, bf16[21,16,128]{2,1,0:T(8,128)(2,1)}, bf16[21,16,128]{2,1,0:T(8,128)(2,1)}, bf16[21,16,128]{2,1,0:T(8,128)...) custom-call(s32[2]{0:T(128)} %pad_add_fusion.place_ref, ...), custom_call_target="tpu_custom_call" | custom-call | tf_op jit(solution)/shard_map/add_first/pallas_call | solution.py:161
  69.1 2.0 %collective-permute-start.6 = (bf16[21,16,128]{2,1,0:T(8,128)(2,1)}, bf16[21,16,128]{2,1,0:T(8,128)(2,1)S(1)}, u32[]{:S(2)}, u32[]{:S(2)}) collective-permute-start(bf16[21,16,128]{2,1,0:T(8,128)(2,1)} %get-tuple-element.39), channel_id=1, source_target_pairs={{0,4},{1,5},{2,6},{3,7},{4,8},{5,9},{6,10},{7,11},{8,12},{9,13},{1... | collective-permute-start | bytes 258056 | tf_op jit(solution)/shard_map/ppermute | solution.py:322
  74.6 1.9 collective-permute-start.11
  76.6 3.1 %collective-permute-done.9.refs_5_ = bf16[21,16,128]{2,1,0:T(8,128)(2,1)S(1)} collective-permute-done((bf16[21,16,128]{2,1,0:T(8,128)(2,1)}, bf16[21,16,128]{2,1,0:T(8,128)(2,1)S(1)}, u32[]{:S(2)}, u32[]{:S(2)}) %collective-permute-start.9) | collective-permute-done | bytes 86048 | tf_op jit(solution)/shard_map/ppermute | solution.py:322
  80.8 1.9 %add_last.1 = (bf16[22,16,128]{2,1,0:T(8,128)(2,1)}, bf16[21,16,128]{2,1,0:T(8,128)(2,1)}) custom-call(f32[8,128]{1,0:T(8,128)} %get-tuple-element.29.square_ref, bf16[21,16,128]{2,1,0:T(8,128)(2,1)} %get-tuple-element.38.refs_0_, bf16[21,16,128]{2,1,0:T(8,128)(2,1)} %copy-done.20, bf16[21,16,128]{2,1,0:T(8,128)(2,1)} %copy-done.21, ...), custom_call_target="tpu_custom_call" | custom-call | tf_op jit(solution)/shard_map/add_last/pallas_call | solution.py:192
  82.8 1.9 %collective-permute-start.17 = (bf16[21,16,128]{2,1,0:T(8,128)(2,1)}, bf16[21,16,128]{2,1,0:T(8,128)(2,1)S(1)}, u32[]{:S(2)}, u32[]{:S(2)}) collective-permute-start(bf16[21,16,128]{2,1,0:T(8,128)(2,1)} %get-tuple-element.47.refs_4_), channel_id=1, source_target_pairs={{0,3},{1,0},{2,1},{3,2},{4,7},{5,4},{6,5},{7,6},{8,11},{9,8},{10,9... | collective-permute-start | bytes 258056 | tf_op jit(solution)/shard_map/ppermute | solution.py:322
  85.4 1.3 collective-permute-start.13
  87.8 4.0 %collective-permute-done.16.refs_6_ = bf16[21,16,128]{2,1,0:T(8,128)(2,1)S(1)} collective-permute-done((bf16[21,16,128]{2,1,0:T(8,128)(2,1)}, bf16[21,16,128]{2,1,0:T(8,128)(2,1)S(1)}, u32[]{:S(2)}, u32[]{:S(2)}) %collective-permute-start.16) | collective-permute-done | bytes 86048 | tf_op jit(solution)/shard_map/ppermute | solution.py:322
  94.0 2.2 %join.1 = (bf16[22,64,128]{2,1,0:T(8,128)(2,1)}, bf16[21,64,128]{2,1,0:T(8,128)(2,1)}) custom-call(s32[2]{0:T(128)} %pad_add_fusion.place_ref, bf16[22,16,128]{2,1,0:T(8,128)(2,1)} %get-tuple-element.46.refs_0_, bf16[22,16,128]{2,1,0:T(8,128)(2,1)} %copy-done.16, bf16[22,16,128]{2,1,0:T(8,128)(2,1)} %copy-done.15, bf16[22,16,128]{2,1,0:T(8,128)(2,1)} %copy-done.14, ...), custom_call_target="tpu_custom_call" | custom-call | tf_op jit(solution)/shard_map/join/pallas_call | solution.py:212
  96.2 2.7 %collective-permute-start.23 = (bf16[21,64,128]{2,1,0:T(8,128)(2,1)}, bf16[21,64,128]{2,1,0:T(8,128)(2,1)S(1)}, u32[]{:S(2)}, u32[]{:S(2)}) collective-permute-start(bf16[21,64,128]{2,1,0:T(8,128)(2,1)} %get-tuple-element.49.refs_4_), channel_id=1, source_target_pairs={{0,12},{1,13},{2,14},{3,15},{4,0},{5,1},{6,2},{7,3},{8,4},{9,5},{1... | collective-permute-start | bytes 1032200 | tf_op jit(solution)/shard_map/ppermute | solution.py:322
  101.5 2.5 %collective-permute-done.23.refs_7_ = bf16[21,64,128]{2,1,0:T(8,128)(2,1)S(1)} collective-permute-done((bf16[21,64,128]{2,1,0:T(8,128)(2,1)}, bf16[21,64,128]{2,1,0:T(8,128)(2,1)S(1)}, u32[]{:S(2)}, u32[]{:S(2)}) %collective-permute-start.23) | collective-permute-done | bytes 344096 | tf_op jit(solution)/shard_map/ppermute | solution.py:322
  104.1 4.9 %collective-permute-done.22.refs_6_ = bf16[21,64,128]{2,1,0:T(8,128)(2,1)S(1)} collective-permute-done((bf16[21,64,128]{2,1,0:T(8,128)(2,1)}, bf16[21,64,128]{2,1,0:T(8,128)(2,1)S(1)}, u32[]{:S(2)}, u32[]{:S(2)}) %collective-permute-start.22) | collective-permute-done | bytes 344096 | tf_op jit(solution)/shard_map/ppermute | solution.py:322
  108.9 5.3 %collective-permute-done.21.refs_5_ = bf16[21,64,128]{2,1,0:T(8,128)(2,1)S(1)} collective-permute-done((bf16[21,64,128]{2,1,0:T(8,128)(2,1)}, bf16[21,64,128]{2,1,0:T(8,128)(2,1)S(1)}, u32[]{:S(2)}, u32[]{:S(2)}) %collective-permute-start.21) | collective-permute-done | bytes 344096 | tf_op jit(solution)/shard_map/ppermute | solution.py:322
  114.2 2.9 %collective-permute-done.18.refs_1_ = bf16[22,64,128]{2,1,0:T(8,128)(2,1)S(1)} collective-permute-done((bf16[22,64,128]{2,1,0:T(8,128)(2,1)}, bf16[22,64,128]{2,1,0:T(8,128)(2,1)S(1)}, u32[]{:S(2)}, u32[]{:S(2)}) %collective-permute-start.18) | collective-permute-done | bytes 360480 | tf_op jit(solution)/shard_map/ppermute | solution.py:322
  117.8 6.4 %step.1 = bf16[1536,256]{1,0:T(8,128)(2,1)} custom-call(s32[2]{0:T(128)} %pad_add_fusion.place_ref, bf16[1536,256]{1,0:T(8,128)(2,1)} %bitcast.9, bf16[22,64,128]{2,1,0:T(8,128)(2,1)} %get-tuple-element.48.refs_0_, bf16[22,64,128]{2,1,0:T(8,128)(2,1)} %copy-done.4, bf16[22,64,128]{2,1,0:T(8,128)(2,1)} %copy-done.3, bf16[22,64,128]{2,1,0:T(8,128)(2,1)} %copy-done.2, ...), custom_call_target="tpu_custom_call" | custom-call | tf_op jit(solution)/shard_map/step/pallas_call | solution.py:274
  124.2 35.4 %all_to_all.15.back_ref = bf16[16,96,256]{2,1,0:T(8,128)(2,1)} all-to-all(bf16[16,96,256]{2,1,0:T(8,128)(2,1)} %bitcast.10), channel_id=1, replica_groups=mesh['fsdp'=16,'grp'=16] {'fsdp'}, dimensions={0} | all-to-all | bytes 1572864 | tf_op jit(solution)/shard_map/all_to_all | solution.py:354
  159.6 2.7 %deal.1 = (bf16[16,96,256]{2,1,0:T(8,128)(2,1)}, bf16[16,96,256]{2,1,0:T(8,128)(2,1)}) custom-call(s32[4,16]{1,0:T(4,128)} %get-tuple-element.27.table_ref, bf16[16,96,256]{2,1,0:T(8,128)(2,1)} %all_to_all.15.back_ref), custom_call_target="tpu_custom_call" | custom-call | tf_op jit(solution)/shard_map/deal/pallas_call | solution.py:303
  162.3 3.5 %all-to-all-start.2 = ((bf16[16,96,256]{2,1,0:T(8,128)(2,1)}), bf16[16,96,256]{2,1,0:T(8,128)(2,1)S(1)}, u32[]{:S(2)}, u32[]{:S(2)}) async-start(bf16[16,96,256]{2,1,0:T(8,128)(2,1)} %get-tuple-element.51), calls=%async_computation.2 | async-start | bytes 1572864 | tf_op jit(solution)/shard_map/all_to_all | solution.py:358
  165.8 1.3 fusion
  167.8 19.8 %all-to-all-done.2 = bf16[16,96,256]{2,1,0:T(8,128)(2,1)S(1)} async-done(((bf16[16,96,256]{2,1,0:T(8,128)(2,1)}), bf16[16,96,256]{2,1,0:T(8,128)(2,1)S(1)}, u32[]{:S(2)}, u32[]{:S(2)}) %all-to-all-start.2) | async-done | bytes 786464 | tf_op jit(solution)/shard_map/all_to_all | solution.py:358
  187.6 1.3 pad_maximum_fusion
  (84 shorter events, 17.6 us)
Async XLA Ops:
  3.6 32.7 %all-to-all-start = ((bf16[16,96,256]{2,1,0:T(8,128)(2,1)}), bf16[16,96,256]{2,1,0:T(8,128)(2,1)S(1)}, u32[]{:S(2)}, u32[]{:S(2)}) async-start(bf16[16,96,256]{2,1,0:T(8,128)(2,1)} %get-tuple-element.28), calls=%async_computation | async-start | bytes 1572864 | tf_op jit(solution)/shard_map/all_to_all | solution.py:343
  41.3 10.6 %collective-permute-start = (bf16[21,64,128]{2,1,0:T(8,128)(2,1)}, bf16[21,64,128]{2,1,0:T(8,128)(2,1)S(1)}, u32[]{:S(2)}, u32[]{:S(2)}) collective-permute-start(bf16[21,64,128]{2,1,0:T(8,128)(2,1)} %get-tuple-element.31), channel_id=1, source_target_pairs={{0,1},{1,2},{2,3},{3,0},{4,5},{5,6},{6,7},{7,4},{8,9},{9,10},{10,1... | collective-permute-start | bytes 1032200 | tf_op jit(solution)/shard_map/ppermute | solution.py:322
  42.5 17.2 %collective-permute-start.1 = (bf16[21,64,128]{2,1,0:T(8,128)(2,1)}, bf16[21,64,128]{2,1,0:T(8,128)(2,1)S(1)}, u32[]{:S(2)}, u32[]{:S(2)}) collective-permute-start(bf16[21,64,128]{2,1,0:T(8,128)(2,1)} %get-tuple-element.32), channel_id=1, source_target_pairs={{0,2},{1,3},{2,0},{3,1},{4,6},{5,7},{6,4},{7,5},{8,10},{9,11},{10,... | collective-permute-start | bytes 1032200 | tf_op jit(solution)/shard_map/ppermute | solution.py:322
  44.9 14.8 %collective-permute-start.2 = (bf16[21,64,128]{2,1,0:T(8,128)(2,1)}, bf16[21,64,128]{2,1,0:T(8,128)(2,1)S(1)}, u32[]{:S(2)}, u32[]{:S(2)}) collective-permute-start(bf16[21,64,128]{2,1,0:T(8,128)(2,1)} %get-tuple-element.33), channel_id=1, source_target_pairs={{0,3},{1,0},{2,1},{3,2},{4,7},{5,4},{6,5},{7,6},{8,11},{9,8},{10,9... | collective-permute-start | bytes 1032200 | tf_op jit(solution)/shard_map/ppermute | solution.py:322
  46.1 13.6 %collective-permute-start.3 = (bf16[21,64,128]{2,1,0:T(8,128)(2,1)}, bf16[21,64,128]{2,1,0:T(8,128)(2,1)S(1)}, u32[]{:S(2)}, u32[]{:S(2)}) collective-permute-start(bf16[21,64,128]{2,1,0:T(8,128)(2,1)} %get-tuple-element.35), channel_id=1, source_target_pairs={{0,4},{1,5},{2,6},{3,7},{4,8},{5,9},{6,10},{7,11},{8,12},{9,13},{1... | collective-permute-start | bytes 1032200 | tf_op jit(solution)/shard_map/ppermute | solution.py:322
  47.4 18.0 %collective-permute-start.4 = (bf16[21,64,128]{2,1,0:T(8,128)(2,1)}, bf16[21,64,128]{2,1,0:T(8,128)(2,1)S(1)}, u32[]{:S(2)}, u32[]{:S(2)}) collective-permute-start(bf16[21,64,128]{2,1,0:T(8,128)(2,1)} %get-tuple-element.36), channel_id=1, source_target_pairs={{0,8},{1,9},{2,10},{3,11},{4,12},{5,13},{6,14},{7,15},{8,0},{9,1},... | collective-permute-start | bytes 1032200 | tf_op jit(solution)/shard_map/ppermute | solution.py:322
  51.8 13.5 %copy-start.5 = (bf16[21,64,128]{2,1,0:T(8,128)(2,1)}, bf16[21,64,128]{2,1,0:T(8,128)(2,1)S(1)}, u32[]{:S(2)}) copy-start(bf16[21,64,128]{2,1,0:T(8,128)(2,1)S(1)} %collective-permute-done.refs_1_) | copy-start | bytes 1032196
  51.8 13.5 %collective-permute-start.5 = (bf16[21,64,128]{2,1,0:T(8,128)(2,1)}, bf16[21,64,128]{2,1,0:T(8,128)(2,1)S(1)}, u32[]{:S(2)}, u32[]{:S(2)}) collective-permute-start(bf16[21,64,128]{2,1,0:T(8,128)(2,1)} %get-tuple-element.37), channel_id=1, source_target_pairs={{0,12},{1,13},{2,14},{3,15},{4,0},{5,1},{6,2},{7,3},{8,4},{9,5},{1... | collective-permute-start | bytes 1032200 | tf_op jit(solution)/shard_map/ppermute | solution.py:322
  59.7 5.6 %copy-start.8 = (bf16[21,64,128]{2,1,0:T(8,128)(2,1)}, bf16[21,64,128]{2,1,0:T(8,128)(2,1)S(1)}, u32[]{:S(2)}) copy-start(bf16[21,64,128]{2,1,0:T(8,128)(2,1)S(1)} %collective-permute-done.3.refs_5_) | copy-start | bytes 1032196
  69.1 5.5 %collective-permute-start.6 = (bf16[21,16,128]{2,1,0:T(8,128)(2,1)}, bf16[21,16,128]{2,1,0:T(8,128)(2,1)S(1)}, u32[]{:S(2)}, u32[]{:S(2)}) collective-permute-start(bf16[21,16,128]{2,1,0:T(8,128)(2,1)} %get-tuple-element.39), channel_id=1, source_target_pairs={{0,4},{1,5},{2,6},{3,7},{4,8},{5,9},{6,10},{7,11},{8,12},{9,13},{1... | collective-permute-start | bytes 258056 | tf_op jit(solution)/shard_map/ppermute | solution.py:322
  71.1 5.3 %collective-permute-start.7 = (bf16[21,16,128]{2,1,0:T(8,128)(2,1)}, bf16[21,16,128]{2,1,0:T(8,128)(2,1)S(1)}, u32[]{:S(2)}, u32[]{:S(2)}) collective-permute-start(bf16[21,16,128]{2,1,0:T(8,128)(2,1)} %get-tuple-element.40), channel_id=1, source_target_pairs={{0,8},{1,9},{2,10},{3,11},{4,12},{5,13},{6,14},{7,15},{8,0},{9,1},... | collective-permute-start | bytes 258056 | tf_op jit(solution)/shard_map/ppermute | solution.py:322
  72.4 4.2 %collective-permute-start.8 = (bf16[21,16,128]{2,1,0:T(8,128)(2,1)}, bf16[21,16,128]{2,1,0:T(8,128)(2,1)S(1)}, u32[]{:S(2)}, u32[]{:S(2)}) collective-permute-start(bf16[21,16,128]{2,1,0:T(8,128)(2,1)} %get-tuple-element.41), channel_id=1, source_target_pairs={{0,12},{1,13},{2,14},{3,15},{4,0},{5,1},{6,2},{7,3},{8,4},{9,5},{1... | collective-permute-start | bytes 258056 | tf_op jit(solution)/shard_map/ppermute | solution.py:322
  73.7 6.1 %collective-permute-start.9 = (bf16[21,16,128]{2,1,0:T(8,128)(2,1)}, bf16[21,16,128]{2,1,0:T(8,128)(2,1)S(1)}, u32[]{:S(2)}, u32[]{:S(2)}) collective-permute-start(bf16[21,16,128]{2,1,0:T(8,128)(2,1)} %get-tuple-element.43), channel_id=1, source_target_pairs={{0,1},{1,2},{2,3},{3,0},{4,5},{5,6},{6,7},{7,4},{8,9},{9,10},{10,1... | collective-permute-start | bytes 258056 | tf_op jit(solution)/shard_map/ppermute | solution.py:322
  74.0 5.8 %collective-permute-start.10 = (bf16[21,16,128]{2,1,0:T(8,128)(2,1)}, bf16[21,16,128]{2,1,0:T(8,128)(2,1)S(1)}, u32[]{:S(2)}, u32[]{:S(2)}) collective-permute-start(bf16[21,16,128]{2,1,0:T(8,128)(2,1)} %get-tuple-element.44), channel_id=1, source_target_pairs={{0,2},{1,3},{2,0},{3,1},{4,6},{5,7},{6,4},{7,5},{8,10},{9,11},{10,... | collective-permute-start | bytes 258056 | tf_op jit(solution)/shard_map/ppermute | solution.py:322
  74.6 5.7 %copy-start.20 = (bf16[21,16,128]{2,1,0:T(8,128)(2,1)}, bf16[21,16,128]{2,1,0:T(8,128)(2,1)S(1)}, u32[]{:S(2)}) copy-start(bf16[21,16,128]{2,1,0:T(8,128)(2,1)S(1)} %collective-permute-done.6.refs_1_) | copy-start | bytes 258052
  74.6 5.6 %collective-permute-start.11 = (bf16[21,16,128]{2,1,0:T(8,128)(2,1)}, bf16[21,16,128]{2,1,0:T(8,128)(2,1)S(1)}, u32[]{:S(2)}, u32[]{:S(2)}) collective-permute-start(bf16[21,16,128]{2,1,0:T(8,128)(2,1)} %get-tuple-element.45), channel_id=1, source_target_pairs={{0,3},{1,0},{2,1},{3,2},{4,7},{5,4},{6,5},{7,6},{8,11},{9,8},{10,9... | collective-permute-start | bytes 258056 | tf_op jit(solution)/shard_map/ppermute | solution.py:322
  82.8 5.0 %collective-permute-start.17 = (bf16[21,16,128]{2,1,0:T(8,128)(2,1)}, bf16[21,16,128]{2,1,0:T(8,128)(2,1)S(1)}, u32[]{:S(2)}, u32[]{:S(2)}) collective-permute-start(bf16[21,16,128]{2,1,0:T(8,128)(2,1)} %get-tuple-element.47.refs_4_), channel_id=1, source_target_pairs={{0,3},{1,0},{2,1},{3,2},{4,7},{5,4},{6,5},{7,6},{8,11},{9,8},{10,9... | collective-permute-start | bytes 258056 | tf_op jit(solution)/shard_map/ppermute | solution.py:322
  84.7 8.0 %collective-permute-start.14 = (bf16[22,16,128]{2,1,0:T(8,128)(2,1)}, bf16[22,16,128]{2,1,0:T(8,128)(2,1)S(1)}, u32[]{:S(2)}, u32[]{:S(2)}) collective-permute-start(bf16[22,16,128]{2,1,0:T(8,128)(2,1)} %get-tuple-element.46.refs_0_), channel_id=1, source_target_pairs={{0,12},{1,13},{2,14},{3,15},{4,0},{5,1},{6,2},{7,3},{8,4},{9,5},{1... | collective-permute-start | bytes 270344 | tf_op jit(solution)/shard_map/ppermute | solution.py:322
  85.4 7.3 %collective-permute-start.13 = (bf16[22,16,128]{2,1,0:T(8,128)(2,1)}, bf16[22,16,128]{2,1,0:T(8,128)(2,1)S(1)}, u32[]{:S(2)}, u32[]{:S(2)}) collective-permute-start(bf16[22,16,128]{2,1,0:T(8,128)(2,1)} %get-tuple-element.46.refs_0_), channel_id=1, source_target_pairs={{0,8},{1,9},{2,10},{3,11},{4,12},{5,13},{6,14},{7,15},{8,0},{9,1},... | collective-permute-start | bytes 270344 | tf_op jit(solution)/shard_map/ppermute | solution.py:322
  86.7 6.0 %collective-permute-start.12 = (bf16[22,16,128]{2,1,0:T(8,128)(2,1)}, bf16[22,16,128]{2,1,0:T(8,128)(2,1)S(1)}, u32[]{:S(2)}, u32[]{:S(2)}) collective-permute-start(bf16[22,16,128]{2,1,0:T(8,128)(2,1)} %get-tuple-element.46.refs_0_), channel_id=1, source_target_pairs={{0,4},{1,5},{2,6},{3,7},{4,8},{5,9},{6,10},{7,11},{8,12},{9,13},{1... | collective-permute-start | bytes 270344 | tf_op jit(solution)/shard_map/ppermute | solution.py:322
  86.7 5.1 %collective-permute-start.16 = (bf16[21,16,128]{2,1,0:T(8,128)(2,1)}, bf16[21,16,128]{2,1,0:T(8,128)(2,1)S(1)}, u32[]{:S(2)}, u32[]{:S(2)}) collective-permute-start(bf16[21,16,128]{2,1,0:T(8,128)(2,1)} %get-tuple-element.47.refs_4_), channel_id=1, source_target_pairs={{0,2},{1,3},{2,0},{3,1},{4,6},{5,7},{6,4},{7,5},{8,10},{9,11},{10,... | collective-permute-start | bytes 258056 | tf_op jit(solution)/shard_map/ppermute | solution.py:322
  87.8 4.9 %collective-permute-start.15 = (bf16[21,16,128]{2,1,0:T(8,128)(2,1)}, bf16[21,16,128]{2,1,0:T(8,128)(2,1)S(1)}, u32[]{:S(2)}, u32[]{:S(2)}) collective-permute-start(bf16[21,16,128]{2,1,0:T(8,128)(2,1)} %get-tuple-element.47.refs_4_), channel_id=1, source_target_pairs={{0,1},{1,2},{2,3},{3,0},{4,5},{5,6},{6,7},{7,4},{8,9},{9,10},{10,1... | collective-permute-start | bytes 258056 | tf_op jit(solution)/shard_map/ppermute | solution.py:322
  96.2 7.9 %collective-permute-start.23 = (bf16[21,64,128]{2,1,0:T(8,128)(2,1)}, bf16[21,64,128]{2,1,0:T(8,128)(2,1)S(1)}, u32[]{:S(2)}, u32[]{:S(2)}) collective-permute-start(bf16[21,64,128]{2,1,0:T(8,128)(2,1)} %get-tuple-element.49.refs_4_), channel_id=1, source_target_pairs={{0,12},{1,13},{2,14},{3,15},{4,0},{5,1},{6,2},{7,3},{8,4},{9,5},{1... | collective-permute-start | bytes 1032200 | tf_op jit(solution)/shard_map/ppermute | solution.py:322
  98.8 15.4 %collective-permute-start.20 = (bf16[22,64,128]{2,1,0:T(8,128)(2,1)}, bf16[22,64,128]{2,1,0:T(8,128)(2,1)S(1)}, u32[]{:S(2)}, u32[]{:S(2)}) collective-permute-start(bf16[22,64,128]{2,1,0:T(8,128)(2,1)} %get-tuple-element.48.refs_0_), channel_id=1, source_target_pairs={{0,3},{1,0},{2,1},{3,2},{4,7},{5,4},{6,5},{7,6},{8,11},{9,8},{10,9... | collective-permute-start | bytes 1081352 | tf_op jit(solution)/shard_map/ppermute | solution.py:322
  99.4 14.8 %collective-permute-start.19 = (bf16[22,64,128]{2,1,0:T(8,128)(2,1)}, bf16[22,64,128]{2,1,0:T(8,128)(2,1)S(1)}, u32[]{:S(2)}, u32[]{:S(2)}) collective-permute-start(bf16[22,64,128]{2,1,0:T(8,128)(2,1)} %get-tuple-element.48.refs_0_), channel_id=1, source_target_pairs={{0,2},{1,3},{2,0},{3,1},{4,6},{5,7},{6,4},{7,5},{8,10},{9,11},{10,... | collective-permute-start | bytes 1081352 | tf_op jit(solution)/shard_map/ppermute | solution.py:322
  100.5 16.6 %collective-permute-start.18 = (bf16[22,64,128]{2,1,0:T(8,128)(2,1)}, bf16[22,64,128]{2,1,0:T(8,128)(2,1)S(1)}, u32[]{:S(2)}, u32[]{:S(2)}) collective-permute-start(bf16[22,64,128]{2,1,0:T(8,128)(2,1)} %get-tuple-element.48.refs_0_), channel_id=1, source_target_pairs={{0,1},{1,2},{2,3},{3,0},{4,5},{5,6},{6,7},{7,4},{8,9},{9,10},{10,1... | collective-permute-start | bytes 1081352 | tf_op jit(solution)/shard_map/ppermute | solution.py:322
  101.0 7.9 %collective-permute-start.22 = (bf16[21,64,128]{2,1,0:T(8,128)(2,1)}, bf16[21,64,128]{2,1,0:T(8,128)(2,1)S(1)}, u32[]{:S(2)}, u32[]{:S(2)}) collective-permute-start(bf16[21,64,128]{2,1,0:T(8,128)(2,1)} %get-tuple-element.49.refs_4_), channel_id=1, source_target_pairs={{0,8},{1,9},{2,10},{3,11},{4,12},{5,13},{6,14},{7,15},{8,0},{9,1},... | collective-permute-start | bytes 1032200 | tf_op jit(solution)/shard_map/ppermute | solution.py:322
  104.0 13.0 %copy-start.11 = (bf16[21,64,128]{2,1,0:T(8,128)(2,1)}, bf16[21,64,128]{2,1,0:T(8,128)(2,1)S(1)}, u32[]{:S(2)}) copy-start(bf16[21,64,128]{2,1,0:T(8,128)(2,1)S(1)} %collective-permute-done.23.refs_7_) | copy-start | bytes 1032196
  104.0 10.1 %collective-permute-start.21 = (bf16[21,64,128]{2,1,0:T(8,128)(2,1)}, bf16[21,64,128]{2,1,0:T(8,128)(2,1)S(1)}, u32[]{:S(2)}, u32[]{:S(2)}) collective-permute-start(bf16[21,64,128]{2,1,0:T(8,128)(2,1)} %get-tuple-element.49.refs_4_), channel_id=1, source_target_pairs={{0,4},{1,5},{2,6},{3,7},{4,8},{5,9},{6,10},{7,11},{8,12},{9,13},{1... | collective-permute-start | bytes 1032200 | tf_op jit(solution)/shard_map/ppermute | solution.py:322
  108.9 8.2 %copy-start.12 = (bf16[21,64,128]{2,1,0:T(8,128)(2,1)}, bf16[21,64,128]{2,1,0:T(8,128)(2,1)S(1)}, u32[]{:S(2)}) copy-start(bf16[21,64,128]{2,1,0:T(8,128)(2,1)S(1)} %collective-permute-done.22.refs_6_) | copy-start | bytes 1032196
  159.6 7.5 %copy-start.1 = (bf16[1536,256]{1,0:T(8,128)(2,1)S(1)}, bf16[1536,256]{1,0:T(8,128)(2,1)}, u32[]{:S(2)}) copy-start(bf16[1536,256]{1,0:T(8,128)(2,1)} %step.1) | copy-start | bytes 2359300
  162.3 25.3 %all-to-all-start.2 = ((bf16[16,96,256]{2,1,0:T(8,128)(2,1)}), bf16[16,96,256]{2,1,0:T(8,128)(2,1)S(1)}, u32[]{:S(2)}, u32[]{:S(2)}) async-start(bf16[16,96,256]{2,1,0:T(8,128)(2,1)} %get-tuple-element.51), calls=%async_computation.2 | async-start | bytes 1572864 | tf_op jit(solution)/shard_map/all_to_all | solution.py:358
  (20 other events, 41.0 us)

commit v2 on v1

v2 whole, which is shorter than its diff:
```python
import functools
import math

import jax
import jax.numpy as jnp
from jax import lax
from jax.experimental import pallas as pl
from jax.experimental.pallas import tpu as pltpu
from jax.sharding import PartitionSpec as P

MOST = 2
SIDE = 4
BLOCK = 256
PIECE = BLOCK // SIDE
SUB = PIECE // SIDE
VMEM_LIMIT = 56 * 1024 * 1024

VMEM = pl.BlockSpec(memory_space=pltpu.VMEM)
SMEM = pl.BlockSpec(memory_space=pltpu.SMEM)


def params():
    return pltpu.CompilerParams(vmem_limit_bytes=VMEM_LIMIT)


def shape_of(*dims, dtype=jnp.bfloat16):
    return jax.ShapeDtypeStruct(dims, dtype)


def part(at, size):
    return pl.ds(pl.multiple_of(lax.rem(at, SIDE) * size, size), size)


def pairs_of(rows):
    side = rows // BLOCK
    return [(i, j) for i in range(side) for j in range(i + 1)]


def plan_kernel(owner_ref, grads_ref, table_ref, packed_ref, empty_ref):
    count = owner_ref.shape[0]

    def clear(g, _):
        table_ref[2, g] = -1
        table_ref[3, g] = 0
        return 0

    lax.fori_loop(0, count, clear, 0)

    def first(e, _):
        g = owner_ref[e]
        seen = table_ref[3, g]
        table_ref[3, g] = seen + 1

        @pl.when(seen == 0)
        def _():
            table_ref[0, g] = e
            table_ref[1, e] = g

        @pl.when(seen > 0)
        def _():
            table_ref[2, g] = e

        return 0

    lax.fori_loop(0, count, first, 0)

    def empties(g, n):
        none = table_ref[3, g] == 0

        @pl.when(none)
        def _():
            empty_ref[n] = g

        return n + none.astype(jnp.int32)

    lax.fori_loop(0, count, empties, 0)

    def second(g, n):
        e = table_ref[2, g]
        two = e >= 0

        @pl.when(two)
        def _():
            h = empty_ref[n]
            table_ref[2, g] = h
            table_ref[0, h] = e
            table_ref[1, e] = h

        return n + two.astype(jnp.int32)

    lax.fori_loop(0, count, second, 0)

    def move(g, _):
        packed_ref[g] = grads_ref[table_ref[0, g]]
        return 0

    lax.fori_loop(0, count, move, 0)


def plan(owner, grads):
    count = grads.shape[0]
    return pl.pallas_call(
        plan_kernel,
        out_shape=(shape_of(4, count, dtype=jnp.int32), shape_of(*grads.shape)),
        in_specs=[SMEM, VMEM],
        out_specs=(SMEM, VMEM),
        scratch_shapes=[pltpu.SMEM((count,), jnp.int32)],
        compiler_params=params(),
        name="plan",
    )(owner, grads)


def gram_kernel(pairs, place_ref, x_ref, *refs):
    outs, square_ref, full = refs[:SIDE], refs[SIDE], refs[SIDE + 1]
    for t, (i, j) in enumerate(pairs):
        full[t] = lax.dot_general(
            x_ref[i * BLOCK : (i + 1) * BLOCK, :],
            x_ref[j * BLOCK : (j + 1) * BLOCK, :],
            (((1,), (1,)), ((), ())),
            preferred_element_type=jnp.float32,
        ).astype(jnp.bfloat16)
        for s in range(SIDE):
            outs[s][t] = full[t, part(place_ref[0] + s, PIECE), :]
    total = jnp.zeros((1, x_ref.shape[1]), jnp.float32)
    for i in range(x_ref.shape[0] // BLOCK):
        values = x_ref[i * BLOCK : (i + 1) * BLOCK, :].astype(jnp.float32)
        total = total + jnp.sum(values * values, axis=0, keepdims=True)
    total = jnp.sum(total, axis=1, keepdims=True)
    square_ref[...] = jnp.broadcast_to(total, square_ref.shape)


def gram_terms(place, x):
    pairs = pairs_of(x.shape[0])
    return pl.pallas_call(
        functools.partial(gram_kernel, pairs),
        out_shape=(shape_of(len(pairs), PIECE, BLOCK),) * SIDE
        + (shape_of(8, BLOCK, dtype=jnp.float32),),
        in_specs=[SMEM, VMEM],
        out_specs=(VMEM,) * (SIDE + 1),
        scratch_shapes=[pltpu.VMEM((len(pairs), BLOCK, BLOCK), jnp.bfloat16)],
        compiler_params=params(),
        name="gram",
    )(place, x)


def add_kernel(place_ref, *refs):
    ins, outs = refs[:SIDE], refs[SIDE:]
    for s in range(SIDE):
        rows = part(place_ref[1] + s, SUB)
        total = ins[0][:, rows, :].astype(jnp.float32)
        for other in ins[1:]:
            total = total + other[:, rows, :].astype(jnp.float32)
        outs[s][...] = total.astype(jnp.bfloat16)


def add_first(place, pieces):
    blocks = pieces[0].shape[0]
    return pl.pallas_call(
        add_kernel,
        out_shape=(shape_of(blocks, SUB, BLOCK),) * SIDE,
        in_specs=[SMEM] + [VMEM] * SIDE,
        out_specs=(VMEM,) * SIDE,
        compiler_params=params(),
        name="add_first",
    )(place, *pieces)


def add_last_kernel(square_ref, *refs):
    ins, out = refs[:SIDE], refs[SIDE]
    blocks = ins[0].shape[0]
    total = ins[0][...].astype(jnp.float32)
    for other in ins[1:]:
        total = total + other[...].astype(jnp.float32)
    out[:blocks] = total.astype(jnp.bfloat16)
    rest = jnp.broadcast_to(square_ref[0:1, :], (SUB, BLOCK))
    row = lax.broadcasted_iota(jnp.int32, (SUB, BLOCK), 0)
    parts = jnp.zeros((SUB, BLOCK), jnp.float32)
    for k in range(3):
        top = lax.reduce_precision(rest, 8, 7)
        parts = jnp.where(row == k, top, parts)
        rest = rest - top
    out[blocks] = parts.astype(jnp.bfloat16)


def add_last(square, pieces):
    blocks = pieces[0].shape[0]
    return pl.pallas_call(
        add_last_kernel,
        out_shape=shape_of(blocks + 1, SUB, BLOCK),
        in_specs=[VMEM] * (SIDE + 1),
        out_specs=VMEM,
        compiler_params=params(),
        name="add_last",
    )(square, *pieces)


def join_kernel(place_ref, *refs):
    ins, out = refs[:SIDE], refs[SIDE]
    for s in range(SIDE):
        out[:, part(place_ref[1] - s + SIDE, SUB), :] = ins[s][...]


def join(place, parts):
    return pl.pallas_call(
        join_kernel,
        out_shape=shape_of(parts[0].shape[0], PIECE, BLOCK),
        in_specs=[SMEM] + [VMEM] * SIDE,
        out_specs=VMEM,
        compiler_params=params(),
        name="join",
    )(place, *parts)


def step_kernel(pairs, rows_all, factor, place_ref, x_ref, *refs):
    ins = refs[:SIDE]
    out_ref, gram, normed, left = refs[SIDE:]
    blocks = len(pairs)
    total = jnp.zeros((1, BLOCK), jnp.float32)
    for s in range(SIDE):
        total = total + jnp.sum(ins[s][blocks].astype(jnp.float32), axis=0, keepdims=True)
    inverse = 1.0 / jnp.sqrt(total / rows_all + 1e-06)
    scale = inverse * inverse
    side = rows_all // BLOCK
    for i in range(side):
        rows = slice(i * BLOCK, (i + 1) * BLOCK)
        normed[rows, :] = (x_ref[rows, :].astype(jnp.float32) * inverse).astype(jnp.bfloat16)
    for t, (i, j) in enumerate(pairs):
        for s in range(SIDE):
            p = lax.rem(place_ref[0] - s + SIDE, SIDE)
            rows = pl.ds(pl.multiple_of(i * BLOCK + p * PIECE, PIECE), PIECE)
            values = ins[s][t].astype(jnp.float32) * scale
            gram[rows, j * BLOCK : (j + 1) * BLOCK] = jnp.where(scale > 0, values, 0.0).astype(
                jnp.bfloat16
            )
    for i, j in pairs:
        if i != j:
            block = gram[i * BLOCK : (i + 1) * BLOCK, j * BLOCK : (j + 1) * BLOCK]
            gram[j * BLOCK : (j + 1) * BLOCK, i * BLOCK : (i + 1) * BLOCK] = block.T
    for i in range(side):
        rows = slice(i * BLOCK, (i + 1) * BLOCK)
        left[rows, :] = jnp.dot(
            gram[rows, :], normed[...], preferred_element_type=jnp.float32
        ).astype(jnp.bfloat16)
    for i in range(side):
        rows = slice(i * BLOCK, (i + 1) * BLOCK)
        right = jnp.dot(gram[rows, :], left[...], preferred_element_type=jnp.float32)
        mixed = (
            3.4445 * normed[rows, :].astype(jnp.float32)
            - 4.775 * left[rows, :].astype(jnp.float32)
            + 2.0315 * right
        )
        out_ref[rows, :] = (factor * mixed).astype(jnp.bfloat16)


def step(place, x, pieces, factor):
    rows, cols = x.shape
    pairs = pairs_of(rows)
    return pl.pallas_call(
        functools.partial(step_kernel, pairs, rows, factor),
        out_shape=shape_of(rows, cols),
        in_specs=[SMEM, VMEM] + [VMEM] * SIDE,
        out_specs=VMEM,
        scratch_shapes=[
            pltpu.VMEM((rows, rows), jnp.bfloat16),
            pltpu.VMEM((rows, cols), jnp.bfloat16),
            pltpu.VMEM((rows, cols), jnp.bfloat16),
        ],
        compiler_params=params(),
        name="step",
    )(place, x, *pieces)


def deal_kernel(table_ref, back_ref, update_ref, second_ref):
    count = back_ref.shape[0]

    def move(e, _):
        update_ref[e] = back_ref[table_ref[1, e]]
        helper = table_ref[2, e]
        block = back_ref[jnp.maximum(helper, 0)]
        second_ref[e] = jnp.where(helper >= 0, block, jnp.zeros_like(block))
        return 0

    lax.fori_loop(0, count, move, 0)


def deal(table, back):
    return pl.pallas_call(
        deal_kernel,
        out_shape=(shape_of(*back.shape),) * 2,
        in_specs=[SMEM, VMEM],
        out_specs=(VMEM,) * 2,
        compiler_params=params(),
        name="deal",
    )(table, back)


def spread(send, order):
    groups, places = lax.axis_size("fsdp"), SIDE * SIDE
    got = [send[0]]
    for amount in range(1, SIDE):
        moves = []
        for at in range(groups * places):
            group, place = divmod(at, places)
            y, x = divmod(place, SIDE)
            if group % 2 == order:
                x = (x + amount) % SIDE
            else:
                y = (y + amount) % SIDE
            moves.append((at, group * places + y * SIDE + x))
        got.append(lax.ppermute(send[amount], ("fsdp", "grp"), moves))
    return got


def on_device(grads, owner):
    count, rows_dev, cols_dev = grads.shape
    groups = lax.axis_size("fsdp")
    rows = rows_dev * groups
    cols = cols_dev * lax.axis_size("grp")
    factor = 0.2 * math.sqrt(max(rows, cols))
    at = lax.axis_index("grp")
    me = lax.axis_index("fsdp")
    along = jnp.stack([lax.rem(at, SIDE), lax.div(at, SIDE)]).astype(jnp.int32)
    place = jnp.where(lax.rem(me, 2) == 0, along, along[::-1])
    table, packed = plan(owner, grads)
    x = lax.all_to_all(packed, "fsdp", split_axis=0, concat_axis=0, tiled=True)
    x = x.reshape(rows, cols_dev)
    *terms, square = gram_terms(place, x)
    parts = add_first(place, spread(terms, 0))
    own = add_last(square, spread(parts, 1))
    own = join(place, spread([own] * SIDE, 1))
    done = step(place, x, spread([own] * SIDE, 0), factor)
    back = lax.all_to_all(
        done.reshape(count, rows_dev, cols_dev), "fsdp", split_axis=0, concat_axis=0, tiled=True
    )
    update, second = deal(table, back)
    second = lax.all_to_all(second, "fsdp", split_axis=0, concat_axis=0, tiled=True)
    first = jnp.where(table[3, me] > 0, done, jnp.zeros_like(done))
    owned = jnp.stack([first, second.reshape(rows, cols_dev)], axis=0)
    return (update, owned)


def solution(mesh):
    return jax.shard_map(
        on_device,
        mesh=mesh,
        in_specs=(P(None, "fsdp", "grp"), P()),
        out_specs=(P(None, "fsdp", "grp"), P("fsdp", None, "grp")),
        check_vma=False,
    )
```

time: 189 us -> 180 us (0.952)
  starting transfers between devices: 42.6 us -> 29.3 us
  waiting for transfers between devices: 78.6 us -> 86 us
  blocking collectives: 35.4 us -> 31.7 us
    ppermute x24 -> x12, starting transfers between devices: 29.1 us -> 15.8 us  [spread(): got.append(lax.ppermute(send[amount], ('fsdp', 'grp'), moves))]
    ppermute x24 -> x12, waiting for transfers between devices: 36.7 us -> 44.2 us  [spread(): got.append(lax.ppermute(send[amount], ('fsdp', 'grp'), moves))]
    all_to_all x1, blocking collectives: 35.4 us -> 31.7 us  [on_device(): lax.all_to_all(done.reshape(count, rows_dev, cols_dev), 'fsdp', split_axi...]
    unnamed x52 -> x28, local copies, waits for them, and re-layouts: 4.4 us -> 4.3 us
  transfers between devices with their start and end apart: 26 -> 14, of which waited for: 14 -> 11; matrix products, arithmetic and copies ran while one was open for 1% -> 2% of each run, Pallas kernels for 0% -> 0%
where the time goes in v2:
time: 180 us; the launch traced here: 179 us
  waiting for transfers between devices  86 us (48%)
  blocking collectives  31.7 us (18%)
  starting transfers between devices  29.3 us (16%)
  Pallas kernels  22.9 us (13%)
  local copies, waits for them, and re-layouts  4.4 us (2%)
  other arithmetic  4.08 us (2%)
    ppermute x12, waiting for transfers between devices, spread(): got.append(lax.ppermute(send[amount], ('fsdp', 'grp'), moves))  44.2 us
    all_to_all x1, blocking collectives, on_device(): lax.all_to_all(done.reshape(count, rows_dev, cols_dev), 'fsdp', split_axi...  31.7 us
    all_to_all x1, waiting for transfers between devices, on_device(): x = lax.all_to_all(packed, 'fsdp', split_axis=0, concat_axis=0, tiled=True)  21.8 us
    all_to_all x1, waiting for transfers between devices, on_device(): lax.all_to_all(second, 'fsdp', split_axis=0, concat_axis=0, tiled=True)  19.9 us
    ppermute x12, starting transfers between devices, spread(): got.append(lax.ppermute(send[amount], ('fsdp', 'grp'), moves))  15.8 us
    all_to_all x1, starting transfers between devices, on_device(): x = lax.all_to_all(packed, 'fsdp', split_axis=0, concat_axis=0, tiled=True)  9.99 us
    pallas_call x1, Pallas kernels, step(): pl.pallas_call(functools.partial(step_kernel, pairs, rows, factor), out_s...  6.58 us
    unnamed x28, local copies, waits for them, and re-layouts  4.3 us
  transfers between devices with their start and end apart: 14, of which 11 were waited for; matrix products, arithmetic and copies ran while one was open for 2% of the time, Pallas kernels for 0%

profile of v2, /device:TPU:1, one launch (start us, length us, event | category | flops | bytes accessed | tf_op | source)
XLA Modules:
  0.0 179.0 jit_solution(16769694269456000569)
XLA Ops:
  0.6 3.0 %plan.1 = (s32[4,16]{1,0:T(4,128)}, bf16[16,96,256]{2,1,0:T(8,128)(2,1)}) custom-call(s32[16]{0:T(128)} %owner_ref.1, bf16[16,96,256]{2,1,0:T(8,128)(2,1)} %grads_ref.1), custom_call_target="tpu_custom_call" | custom-call | tf_op jit(solution)/shard_map/plan/pallas_call | solution.py:102
  3.6 10.0 %all-to-all-start = ((bf16[16,96,256]{2,1,0:T(8,128)(2,1)}), bf16[16,96,256]{2,1,0:T(8,128)(2,1)S(1)}, u32[]{:S(2)}, u32[]{:S(2)}) async-start(bf16[16,96,256]{2,1,0:T(8,128)(2,1)} %get-tuple-element.16), calls=%async_computation | async-start | bytes 1572864 | tf_op jit(solution)/shard_map/all_to_all | solution.py:325
  14.4 21.8 %all-to-all-done = bf16[16,96,256]{2,1,0:T(8,128)(2,1)S(1)} async-done(((bf16[16,96,256]{2,1,0:T(8,128)(2,1)}), bf16[16,96,256]{2,1,0:T(8,128)(2,1)S(1)}, u32[]{:S(2)}, u32[]{:S(2)}) %all-to-all-start) | async-done | bytes 786464 | tf_op jit(solution)/shard_map/all_to_all | solution.py:325
  37.1 3.7 %gram.1 = (bf16[21,64,256]{2,1,0:T(8,128)(2,1)}, bf16[21,64,256]{2,1,0:T(8,128)(2,1)}, bf16[21,64,256]{2,1,0:T(8,128)(2,1)}, bf16[21,64,256]{2,1,0:T(8,128)(2,1)}, f32[8,256]{1,0:T(8,128)}) custom-call(s32[2]{0:T(128)} %broadcast_select_fusion.place_ref, bf16[1536,256]{1,0:T(8,128)(2,1)} %bitcast.8), custom_call_target="tpu_custom_call" | custom-call | tf_op jit(solution)/shard_map/gram/pallas_call | solution.py:134
  40.9 1.3 collective-permute-start
  42.2 2.6 %collective-permute-start.1 = (bf16[21,64,256]{2,1,0:T(8,128)(2,1)}, bf16[21,64,256]{2,1,0:T(8,128)(2,1)S(1)}, u32[]{:S(2)}, u32[]{:S(2)}) collective-permute-start(bf16[21,64,256]{2,1,0:T(8,128)(2,1)} %get-tuple-element.20), channel_id=1, source_target_pairs={{0,2},{1,3},{2,0},{3,1},{4,6},{5,7},{6,4},{7,5},{8,10},{9,11},{10,... | collective-permute-start | bytes 2064392 | tf_op jit(solution)/shard_map/ppermute | solution.py:310
  44.8 1.1 collective-permute-start.2
  45.9 6.6 %collective-permute-done.refs_1_ = bf16[21,64,256]{2,1,0:T(8,128)(2,1)S(1)} collective-permute-done((bf16[21,64,256]{2,1,0:T(8,128)(2,1)}, bf16[21,64,256]{2,1,0:T(8,128)(2,1)S(1)}, u32[]{:S(2)}, u32[]{:S(2)}) %collective-permute-start) | collective-permute-done | bytes 688160 | tf_op jit(solution)/shard_map/ppermute | solution.py:310
  52.4 8.3 %collective-permute-done.1.refs_2_ = bf16[21,64,256]{2,1,0:T(8,128)(2,1)S(1)} collective-permute-done((bf16[21,64,256]{2,1,0:T(8,128)(2,1)}, bf16[21,64,256]{2,1,0:T(8,128)(2,1)S(1)}, u32[]{:S(2)}, u32[]{:S(2)}) %collective-permute-start.1) | collective-permute-done | bytes 688160 | tf_op jit(solution)/shard_map/ppermute | solution.py:310
  61.8 2.9 %add_first.1 = (bf16[21,16,256]{2,1,0:T(8,128)(2,1)}, bf16[21,16,256]{2,1,0:T(8,128)(2,1)}, bf16[21,16,256]{2,1,0:T(8,128)(2,1)}, bf16[21,16,256]{2,1,0:T(8,128)(2,1)}) custom-call(s32[2]{0:T(128)} %broadcast_select_fusion.place_ref, bf16[21,64,256]{2,1,0:T(8,128)(2,1)} %get-tuple-element.18.refs_0_, bf16[21,64,256]{2,1,0:T(8,128)(2,1)} %copy-done.5, ...), custom_call_target="tpu_custom_call" | custom-call | tf_op jit(solution)/shard_map/add_first/pallas_call | solution.py:158
  64.7 1.2 collective-permute-start.3
  65.9 2.5 %collective-permute-start.4 = (bf16[21,16,256]{2,1,0:T(8,128)(2,1)}, bf16[21,16,256]{2,1,0:T(8,128)(2,1)S(1)}, u32[]{:S(2)}, u32[]{:S(2)}) collective-permute-start(bf16[21,16,256]{2,1,0:T(8,128)(2,1)} %get-tuple-element.24), channel_id=1, source_target_pairs={{0,8},{1,9},{2,10},{3,11},{4,12},{5,13},{6,14},{7,15},{8,0},{9,1},... | collective-permute-start | bytes 516104 | tf_op jit(solution)/shard_map/ppermute | solution.py:310
  68.3 1.1 collective-permute-start.5
  70.4 2.9 %collective-permute-done.4.refs_2_ = bf16[21,16,256]{2,1,0:T(8,128)(2,1)S(1)} collective-permute-done((bf16[21,16,256]{2,1,0:T(8,128)(2,1)}, bf16[21,16,256]{2,1,0:T(8,128)(2,1)S(1)}, u32[]{:S(2)}, u32[]{:S(2)}) %collective-permute-start.4) | collective-permute-done | bytes 172064 | tf_op jit(solution)/shard_map/ppermute | solution.py:310
  73.9 2.0 %add_last.1.refs_0_ = bf16[22,16,256]{2,1,0:T(8,128)(2,1)} custom-call(f32[8,256]{1,0:T(8,128)} %get-tuple-element.17.square_ref, bf16[21,16,256]{2,1,0:T(8,128)(2,1)} %get-tuple-element.22.refs_0_, bf16[21,16,256]{2,1,0:T(8,128)(2,1)} %copy-done.11, bf16[21,16,256]{2,1,0:T(8,128)(2,1)} %copy-done.12, bf16[21,16,256]{2,1,0:T(8,128)(2,1)} %copy-done.13), custom_call_target="tpu_custom_call" | custom-call | tf_op jit(solution)/shard_map/add_last/pallas_call | solution.py:187
  75.9 1.9 %collective-permute-start.8 = (bf16[22,16,256]{2,1,0:T(8,128)(2,1)}, bf16[22,16,256]{2,1,0:T(8,128)(2,1)S(1)}, u32[]{:S(2)}, u32[]{:S(2)}) collective-permute-start(bf16[22,16,256]{2,1,0:T(8,128)(2,1)} %add_last.1.refs_0_), channel_id=1, source_target_pairs={{0,12},{1,13},{2,14},{3,15},{4,0},{5,1},{6,2},{7,3},{8,4},{9,5},{1... | collective-permute-start | bytes 540680 | tf_op jit(solution)/shard_map/ppermute | solution.py:310
  77.8 1.1 collective-permute-start.7
  79.3 3.3 %collective-permute-done.8.refs_3_ = bf16[22,16,256]{2,1,0:T(8,128)(2,1)S(1)} collective-permute-done((bf16[22,16,256]{2,1,0:T(8,128)(2,1)}, bf16[22,16,256]{2,1,0:T(8,128)(2,1)S(1)}, u32[]{:S(2)}, u32[]{:S(2)}) %collective-permute-start.8) | collective-permute-done | bytes 180256 | tf_op jit(solution)/shard_map/ppermute | solution.py:310
  82.6 1.6 collective-permute-done.7.refs_2_
  84.2 1.9 %collective-permute-done.6.refs_1_ = bf16[22,16,256]{2,1,0:T(8,128)(2,1)S(1)} collective-permute-done((bf16[22,16,256]{2,1,0:T(8,128)(2,1)}, bf16[22,16,256]{2,1,0:T(8,128)(2,1)S(1)}, u32[]{:S(2)}, u32[]{:S(2)}) %collective-permute-start.6) | collective-permute-done | bytes 180256 | tf_op jit(solution)/shard_map/ppermute | solution.py:310
  86.8 2.1 %join.1.refs_0_ = bf16[22,64,256]{2,1,0:T(8,128)(2,1)} custom-call(s32[2]{0:T(128)} %broadcast_select_fusion.place_ref, bf16[22,16,256]{2,1,0:T(8,128)(2,1)} %add_last.1.refs_0_, bf16[22,16,256]{2,1,0:T(8,128)(2,1)} %copy-done.10, bf16[22,16,256]{2,1,0:T(8,128)(2,1)} %copy-done.9, bf16[22,16,256]{2,1,0:T(8,128)(2,1)} %copy-done.8), custom_call_target="tpu_custom_call" | custom-call | tf_op jit(solution)/shard_map/join/pallas_call | solution.py:204
  88.9 1.5 collective-permute-start.11
  91.5 15.2 %collective-permute-done.11.refs_3_ = bf16[22,64,256]{2,1,0:T(8,128)(2,1)S(1)} collective-permute-done((bf16[22,64,256]{2,1,0:T(8,128)(2,1)}, bf16[22,64,256]{2,1,0:T(8,128)(2,1)S(1)}, u32[]{:S(2)}, u32[]{:S(2)}) %collective-permute-start.11) | collective-permute-done | bytes 720928 | tf_op jit(solution)/shard_map/ppermute | solution.py:310
  106.7 3.6 %collective-permute-done.9.refs_1_ = bf16[22,64,256]{2,1,0:T(8,128)(2,1)S(1)} collective-permute-done((bf16[22,64,256]{2,1,0:T(8,128)(2,1)}, bf16[22,64,256]{2,1,0:T(8,128)(2,1)S(1)}, u32[]{:S(2)}, u32[]{:S(2)}) %collective-permute-start.9) | collective-permute-done | bytes 720928 | tf_op jit(solution)/shard_map/ppermute | solution.py:310
  110.3 0.9 copy-done.4
  111.2 6.6 %step.1 = bf16[1536,256]{1,0:T(8,128)(2,1)} custom-call(s32[2]{0:T(128)} %broadcast_select_fusion.place_ref, bf16[1536,256]{1,0:T(8,128)(2,1)} %bitcast.9, bf16[22,64,256]{2,1,0:T(8,128)(2,1)} %join.1.refs_0_, bf16[22,64,256]{2,1,0:T(8,128)(2,1)} %copy-done.4, bf16[22,64,256]{2,1,0:T(8,128)(2,1)} %copy-done.3, bf16[22,64,256]{2,1,0:T(8,128)(2,1)} %copy-done.2), custom_call_target="tpu_custom_call" | custom-call | tf_op jit(solution)/shard_map/step/pallas_call | solution.py:258
  117.8 31.7 %all_to_all.15.back_ref = bf16[16,96,256]{2,1,0:T(8,128)(2,1)} all-to-all(bf16[16,96,256]{2,1,0:T(8,128)(2,1)} %bitcast.10), channel_id=1, replica_groups=mesh['fsdp'=16,'grp'=16] {'fsdp'}, dimensions={0} | all-to-all | bytes 1572864 | tf_op jit(solution)/shard_map/all_to_all | solution.py:332
  149.5 2.7 %deal.1 = (bf16[16,96,256]{2,1,0:T(8,128)(2,1)}, bf16[16,96,256]{2,1,0:T(8,128)(2,1)}) custom-call(s32[4,16]{1,0:T(4,128)} %get-tuple-element.15.table_ref, bf16[16,96,256]{2,1,0:T(8,128)(2,1)} %all_to_all.15.back_ref), custom_call_target="tpu_custom_call" | custom-call | tf_op jit(solution)/shard_map/deal/pallas_call | solution.py:287
  152.2 3.5 %all-to-all-start.2 = ((bf16[16,96,256]{2,1,0:T(8,128)(2,1)}), bf16[16,96,256]{2,1,0:T(8,128)(2,1)S(1)}, u32[]{:S(2)}, u32[]{:S(2)}) async-start(bf16[16,96,256]{2,1,0:T(8,128)(2,1)} %get-tuple-element.27), calls=%async_computation.2 | async-start | bytes 1572864 | tf_op jit(solution)/shard_map/all_to_all | solution.py:336
  155.7 1.3 fusion
  157.8 19.9 %all-to-all-done.2 = bf16[16,96,256]{2,1,0:T(8,128)(2,1)S(1)} async-done(((bf16[16,96,256]{2,1,0:T(8,128)(2,1)}), bf16[16,96,256]{2,1,0:T(8,128)(2,1)S(1)}, u32[]{:S(2)}, u32[]{:S(2)}) %all-to-all-start.2) | async-done | bytes 786464 | tf_op jit(solution)/shard_map/all_to_all | solution.py:336
  177.7 1.3 pad_maximum_fusion
  (38 shorter events, 7.2 us)
Async XLA Ops:
  3.6 32.7 %all-to-all-start = ((bf16[16,96,256]{2,1,0:T(8,128)(2,1)}), bf16[16,96,256]{2,1,0:T(8,128)(2,1)S(1)}, u32[]{:S(2)}, u32[]{:S(2)}) async-start(bf16[16,96,256]{2,1,0:T(8,128)(2,1)} %get-tuple-element.16), calls=%async_computation | async-start | bytes 1572864 | tf_op jit(solution)/shard_map/all_to_all | solution.py:325
  36.3 0.9 copy-start
  40.9 11.6 %collective-permute-start = (bf16[21,64,256]{2,1,0:T(8,128)(2,1)}, bf16[21,64,256]{2,1,0:T(8,128)(2,1)S(1)}, u32[]{:S(2)}, u32[]{:S(2)}) collective-permute-start(bf16[21,64,256]{2,1,0:T(8,128)(2,1)} %get-tuple-element.19), channel_id=1, source_target_pairs={{0,1},{1,2},{2,3},{3,0},{4,5},{5,6},{6,7},{7,4},{8,9},{9,10},{10,1... | collective-permute-start | bytes 2064392 | tf_op jit(solution)/shard_map/ppermute | solution.py:310
  42.2 18.5 %collective-permute-start.1 = (bf16[21,64,256]{2,1,0:T(8,128)(2,1)}, bf16[21,64,256]{2,1,0:T(8,128)(2,1)S(1)}, u32[]{:S(2)}, u32[]{:S(2)}) collective-permute-start(bf16[21,64,256]{2,1,0:T(8,128)(2,1)} %get-tuple-element.20), channel_id=1, source_target_pairs={{0,2},{1,3},{2,0},{3,1},{4,6},{5,7},{6,4},{7,5},{8,10},{9,11},{10,... | collective-permute-start | bytes 2064392 | tf_op jit(solution)/shard_map/ppermute | solution.py:310
  44.8 15.9 %collective-permute-start.2 = (bf16[21,64,256]{2,1,0:T(8,128)(2,1)}, bf16[21,64,256]{2,1,0:T(8,128)(2,1)S(1)}, u32[]{:S(2)}, u32[]{:S(2)}) collective-permute-start(bf16[21,64,256]{2,1,0:T(8,128)(2,1)} %get-tuple-element.21), channel_id=1, source_target_pairs={{0,3},{1,0},{2,1},{3,2},{4,7},{5,4},{6,5},{7,6},{8,11},{9,8},{10,9... | collective-permute-start | bytes 2064392 | tf_op jit(solution)/shard_map/ppermute | solution.py:310
  52.4 8.3 %copy-start.5 = (bf16[21,64,256]{2,1,0:T(8,128)(2,1)}, bf16[21,64,256]{2,1,0:T(8,128)(2,1)S(1)}, u32[]{:S(2)}) copy-start(bf16[21,64,256]{2,1,0:T(8,128)(2,1)S(1)} %collective-permute-done.refs_1_) | copy-start | bytes 2064388
  60.7 0.9 copy-start.6
  60.7 1.1 copy-start.7
  64.7 5.7 %collective-permute-start.3 = (bf16[21,16,256]{2,1,0:T(8,128)(2,1)}, bf16[21,16,256]{2,1,0:T(8,128)(2,1)S(1)}, u32[]{:S(2)}, u32[]{:S(2)}) collective-permute-start(bf16[21,16,256]{2,1,0:T(8,128)(2,1)} %get-tuple-element.23), channel_id=1, source_target_pairs={{0,4},{1,5},{2,6},{3,7},{4,8},{5,9},{6,10},{7,11},{8,12},{9,13},{1... | collective-permute-start | bytes 516104 | tf_op jit(solution)/shard_map/ppermute | solution.py:310
  65.9 7.3 %collective-permute-start.4 = (bf16[21,16,256]{2,1,0:T(8,128)(2,1)}, bf16[21,16,256]{2,1,0:T(8,128)(2,1)S(1)}, u32[]{:S(2)}, u32[]{:S(2)}) collective-permute-start(bf16[21,16,256]{2,1,0:T(8,128)(2,1)} %get-tuple-element.24), channel_id=1, source_target_pairs={{0,8},{1,9},{2,10},{3,11},{4,12},{5,13},{6,14},{7,15},{8,0},{9,1},... | collective-permute-start | bytes 516104 | tf_op jit(solution)/shard_map/ppermute | solution.py:310
  68.3 4.9 %collective-permute-start.5 = (bf16[21,16,256]{2,1,0:T(8,128)(2,1)}, bf16[21,16,256]{2,1,0:T(8,128)(2,1)S(1)}, u32[]{:S(2)}, u32[]{:S(2)}) collective-permute-start(bf16[21,16,256]{2,1,0:T(8,128)(2,1)} %get-tuple-element.25), channel_id=1, source_target_pairs={{0,12},{1,13},{2,14},{3,15},{4,0},{5,1},{6,2},{7,3},{8,4},{9,5},{1... | collective-permute-start | bytes 516104 | tf_op jit(solution)/shard_map/ppermute | solution.py:310
  70.4 2.9 %copy-start.11 = (bf16[21,16,256]{2,1,0:T(8,128)(2,1)}, bf16[21,16,256]{2,1,0:T(8,128)(2,1)S(1)}, u32[]{:S(2)}) copy-start(bf16[21,16,256]{2,1,0:T(8,128)(2,1)S(1)} %collective-permute-done.3.refs_1_) | copy-start | bytes 516100
  73.2 0.7 copy-start.12
  73.2 0.7 copy-start.13
  75.9 6.7 %collective-permute-start.8 = (bf16[22,16,256]{2,1,0:T(8,128)(2,1)}, bf16[22,16,256]{2,1,0:T(8,128)(2,1)S(1)}, u32[]{:S(2)}, u32[]{:S(2)}) collective-permute-start(bf16[22,16,256]{2,1,0:T(8,128)(2,1)} %add_last.1.refs_0_), channel_id=1, source_target_pairs={{0,12},{1,13},{2,14},{3,15},{4,0},{5,1},{6,2},{7,3},{8,4},{9,5},{1... | collective-permute-start | bytes 540680 | tf_op jit(solution)/shard_map/ppermute | solution.py:310
  77.8 6.4 %collective-permute-start.7 = (bf16[22,16,256]{2,1,0:T(8,128)(2,1)}, bf16[22,16,256]{2,1,0:T(8,128)(2,1)S(1)}, u32[]{:S(2)}, u32[]{:S(2)}) collective-permute-start(bf16[22,16,256]{2,1,0:T(8,128)(2,1)} %add_last.1.refs_0_), channel_id=1, source_target_pairs={{0,8},{1,9},{2,10},{3,11},{4,12},{5,13},{6,14},{7,15},{8,0},{9,1},... | collective-permute-start | bytes 540680 | tf_op jit(solution)/shard_map/ppermute | solution.py:310
  79.0 7.2 %collective-permute-start.6 = (bf16[22,16,256]{2,1,0:T(8,128)(2,1)}, bf16[22,16,256]{2,1,0:T(8,128)(2,1)S(1)}, u32[]{:S(2)}, u32[]{:S(2)}) collective-permute-start(bf16[22,16,256]{2,1,0:T(8,128)(2,1)} %add_last.1.refs_0_), channel_id=1, source_target_pairs={{0,4},{1,5},{2,6},{3,7},{4,8},{5,9},{6,10},{7,11},{8,12},{9,13},{1... | collective-permute-start | bytes 540680 | tf_op jit(solution)/shard_map/ppermute | solution.py:310
  82.6 3.6 %copy-start.8 = (bf16[22,16,256]{2,1,0:T(8,128)(2,1)}, bf16[22,16,256]{2,1,0:T(8,128)(2,1)S(1)}, u32[]{:S(2)}) copy-start(bf16[22,16,256]{2,1,0:T(8,128)(2,1)S(1)} %collective-permute-done.8.refs_3_) | copy-start | bytes 540676
  84.2 1.9 %copy-start.9 = (bf16[22,16,256]{2,1,0:T(8,128)(2,1)}, bf16[22,16,256]{2,1,0:T(8,128)(2,1)S(1)}, u32[]{:S(2)}) copy-start(bf16[22,16,256]{2,1,0:T(8,128)(2,1)S(1)} %collective-permute-done.7.refs_2_) | copy-start | bytes 540676
  86.1 0.7 copy-start.10
  88.9 17.8 %collective-permute-start.11 = (bf16[22,64,256]{2,1,0:T(8,128)(2,1)}, bf16[22,64,256]{2,1,0:T(8,128)(2,1)S(1)}, u32[]{:S(2)}, u32[]{:S(2)}) collective-permute-start(bf16[22,64,256]{2,1,0:T(8,128)(2,1)} %join.1.refs_0_), channel_id=1, source_target_pairs={{0,3},{1,0},{2,1},{3,2},{4,7},{5,4},{6,5},{7,6},{8,11},{9,8},{10,9... | collective-permute-start | bytes 2162696 | tf_op jit(solution)/shard_map/ppermute | solution.py:310
  90.4 16.3 %collective-permute-start.10 = (bf16[22,64,256]{2,1,0:T(8,128)(2,1)}, bf16[22,64,256]{2,1,0:T(8,128)(2,1)S(1)}, u32[]{:S(2)}, u32[]{:S(2)}) collective-permute-start(bf16[22,64,256]{2,1,0:T(8,128)(2,1)} %join.1.refs_0_), channel_id=1, source_target_pairs={{0,2},{1,3},{2,0},{3,1},{4,6},{5,7},{6,4},{7,5},{8,10},{9,11},{10,... | collective-permute-start | bytes 2162696 | tf_op jit(solution)/shard_map/ppermute | solution.py:310
  91.0 19.3 %collective-permute-start.9 = (bf16[22,64,256]{2,1,0:T(8,128)(2,1)}, bf16[22,64,256]{2,1,0:T(8,128)(2,1)S(1)}, u32[]{:S(2)}, u32[]{:S(2)}) collective-permute-start(bf16[22,64,256]{2,1,0:T(8,128)(2,1)} %join.1.refs_0_), channel_id=1, source_target_pairs={{0,1},{1,2},{2,3},{3,0},{4,5},{5,6},{6,7},{7,4},{8,9},{9,10},{10,1... | collective-permute-start | bytes 2162696 | tf_op jit(solution)/shard_map/ppermute | solution.py:310
  106.7 3.6 %copy-start.2 = (bf16[22,64,256]{2,1,0:T(8,128)(2,1)}, bf16[22,64,256]{2,1,0:T(8,128)(2,1)S(1)}, u32[]{:S(2)}) copy-start(bf16[22,64,256]{2,1,0:T(8,128)(2,1)S(1)} %collective-permute-done.11.refs_3_) | copy-start | bytes 2162692
  106.7 3.6 %copy-start.3 = (bf16[22,64,256]{2,1,0:T(8,128)(2,1)}, bf16[22,64,256]{2,1,0:T(8,128)(2,1)S(1)}, u32[]{:S(2)}) copy-start(bf16[22,64,256]{2,1,0:T(8,128)(2,1)S(1)} %collective-permute-done.10.refs_2_) | copy-start | bytes 2162692
  110.3 0.9 copy-start.4
  149.5 7.5 %copy-start.1 = (bf16[1536,256]{1,0:T(8,128)(2,1)S(1)}, bf16[1536,256]{1,0:T(8,128)(2,1)}, u32[]{:S(2)}) copy-start(bf16[1536,256]{1,0:T(8,128)(2,1)} %step.1) | copy-start | bytes 2359300
  152.2 25.5 %all-to-all-start.2 = ((bf16[16,96,256]{2,1,0:T(8,128)(2,1)}), bf16[16,96,256]{2,1,0:T(8,128)(2,1)S(1)}, u32[]{:S(2)}, u32[]{:S(2)}) async-start(bf16[16,96,256]{2,1,0:T(8,128)(2,1)} %get-tuple-element.27), calls=%async_computation.2 | async-start | bytes 1572864 | tf_op jit(solution)/shard_map/all_to_all | solution.py:336

commit v3 on v2

--- a/solution.py
+++ b/solution.py
@@ -12,7 +12,6 @@
 SIDE = 4
 BLOCK = 256
 PIECE = BLOCK // SIDE
-SUB = PIECE // SIDE
 VMEM_LIMIT = 56 * 1024 * 1024
 
 VMEM = pl.BlockSpec(memory_space=pltpu.VMEM)
@@ -110,8 +109,8 @@
     )(owner, grads)
 
 
-def gram_kernel(pairs, place_ref, x_ref, *refs):
-    outs, square_ref, full = refs[:SIDE], refs[SIDE], refs[SIDE + 1]
+def gram_kernel(pairs, squares, place_ref, x_ref, *refs):
+    outs, full = refs[:SIDE], refs[-1]
     for t, (i, j) in enumerate(pairs):
         full[t] = lax.dot_general(
             x_ref[i * BLOCK : (i + 1) * BLOCK, :],
@@ -121,100 +120,80 @@
         ).astype(jnp.bfloat16)
         for s in range(SIDE):
             outs[s][t] = full[t, part(place_ref[0] + s, PIECE), :]
-    total = jnp.zeros((1, x_ref.shape[1]), jnp.float32)
-    for i in range(x_ref.shape[0] // BLOCK):
-        values = x_ref[i * BLOCK : (i + 1) * BLOCK, :].astype(jnp.float32)
-        total = total + jnp.sum(values * values, axis=0, keepdims=True)
-    total = jnp.sum(total, axis=1, keepdims=True)
-    square_ref[...] = jnp.broadcast_to(total, square_ref.shape)
-
-
-def gram_terms(place, x):
-    pairs = pairs_of(x.shape[0])
-    return pl.pallas_call(
-        functools.partial(gram_kernel, pairs),
-        out_shape=(shape_of(len(pairs), PIECE, BLOCK),) * SIDE
-        + (shape_of(8, BLOCK, dtype=jnp.float32),),
+    if squares:
+        square_ref = refs[SIDE]
+        total = jnp.zeros((1, x_ref.shape[1]), jnp.float32)
+        for i in range(x_ref.shape[0] // BLOCK):
+            values = x_ref[i * BLOCK : (i + 1) * BLOCK, :].astype(jnp.float32)
+            total = total + jnp.sum(values * values, axis=0, keepdims=True)
+        total = jnp.sum(total, axis=1, keepdims=True)
+        square_ref[...] = jnp.broadcast_to(total, square_ref.shape)
+
+
+def gram_terms(place, x, pairs, squares):
+    out_shape = (shape_of(len(pairs), PIECE, BLOCK),) * SIDE
+    if squares:
+        out_shape += (shape_of(8, BLOCK, dtype=jnp.float32),)
+    return pl.pallas_call(
+        functools.partial(gram_kernel, pairs, squares),
+        out_shape=out_shape,
         in_specs=[SMEM, VMEM],
-        out_specs=(VMEM,) * (SIDE + 1),
+        out_specs=(VMEM,) * len(out_shape),
         scratch_shapes=[pltpu.VMEM((len(pairs), BLOCK, BLOCK), jnp.bfloat16)],
         compiler_params=params(),
+        cost_estimate=pl.CostEstimate(
+            flops=2 * len(pairs) * BLOCK**3, bytes_accessed=4 * 1024 * 1024, transcendentals=0
+        ),
         name="gram",
     )(place, x)
 
 
-def add_kernel(place_ref, *refs):
-    ins, outs = refs[:SIDE], refs[SIDE:]
-    for s in range(SIDE):
-        rows = part(place_ref[1] + s, SUB)
-        total = ins[0][:, rows, :].astype(jnp.float32)
-        for other in ins[1:]:
-            total = total + other[:, rows, :].astype(jnp.float32)
-        outs[s][...] = total.astype(jnp.bfloat16)
-
-
-def add_first(place, pieces):
-    blocks = pieces[0].shape[0]
-    return pl.pallas_call(
-        add_kernel,
-        out_shape=(shape_of(blocks, SUB, BLOCK),) * SIDE,
-        in_specs=[SMEM] + [VMEM] * SIDE,
-        out_specs=(VMEM,) * SIDE,
-        compiler_params=params(),
-        name="add_first",
-    )(place, *pieces)
-
-
-def add_last_kernel(square_ref, *refs):
-    ins, out = refs[:SIDE], refs[SIDE]
-    blocks = ins[0].shape[0]
-    total = ins[0][...].astype(jnp.float32)
-    for other in ins[1:]:
-        total = total + other[...].astype(jnp.float32)
-    out[:blocks] = total.astype(jnp.bfloat16)
-    rest = jnp.broadcast_to(square_ref[0:1, :], (SUB, BLOCK))
-    row = lax.broadcasted_iota(jnp.int32, (SUB, BLOCK), 0)
-    parts = jnp.zeros((SUB, BLOCK), jnp.float32)
+def split(number, shape):
+    rest = jnp.broadcast_to(number, shape)
+    row = lax.broadcasted_iota(jnp.int32, shape, 0)
+    parts = jnp.zeros(shape, jnp.float32)
     for k in range(3):
         top = lax.reduce_precision(rest, 8, 7)
         parts = jnp.where(row == k, top, parts)
         rest = rest - top
-    out[blocks] = parts.astype(jnp.bfloat16)
-
-
-def add_last(square, pieces):
-    blocks = pieces[0].shape[0]
-    return pl.pallas_call(
-        add_last_kernel,
-        out_shape=shape_of(blocks + 1, SUB, BLOCK),
-        in_specs=[VMEM] * (SIDE + 1),
+    return parts.astype(jnp.bfloat16)
+
+
+def add_kernel(blocks, squares, carried, *refs):
+    ins, out = refs[:SIDE], refs[-1]
+    total = ins[0][:blocks].astype(jnp.float32)
+    for other in ins[1:]:
+        total = total + other[:blocks].astype(jnp.float32)
+    out[:blocks] = total.astype(jnp.bfloat16)
+    if squares:
+        out[blocks] = split(refs[SIDE][0:1, :], (PIECE, BLOCK))
+    if carried:
+        number = jnp.zeros((1, BLOCK), jnp.float32)
+        for piece in ins:
+            number = number + jnp.sum(piece[blocks].astype(jnp.float32), axis=0, keepdims=True)
+        out[blocks] = split(number, (PIECE, BLOCK))
+
+
+def add(pieces, square=None, carried=False):
+    extra = () if square is None else (square,)
+    blocks = pieces[0].shape[0] - carried
+    return pl.pallas_call(
+        functools.partial(add_kernel, blocks, square is not None, carried),
+        out_shape=shape_of(blocks + (square is not None or carried), PIECE, BLOCK),
+        in_specs=[VMEM] * (SIDE + len(extra)),
         out_specs=VMEM,
         compiler_params=params(),
-        name="add_last",
-    )(square, *pieces)
-
-
-def join_kernel(place_ref, *refs):
-    ins, out = refs[:SIDE], refs[SIDE]
-    for s in range(SIDE):
-        out[:, part(place_ref[1] - s + SIDE, SUB), :] = ins[s][...]
-
-
-def join(place, parts):
-    return pl.pallas_call(
-        join_kernel,
-        out_shape=shape_of(parts[0].shape[0], PIECE, BLOCK),
-        in_specs=[SMEM] + [VMEM] * SIDE,
-        out_specs=VMEM,
-        compiler_params=params(),
-        name="join",
-    )(place, *parts)
+        cost_estimate=pl.CostEstimate(
+            flops=4 * blocks * PIECE * BLOCK, bytes_accessed=4 * 1024 * 1024, transcendentals=0
+        ),
+        name="add",
+    )(*pieces, *extra)
 
 
 def step_kernel(pairs, rows_all, factor, place_ref, x_ref, *refs):
-    ins = refs[:SIDE]
-    out_ref, gram, normed, left = refs[SIDE:]
-    blocks = len(pairs)
+    ins = refs[: 2 * SIDE]
+    out_ref, gram, normed, left = refs[2 * SIDE :]
+    blocks = ins[0].shape[0] - 1
     total = jnp.zeros((1, BLOCK), jnp.float32)
     for s in range(SIDE):
         total = total + jnp.sum(ins[s][blocks].astype(jnp.float32), axis=0, keepdims=True)
@@ -225,10 +204,11 @@
         rows = slice(i * BLOCK, (i + 1) * BLOCK)
         normed[rows, :] = (x_ref[rows, :].astype(jnp.float32) * inverse).astype(jnp.bfloat16)
     for t, (i, j) in enumerate(pairs):
+        source, u = (ins[:SIDE], t) if t < blocks else (ins[SIDE:], t - blocks)
         for s in range(SIDE):
             p = lax.rem(place_ref[0] - s + SIDE, SIDE)
             rows = pl.ds(pl.multiple_of(i * BLOCK + p * PIECE, PIECE), PIECE)
-            values = ins[s][t].astype(jnp.float32) * scale
+            values = source[s][u].astype(jnp.float32) * scale
             gram[rows, j * BLOCK : (j + 1) * BLOCK] = jnp.where(scale > 0, values, 0.0).astype(
                 jnp.bfloat16
             )
@@ -258,7 +238,7 @@
     return pl.pallas_call(
         functools.partial(step_kernel, pairs, rows, factor),
         out_shape=shape_of(rows, cols),
-        in_specs=[SMEM, VMEM] + [VMEM] * SIDE,
+        in_specs=[SMEM, VMEM] + [VMEM] * (2 * SIDE),
         out_specs=VMEM,
         scratch_shapes=[
             pltpu.VMEM((rows, rows), jnp.bfloat16),
@@ -324,11 +304,16 @@
     table, packed = plan(owner, grads)
     x = lax.all_to_all(packed, "fsdp", split_axis=0, concat_axis=0, tiled=True)
     x = x.reshape(rows, cols_dev)
-    *terms, square = gram_terms(place, x)
-    parts = add_first(place, spread(terms, 0))
-    own = add_last(square, spread(parts, 1))
-    own = join(place, spread([own] * SIDE, 1))
-    done = step(place, x, spread([own] * SIDE, 0), factor)
+    pairs = pairs_of(rows)
+    cut = len(pairs) // 2
+    *early, square = gram_terms(place, x, pairs[:cut], True)
+    late = gram_terms(place, x, pairs[cut:], False)
+    early = add(spread(early, 0), square)
+    late = add(spread(late, 0))
+    early = add(spread([early] * SIDE, 1), carried=True)
+    late = add(spread([late] * SIDE, 1))
+    pieces = spread([early] * SIDE, 0) + spread([late] * SIDE, 0)
+    done = step(place, x, pieces, factor)
     back = lax.all_to_all(
         done.reshape(count, rows_dev, cols_dev), "fsdp", split_axis=0, concat_axis=0, tiled=True
     )

time: 180 us -> 175 us (0.972)
  waiting for transfers between devices: 86 us -> 63.1 us
  blocking collectives: 31.7 us -> 39.1 us
  starting transfers between devices: 29.3 us -> 36.3 us
  Pallas kernels: 22.9 us -> 26.8 us
    ppermute x12 -> x18, waiting for transfers between devices: 44.2 us -> 21.2 us  [spread(): got.append(lax.ppermute(send[amount], ('fsdp', 'grp'), moves))]
    all_to_all x1, blocking collectives: 31.7 us -> 39.1 us  [on_device(): lax.all_to_all(done.reshape(count, rows_dev, cols_dev), 'fsdp', split_axi...]
    ppermute x12 -> x18, starting transfers between devices: 15.8 us -> 22.8 us  [spread(): got.append(lax.ppermute(send[amount], ('fsdp', 'grp'), moves))]
    pallas_call x4 -> x6, Pallas kernels: 10.7 us -> 14.6 us  [the longest x4 8.88 us: add(): pl.pallas_call(functools.partial(add_kernel, blocks, square is not None,...]
    unnamed x28 -> x40, local copies, waits for them, and re-layouts: 4.3 us -> 4.73 us
  transfers between devices with their start and end apart: 14 -> 20, of which waited for: 11 -> 12; matrix products, arithmetic and copies ran while one was open for 2% -> 2% of each run, Pallas kernels for 0% -> 7%
where the time goes in v3:
time: 175 us
  waiting for transfers between devices  63.1 us (36%)
  blocking collectives  39.1 us (22%)
  starting transfers between devices  36.3 us (21%)
  Pallas kernels  26.8 us (15%)
  local copies, waits for them, and re-layouts  4.82 us (3%)
  other arithmetic  3.91 us (2%)
    all_to_all x1, blocking collectives, on_device(): lax.all_to_all(done.reshape(count, rows_dev, cols_dev), 'fsdp', split_axi...  39.1 us
    ppermute x18, starting transfers between devices, spread(): got.append(lax.ppermute(send[amount], ('fsdp', 'grp'), moves))  22.8 us
    all_to_all x1, waiting for transfers between devices, on_device(): x = lax.all_to_all(packed, 'fsdp', split_axis=0, concat_axis=0, tiled=True)  21.8 us
    ppermute x18, waiting for transfers between devices, spread(): got.append(lax.ppermute(send[amount], ('fsdp', 'grp'), moves))  21.2 us
    all_to_all x1, waiting for transfers between devices, on_device(): lax.all_to_all(second, 'fsdp', split_axis=0, concat_axis=0, tiled=True)  20.1 us
    all_to_all x1, starting transfers between devices, on_device(): x = lax.all_to_all(packed, 'fsdp', split_axis=0, concat_axis=0, tiled=True)  9.99 us
    pallas_call x4, Pallas kernels, add(): pl.pallas_call(functools.partial(add_kernel, blocks, square is not None,...  8.88 us
    pallas_call x1, Pallas kernels, step(): pl.pallas_call(functools.partial(step_kernel, pairs, rows, factor), out_s...  6.56 us
  transfers between devices with their start and end apart: 20, of which 12 were waited for; matrix products, arithmetic and copies ran while one was open for 2% of the time, Pallas kernels for 7%

profile of v3, /device:TPU:1, one launch (start us, length us, event | category | flops | bytes accessed | tf_op | source)
XLA Modules:
  0.0 174.7 jit_solution(18139110717722361334)
XLA Ops:
  0.6 3.0 %plan.1 = (s32[4,16]{1,0:T(4,128)}, bf16[16,96,256]{2,1,0:T(8,128)(2,1)}) custom-call(s32[16]{0:T(128)} %owner_ref.1, bf16[16,96,256]{2,1,0:T(8,128)(2,1)} %grads_ref.1), custom_call_target="tpu_custom_call" | custom-call | tf_op jit(solution)/shard_map/plan/pallas_call | solution.py:101
  3.6 10.0 %all-to-all-start = ((bf16[16,96,256]{2,1,0:T(8,128)(2,1)}), bf16[16,96,256]{2,1,0:T(8,128)(2,1)S(1)}, u32[]{:S(2)}, u32[]{:S(2)}) async-start(bf16[16,96,256]{2,1,0:T(8,128)(2,1)} %get-tuple-element.16), calls=%async_computation | async-start | bytes 1572864 | tf_op jit(solution)/shard_map/all_to_all | solution.py:305
  14.4 21.8 %all-to-all-done = bf16[16,96,256]{2,1,0:T(8,128)(2,1)S(1)} async-done(((bf16[16,96,256]{2,1,0:T(8,128)(2,1)}), bf16[16,96,256]{2,1,0:T(8,128)(2,1)S(1)}, u32[]{:S(2)}, u32[]{:S(2)}) %all-to-all-start) | async-done | bytes 786464 | tf_op jit(solution)/shard_map/all_to_all | solution.py:305
  37.1 2.9 %gram.3 = (bf16[11,64,256]{2,1,0:T(8,128)(2,1)}, bf16[11,64,256]{2,1,0:T(8,128)(2,1)}, bf16[11,64,256]{2,1,0:T(8,128)(2,1)}, bf16[11,64,256]{2,1,0:T(8,128)(2,1)}) custom-call(s32[2]{0:T(128)} %broadcast_select_fusion.place_ref, bf16[1536,256]{1,0:T(8,128)(2,1)} %bitcast.9), custom_call_target="tpu_custom_call" | custom-call | flops 369098752 | bytes 4194304 | tf_op jit(solution)/shard_map/gram/pallas_call | solution.py:137
  40.0 1.3 collective-permute-start.9
  41.3 2.8 %gram.2 = (bf16[10,64,256]{2,1,0:T(8,128)(2,1)}, bf16[10,64,256]{2,1,0:T(8,128)(2,1)}, bf16[10,64,256]{2,1,0:T(8,128)(2,1)}, bf16[10,64,256]{2,1,0:T(8,128)(2,1)}, f32[8,256]{1,0:T(8,128)}) custom-call(s32[2]{0:T(128)} %broadcast_select_fusion.place_ref, bf16[1536,256]{1,0:T(8,128)(2,1)} %bitcast.10), custom_call_target="tpu_custom_call" | custom-call | flops 335544320 | bytes 4194304 | tf_op jit(solution)/shard_map/gram/pallas_call | solution.py:137
  44.1 1.3 collective-permute-start
  45.4 1.3 collective-permute-start.1
  46.8 2.1 %collective-permute-start.2 = (bf16[10,64,256]{2,1,0:T(8,128)(2,1)}, bf16[10,64,256]{2,1,0:T(8,128)(2,1)S(1)}, u32[]{:S(2)}, u32[]{:S(2)}) collective-permute-start(bf16[10,64,256]{2,1,0:T(8,128)(2,1)} %get-tuple-element.20), channel_id=1, source_target_pairs={{0,3},{1,0},{2,1},{3,2},{4,7},{5,4},{6,5},{7,6},{8,11},{9,8},{10,9... | collective-permute-start | bytes 983048 | tf_op jit(solution)/shard_map/ppermute | solution.py:290
  49.2 2.6 %collective-permute-done.refs_1_ = bf16[10,64,256]{2,1,0:T(8,128)(2,1)S(1)} collective-permute-done((bf16[10,64,256]{2,1,0:T(8,128)(2,1)}, bf16[10,64,256]{2,1,0:T(8,128)(2,1)S(1)}, u32[]{:S(2)}, u32[]{:S(2)}) %collective-permute-start) | collective-permute-done | bytes 327712 | tf_op jit(solution)/shard_map/ppermute | solution.py:290
  53.1 3.2 %collective-permute-done.1.refs_2_ = bf16[10,64,256]{2,1,0:T(8,128)(2,1)S(1)} collective-permute-done((bf16[10,64,256]{2,1,0:T(8,128)(2,1)}, bf16[10,64,256]{2,1,0:T(8,128)(2,1)S(1)}, u32[]{:S(2)}, u32[]{:S(2)}) %collective-permute-start.1) | collective-permute-done | bytes 327712 | tf_op jit(solution)/shard_map/ppermute | solution.py:290
  57.2 2.2 %add.12.refs_0_ = bf16[11,64,256]{2,1,0:T(8,128)(2,1)} custom-call(bf16[10,64,256]{2,1,0:T(8,128)(2,1)} %get-tuple-element.17.refs_0_, bf16[10,64,256]{2,1,0:T(8,128)(2,1)} %copy-done.17, bf16[10,64,256]{2,1,0:T(8,128)(2,1)} %copy-done.18, bf16[10,64,256]{2,1,0:T(8,128)(2,1)} %copy-done.19, f32[8,256]{1,0:T(8,128)} %get-tuple-element.21.refs_4_), custom_call_target="tpu_custom_call" | custom-call | flops 655360 | bytes 4194304 | tf_op jit(solution)/shard_map/add/pallas_call | solution.py:180
  59.3 2.5 %collective-permute-start.5 = (bf16[11,64,256]{2,1,0:T(8,128)(2,1)}, bf16[11,64,256]{2,1,0:T(8,128)(2,1)S(1)}, u32[]{:S(2)}, u32[]{:S(2)}) collective-permute-start(bf16[11,64,256]{2,1,0:T(8,128)(2,1)} %add.12.refs_0_), channel_id=1, source_target_pairs={{0,12},{1,13},{2,14},{3,15},{4,0},{5,1},{6,2},{7,3},{8,4},{9,5},{1... | collective-permute-start | bytes 1081352 | tf_op jit(solution)/shard_map/ppermute | solution.py:290
  62.7 3.0 %collective-permute-done.11.refs_3_ = bf16[11,64,256]{2,1,0:T(8,128)(2,1)S(1)} collective-permute-done((bf16[11,64,256]{2,1,0:T(8,128)(2,1)}, bf16[11,64,256]{2,1,0:T(8,128)(2,1)S(1)}, u32[]{:S(2)}, u32[]{:S(2)}) %collective-permute-start.11) | collective-permute-done | bytes 360480 | tf_op jit(solution)/shard_map/ppermute | solution.py:290
  66.4 2.2 %add.14.refs_0_ = bf16[11,64,256]{2,1,0:T(8,128)(2,1)} custom-call(bf16[11,64,256]{2,1,0:T(8,128)(2,1)} %get-tuple-element.22.refs_0_, bf16[11,64,256]{2,1,0:T(8,128)(2,1)} %copy-done.2, bf16[11,64,256]{2,1,0:T(8,128)(2,1)} %copy-done.3, bf16[11,64,256]{2,1,0:T(8,128)(2,1)} %copy-done.7), custom_call_target="tpu_custom_call" | custom-call | flops 720896 | bytes 4194304 | tf_op jit(solution)/shard_map/add/pallas_call | solution.py:180
  68.6 2.6 %collective-permute-start.14 = (bf16[11,64,256]{2,1,0:T(8,128)(2,1)}, bf16[11,64,256]{2,1,0:T(8,128)(2,1)S(1)}, u32[]{:S(2)}, u32[]{:S(2)}) collective-permute-start(bf16[11,64,256]{2,1,0:T(8,128)(2,1)} %add.14.refs_0_), channel_id=1, source_target_pairs={{0,12},{1,13},{2,14},{3,15},{4,0},{5,1},{6,2},{7,3},{8,4},{9,5},{1... | collective-permute-start | bytes 1081352 | tf_op jit(solution)/shard_map/ppermute | solution.py:290
  72.5 1.4 collective-permute-done.3.refs_1_
  74.7 2.2 %add.13.refs_0_ = bf16[11,64,256]{2,1,0:T(8,128)(2,1)} custom-call(bf16[11,64,256]{2,1,0:T(8,128)(2,1)} %add.12.refs_0_, bf16[11,64,256]{2,1,0:T(8,128)(2,1)} %copy-done.9, bf16[11,64,256]{2,1,0:T(8,128)(2,1)} %copy-done.5, bf16[11,64,256]{2,1,0:T(8,128)(2,1)} %copy-done.4), custom_call_target="tpu_custom_call" | custom-call | flops 655360 | bytes 4194304 | tf_op jit(solution)/shard_map/add/pallas_call | solution.py:180
  76.9 1.9 %collective-permute-start.8 = (bf16[11,64,256]{2,1,0:T(8,128)(2,1)}, bf16[11,64,256]{2,1,0:T(8,128)(2,1)S(1)}, u32[]{:S(2)}, u32[]{:S(2)}) collective-permute-start(bf16[11,64,256]{2,1,0:T(8,128)(2,1)} %add.13.refs_0_), channel_id=1, source_target_pairs={{0,3},{1,0},{2,1},{3,2},{4,7},{5,4},{6,5},{7,6},{8,11},{9,8},{10,9... | collective-permute-start | bytes 1081352 | tf_op jit(solution)/shard_map/ppermute | solution.py:290
  79.7 1.5 collective-permute-start.6
  81.2 1.8 %collective-permute-done.12.refs_1_ = bf16[11,64,256]{2,1,0:T(8,128)(2,1)S(1)} collective-permute-done((bf16[11,64,256]{2,1,0:T(8,128)(2,1)}, bf16[11,64,256]{2,1,0:T(8,128)(2,1)S(1)}, u32[]{:S(2)}, u32[]{:S(2)}) %collective-permute-start.12) | collective-permute-done | bytes 360480 | tf_op jit(solution)/shard_map/ppermute | solution.py:290
  83.8 2.2 %add.15.refs_4_ = bf16[11,64,256]{2,1,0:T(8,128)(2,1)} custom-call(bf16[11,64,256]{2,1,0:T(8,128)(2,1)} %add.14.refs_0_, bf16[11,64,256]{2,1,0:T(8,128)(2,1)} %copy-done.10, bf16[11,64,256]{2,1,0:T(8,128)(2,1)} %copy-done.8, bf16[11,64,256]{2,1,0:T(8,128)(2,1)} %copy-done.6), custom_call_target="tpu_custom_call" | custom-call | flops 720896 | bytes 4194304 | tf_op jit(solution)/shard_map/add/pallas_call | solution.py:180
  86.7 2.6 %collective-permute-start.16 = (bf16[11,64,256]{2,1,0:T(8,128)(2,1)}, bf16[11,64,256]{2,1,0:T(8,128)(2,1)S(1)}, u32[]{:S(2)}, u32[]{:S(2)}) collective-permute-start(bf16[11,64,256]{2,1,0:T(8,128)(2,1)} %add.15.refs_4_), channel_id=1, source_target_pairs={{0,2},{1,3},{2,0},{3,1},{4,6},{5,7},{6,4},{7,5},{8,10},{9,11},{10,... | collective-permute-start | bytes 1081352 | tf_op jit(solution)/shard_map/ppermute | solution.py:290
  90.9 1.6 collective-permute-done.17.refs_7_
  92.6 2.2 %collective-permute-done.16.refs_6_ = bf16[11,64,256]{2,1,0:T(8,128)(2,1)S(1)} collective-permute-done((bf16[11,64,256]{2,1,0:T(8,128)(2,1)}, bf16[11,64,256]{2,1,0:T(8,128)(2,1)S(1)}, u32[]{:S(2)}, u32[]{:S(2)}) %collective-permute-start.16) | collective-permute-done | bytes 360480 | tf_op jit(solution)/shard_map/ppermute | solution.py:290
  94.8 4.0 %collective-permute-done.15.refs_5_ = bf16[11,64,256]{2,1,0:T(8,128)(2,1)S(1)} collective-permute-done((bf16[11,64,256]{2,1,0:T(8,128)(2,1)}, bf16[11,64,256]{2,1,0:T(8,128)(2,1)S(1)}, u32[]{:S(2)}, u32[]{:S(2)}) %collective-permute-start.15) | collective-permute-done | bytes 360480 | tf_op jit(solution)/shard_map/ppermute | solution.py:290
  99.6 6.6 %step.1 = bf16[1536,256]{1,0:T(8,128)(2,1)} custom-call(s32[2]{0:T(128)} %broadcast_select_fusion.place_ref, bf16[1536,256]{1,0:T(8,128)(2,1)} %bitcast.11, bf16[11,64,256]{2,1,0:T(8,128)(2,1)} %add.13.refs_0_, bf16[11,64,256]{2,1,0:T(8,128)(2,1)} %copy-done.13, bf16[11,64,256]{2,1,0:T(8,128)(2,1)} %copy-done.12, bf16[11,64,256]{2,1,0:T(8,128)(2,1)} %copy-done.11, ...), custom_call_target="tpu_custom_call" | custom-call | tf_op jit(solution)/shard_map/step/pallas_call | solution.py:238
  106.2 39.1 %all_to_all.15.back_ref = bf16[16,96,256]{2,1,0:T(8,128)(2,1)} all-to-all(bf16[16,96,256]{2,1,0:T(8,128)(2,1)} %bitcast.8), channel_id=1, replica_groups=mesh['fsdp'=16,'grp'=16] {'fsdp'}, dimensions={0} | all-to-all | bytes 1572864 | tf_op jit(solution)/shard_map/all_to_all | solution.py:317
  145.2 2.6 %deal.1 = (bf16[16,96,256]{2,1,0:T(8,128)(2,1)}, bf16[16,96,256]{2,1,0:T(8,128)(2,1)}) custom-call(s32[4,16]{1,0:T(4,128)} %get-tuple-element.15.table_ref, bf16[16,96,256]{2,1,0:T(8,128)(2,1)} %all_to_all.15.back_ref), custom_call_target="tpu_custom_call" | custom-call | tf_op jit(solution)/shard_map/deal/pallas_call | solution.py:267
  147.9 3.5 %all-to-all-start.2 = ((bf16[16,96,256]{2,1,0:T(8,128)(2,1)}), bf16[16,96,256]{2,1,0:T(8,128)(2,1)S(1)}, u32[]{:S(2)}, u32[]{:S(2)}) async-start(bf16[16,96,256]{2,1,0:T(8,128)(2,1)} %get-tuple-element.27), calls=%async_computation.2 | async-start | bytes 1572864 | tf_op jit(solution)/shard_map/all_to_all | solution.py:321
  153.3 20.1 %all-to-all-done.2 = bf16[16,96,256]{2,1,0:T(8,128)(2,1)S(1)} async-done(((bf16[16,96,256]{2,1,0:T(8,128)(2,1)}), bf16[16,96,256]{2,1,0:T(8,128)(2,1)S(1)}, u32[]{:S(2)}, u32[]{:S(2)}) %all-to-all-start.2) | async-done | bytes 786464 | tf_op jit(solution)/shard_map/all_to_all | solution.py:321
  173.4 1.3 pad_maximum_fusion
  (64 shorter events, 14.5 us)
Async XLA Ops:
  3.6 32.7 %all-to-all-start = ((bf16[16,96,256]{2,1,0:T(8,128)(2,1)}), bf16[16,96,256]{2,1,0:T(8,128)(2,1)S(1)}, u32[]{:S(2)}, u32[]{:S(2)}) async-start(bf16[16,96,256]{2,1,0:T(8,128)(2,1)} %get-tuple-element.16), calls=%async_computation | async-start | bytes 1572864 | tf_op jit(solution)/shard_map/all_to_all | solution.py:305
  40.0 22.0 %collective-permute-start.9 = (bf16[11,64,256]{2,1,0:T(8,128)(2,1)}, bf16[11,64,256]{2,1,0:T(8,128)(2,1)S(1)}, u32[]{:S(2)}, u32[]{:S(2)}) collective-permute-start(bf16[11,64,256]{2,1,0:T(8,128)(2,1)} %get-tuple-element.23), channel_id=1, source_target_pairs={{0,1},{1,2},{2,3},{3,0},{4,5},{5,6},{6,7},{7,4},{8,9},{9,10},{10,1... | collective-permute-start | bytes 1081352 | tf_op jit(solution)/shard_map/ppermute | solution.py:290
  44.1 7.6 %collective-permute-start = (bf16[10,64,256]{2,1,0:T(8,128)(2,1)}, bf16[10,64,256]{2,1,0:T(8,128)(2,1)S(1)}, u32[]{:S(2)}, u32[]{:S(2)}) collective-permute-start(bf16[10,64,256]{2,1,0:T(8,128)(2,1)} %get-tuple-element.18), channel_id=1, source_target_pairs={{0,1},{1,2},{2,3},{3,0},{4,5},{5,6},{6,7},{7,4},{8,9},{9,10},{10,1... | collective-permute-start | bytes 983048 | tf_op jit(solution)/shard_map/ppermute | solution.py:290
  45.4 10.9 %collective-permute-start.1 = (bf16[10,64,256]{2,1,0:T(8,128)(2,1)}, bf16[10,64,256]{2,1,0:T(8,128)(2,1)S(1)}, u32[]{:S(2)}, u32[]{:S(2)}) collective-permute-start(bf16[10,64,256]{2,1,0:T(8,128)(2,1)} %get-tuple-element.19), channel_id=1, source_target_pairs={{0,2},{1,3},{2,0},{3,1},{4,6},{5,7},{6,4},{7,5},{8,10},{9,11},{10,... | collective-permute-start | bytes 983048 | tf_op jit(solution)/shard_map/ppermute | solution.py:290
  46.8 9.5 %collective-permute-start.2 = (bf16[10,64,256]{2,1,0:T(8,128)(2,1)}, bf16[10,64,256]{2,1,0:T(8,128)(2,1)S(1)}, u32[]{:S(2)}, u32[]{:S(2)}) collective-permute-start(bf16[10,64,256]{2,1,0:T(8,128)(2,1)} %get-tuple-element.20), channel_id=1, source_target_pairs={{0,3},{1,0},{2,1},{3,2},{4,7},{5,4},{6,5},{7,6},{8,11},{9,8},{10,9... | collective-permute-start | bytes 983048 | tf_op jit(solution)/shard_map/ppermute | solution.py:290
  48.8 13.8 %collective-permute-start.10 = (bf16[11,64,256]{2,1,0:T(8,128)(2,1)}, bf16[11,64,256]{2,1,0:T(8,128)(2,1)S(1)}, u32[]{:S(2)}, u32[]{:S(2)}) collective-permute-start(bf16[11,64,256]{2,1,0:T(8,128)(2,1)} %get-tuple-element.24), channel_id=1, source_target_pairs={{0,2},{1,3},{2,0},{3,1},{4,6},{5,7},{6,4},{7,5},{8,10},{9,11},{10,... | collective-permute-start | bytes 1081352 | tf_op jit(solution)/shard_map/ppermute | solution.py:290
  51.8 4.5 %copy-start.17 = (bf16[10,64,256]{2,1,0:T(8,128)(2,1)}, bf16[10,64,256]{2,1,0:T(8,128)(2,1)S(1)}, u32[]{:S(2)}) copy-start(bf16[10,64,256]{2,1,0:T(8,128)(2,1)S(1)} %collective-permute-done.refs_1_) | copy-start | bytes 983044
  51.8 13.8 %collective-permute-start.11 = (bf16[11,64,256]{2,1,0:T(8,128)(2,1)}, bf16[11,64,256]{2,1,0:T(8,128)(2,1)S(1)}, u32[]{:S(2)}, u32[]{:S(2)}) collective-permute-start(bf16[11,64,256]{2,1,0:T(8,128)(2,1)} %get-tuple-element.25), channel_id=1, source_target_pairs={{0,3},{1,0},{2,1},{3,2},{4,7},{5,4},{6,5},{7,6},{8,11},{9,8},{10,9... | collective-permute-start | bytes 1081352 | tf_op jit(solution)/shard_map/ppermute | solution.py:290
  59.3 12.3 %collective-permute-start.5 = (bf16[11,64,256]{2,1,0:T(8,128)(2,1)}, bf16[11,64,256]{2,1,0:T(8,128)(2,1)S(1)}, u32[]{:S(2)}, u32[]{:S(2)}) collective-permute-start(bf16[11,64,256]{2,1,0:T(8,128)(2,1)} %add.12.refs_0_), channel_id=1, source_target_pairs={{0,12},{1,13},{2,14},{3,15},{4,0},{5,1},{6,2},{7,3},{8,4},{9,5},{1... | collective-permute-start | bytes 1081352 | tf_op jit(solution)/shard_map/ppermute | solution.py:290
  61.8 10.6 %collective-permute-start.4 = (bf16[11,64,256]{2,1,0:T(8,128)(2,1)}, bf16[11,64,256]{2,1,0:T(8,128)(2,1)S(1)}, u32[]{:S(2)}, u32[]{:S(2)}) collective-permute-start(bf16[11,64,256]{2,1,0:T(8,128)(2,1)} %add.12.refs_0_), channel_id=1, source_target_pairs={{0,8},{1,9},{2,10},{3,11},{4,12},{5,13},{6,14},{7,15},{8,0},{9,1},... | collective-permute-start | bytes 1081352 | tf_op jit(solution)/shard_map/ppermute | solution.py:290
  62.0 3.6 %copy-start.2 = (bf16[11,64,256]{2,1,0:T(8,128)(2,1)}, bf16[11,64,256]{2,1,0:T(8,128)(2,1)S(1)}, u32[]{:S(2)}) copy-start(bf16[11,64,256]{2,1,0:T(8,128)(2,1)S(1)} %collective-permute-done.9.refs_1_) | copy-start | bytes 1081348
  62.1 11.8 %collective-permute-start.3 = (bf16[11,64,256]{2,1,0:T(8,128)(2,1)}, bf16[11,64,256]{2,1,0:T(8,128)(2,1)S(1)}, u32[]{:S(2)}, u32[]{:S(2)}) collective-permute-start(bf16[11,64,256]{2,1,0:T(8,128)(2,1)} %add.12.refs_0_), channel_id=1, source_target_pairs={{0,4},{1,5},{2,6},{3,7},{4,8},{5,9},{6,10},{7,11},{8,12},{9,13},{1... | collective-permute-start | bytes 1081352 | tf_op jit(solution)/shard_map/ppermute | solution.py:290
  62.7 3.0 %copy-start.3 = (bf16[11,64,256]{2,1,0:T(8,128)(2,1)}, bf16[11,64,256]{2,1,0:T(8,128)(2,1)S(1)}, u32[]{:S(2)}) copy-start(bf16[11,64,256]{2,1,0:T(8,128)(2,1)S(1)} %collective-permute-done.10.refs_2_) | copy-start | bytes 1081348
  68.6 11.1 %collective-permute-start.14 = (bf16[11,64,256]{2,1,0:T(8,128)(2,1)}, bf16[11,64,256]{2,1,0:T(8,128)(2,1)S(1)}, u32[]{:S(2)}, u32[]{:S(2)}) collective-permute-start(bf16[11,64,256]{2,1,0:T(8,128)(2,1)} %add.14.refs_0_), channel_id=1, source_target_pairs={{0,12},{1,13},{2,14},{3,15},{4,0},{5,1},{6,2},{7,3},{8,4},{9,5},{1... | collective-permute-start | bytes 1081352 | tf_op jit(solution)/shard_map/ppermute | solution.py:290
  71.2 10.0 %collective-permute-start.13 = (bf16[11,64,256]{2,1,0:T(8,128)(2,1)}, bf16[11,64,256]{2,1,0:T(8,128)(2,1)S(1)}, u32[]{:S(2)}, u32[]{:S(2)}) collective-permute-start(bf16[11,64,256]{2,1,0:T(8,128)(2,1)} %add.14.refs_0_), channel_id=1, source_target_pairs={{0,8},{1,9},{2,10},{3,11},{4,12},{5,13},{6,14},{7,15},{8,0},{9,1},... | collective-permute-start | bytes 1081352 | tf_op jit(solution)/shard_map/ppermute | solution.py:290
  71.6 2.3 %copy-start.4 = (bf16[11,64,256]{2,1,0:T(8,128)(2,1)}, bf16[11,64,256]{2,1,0:T(8,128)(2,1)S(1)}, u32[]{:S(2)}) copy-start(bf16[11,64,256]{2,1,0:T(8,128)(2,1)S(1)} %collective-permute-done.5.refs_3_) | copy-start | bytes 1081348
  71.6 11.4 %collective-permute-start.12 = (bf16[11,64,256]{2,1,0:T(8,128)(2,1)}, bf16[11,64,256]{2,1,0:T(8,128)(2,1)S(1)}, u32[]{:S(2)}, u32[]{:S(2)}) collective-permute-start(bf16[11,64,256]{2,1,0:T(8,128)(2,1)} %add.14.refs_0_), channel_id=1, source_target_pairs={{0,4},{1,5},{2,6},{3,7},{4,8},{5,9},{6,10},{7,11},{8,12},{9,13},{1... | collective-permute-start | bytes 1081352 | tf_op jit(solution)/shard_map/ppermute | solution.py:290
  76.9 12.4 %collective-permute-start.8 = (bf16[11,64,256]{2,1,0:T(8,128)(2,1)}, bf16[11,64,256]{2,1,0:T(8,128)(2,1)S(1)}, u32[]{:S(2)}, u32[]{:S(2)}) collective-permute-start(bf16[11,64,256]{2,1,0:T(8,128)(2,1)} %add.13.refs_0_), channel_id=1, source_target_pairs={{0,3},{1,0},{2,1},{3,2},{4,7},{5,4},{6,5},{7,6},{8,11},{9,8},{10,9... | collective-permute-start | bytes 1081352 | tf_op jit(solution)/shard_map/ppermute | solution.py:290
  78.8 11.2 %collective-permute-start.7 = (bf16[11,64,256]{2,1,0:T(8,128)(2,1)}, bf16[11,64,256]{2,1,0:T(8,128)(2,1)S(1)}, u32[]{:S(2)}, u32[]{:S(2)}) collective-permute-start(bf16[11,64,256]{2,1,0:T(8,128)(2,1)} %add.13.refs_0_), channel_id=1, source_target_pairs={{0,2},{1,3},{2,0},{3,1},{4,6},{5,7},{6,4},{7,5},{8,10},{9,11},{10,... | collective-permute-start | bytes 1081352 | tf_op jit(solution)/shard_map/ppermute | solution.py:290
  79.7 3.3 %copy-start.6 = (bf16[11,64,256]{2,1,0:T(8,128)(2,1)}, bf16[11,64,256]{2,1,0:T(8,128)(2,1)S(1)}, u32[]{:S(2)}) copy-start(bf16[11,64,256]{2,1,0:T(8,128)(2,1)S(1)} %collective-permute-done.14.refs_3_) | copy-start | bytes 1081348
  79.7 11.2 %collective-permute-start.6 = (bf16[11,64,256]{2,1,0:T(8,128)(2,1)}, bf16[11,64,256]{2,1,0:T(8,128)(2,1)S(1)}, u32[]{:S(2)}, u32[]{:S(2)}) collective-permute-start(bf16[11,64,256]{2,1,0:T(8,128)(2,1)} %add.13.refs_0_), channel_id=1, source_target_pairs={{0,1},{1,2},{2,3},{3,0},{4,5},{5,6},{6,7},{7,4},{8,9},{9,10},{10,1... | collective-permute-start | bytes 1081352 | tf_op jit(solution)/shard_map/ppermute | solution.py:290
  81.2 1.8 %copy-start.8 = (bf16[11,64,256]{2,1,0:T(8,128)(2,1)}, bf16[11,64,256]{2,1,0:T(8,128)(2,1)S(1)}, u32[]{:S(2)}) copy-start(bf16[11,64,256]{2,1,0:T(8,128)(2,1)S(1)} %collective-permute-done.13.refs_2_) | copy-start | bytes 1081348
  86.0 6.6 %collective-permute-start.17 = (bf16[11,64,256]{2,1,0:T(8,128)(2,1)}, bf16[11,64,256]{2,1,0:T(8,128)(2,1)S(1)}, u32[]{:S(2)}, u32[]{:S(2)}) collective-permute-start(bf16[11,64,256]{2,1,0:T(8,128)(2,1)} %add.15.refs_4_), channel_id=1, source_target_pairs={{0,3},{1,0},{2,1},{3,2},{4,7},{5,4},{6,5},{7,6},{8,11},{9,8},{10,9... | collective-permute-start | bytes 1081352 | tf_op jit(solution)/shard_map/ppermute | solution.py:290
  86.7 8.1 %collective-permute-start.16 = (bf16[11,64,256]{2,1,0:T(8,128)(2,1)}, bf16[11,64,256]{2,1,0:T(8,128)(2,1)S(1)}, u32[]{:S(2)}, u32[]{:S(2)}) collective-permute-start(bf16[11,64,256]{2,1,0:T(8,128)(2,1)} %add.15.refs_4_), channel_id=1, source_target_pairs={{0,2},{1,3},{2,0},{3,1},{4,6},{5,7},{6,4},{7,5},{8,10},{9,11},{10,... | collective-permute-start | bytes 1081352 | tf_op jit(solution)/shard_map/ppermute | solution.py:290
  89.3 9.6 %copy-start.11 = (bf16[11,64,256]{2,1,0:T(8,128)(2,1)}, bf16[11,64,256]{2,1,0:T(8,128)(2,1)S(1)}, u32[]{:S(2)}) copy-start(bf16[11,64,256]{2,1,0:T(8,128)(2,1)S(1)} %collective-permute-done.8.refs_3_) | copy-start | bytes 1081348
  89.3 9.6 %collective-permute-start.15 = (bf16[11,64,256]{2,1,0:T(8,128)(2,1)}, bf16[11,64,256]{2,1,0:T(8,128)(2,1)S(1)}, u32[]{:S(2)}, u32[]{:S(2)}) collective-permute-start(bf16[11,64,256]{2,1,0:T(8,128)(2,1)} %add.15.refs_4_), channel_id=1, source_target_pairs={{0,1},{1,2},{2,3},{3,0},{4,5},{5,6},{6,7},{7,4},{8,9},{9,10},{10,1... | collective-permute-start | bytes 1081352 | tf_op jit(solution)/shard_map/ppermute | solution.py:290
  89.9 8.9 %copy-start.12 = (bf16[11,64,256]{2,1,0:T(8,128)(2,1)}, bf16[11,64,256]{2,1,0:T(8,128)(2,1)S(1)}, u32[]{:S(2)}) copy-start(bf16[11,64,256]{2,1,0:T(8,128)(2,1)S(1)} %collective-permute-done.7.refs_2_) | copy-start | bytes 1081348
  90.9 7.9 %copy-start.13 = (bf16[11,64,256]{2,1,0:T(8,128)(2,1)}, bf16[11,64,256]{2,1,0:T(8,128)(2,1)S(1)}, u32[]{:S(2)}) copy-start(bf16[11,64,256]{2,1,0:T(8,128)(2,1)S(1)} %collective-permute-done.6.refs_1_) | copy-start | bytes 1081348
  92.6 6.3 %copy-start.14 = (bf16[11,64,256]{2,1,0:T(8,128)(2,1)}, bf16[11,64,256]{2,1,0:T(8,128)(2,1)S(1)}, u32[]{:S(2)}) copy-start(bf16[11,64,256]{2,1,0:T(8,128)(2,1)S(1)} %collective-permute-done.17.refs_7_) | copy-start | bytes 1081348
  94.8 4.1 %copy-start.15 = (bf16[11,64,256]{2,1,0:T(8,128)(2,1)}, bf16[11,64,256]{2,1,0:T(8,128)(2,1)S(1)}, u32[]{:S(2)}) copy-start(bf16[11,64,256]{2,1,0:T(8,128)(2,1)S(1)} %collective-permute-done.16.refs_6_) | copy-start | bytes 1081348
  145.2 7.4 %copy-start = (bf16[1536,256]{1,0:T(8,128)(2,1)S(1)}, bf16[1536,256]{1,0:T(8,128)(2,1)}, u32[]{:S(2)}) copy-start(bf16[1536,256]{1,0:T(8,128)(2,1)} %step.1) | copy-start | bytes 2359300
  147.9 25.5 %all-to-all-start.2 = ((bf16[16,96,256]{2,1,0:T(8,128)(2,1)}), bf16[16,96,256]{2,1,0:T(8,128)(2,1)S(1)}, u32[]{:S(2)}, u32[]{:S(2)}) async-start(bf16[16,96,256]{2,1,0:T(8,128)(2,1)} %get-tuple-element.27), calls=%async_computation.2 | async-start | bytes 1572864 | tf_op jit(solution)/shard_map/all_to_all | solution.py:321
  (8 other events, 6.9 us)

commit v4 on v3

v4 whole, which is shorter than its diff:
```python
import functools
import math

import jax
import jax.numpy as jnp
from jax import lax
from jax.experimental import pallas as pl
from jax.experimental.pallas import tpu as pltpu
from jax.sharding import PartitionSpec as P

MOST = 2
SIDE = 4
BLOCK = 256
PIECE = BLOCK // SIDE
VMEM_LIMIT = 56 * 1024 * 1024

VMEM = pl.BlockSpec(memory_space=pltpu.VMEM)
SMEM = pl.BlockSpec(memory_space=pltpu.SMEM)
ANY = pl.BlockSpec(memory_space=pl.ANY)


def params():
    return pltpu.CompilerParams(vmem_limit_bytes=VMEM_LIMIT)


def shape_of(*dims, dtype=jnp.bfloat16):
    return jax.ShapeDtypeStruct(dims, dtype)


def cost(flops, size):
    return pl.CostEstimate(flops=flops, bytes_accessed=size, transcendentals=0)


def part(at, size):
    return pl.ds(pl.multiple_of(lax.rem(at, SIDE) * size, size), size)


def pairs_of(rows):
    side = rows // BLOCK
    return [(i, j) for i in range(side) for j in range(i + 1)]


def move_all(moves, sems):
    copies = [pltpu.make_async_copy(a, b, sems.at[k]) for k, (a, b) in enumerate(moves)]
    for copy in copies:
        copy.start()
    for copy in copies:
        copy.wait()


def choose_all(moves, sems):
    copies = []
    for k, (choice, a, b, to) in enumerate(moves):
        yes = pltpu.make_async_copy(a, to, sems.at[k])
        no = pltpu.make_async_copy(b, to, sems.at[k])
        pl.when(choice)(yes.start)
        pl.when(jnp.logical_not(choice))(no.start)
        copies.append(yes)
    for copy in copies:
        copy.wait()


def group_at(spot_ref, away, other, planes):
    core = spot_ref[1]
    return 2 * lax.rem(spot_ref[0] + away, planes) + (1 - core if other else core)


def plan_kernel(owner_ref, spot_ref, grads_ref, table_ref, *refs):
    outs, empty_ref, sems = refs[:-2], refs[-2], refs[-1]
    count, planes = owner_ref.shape[0], len(outs)

    def clear(g, _):
        table_ref[1, g] = 0
        table_ref[2, g] = -1
        return 0

    lax.fori_loop(0, count, clear, 0)

    def first(e, _):
        g = owner_ref[e]
        seen = table_ref[1, g]
        table_ref[1, g] = seen + 1

        @pl.when(seen == 0)
        def _():
            table_ref[0, g] = e

        @pl.when(seen > 0)
        def _():
            table_ref[2, g] = e

        return 0

    lax.fori_loop(0, count, first, 0)

    def empties(g, n):
        none = table_ref[1, g] == 0

        @pl.when(none)
        def _():
            empty_ref[n] = g

        return n + none.astype(jnp.int32)

    lax.fori_loop(0, count, empties, 0)

    def second(g, n):
        e = table_ref[2, g]
        two = e >= 0

        @pl.when(two)
        def _():
            h = empty_ref[n]
            table_ref[2, g] = h
            table_ref[0, h] = e

        return n + two.astype(jnp.int32)

    lax.fori_loop(0, count, second, 0)
    moves = []
    for away in range(planes):
        for other in range(2):
            e = table_ref[0, group_at(spot_ref, away, other, planes)]
            moves.append((grads_ref.at[e], outs[away].at[other]))
    move_all(moves, sems)


def plan(owner, spot, grads):
    count, rows, cols = grads.shape
    planes = count // 2
    return pl.pallas_call(
        plan_kernel,
        out_shape=(shape_of(3, count, dtype=jnp.int32),) + (shape_of(2, rows, cols),) * planes,
        in_specs=[SMEM, SMEM, ANY],
        out_specs=(SMEM,) + (ANY,) * planes,
        scratch_shapes=[pltpu.SMEM((count,), jnp.int32), pltpu.SemaphoreType.DMA((count,))],
        compiler_params=params(),
        name="plan",
    )(owner, spot, grads)


def sort_kernel(*refs):
    ins, (own_ref, give_ref, sems) = refs[:-3], refs[-3:]
    moves = [(ref.at[0], own_ref.at[k]) for k, ref in enumerate(ins)]
    moves += [(ref.at[1], give_ref.at[k]) for k, ref in enumerate(ins)]
    move_all(moves, sems)


def sort(blocks):
    planes = len(blocks)
    _, rows, cols = blocks[0].shape
    return pl.pallas_call(
        sort_kernel,
        out_shape=(shape_of(planes, rows, cols),) * 2,
        in_specs=[ANY] * planes,
        out_specs=(ANY,) * 2,
        scratch_shapes=[pltpu.SemaphoreType.DMA((2 * planes,))],
        compiler_params=params(),
        name="sort",
    )(*blocks)


def split(number, shape):
    rest = jnp.broadcast_to(number, shape)
    row = lax.broadcasted_iota(jnp.int32, shape, 0)
    parts = jnp.zeros(shape, jnp.float32)
    for k in range(3):
        top = lax.reduce_precision(rest, 8, 7)
        parts = jnp.where(row == k, top, parts)
        rest = rest - top
    return parts.astype(jnp.bfloat16)


def gram_kernel(low, squares, place_ref, *refs):
    lists = [refs[k : k + SIDE] for k in range(0, len(refs) - 2, SIDE)]
    out_ref, picked = refs[-2:]
    each = lists[0][0].shape[0] // BLOCK
    side = each * len(lists)
    rows = part(place_ref[0], PIECE)

    def block(s, i):
        start = (i % each) * BLOCK
        return lists[i // each][s][start : start + BLOCK, :]

    for s in range(SIDE):
        for i in range(low, side):
            start = pl.multiple_of((i % each) * BLOCK + lax.rem(place_ref[0], SIDE) * PIECE, PIECE)
            picked[s, (i - low) * PIECE : (i - low + 1) * PIECE, :] = lists[i // each][s][
                pl.ds(start, PIECE), :
            ]
    index = {pair: t for t, pair in enumerate(p for p in pairs_of(side * BLOCK) if p[0] >= low)}
    for j in range(side):
        top = max(j, low)
        total = jnp.zeros(((side - top) * PIECE, BLOCK), jnp.float32)
        for s in range(SIDE):
            total = total + lax.dot_general(
                picked[s, (top - low) * PIECE :, :],
                block(s, j),
                (((1,), (1,)), ((), ())),
                preferred_element_type=jnp.float32,
            )
        total = total.astype(jnp.bfloat16)
        for i in range(top, side):
            out_ref[index[i, j]] = total[(i - top) * PIECE : (i - top + 1) * PIECE, :]
    if squares:
        total = jnp.zeros((1, BLOCK), jnp.float32)
        for i in range(side):
            values = block(0, i).astype(jnp.float32)
            total = total + jnp.sum(values * values, axis=0, keepdims=True)
        total = jnp.sum(total, axis=1, keepdims=True)
        out_ref[len(index)] = split(total, (PIECE, BLOCK))


def gram_quarter(place, lists, low, squares):
    side = len(lists) * lists[0][0].shape[0] // BLOCK
    blocks = len([p for p in pairs_of(side * BLOCK) if p[0] >= low])
    return pl.pallas_call(
        functools.partial(gram_kernel, low, squares),
        out_shape=shape_of(blocks + squares, PIECE, BLOCK),
        in_specs=[SMEM] + [VMEM] * (SIDE * len(lists)),
        out_specs=VMEM,
        scratch_shapes=[pltpu.VMEM((SIDE, (side - low) * PIECE, BLOCK), jnp.bfloat16)],
        compiler_params=params(),
        cost_estimate=cost(2 * blocks * BLOCK**3, 4 * 1024 * 1024),
        name="gram",
    )(place, *[x for xs in lists for x in xs])


def add_kernel(blocks, carried, *refs):
    ins, out = refs[:SIDE], refs[-1]
    total = ins[0][:blocks].astype(jnp.float32)
    for other in ins[1:]:
        total = total + other[:blocks].astype(jnp.float32)
    out[:blocks] = total.astype(jnp.bfloat16)
    if carried:
        number = jnp.zeros((1, BLOCK), jnp.float32)
        for piece in ins:
            number = number + jnp.sum(piece[blocks].astype(jnp.float32), axis=0, keepdims=True)
        out[blocks] = split(number, (PIECE, BLOCK))


def add(pieces, carried):
    blocks = pieces[0].shape[0] - carried
    return pl.pallas_call(
        functools.partial(add_kernel, blocks, carried),
        out_shape=shape_of(blocks + carried, PIECE, BLOCK),
        in_specs=[VMEM] * SIDE,
        out_specs=VMEM,
        compiler_params=params(),
        cost_estimate=cost(4 * blocks * PIECE * BLOCK, 4 * 1024 * 1024),
        name="add",
    )(*pieces)


def step_kernel(pairs, factor, planes, place_ref, own_ref, got_ref, *refs):
    early, late = refs[:SIDE], refs[SIDE : 2 * SIDE]
    outs, (gram, normed, left) = refs[2 * SIDE : -3], refs[-3:]
    half = own_ref.shape[0]
    blocks = early[0].shape[0]
    total = jnp.zeros((1, BLOCK), jnp.float32)
    for s in range(SIDE):
        total = total + jnp.sum(
            late[s][len(pairs) - blocks].astype(jnp.float32), axis=0, keepdims=True
        )
    inverse = 1.0 / jnp.sqrt(total / (2 * half) + 1e-06)
    scale = inverse * inverse
    side = 2 * half // BLOCK
    for k, ref in enumerate((own_ref, got_ref)):
        for i in range(half // BLOCK):
            values = ref[i * BLOCK : (i + 1) * BLOCK, :].astype(jnp.float32) * inverse
            normed[k * half + i * BLOCK : k * half + (i + 1) * BLOCK, :] = values.astype(
                jnp.bfloat16
            )
    for t, (i, j) in enumerate(pairs):
        source, u = (early, t) if t < blocks else (late, t - blocks)
        for s in range(SIDE):
            p = lax.rem(place_ref[0] - s + SIDE, SIDE)
            rows = pl.ds(pl.multiple_of(i * BLOCK + p * PIECE, PIECE), PIECE)
            values = source[s][u].astype(jnp.float32) * scale
            gram[rows, j * BLOCK : (j + 1) * BLOCK] = jnp.where(scale > 0, values, 0.0).astype(
                jnp.bfloat16
            )
    for i, j in pairs:
        if i != j:
            block = gram[i * BLOCK : (i + 1) * BLOCK, j * BLOCK : (j + 1) * BLOCK]
            gram[j * BLOCK : (j + 1) * BLOCK, i * BLOCK : (i + 1) * BLOCK] = block.T
    for i in range(side):
        rows = slice(i * BLOCK, (i + 1) * BLOCK)
        left[rows, :] = jnp.dot(
            gram[rows, :], normed[...], preferred_element_type=jnp.float32
        ).astype(jnp.bfloat16)
    each = half // planes
    for k in range(2):
        for away in range(0, planes, 2):
            rows = slice(k * half + away * each, k * half + (away + 2) * each)
            right = jnp.dot(gram[rows, :], left[...], preferred_element_type=jnp.float32)
            mixed = (
                3.4445 * normed[rows, :].astype(jnp.float32)
                - 4.775 * left[rows, :].astype(jnp.float32)
                + 2.0315 * right
            )
            values = (factor * mixed).astype(jnp.bfloat16)
            outs[away][k] = values[:each]
            outs[away + 1][k] = values[each:]


def step(place, own, got, early, late, factor, planes):
    half, cols = own.shape
    rows = 2 * half
    return pl.pallas_call(
        functools.partial(step_kernel, pairs_of(rows), factor, planes),
        out_shape=(shape_of(2, half // planes, cols),) * planes,
        in_specs=[SMEM] + [VMEM] * (2 + 2 * SIDE),
        out_specs=(VMEM,) * planes,
        scratch_shapes=[
            pltpu.VMEM((rows, rows), jnp.bfloat16),
            pltpu.VMEM((rows, cols), jnp.bfloat16),
            pltpu.VMEM((rows, cols), jnp.bfloat16),
        ],
        compiler_params=params(),
        cost_estimate=cost(4 * rows * rows * cols, 6 * 1024 * 1024),
        name="step",
    )(place, own, got, *early, *late)


def helper_of(table_ref, spot_ref, group, planes):
    helper = table_ref[2, group]
    there = helper >= 0
    helper = jnp.maximum(helper, 0)
    mine = jnp.logical_and(there, lax.rem(helper, 2) == spot_ref[1])
    return there, mine, lax.rem(lax.div(helper, 2) - spot_ref[0] + planes, planes)


def pick_kernel(planes, table_ref, spot_ref, *refs):
    ins = refs[:planes]
    mine_ref, give_ref, rest_ref, held, sems = refs[planes:]
    move_all([(ref, held.at[k]) for k, ref in enumerate(ins)], sems)
    moves = [(held.at[k, 1], rest_ref.at[k]) for k in range(planes)]
    for away in range(planes):
        for other, out in enumerate((mine_ref, give_ref)):
            group = group_at(spot_ref, away, other, planes)
            _, mine, up = helper_of(table_ref, spot_ref, group, planes)
            moves.append((held.at[jnp.where(mine, up, planes)], out.at[away]))
    held[planes] = jnp.zeros(held.shape[1:], held.dtype)
    move_all(moves, sems)


def pick(table, spot, back):
    planes = len(back)
    block = back[0].shape
    return pl.pallas_call(
        functools.partial(pick_kernel, planes),
        out_shape=(shape_of(planes, *block),) * 2 + (shape_of(planes, *block[1:]),),
        in_specs=[SMEM] * 2 + [ANY] * planes,
        out_specs=(ANY,) * 3,
        scratch_shapes=[
            pltpu.VMEM((planes + 1, *block), jnp.bfloat16),
            pltpu.SemaphoreType.DMA((3 * planes,)),
        ],
        compiler_params=params(),
        name="pick",
    )(table, spot, *back)


def merge_kernel(planes, table_ref, spot_ref, mine_ref, got_ref, *refs):
    outs, sems = refs[:planes], refs[planes]
    moves = []
    for away in range(planes):
        group = group_at(spot_ref, away, 0, planes)
        there, mine, _ = helper_of(table_ref, spot_ref, group, planes)
        here = jnp.logical_or(mine, jnp.logical_not(there))
        for k in range(2):
            moves.append((here, mine_ref.at[away, k], got_ref.at[away, 1 - k], outs[away].at[k]))
    choose_all(moves, sems)


def merge(table, spot, mine, got):
    planes = mine.shape[0]
    return pl.pallas_call(
        functools.partial(merge_kernel, planes),
        out_shape=(shape_of(*mine.shape[1:]),) * planes,
        in_specs=[SMEM] * 2 + [ANY] * 2,
        out_specs=(ANY,) * planes,
        scratch_shapes=[pltpu.SemaphoreType.DMA((2 * planes,))],
        compiler_params=params(),
        name="merge",
    )(table, spot, mine, got)


def update_kernel(planes, table_ref, spot_ref, *refs):
    ins, rest_ref, out_ref, sems = refs[:planes], *refs[planes:]
    moves = []
    for away in range(planes):
        e = table_ref[0, group_at(spot_ref, away, 0, planes)]
        moves.append((ins[away].at[0], out_ref.at[e]))
        e = table_ref[0, group_at(spot_ref, away, 1, planes)]
        moves.append((rest_ref.at[away], out_ref.at[e]))
    move_all(moves, sems)


def update_of(table, spot, back, rest):
    planes, rows, cols = rest.shape
    return pl.pallas_call(
        functools.partial(update_kernel, planes),
        out_shape=shape_of(2 * planes, rows, cols),
        in_specs=[SMEM] * 2 + [ANY] * (planes + 1),
        out_specs=ANY,
        scratch_shapes=[pltpu.SemaphoreType.DMA((2 * planes,))],
        compiler_params=params(),
        name="update",
    )(table, spot, *back, rest)


def slot_moves(spot_ref, ins, out_ref, slot):
    planes = len(ins)
    moves = []
    for away, ref in enumerate(ins):
        for k in range(2):
            rows = ref.shape[1]
            start = group_at(spot_ref, planes - away, k, planes) * rows
            to = out_ref.at[slot, pl.ds(pl.multiple_of(start, rows), rows)]
            moves.append((ref.at[k], to))
    return moves


def first_kernel(planes, table_ref, spot_ref, *refs):
    ins, out_ref, zero, sems = refs[:planes], *refs[planes:]
    zero[...] = jnp.zeros(zero.shape, zero.dtype)
    owns = table_ref[1, group_at(spot_ref, 0, 0, planes)] > 0
    moves = slot_moves(spot_ref, ins, out_ref, 0)
    choose_all([(owns, a, zero, b) for a, b in moves], sems)


def second_kernel(planes, spot_ref, *refs):
    ins, _, out_ref, sems = refs[:planes], *refs[planes:]
    move_all(slot_moves(spot_ref, ins, out_ref, 1), sems)


def first_slot(table, spot, done):
    planes = len(done)
    _, rows, cols = done[0].shape
    return pl.pallas_call(
        functools.partial(first_kernel, planes),
        out_shape=shape_of(MOST, 2 * planes * rows, cols),
        in_specs=[SMEM] * 2 + [ANY] * planes,
        out_specs=ANY,
        scratch_shapes=[
            pltpu.VMEM((rows, cols), jnp.bfloat16),
            pltpu.SemaphoreType.DMA((2 * planes,)),
        ],
        compiler_params=params(),
        name="first_slot",
    )(table, spot, *done)


def second_slot(spot, came, owned):
    planes = len(came)
    return pl.pallas_call(
        functools.partial(second_kernel, planes),
        out_shape=shape_of(*owned.shape),
        in_specs=[SMEM] + [ANY] * (planes + 1),
        out_specs=ANY,
        scratch_shapes=[pltpu.SemaphoreType.DMA((2 * planes,))],
        input_output_aliases={planes + 1: 0},
        compiler_params=params(),
        name="second_slot",
    )(spot, *came, owned)


def spread(value, order):
    groups, places = lax.axis_size("fsdp"), SIDE * SIDE
    got = [value] * SIDE
    for amount in (1, 3, 2):
        moves = []
        for at in range(groups * places):
            group, place = divmod(at, places)
            y, x = divmod(place, SIDE)
            if group % 2 == order:
                x = (x + amount) % SIDE
            else:
                y = (y + amount) % SIDE
            moves.append((at, group * places + y * SIDE + x))
        got[amount] = lax.ppermute(value, ("fsdp", "grp"), moves)
    return got


def over_planes(blocks, sign):
    planes = len(blocks)
    got = list(blocks)
    for away in sorted(range(1, planes), key=lambda a: -min(a, planes - a)):
        moves = []
        for group in range(2 * planes):
            plane, core = divmod(group, 2)
            moves.append((group, 2 * ((plane + sign * away) % planes) + core))
        got[away] = lax.ppermute(blocks[away], "fsdp", moves)
    return got


def swap(value):
    groups = lax.axis_size("fsdp")
    return lax.ppermute(value, "fsdp", [(g, g ^ 1) for g in range(groups)])


def on_device(grads, owner):
    count, rows_dev, cols_dev = grads.shape
    groups = lax.axis_size("fsdp")
    planes = groups // 2
    rows = rows_dev * groups
    cols = cols_dev * lax.axis_size("grp")
    factor = 0.2 * math.sqrt(max(rows, cols))
    at = lax.axis_index("grp")
    me = lax.axis_index("fsdp")
    along = jnp.stack([lax.rem(at, SIDE), lax.div(at, SIDE)]).astype(jnp.int32)
    place = jnp.where(lax.rem(me, 2) == 0, along, along[::-1])
    spot = jnp.stack([lax.div(me, 2), lax.rem(me, 2)]).astype(jnp.int32)
    table, *sends = plan(owner, spot, grads)
    own, give = sort(over_planes(sends, 1))
    got = swap(give)
    own, got = own.reshape(rows // 2, cols_dev), got.reshape(rows // 2, cols_dev)
    owns, gots = spread(own, 0), spread(got, 0)
    early = gram_quarter(place, [owns], 0, False)
    late = gram_quarter(place, [owns, gots], rows // 2 // BLOCK, True)
    early = add(spread(early, 1), False)
    late = add(spread(late, 1), True)
    done = step(place, own, got, spread(early, 0), spread(late, 0), factor, planes)
    back = over_planes(done, -1)
    mine, give, rest = pick(table, spot, back)
    sends = merge(table, spot, mine, swap(give))
    came = over_planes(sends, 1)
    update = update_of(table, spot, back, swap(rest))
    owned = second_slot(spot, came, first_slot(table, spot, done))
    return (update, owned)


def solution(mesh):
    return jax.shard_map(
        on_device,
        mesh=mesh,
        in_specs=(P(None, "fsdp", "grp"), P()),
        out_specs=(P(None, "fsdp", "grp"), P("fsdp", None, "grp")),
        check_vma=False,
    )
```

time: 175 us -> 319 us (1.82)
  Pallas kernels: 26.8 us -> 176 us
  blocking collectives: 39.1 us -> 0 us
  starting transfers between devices: 36.3 us -> 64 us
  local copies, waits for them, and re-layouts: 4.82 us -> 9.11 us
  waiting for transfers between devices: 63.1 us -> 66.9 us
    pallas_call x9 -> x12, Pallas kernels: 26.8 us -> 176 us  [the longest x1 27.1 us: plan(): pl.pallas_call(plan_kernel, out_shape=(shape_of(3, count, dtype=jnp.int32...]
    ppermute x18 -> x42, waiting for transfers between devices: 21.2 us -> 66.9 us  [the longest x18 36.5 us: spread(): got[amount] = lax.ppermute(value, ('fsdp', 'grp'), moves)]
    all_to_all x2 -> x0, waiting for transfers between devices: 41.9 us -> none  [the longest x1 21.8 us: on_device(): x = lax.all_to_all(packed, 'fsdp', split_axis=0, concat_axis=0, tiled=True)]
    ppermute x18 -> x42, starting transfers between devices: 22.8 us -> 64 us  [the longest x21 42.3 us: over_planes(): got[away] = lax.ppermute(blocks[away], 'fsdp', moves)]
    all_to_all x1 -> x0, blocking collectives: 39.1 us -> none  [on_device(): lax.all_to_all(done.reshape(count, rows_dev, cols_dev), 'fsdp', split_axi...]
    all_to_all x2 -> x0, starting transfers between devices: 13.5 us -> none  [the longest x1 9.99 us: on_device(): x = lax.all_to_all(packed, 'fsdp', split_axis=0, concat_axis=0, tiled=True)]
    unnamed x40 -> x84, local copies, waits for them, and re-layouts: 4.73 us -> 9.01 us
  transfers between devices with their start and end apart: 20 -> 42, of which waited for: 12 -> 17; matrix products, arithmetic and copies ran while one was open for 2% -> 0% of each run, Pallas kernels for 7% -> 27%
where the time goes in v4:
time: 319 us
  Pallas kernels  176 us (55%)
  waiting for transfers between devices  66.9 us (21%)
  starting transfers between devices  64 us (20%)
  local copies, waits for them, and re-layouts  9.11 us (3%)
    ppermute x21, starting transfers between devices, over_planes(): got[away] = lax.ppermute(blocks[away], 'fsdp', moves)  42.3 us
    ppermute x18, waiting for transfers between devices, spread(): got[amount] = lax.ppermute(value, ('fsdp', 'grp'), moves)  36.5 us
    ppermute x21, waiting for transfers between devices, over_planes(): got[away] = lax.ppermute(blocks[away], 'fsdp', moves)  28.3 us
    pallas_call x1, Pallas kernels, plan(): pl.pallas_call(plan_kernel, out_shape=(shape_of(3, count, dtype=jnp.int32...  27.1 us
    pallas_call x1, Pallas kernels, update_of(): pl.pallas_call(functools.partial(update_kernel, planes), out_shape=shape_...  25.8 us
    pallas_call x1, Pallas kernels, merge(): pl.pallas_call(functools.partial(merge_kernel, planes), out_shape=(shape_...  25.8 us
    pallas_call x1, Pallas kernels, first_slot(): pl.pallas_call(functools.partial(first_kernel, planes), out_shape=shape_o...  25.8 us
    pallas_call x1, Pallas kernels, second_slot(): pl.pallas_call(functools.partial(second_kernel, planes), out_shape=shape_...  25.7 us
  transfers between devices with their start and end apart: 42, of which 17 were waited for; matrix products, arithmetic and copies ran while one was open for 0% of the time, Pallas kernels for 27%

profile of v4, /device:TPU:1, one launch (start us, length us, event | category | flops | bytes accessed | tf_op | source)
XLA Modules:
  0.0 318.7 jit_solution(757229869108696436)
XLA Ops:
  1.3 27.1 %plan.1 = (s32[3,16]{1,0:T(4,128)}, bf16[2,96,256]{2,1,0:T(8,128)(2,1)}, bf16[2,96,256]{2,1,0:T(8,128)(2,1)}, bf16[2,96,256]{2,1,0:T(8,128)(2,1)}, bf16[2,96,256...) custom-call(s32[16]{0:T(128)} %owner_ref.1, ...), custom_call_target="tpu_custom_call" | custom-call | tf_op jit(solution)/shard_map/plan/pallas_call | solution.py:131
  28.4 2.5 collective-permute-start
  31.0 3.0 collective-permute-start.1
  33.9 3.8 %collective-permute-start.2 = (bf16[2,96,256]{2,1,0:T(8,128)(2,1)}, bf16[2,96,256]{2,1,0:T(8,128)(2,1)S(1)}, u32[]{:S(2)}, u32[]{:S(2)}) collective-permute-start(bf16[2,96,256]{2,1,0:T(8,128)(2,1)} %get-tuple-element.36), channel_id=1, source_target_pairs={{0,96},{16,112},{32,128},{48,144},{64,160},{80,176},{96,192},{112,... | collective-permute-start | bytes 294920 | tf_op jit(solution)/shard_map/ppermute | solution.py:495
  38.2 4.5 %collective-permute-start.4 = (bf16[2,96,256]{2,1,0:T(8,128)(2,1)}, bf16[2,96,256]{2,1,0:T(8,128)(2,1)S(1)}, u32[]{:S(2)}, u32[]{:S(2)}) collective-permute-start(bf16[2,96,256]{2,1,0:T(8,128)(2,1)} %get-tuple-element.38), channel_id=1, source_target_pairs={{0,160},{16,176},{32,192},{48,208},{64,224},{80,240},{96,0},{112,1... | collective-permute-start | bytes 294920 | tf_op jit(solution)/shard_map/ppermute | solution.py:495
  42.6 2.4 collective-permute-start.5
  51.3 6.5 %collective-permute-done.5.refs_6_ = bf16[2,96,256]{2,1,0:T(8,128)(2,1)S(1)} collective-permute-done((bf16[2,96,256]{2,1,0:T(8,128)(2,1)}, bf16[2,96,256]{2,1,0:T(8,128)(2,1)S(1)}, u32[]{:S(2)}, u32[]{:S(2)}) %collective-permute-start.5) | collective-permute-done | bytes 98336 | tf_op jit(solution)/shard_map/ppermute | solution.py:495
  59.2 25.1 %sort.1 = (bf16[8,96,256]{2,1,0:T(8,128)(2,1)}, bf16[8,96,256]{2,1,0:T(8,128)(2,1)}) custom-call(bf16[2,96,256]{2,1,0:T(8,128)(2,1)} %get-tuple-element.33.refs_0_, bf16[2,96,256]{2,1,0:T(8,128)(2,1)} %copy-done.22, bf16[2,96,256]{2,1,0:T(8,128)(2,1)} %copy-done.23, bf16[2,96,256]{2,1,0:T(8,128)(2,1)} %copy-done.24, bf16[2,96,256]{2,1,0:T(8,128)(2,1)} %copy-done.25, ...), custom_call_target="tpu_custom_call" | custom-call | tf_op jit(solution)/shard_map/sort/pallas_call | solution.py:152
  86.3 2.6 collective-permute-start.9
  95.7 3.1 collective-permute-done.9.refs_2_
  98.9 3.5 %collective-permute-done.17.refs_5_ = bf16[768,256]{1,0:T(8,128)(2,1)S(1)} collective-permute-done((bf16[768,256]{1,0:T(8,128)(2,1)S(1)}, bf16[768,256]{1,0:T(8,128)(2,1)S(1)}, u32[]{:S(2)}, u32[]{:S(2)}) %collective-permute-start.17) | collective-permute-done | bytes 393248 | tf_op jit(solution)/shard_map/ppermute | solution.py:483
  102.4 4.9 %collective-permute-done.18.refs_6_ = bf16[768,256]{1,0:T(8,128)(2,1)S(1)} collective-permute-done((bf16[768,256]{1,0:T(8,128)(2,1)S(1)}, bf16[768,256]{1,0:T(8,128)(2,1)S(1)}, u32[]{:S(2)}, u32[]{:S(2)}) %collective-permute-start.18) | collective-permute-done | bytes 393248 | tf_op jit(solution)/shard_map/ppermute | solution.py:483
  108.8 3.8 %gram.3.refs_0_ = bf16[16,64,256]{2,1,0:T(8,128)(2,1)} custom-call(s32[2]{0:T(128)} %broadcast_select_fusion.place_ref, bf16[768,256]{1,0:T(8,128)(2,1)} %bitcast.9, bf16[768,256]{1,0:T(8,128)(2,1)} %copy-done, bf16[768,256]{1,0:T(8,128)(2,1)} %copy-done.1, bf16[768,256]{1,0:T(8,128)(2,1)} %copy-done.2, bf16[768,256]{1,0:T(8,128)(2,1)} %bitcast.15, ...), custom_call_target="tpu_custom_call" | custom-call | flops 503316480 | bytes 4194304 | tf_op jit(solution)/shard_map/gram/pallas_call | solution.py:217
  113.5 2.4 collective-permute-start.21
  117.1 2.7 gram.2.refs_0_
  123.3 5.4 %collective-permute-done.21.refs_2_ = bf16[16,64,256]{2,1,0:T(8,128)(2,1)S(1)} collective-permute-done((bf16[16,64,256]{2,1,0:T(8,128)(2,1)}, bf16[16,64,256]{2,1,0:T(8,128)(2,1)S(1)}, u32[]{:S(2)}, u32[]{:S(2)}) %collective-permute-start.21) | collective-permute-done | bytes 524320 | tf_op jit(solution)/shard_map/ppermute | solution.py:483
  130.2 2.6 add.9.refs_4_
  141.3 11.1 %collective-permute-done.14.refs_1_ = bf16[6,64,256]{2,1,0:T(8,128)(2,1)S(1)} collective-permute-done((bf16[6,64,256]{2,1,0:T(8,128)(2,1)}, bf16[6,64,256]{2,1,0:T(8,128)(2,1)S(1)}, u32[]{:S(2)}, u32[]{:S(2)}) %collective-permute-start.14) | collective-permute-done | bytes 196640 | tf_op jit(solution)/shard_map/ppermute | solution.py:483
  152.4 5.0 %collective-permute-done.16.refs_3_ = bf16[6,64,256]{2,1,0:T(8,128)(2,1)S(1)} collective-permute-done((bf16[6,64,256]{2,1,0:T(8,128)(2,1)}, bf16[6,64,256]{2,1,0:T(8,128)(2,1)S(1)}, u32[]{:S(2)}, u32[]{:S(2)}) %collective-permute-start.16) | collective-permute-done | bytes 196640 | tf_op jit(solution)/shard_map/ppermute | solution.py:483
  159.2 6.4 %step.1 = (bf16[2,96,256]{2,1,0:T(8,128)(2,1)}, bf16[2,96,256]{2,1,0:T(8,128)(2,1)}, bf16[2,96,256]{2,1,0:T(8,128)(2,1)}, bf16[2,96,256]{2,1,0:T(8,128)(2,1)}, b...) custom-call(s32[2]{0:T(128)} %broadcast_select_fusion.place_ref, ...), custom_call_target="tpu_custom_call" | custom-call | flops 2415919104 | bytes 6291456 | tf_op jit(solution)/shard_map/step/pallas_call | solution.py:310
  165.7 2.4 collective-permute-start.26
  168.2 3.4 %collective-permute-start.28 = (bf16[2,96,256]{2,1,0:T(8,128)(2,1)}, bf16[2,96,256]{2,1,0:T(8,128)(2,1)S(1)}, u32[]{:S(2)}, u32[]{:S(2)}) collective-permute-start(bf16[2,96,256]{2,1,0:T(8,128)(2,1)} %get-tuple-element.46.refs_3_), channel_id=1, source_target_pairs={{0,160},{16,176},{32,192},{48,208},{64,224},{80,240},{96,0},{112,1... | collective-permute-start | bytes 294920 | tf_op jit(solution)/shard_map/ppermute | solution.py:495
  178.0 2.4 collective-permute-done.29.refs_4_
  180.4 8.0 %collective-permute-done.30.refs_5_ = bf16[2,96,256]{2,1,0:T(8,128)(2,1)S(1)} collective-permute-done((bf16[2,96,256]{2,1,0:T(8,128)(2,1)}, bf16[2,96,256]{2,1,0:T(8,128)(2,1)S(1)}, u32[]{:S(2)}, u32[]{:S(2)}) %collective-permute-start.30) | collective-permute-done | bytes 98336 | tf_op jit(solution)/shard_map/ppermute | solution.py:495
  188.5 5.0 %collective-permute-done.32.refs_7_ = bf16[2,96,256]{2,1,0:T(8,128)(2,1)S(1)} collective-permute-done((bf16[2,96,256]{2,1,0:T(8,128)(2,1)}, bf16[2,96,256]{2,1,0:T(8,128)(2,1)S(1)}, u32[]{:S(2)}, u32[]{:S(2)}) %collective-permute-start.32) | collective-permute-done | bytes 98336 | tf_op jit(solution)/shard_map/ppermute | solution.py:495
  194.2 3.4 %pick.1 = (bf16[8,2,96,256]{3,2,1,0:T(8,128)(2,1)}, bf16[8,2,96,256]{3,2,1,0:T(8,128)(2,1)}, bf16[8,96,256]{2,1,0:T(8,128)(2,1)}) custom-call(s32[3,16]{1,0:T(4,128)} %get-tuple-element.32.table_ref, s32[2]{0:T(128)} %pad_add_fusion.spot_ref, bf16[2,96,256]{2,1,0:T(8,128)(2,1)} %get-tuple-element.43.refs_0_, bf16[2,96,256]{2,1,0:T(8,128)(2,1)} %copy-done.7, ...), custom_call_target="tpu_custom_call" | custom-call | tf_op jit(solution)/shard_map/pick/pallas_call | solution.py:351
  201.8 25.8 %merge.1 = (bf16[2,96,256]{2,1,0:T(8,128)(2,1)}, bf16[2,96,256]{2,1,0:T(8,128)(2,1)}, bf16[2,96,256]{2,1,0:T(8,128)(2,1)}, bf16[2,96,256]{2,1,0:T(8,128)(2,1)}, ...) custom-call(s32[3,16]{1,0:T(4,128)} %get-tuple-element.32.table_ref,, ...), custom_call_target="tpu_custom_call" | custom-call | tf_op jit(solution)/shard_map/merge/pallas_call | solution.py:379
  229.0 2.4 collective-permute-start.37
  235.7 2.7 collective-permute-start.40
  240.4 25.8 %first_slot.1.refs_8_ = bf16[2,1536,256]{2,1,0:T(8,128)(2,1)} custom-call(s32[3,16]{1,0:T(4,128)} %get-tuple-element.32.table_ref, s32[2]{0:T(128)} %pad_add_fusion.spot_ref, bf16[2,96,256]{2,1,0:T(8,128)(2,1)} %get-tuple-element.43.refs_0_, bf16[2,96,256]{2,1,0:T(8,128)(2,1)} %get-tuple-element.44.refs_1_, bf16[2,96,256]{2,1,0:T(8,128)(2,1)} %get-tuple-element.45.refs_2_, ...), custom_call_target="tpu_custom_call" | custom-call | tf_op jit(solution)/shard_map/first_slot/pallas_call | solution.py:442
  266.2 25.8 %update.1 = bf16[16,96,256]{2,1,0:T(8,128)(2,1)} custom-call(s32[3,16]{1,0:T(4,128)} %get-tuple-element.32.table_ref, s32[2]{0:T(128)} %pad_add_fusion.spot_ref, bf16[2,96,256]{2,1,0:T(8,128)(2,1)} %get-tuple-element.43.refs_0_, bf16[2,96,256]{2,1,0:T(8,128)(2,1)} %copy-done.7, bf16[2,96,256]{2,1,0:T(8,128)(2,1)} %copy-done.8, ...), custom_call_target="tpu_custom_call" | custom-call | tf_op jit(solution)/shard_map/update/pallas_call | solution.py:403
  292.8 25.7 %second_slot.1 = bf16[2,1536,256]{2,1,0:T(8,128)(2,1)} custom-call(s32[2]{0:T(128)} %pad_add_fusion.spot_ref, bf16[2,96,256]{2,1,0:T(8,128)(2,1)} %get-tuple-element.54.refs_0_, bf16[2,96,256]{2,1,0:T(8,128)(2,1)} %copy-done.29, bf16[2,96,256]{2,1,0:T(8,128)(2,1)} %copy-done.30, bf16[2,96,256]{2,1,0:T(8,128)(2,1)} %copy-done.31, ...), custom_call_target="tpu_custom_call", output_to_operand_aliasing={{}: (9, {})} | custom-call | tf_op jit(solution)/shard_map/second_slot/pallas_call | solution.py:458
  (152 shorter events, 56.3 us)
Async XLA Ops:
  28.4 14.2 %collective-permute-start = (bf16[2,96,256]{2,1,0:T(8,128)(2,1)}, bf16[2,96,256]{2,1,0:T(8,128)(2,1)S(1)}, u32[]{:S(2)}, u32[]{:S(2)}) collective-permute-start(bf16[2,96,256]{2,1,0:T(8,128)(2,1)} %get-tuple-element.34), channel_id=1, source_target_pairs={{0,32},{16,48},{32,64},{48,80},{64,96},{80,112},{96,128},{112,144}... | collective-permute-start | bytes 294920 | tf_op jit(solution)/shard_map/ppermute | solution.py:495
  31.0 14.1 %collective-permute-start.1 = (bf16[2,96,256]{2,1,0:T(8,128)(2,1)}, bf16[2,96,256]{2,1,0:T(8,128)(2,1)S(1)}, u32[]{:S(2)}, u32[]{:S(2)}) collective-permute-start(bf16[2,96,256]{2,1,0:T(8,128)(2,1)} %get-tuple-element.35), channel_id=1, source_target_pairs={{0,64},{16,80},{32,96},{48,112},{64,128},{80,144},{96,160},{112,17... | collective-permute-start | bytes 294920 | tf_op jit(solution)/shard_map/ppermute | solution.py:495
  33.9 14.0 %collective-permute-start.2 = (bf16[2,96,256]{2,1,0:T(8,128)(2,1)}, bf16[2,96,256]{2,1,0:T(8,128)(2,1)S(1)}, u32[]{:S(2)}, u32[]{:S(2)}) collective-permute-start(bf16[2,96,256]{2,1,0:T(8,128)(2,1)} %get-tuple-element.36), channel_id=1, source_target_pairs={{0,96},{16,112},{32,128},{48,144},{64,160},{80,176},{96,192},{112,... | collective-permute-start | bytes 294920 | tf_op jit(solution)/shard_map/ppermute | solution.py:495
  37.7 12.5 %collective-permute-start.3 = (bf16[2,96,256]{2,1,0:T(8,128)(2,1)}, bf16[2,96,256]{2,1,0:T(8,128)(2,1)S(1)}, u32[]{:S(2)}, u32[]{:S(2)}) collective-permute-start(bf16[2,96,256]{2,1,0:T(8,128)(2,1)} %get-tuple-element.37), channel_id=1, source_target_pairs={{0,128},{16,144},{32,160},{48,176},{64,192},{80,208},{96,224},{112... | collective-permute-start | bytes 294920 | tf_op jit(solution)/shard_map/ppermute | solution.py:495
  38.2 13.1 %collective-permute-start.4 = (bf16[2,96,256]{2,1,0:T(8,128)(2,1)}, bf16[2,96,256]{2,1,0:T(8,128)(2,1)S(1)}, u32[]{:S(2)}, u32[]{:S(2)}) collective-permute-start(bf16[2,96,256]{2,1,0:T(8,128)(2,1)} %get-tuple-element.38), channel_id=1, source_target_pairs={{0,160},{16,176},{32,192},{48,208},{64,224},{80,240},{96,0},{112,1... | collective-permute-start | bytes 294920 | tf_op jit(solution)/shard_map/ppermute | solution.py:495
  42.6 15.1 %collective-permute-start.5 = (bf16[2,96,256]{2,1,0:T(8,128)(2,1)}, bf16[2,96,256]{2,1,0:T(8,128)(2,1)S(1)}, u32[]{:S(2)}, u32[]{:S(2)}) collective-permute-start(bf16[2,96,256]{2,1,0:T(8,128)(2,1)} %get-tuple-element.39), channel_id=1, source_target_pairs={{0,192},{16,208},{32,224},{48,240},{64,0},{80,16},{96,32},{112,48}... | collective-permute-start | bytes 294920 | tf_op jit(solution)/shard_map/ppermute | solution.py:495
  45.0 13.5 %collective-permute-start.6 = (bf16[2,96,256]{2,1,0:T(8,128)(2,1)}, bf16[2,96,256]{2,1,0:T(8,128)(2,1)S(1)}, u32[]{:S(2)}, u32[]{:S(2)}) collective-permute-start(bf16[2,96,256]{2,1,0:T(8,128)(2,1)} %get-tuple-element.40), channel_id=1, source_target_pairs={{0,224},{16,240},{32,0},{48,16},{64,32},{80,48},{96,64},{112,80},{... | collective-permute-start | bytes 294920 | tf_op jit(solution)/shard_map/ppermute | solution.py:495
  86.3 12.5 %collective-permute-start.9 = (bf16[768,256]{1,0:T(8,128)(2,1)}, bf16[768,256]{1,0:T(8,128)(2,1)S(1)}, u32[]{:S(2)}, u32[]{:S(2)}) collective-permute-start(bf16[768,256]{1,0:T(8,128)(2,1)} %bitcast.7), channel_id=1, source_target_pairs={{0,2},{1,3},{2,0},{3,1},{4,6},{5,7},{6,4},{7,5},{8,10},{9,11},{10,... | collective-permute-start | bytes 1179656 | tf_op jit(solution)/shard_map/ppermute | solution.py:483
  90.0 12.3 %collective-permute-start.17 = (bf16[768,256]{1,0:T(8,128)(2,1)S(1)}, bf16[768,256]{1,0:T(8,128)(2,1)S(1)}, u32[]{:S(2)}, u32[]{:S(2)}) collective-permute-start(bf16[768,256]{1,0:T(8,128)(2,1)S(1)} %bitcast.12), channel_id=1, source_target_pairs={{0,1},{1,2},{2,3},{3,0},{4,5},{5,6},{6,7},{7,4},{8,9},{9,10},{10,1... | collective-permute-start | bytes 1179656 | tf_op jit(solution)/shard_map/ppermute | solution.py:483
  90.4 16.9 %collective-permute-start.18 = (bf16[768,256]{1,0:T(8,128)(2,1)S(1)}, bf16[768,256]{1,0:T(8,128)(2,1)S(1)}, u32[]{:S(2)}, u32[]{:S(2)}) collective-permute-start(bf16[768,256]{1,0:T(8,128)(2,1)S(1)} %bitcast.13), channel_id=1, source_target_pairs={{0,2},{1,3},{2,0},{3,1},{4,6},{5,7},{6,4},{7,5},{8,10},{9,11},{10,... | collective-permute-start | bytes 1179656 | tf_op jit(solution)/shard_map/ppermute | solution.py:483
  93.4 13.9 %collective-permute-start.19 = (bf16[768,256]{1,0:T(8,128)(2,1)S(1)}, bf16[768,256]{1,0:T(8,128)(2,1)S(1)}, u32[]{:S(2)}, u32[]{:S(2)}) collective-permute-start(bf16[768,256]{1,0:T(8,128)(2,1)S(1)} %bitcast.14), channel_id=1, source_target_pairs={{0,3},{1,0},{2,1},{3,2},{4,7},{5,4},{6,5},{7,6},{8,11},{9,8},{10,9... | collective-permute-start | bytes 1179656 | tf_op jit(solution)/shard_map/ppermute | solution.py:483
  113.5 15.2 %collective-permute-start.21 = (bf16[16,64,256]{2,1,0:T(8,128)(2,1)}, bf16[16,64,256]{2,1,0:T(8,128)(2,1)S(1)}, u32[]{:S(2)}, u32[]{:S(2)}) collective-permute-start(bf16[16,64,256]{2,1,0:T(8,128)(2,1)} %gram.3.refs_0_), channel_id=1, source_target_pairs={{0,8},{1,9},{2,10},{3,11},{4,12},{5,13},{6,14},{7,15},{8,0},{9,1},... | collective-permute-start | bytes 1572872 | tf_op jit(solution)/shard_map/ppermute | solution.py:483
  115.9 12.7 %collective-permute-start.22 = (bf16[16,64,256]{2,1,0:T(8,128)(2,1)}, bf16[16,64,256]{2,1,0:T(8,128)(2,1)S(1)}, u32[]{:S(2)}, u32[]{:S(2)}) collective-permute-start(bf16[16,64,256]{2,1,0:T(8,128)(2,1)} %gram.3.refs_0_), channel_id=1, source_target_pairs={{0,12},{1,13},{2,14},{3,15},{4,0},{5,1},{6,2},{7,3},{8,4},{9,5},{1... | collective-permute-start | bytes 1572872 | tf_op jit(solution)/shard_map/ppermute | solution.py:483
  119.7 15.4 %collective-permute-start.11 = (bf16[6,64,256]{2,1,0:T(8,128)(2,1)}, bf16[6,64,256]{2,1,0:T(8,128)(2,1)S(1)}, u32[]{:S(2)}, u32[]{:S(2)}) collective-permute-start(bf16[6,64,256]{2,1,0:T(8,128)(2,1)} %gram.2.refs_0_), channel_id=1, source_target_pairs={{0,4},{1,5},{2,6},{3,7},{4,8},{5,9},{6,10},{7,11},{8,12},{9,13},{1... | collective-permute-start | bytes 589832 | tf_op jit(solution)/shard_map/ppermute | solution.py:483
  120.0 16.5 %collective-permute-start.12 = (bf16[6,64,256]{2,1,0:T(8,128)(2,1)}, bf16[6,64,256]{2,1,0:T(8,128)(2,1)S(1)}, u32[]{:S(2)}, u32[]{:S(2)}) collective-permute-start(bf16[6,64,256]{2,1,0:T(8,128)(2,1)} %gram.2.refs_0_), channel_id=1, source_target_pairs={{0,8},{1,9},{2,10},{3,11},{4,12},{5,13},{6,14},{7,15},{8,0},{9,1},... | collective-permute-start | bytes 589832 | tf_op jit(solution)/shard_map/ppermute | solution.py:483
  122.3 14.3 %collective-permute-start.13 = (bf16[6,64,256]{2,1,0:T(8,128)(2,1)}, bf16[6,64,256]{2,1,0:T(8,128)(2,1)S(1)}, u32[]{:S(2)}, u32[]{:S(2)}) collective-permute-start(bf16[6,64,256]{2,1,0:T(8,128)(2,1)} %gram.2.refs_0_), channel_id=1, source_target_pairs={{0,12},{1,13},{2,14},{3,15},{4,0},{5,1},{6,2},{7,3},{8,4},{9,5},{1... | collective-permute-start | bytes 589832 | tf_op jit(solution)/shard_map/ppermute | solution.py:483
  132.8 24.6 %collective-permute-start.23 = (bf16[16,64,256]{2,1,0:T(8,128)(2,1)}, bf16[16,64,256]{2,1,0:T(8,128)(2,1)S(1)}, u32[]{:S(2)}, u32[]{:S(2)}) collective-permute-start(bf16[16,64,256]{2,1,0:T(8,128)(2,1)} %add.9.refs_4_), channel_id=1, source_target_pairs={{0,1},{1,2},{2,3},{3,0},{4,5},{5,6},{6,7},{7,4},{8,9},{9,10},{10,1... | collective-permute-start | bytes 1572872 | tf_op jit(solution)/shard_map/ppermute | solution.py:483
  133.5 23.9 %collective-permute-start.24 = (bf16[16,64,256]{2,1,0:T(8,128)(2,1)}, bf16[16,64,256]{2,1,0:T(8,128)(2,1)S(1)}, u32[]{:S(2)}, u32[]{:S(2)}) collective-permute-start(bf16[16,64,256]{2,1,0:T(8,128)(2,1)} %add.9.refs_4_), channel_id=1, source_target_pairs={{0,2},{1,3},{2,0},{3,1},{4,6},{5,7},{6,4},{7,5},{8,10},{9,11},{10,... | collective-permute-start | bytes 1572872 | tf_op jit(solution)/shard_map/ppermute | solution.py:483
  135.1 22.3 %collective-permute-start.25 = (bf16[16,64,256]{2,1,0:T(8,128)(2,1)}, bf16[16,64,256]{2,1,0:T(8,128)(2,1)S(1)}, u32[]{:S(2)}, u32[]{:S(2)}) collective-permute-start(bf16[16,64,256]{2,1,0:T(8,128)(2,1)} %add.9.refs_4_), channel_id=1, source_target_pairs={{0,3},{1,0},{2,1},{3,2},{4,7},{5,4},{6,5},{7,6},{8,11},{9,8},{10,9... | collective-permute-start | bytes 1572872 | tf_op jit(solution)/shard_map/ppermute | solution.py:483
  139.9 12.5 %collective-permute-start.14 = (bf16[6,64,256]{2,1,0:T(8,128)(2,1)}, bf16[6,64,256]{2,1,0:T(8,128)(2,1)S(1)}, u32[]{:S(2)}, u32[]{:S(2)}) collective-permute-start(bf16[6,64,256]{2,1,0:T(8,128)(2,1)} %add.8.refs_0_), channel_id=1, source_target_pairs={{0,1},{1,2},{2,3},{3,0},{4,5},{5,6},{6,7},{7,4},{8,9},{9,10},{10,1... | collective-permute-start | bytes 589832 | tf_op jit(solution)/shard_map/ppermute | solution.py:483
  140.0 12.5 %collective-permute-start.15 = (bf16[6,64,256]{2,1,0:T(8,128)(2,1)}, bf16[6,64,256]{2,1,0:T(8,128)(2,1)S(1)}, u32[]{:S(2)}, u32[]{:S(2)}) collective-permute-start(bf16[6,64,256]{2,1,0:T(8,128)(2,1)} %add.8.refs_0_), channel_id=1, source_target_pairs={{0,2},{1,3},{2,0},{3,1},{4,6},{5,7},{6,4},{7,5},{8,10},{9,11},{10,... | collective-permute-start | bytes 589832 | tf_op jit(solution)/shard_map/ppermute | solution.py:483
  165.7 10.1 %collective-permute-start.26 = (bf16[2,96,256]{2,1,0:T(8,128)(2,1)}, bf16[2,96,256]{2,1,0:T(8,128)(2,1)S(1)}, u32[]{:S(2)}, u32[]{:S(2)}) collective-permute-start(bf16[2,96,256]{2,1,0:T(8,128)(2,1)} %get-tuple-element.44.refs_1_), channel_id=1, source_target_pairs={{0,224},{16,240},{32,0},{48,16},{64,32},{80,48},{96,64},{112,80},{... | collective-permute-start | bytes 294920 | tf_op jit(solution)/shard_map/ppermute | solution.py:495
  173.8 14.7 %collective-permute-start.30 = (bf16[2,96,256]{2,1,0:T(8,128)(2,1)}, bf16[2,96,256]{2,1,0:T(8,128)(2,1)S(1)}, u32[]{:S(2)}, u32[]{:S(2)}) collective-permute-start(bf16[2,96,256]{2,1,0:T(8,128)(2,1)} %get-tuple-element.48.refs_5_), channel_id=1, source_target_pairs={{0,96},{16,112},{32,128},{48,144},{64,160},{80,176},{96,192},{112,... | collective-permute-start | bytes 294920 | tf_op jit(solution)/shard_map/ppermute | solution.py:495
  175.8 12.6 %collective-permute-start.31 = (bf16[2,96,256]{2,1,0:T(8,128)(2,1)}, bf16[2,96,256]{2,1,0:T(8,128)(2,1)S(1)}, u32[]{:S(2)}, u32[]{:S(2)}) collective-permute-start(bf16[2,96,256]{2,1,0:T(8,128)(2,1)} %get-tuple-element.49.refs_6_), channel_id=1, source_target_pairs={{0,64},{16,80},{32,96},{48,112},{64,128},{80,144},{96,160},{112,17... | collective-permute-start | bytes 294920 | tf_op jit(solution)/shard_map/ppermute | solution.py:495
  177.9 15.6 %collective-permute-start.32 = (bf16[2,96,256]{2,1,0:T(8,128)(2,1)}, bf16[2,96,256]{2,1,0:T(8,128)(2,1)S(1)}, u32[]{:S(2)}, u32[]{:S(2)}) collective-permute-start(bf16[2,96,256]{2,1,0:T(8,128)(2,1)} %get-tuple-element.50.refs_7_), channel_id=1, source_target_pairs={{0,32},{16,48},{32,64},{48,80},{64,96},{80,112},{96,128},{112,144}... | collective-permute-start | bytes 294920 | tf_op jit(solution)/shard_map/ppermute | solution.py:495
  198.8 34.7 %collective-permute-start.33 = (bf16[8,96,256]{2,1,0:T(8,128)(2,1)}, bf16[8,96,256]{2,1,0:T(8,128)(2,1)S(1)}, u32[]{:S(2)}, u32[]{:S(2)}) collective-permute-start(bf16[8,96,256]{2,1,0:T(8,128)(2,1)} %get-tuple-element.51), channel_id=1, source_target_pairs={{0,16},{16,0},{32,48},{48,32},{64,80},{80,64},{96,112},{112,96},{1... | collective-permute-start | bytes 1179656 | tf_op jit(solution)/shard_map/ppermute | solution.py:501
  227.7 10.7 %collective-permute-start.36 = (bf16[2,96,256]{2,1,0:T(8,128)(2,1)}, bf16[2,96,256]{2,1,0:T(8,128)(2,1)S(1)}, u32[]{:S(2)}, u32[]{:S(2)}) collective-permute-start(bf16[2,96,256]{2,1,0:T(8,128)(2,1)} %get-tuple-element.56), channel_id=1, source_target_pairs={{0,64},{16,80},{32,96},{48,112},{64,128},{80,144},{96,160},{112,17... | collective-permute-start | bytes 294920 | tf_op jit(solution)/shard_map/ppermute | solution.py:495
  229.0 63.0 %collective-permute-start.37 = (bf16[2,96,256]{2,1,0:T(8,128)(2,1)}, bf16[2,96,256]{2,1,0:T(8,128)(2,1)S(1)}, u32[]{:S(2)}, u32[]{:S(2)}) collective-permute-start(bf16[2,96,256]{2,1,0:T(8,128)(2,1)} %get-tuple-element.57), channel_id=1, source_target_pairs={{0,96},{16,112},{32,128},{48,144},{64,160},{80,176},{96,192},{112,... | collective-permute-start | bytes 294920 | tf_op jit(solution)/shard_map/ppermute | solution.py:495
  231.4 60.7 %collective-permute-start.38 = (bf16[2,96,256]{2,1,0:T(8,128)(2,1)}, bf16[2,96,256]{2,1,0:T(8,128)(2,1)S(1)}, u32[]{:S(2)}, u32[]{:S(2)}) collective-permute-start(bf16[2,96,256]{2,1,0:T(8,128)(2,1)} %get-tuple-element.58), channel_id=1, source_target_pairs={{0,128},{16,144},{32,160},{48,176},{64,192},{80,208},{96,224},{112... | collective-permute-start | bytes 294920 | tf_op jit(solution)/shard_map/ppermute | solution.py:495
  233.5 58.6 %collective-permute-start.39 = (bf16[2,96,256]{2,1,0:T(8,128)(2,1)}, bf16[2,96,256]{2,1,0:T(8,128)(2,1)S(1)}, u32[]{:S(2)}, u32[]{:S(2)}) collective-permute-start(bf16[2,96,256]{2,1,0:T(8,128)(2,1)} %get-tuple-element.59), channel_id=1, source_target_pairs={{0,160},{16,176},{32,192},{48,208},{64,224},{80,240},{96,0},{112,1... | collective-permute-start | bytes 294920 | tf_op jit(solution)/shard_map/ppermute | solution.py:495
  235.7 56.3 %collective-permute-start.40 = (bf16[2,96,256]{2,1,0:T(8,128)(2,1)}, bf16[2,96,256]{2,1,0:T(8,128)(2,1)S(1)}, u32[]{:S(2)}, u32[]{:S(2)}) collective-permute-start(bf16[2,96,256]{2,1,0:T(8,128)(2,1)} %get-tuple-element.60), channel_id=1, source_target_pairs={{0,192},{16,208},{32,224},{48,240},{64,0},{80,16},{96,32},{112,48}... | collective-permute-start | bytes 294920 | tf_op jit(solution)/shard_map/ppermute | solution.py:495
  238.4 53.7 %collective-permute-start.41 = (bf16[2,96,256]{2,1,0:T(8,128)(2,1)}, bf16[2,96,256]{2,1,0:T(8,128)(2,1)S(1)}, u32[]{:S(2)}, u32[]{:S(2)}) collective-permute-start(bf16[2,96,256]{2,1,0:T(8,128)(2,1)} %get-tuple-element.61), channel_id=1, source_target_pairs={{0,224},{16,240},{32,0},{48,16},{64,32},{80,48},{96,64},{112,80},{... | collective-permute-start | bytes 294920 | tf_op jit(solution)/shard_map/ppermute | solution.py:495
  (52 other events, 434.2 us)

commit v5 on v4

v5 whole, which is shorter than its diff:
```python
import functools
import math

import jax
import jax.numpy as jnp
from jax import lax
from jax.experimental import pallas as pl
from jax.experimental.pallas import tpu as pltpu
from jax.sharding import PartitionSpec as P

MOST = 2
SIDE = 4
BLOCK = 256
PIECE = BLOCK // SIDE
MIB = 1024 * 1024

VMEM = pl.BlockSpec(memory_space=pltpu.VMEM)
SMEM = pl.BlockSpec(memory_space=pltpu.SMEM)
ANY = pl.BlockSpec(memory_space=pl.ANY)


def params(mib):
    return pltpu.CompilerParams(vmem_limit_bytes=mib * MIB)


def shape_of(*dims, dtype=jnp.bfloat16):
    return jax.ShapeDtypeStruct(dims, dtype)


def cost(flops, size):
    return pl.CostEstimate(flops=flops, bytes_accessed=size, transcendentals=0)


def part(at, size):
    return pl.ds(pl.multiple_of(lax.rem(at, SIDE) * size, size), size)


def pairs_of(rows):
    side = rows // BLOCK
    return [(i, j) for i in range(side) for j in range(i + 1)]


def move_all(moves, sems):
    copies = [pltpu.make_async_copy(a, b, sems.at[k]) for k, (a, b) in enumerate(moves)]
    for copy in copies:
        copy.start()
    for copy in copies:
        copy.wait()


def group_at(spot_ref, away, other, planes):
    core = spot_ref[1]
    return 2 * lax.rem(spot_ref[0] + away, planes) + (1 - core if other else core)


def plan_kernel(owner_ref, spot_ref, grads_ref, table_ref, *refs):
    outs, empty_ref = refs[:-1], refs[-1]
    count, planes = owner_ref.shape[0], len(outs)

    def clear(g, _):
        table_ref[1, g] = 0
        table_ref[2, g] = -1
        table_ref[3, g] = -1
        return 0

    lax.fori_loop(0, count, clear, 0)

    def first(e, _):
        g = owner_ref[e]
        seen = table_ref[1, g]
        table_ref[1, g] = seen + 1

        @pl.when(seen == 0)
        def _():
            table_ref[0, g] = e

        @pl.when(seen > 0)
        def _():
            table_ref[2, g] = e

        return 0

    lax.fori_loop(0, count, first, 0)

    def empties(g, n):
        none = table_ref[1, g] == 0

        @pl.when(none)
        def _():
            empty_ref[n] = g

        return n + none.astype(jnp.int32)

    lax.fori_loop(0, count, empties, 0)

    def second(g, n):
        e = table_ref[2, g]
        two = e >= 0

        @pl.when(two)
        def _():
            h = empty_ref[n]
            table_ref[2, g] = h
            table_ref[0, h] = e
            table_ref[3, h] = g

        return n + two.astype(jnp.int32)

    lax.fori_loop(0, count, second, 0)
    for away in range(planes):
        for other in range(2):
            outs[away][other] = grads_ref[table_ref[0, group_at(spot_ref, away, other, planes)]]


def plan(owner, spot, grads):
    count, rows, cols = grads.shape
    planes = count // 2
    return pl.pallas_call(
        plan_kernel,
        out_shape=(shape_of(4, count, dtype=jnp.int32),) + (shape_of(2, rows, cols),) * planes,
        in_specs=[SMEM, SMEM, VMEM],
        out_specs=(SMEM,) + (VMEM,) * planes,
        scratch_shapes=[pltpu.SMEM((count,), jnp.int32)],
        compiler_params=params(8),
        name="plan",
    )(owner, spot, grads)


def sort_kernel(*refs):
    ins, (own_ref, give_ref) = in_place(refs[:-2]), refs[-2:]
    for k, ref in enumerate(ins):
        own_ref[k] = ref[0]
        give_ref[k] = ref[1]


def sort(blocks):
    planes = len(blocks)
    _, rows, cols = blocks[0].shape
    return pl.pallas_call(
        sort_kernel,
        out_shape=(shape_of(planes, rows, cols),) * 2,
        in_specs=[VMEM] * planes,
        out_specs=(VMEM,) * 2,
        compiler_params=params(8),
        name="sort",
    )(*in_turn(blocks))


def split(number, shape):
    rest = jnp.broadcast_to(number, shape)
    row = lax.broadcasted_iota(jnp.int32, shape, 0)
    parts = jnp.zeros(shape, jnp.float32)
    for k in range(3):
        top = lax.reduce_precision(rest, 8, 7)
        parts = jnp.where(row == k, top, parts)
        rest = rest - top
    return parts.astype(jnp.bfloat16)


def gram_kernel(place_ref, *refs):
    lists = in_lists(refs[: 2 * SIDE])
    *outs, picked = refs[2 * SIDE :]
    each = lists[0][0].shape[0] // BLOCK
    side = 2 * each
    turn = lax.rem(place_ref[0], SIDE) * PIECE

    def block(s, i):
        start = (i % each) * BLOCK
        return lists[i // each][s][start : start + BLOCK, :]

    for s in range(SIDE):
        for i in range(side):
            start = pl.multiple_of((i % each) * BLOCK + turn, PIECE)
            picked[s, i * PIECE : (i + 1) * PIECE, :] = lists[i // each][s][pl.ds(start, PIECE), :]
    index = {pair: t for t, pair in enumerate(pairs_of(side * BLOCK))}
    cut = outs[0].shape[0]
    for j in range(side):
        total = jnp.zeros(((side - j) * PIECE, BLOCK), jnp.float32)
        for s in range(SIDE):
            total = total + lax.dot_general(
                picked[s, j * PIECE :, :],
                block(s, j),
                (((1,), (1,)), ((), ())),
                preferred_element_type=jnp.float32,
            )
        total = total.astype(jnp.bfloat16)
        for i in range(j, side):
            t = index[i, j]
            outs[t // cut][t % cut] = total[(i - j) * PIECE : (i - j + 1) * PIECE, :]
    total = jnp.zeros((1, BLOCK), jnp.float32)
    for i in range(side):
        values = block(0, i).astype(jnp.float32)
        total = total + jnp.sum(values * values, axis=0, keepdims=True)
    total = jnp.sum(total, axis=1, keepdims=True)
    outs[1][outs[1].shape[0] - 1] = split(total, (PIECE, BLOCK))


def gram_quarter(place, lists):
    rows = 2 * lists[0][0].shape[0]
    blocks = len(pairs_of(rows))
    cut = (blocks + 1) // 2
    return pl.pallas_call(
        gram_kernel,
        out_shape=(shape_of(cut, PIECE, BLOCK), shape_of(blocks + 1 - cut, PIECE, BLOCK)),
        in_specs=[SMEM] + [VMEM] * (2 * SIDE),
        out_specs=(VMEM,) * 2,
        scratch_shapes=[pltpu.VMEM((SIDE, rows // SIDE, BLOCK), jnp.bfloat16)],
        compiler_params=params(16),
        cost_estimate=cost(2 * blocks * BLOCK**3, 4 * MIB),
        name="gram",
    )(place, *out_of_lists(lists))


def add_kernel(*refs):
    lists, outs = in_lists(refs[: 2 * SIDE]), refs[2 * SIDE :]
    for ins, out in zip(lists, outs):
        total = ins[0][...].astype(jnp.float32)
        for other in ins[1:]:
            total = total + other[...].astype(jnp.float32)
        out[...] = total.astype(jnp.bfloat16)
    last = outs[1].shape[0] - 1
    number = jnp.zeros((1, BLOCK), jnp.float32)
    for piece in lists[1]:
        number = number + jnp.sum(piece[last].astype(jnp.float32), axis=0, keepdims=True)
    outs[1][last] = split(number, (PIECE, BLOCK))


def add(lists):
    return pl.pallas_call(
        add_kernel,
        out_shape=tuple(shape_of(*pieces[0].shape) for pieces in lists),
        in_specs=[VMEM] * (2 * SIDE),
        out_specs=(VMEM,) * 2,
        compiler_params=params(12),
        name="add",
    )(*out_of_lists(lists))


def step_kernel(pairs, factor, planes, place_ref, own_ref, got_ref, *refs):
    early, late = in_lists(refs[: 2 * SIDE])
    outs, (gram, normed, left) = refs[2 * SIDE : -3], refs[-3:]
    half = own_ref.shape[0]
    blocks = early[0].shape[0]
    total = jnp.zeros((1, BLOCK), jnp.float32)
    for s in range(SIDE):
        total = total + jnp.sum(
            late[s][len(pairs) - blocks].astype(jnp.float32), axis=0, keepdims=True
        )
    inverse = 1.0 / jnp.sqrt(total / (2 * half) + 1e-06)
    scale = inverse * inverse
    side = 2 * half // BLOCK
    for k, ref in enumerate((own_ref, got_ref)):
        for i in range(half // BLOCK):
            values = ref[i * BLOCK : (i + 1) * BLOCK, :].astype(jnp.float32) * inverse
            normed[k * half + i * BLOCK : k * half + (i + 1) * BLOCK, :] = values.astype(
                jnp.bfloat16
            )
    for t, (i, j) in enumerate(pairs):
        source, u = (early, t) if t < blocks else (late, t - blocks)
        for s in range(SIDE):
            p = lax.rem(place_ref[0] - s + SIDE, SIDE)
            rows = pl.ds(pl.multiple_of(i * BLOCK + p * PIECE, PIECE), PIECE)
            values = source[s][u].astype(jnp.float32) * scale
            gram[rows, j * BLOCK : (j + 1) * BLOCK] = jnp.where(scale > 0, values, 0.0).astype(
                jnp.bfloat16
            )
    for i, j in pairs:
        if i != j:
            block = gram[i * BLOCK : (i + 1) * BLOCK, j * BLOCK : (j + 1) * BLOCK]
            gram[j * BLOCK : (j + 1) * BLOCK, i * BLOCK : (i + 1) * BLOCK] = block.T
    for i in range(side):
        rows = slice(i * BLOCK, (i + 1) * BLOCK)
        left[rows, :] = jnp.dot(
            gram[rows, :], normed[...], preferred_element_type=jnp.float32
        ).astype(jnp.bfloat16)
    each = half // planes
    for k in range(2):
        for away in range(0, planes, 2):
            rows = slice(k * half + away * each, k * half + (away + 2) * each)
            right = jnp.dot(gram[rows, :], left[...], preferred_element_type=jnp.float32)
            mixed = (
                3.4445 * normed[rows, :].astype(jnp.float32)
                - 4.775 * left[rows, :].astype(jnp.float32)
                + 2.0315 * right
            )
            values = (factor * mixed).astype(jnp.bfloat16)
            outs[away][k] = values[:each]
            outs[away + 1][k] = values[each:]


def step(place, own, got, lists, factor, planes):
    half, cols = own.shape
    rows = 2 * half
    return pl.pallas_call(
        functools.partial(step_kernel, pairs_of(rows), factor, planes),
        out_shape=(shape_of(2, half // planes, cols),) * planes,
        in_specs=[SMEM] + [VMEM] * (2 + 2 * SIDE),
        out_specs=(VMEM,) * planes,
        scratch_shapes=[
            pltpu.VMEM((rows, rows), jnp.bfloat16),
            pltpu.VMEM((rows, cols), jnp.bfloat16),
            pltpu.VMEM((rows, cols), jnp.bfloat16),
        ],
        compiler_params=params(28),
        cost_estimate=cost(4 * rows * rows * cols, 6 * 1024 * 1024),
        name="step",
    )(place, own, got, *out_of_lists(lists))


def pick_kernel(planes, table_ref, spot_ref, *refs):
    ins, (mine_ref, give_ref, rest_ref) = in_place(refs[:planes]), refs[planes:]
    for up, ref in enumerate(ins):
        owner = table_ref[3, group_at(spot_ref, up, 0, planes)]
        away = lax.rem(lax.div(jnp.maximum(owner, 0), 2) - spot_ref[0] + planes, planes)
        here = lax.rem(jnp.maximum(owner, 0), 2) == spot_ref[1]

        @pl.when(jnp.logical_and(owner >= 0, here))
        def _():
            mine_ref[away] = ref[...]

        @pl.when(jnp.logical_and(owner >= 0, jnp.logical_not(here)))
        def _():
            give_ref[away] = ref[...]

        rest_ref[up] = ref[1]


def pick(table, spot, back):
    planes = len(back)
    block = back[0].shape
    return pl.pallas_call(
        functools.partial(pick_kernel, planes),
        out_shape=(shape_of(planes, *block),) * 2 + (shape_of(planes, *block[1:]),),
        in_specs=[SMEM] * 2 + [VMEM] * planes,
        out_specs=(VMEM,) * 3,
        compiler_params=params(8),
        name="pick",
    )(table, spot, *in_turn(back))


def merge_kernel(planes, table_ref, spot_ref, mine_ref, got_ref, *outs):
    for away, out in enumerate(outs):
        helper = table_ref[2, group_at(spot_ref, away, 0, planes)]
        here = lax.rem(jnp.maximum(helper, 0), 2) == spot_ref[1]

        @pl.when(helper < 0)
        def _():
            out[...] = jnp.zeros(out.shape, out.dtype)

        @pl.when(jnp.logical_and(helper >= 0, here))
        def _():
            out[...] = mine_ref[away]

        @pl.when(jnp.logical_and(helper >= 0, jnp.logical_not(here)))
        def _():
            out[0] = got_ref[away, 1]
            out[1] = got_ref[away, 0]


def merge(table, spot, mine, got):
    planes = mine.shape[0]
    return pl.pallas_call(
        functools.partial(merge_kernel, planes),
        out_shape=(shape_of(*mine.shape[1:]),) * planes,
        in_specs=[SMEM] * 2 + [VMEM] * 2,
        out_specs=(VMEM,) * planes,
        compiler_params=params(8),
        name="merge",
    )(table, spot, mine, got)


def update_kernel(planes, table_ref, spot_ref, *refs):
    ins, (rest_ref, out_ref, sems) = in_place(refs[:planes]), refs[planes:]
    moves = []
    for away in range(planes):
        e = table_ref[0, group_at(spot_ref, away, 0, planes)]
        moves.append((ins[away].at[0], out_ref.at[e]))
        e = table_ref[0, group_at(spot_ref, away, 1, planes)]
        moves.append((rest_ref.at[away], out_ref.at[e]))
    move_all(moves, sems)


def update_of(table, spot, back, rest):
    planes, rows, cols = rest.shape
    return pl.pallas_call(
        functools.partial(update_kernel, planes),
        out_shape=shape_of(2 * planes, rows, cols),
        in_specs=[SMEM] * 2 + [VMEM] * (planes + 1),
        out_specs=ANY,
        scratch_shapes=[pltpu.SemaphoreType.DMA((2 * planes,))],
        compiler_params=params(8),
        name="update",
    )(table, spot, *in_turn(back), rest)


def slot_moves(spot_ref, ins, out_ref, slot):
    planes = len(ins)
    moves = []
    for away, ref in enumerate(ins):
        for k in range(2):
            rows = ref.shape[1]
            start = group_at(spot_ref, planes - away, k, planes) * rows
            to = out_ref.at[slot, pl.ds(pl.multiple_of(start, rows), rows)]
            moves.append((ref.at[k], to))
    return moves


def first_kernel(planes, table_ref, spot_ref, *refs):
    ins, (out_ref, zero, sems) = refs[:planes], refs[planes:]
    moves = slot_moves(spot_ref, ins, out_ref, 0)
    owns = table_ref[1, group_at(spot_ref, 0, 0, planes)] > 0

    @pl.when(owns)
    def _():
        move_all(moves, sems)

    @pl.when(jnp.logical_not(owns))
    def _():
        zero[...] = jnp.zeros(zero.shape, zero.dtype)
        move_all([(zero, b) for _, b in moves], sems)


def second_kernel(planes, spot_ref, *refs):
    ins, (_, out_ref, sems) = in_place(refs[:planes]), refs[planes:]
    move_all(slot_moves(spot_ref, ins, out_ref, 1), sems)


def first_slot(table, spot, done):
    planes = len(done)
    _, rows, cols = done[0].shape
    return pl.pallas_call(
        functools.partial(first_kernel, planes),
        out_shape=shape_of(MOST, 2 * planes * rows, cols),
        in_specs=[SMEM] * 2 + [VMEM] * planes,
        out_specs=ANY,
        scratch_shapes=[
            pltpu.VMEM((rows, cols), jnp.bfloat16),
            pltpu.SemaphoreType.DMA((2 * planes,)),
        ],
        compiler_params=params(8),
        name="first_slot",
    )(table, spot, *done)


def second_slot(spot, came, owned):
    planes = len(came)
    return pl.pallas_call(
        functools.partial(second_kernel, planes),
        out_shape=shape_of(*owned.shape),
        in_specs=[SMEM] + [VMEM] * planes + [ANY],
        out_specs=ANY,
        scratch_shapes=[pltpu.SemaphoreType.DMA((2 * planes,))],
        input_output_aliases={planes + 1: 0},
        compiler_params=params(8),
        name="second_slot",
    )(spot, *in_turn(came), owned)


def neighbour(value, order, amount):
    groups, places = lax.axis_size("fsdp"), SIDE * SIDE
    moves = []
    for at in range(groups * places):
        group, place = divmod(at, places)
        y, x = divmod(place, SIDE)
        if group % 2 == order:
            x = (x + amount) % SIDE
        else:
            y = (y + amount) % SIDE
        moves.append((at, group * places + y * SIDE + x))
    return lax.ppermute(value, ("fsdp", "grp"), moves)


def gather(first, second, order):
    one = [first, neighbour(first, order, 1), None, neighbour(first, order, -1)]
    two = [second, neighbour(second, order, 1), None, neighbour(second, order, -1)]
    one[2] = neighbour(one[1], order, 1)
    two[2] = neighbour(two[3], order, -1)
    return one, two


TRAVEL = ((0, 0), (1, 0), (0, 1), (1, 3), (0, 3), (1, 1), (0, 2), (1, 2))


def out_of_lists(lists):
    return [lists[k][s] for k, s in TRAVEL]


def in_lists(refs):
    return [[refs[TRAVEL.index((k, s))] for s in range(SIDE)] for k in range(2)]


def over_planes(blocks, sign):
    planes = len(blocks)
    got = list(blocks)
    for away in nearest_first(planes)[1:]:
        moves = []
        for group in range(2 * planes):
            plane, core = divmod(group, 2)
            moves.append((group, 2 * ((plane + sign * away) % planes) + core))
        got[away] = lax.ppermute(blocks[away], "fsdp", moves)
    return got


def nearest_first(planes):
    return sorted(range(planes), key=lambda a: min(a, planes - a))


def in_turn(blocks):
    return [blocks[away] for away in nearest_first(len(blocks))]


def in_place(refs):
    order = nearest_first(len(refs))
    return [refs[order.index(away)] for away in range(len(refs))]


def swap(value):
    groups = lax.axis_size("fsdp")
    return lax.ppermute(value, "fsdp", [(g, g ^ 1) for g in range(groups)])


def on_device(grads, owner):
    count, rows_dev, cols_dev = grads.shape
    groups = lax.axis_size("fsdp")
    planes = groups // 2
    rows = rows_dev * groups
    cols = cols_dev * lax.axis_size("grp")
    factor = 0.2 * math.sqrt(max(rows, cols))
    at = lax.axis_index("grp")
    me = lax.axis_index("fsdp")
    along = jnp.stack([lax.rem(at, SIDE), lax.div(at, SIDE)]).astype(jnp.int32)
    place = jnp.where(lax.rem(me, 2) == 0, along, along[::-1])
    spot = jnp.stack([lax.div(me, 2), lax.rem(me, 2)]).astype(jnp.int32)
    table, *sends = plan(owner, spot, grads)
    own, give = sort(over_planes(sends, 1))
    got = swap(give)
    own, got = own.reshape(rows // 2, cols_dev), got.reshape(rows // 2, cols_dev)
    parts = gram_quarter(place, gather(own, got, 0))
    parts = add(gather(*parts, 1))
    done = step(place, own, got, gather(*parts, 0), factor, planes)
    back = over_planes(done, -1)
    mine, give, rest = pick(table, spot, back)
    sends = merge(table, spot, mine, swap(give))
    came = over_planes(sends, 1)
    update = update_of(table, spot, back, swap(rest))
    owned = second_slot(spot, came, first_slot(table, spot, done))
    return (update, owned)


def solution(mesh):
    return jax.shard_map(
        on_device,
        mesh=mesh,
        in_specs=(P(None, "fsdp", "grp"), P()),
        out_specs=(P(None, "fsdp", "grp"), P("fsdp", None, "grp")),
        check_vma=False,
    )
```

time: 319 us -> 143 us (0.45)
  the two profiles are of different devices: /device:TPU:1 before, /device:TPU:62 now
where the time goes in v5:
time: 143 us
  starting transfers between devices  66.8 us (47%)
  waiting for transfers between devices  58.8 us (41%)
  Pallas kernels  14.7 us (10%)
  local copies, waits for them, and re-layouts  1.88 us (1%)
    ppermute x21, starting transfers between devices, over_planes(): got[away] = lax.ppermute(blocks[away], 'fsdp', moves)  45.2 us
    ppermute x18, waiting for transfers between devices, neighbour(): return lax.ppermute(value, ('fsdp', 'grp'), moves)  32.4 us
    ppermute x21, waiting for transfers between devices, over_planes(): got[away] = lax.ppermute(blocks[away], 'fsdp', moves)  23.5 us
    ppermute x18, starting transfers between devices, neighbour(): return lax.ppermute(value, ('fsdp', 'grp'), moves)  20.9 us
    pallas_call x1, Pallas kernels, step(): pl.pallas_call(functools.partial(step_kernel, pairs_of(rows), factor, pla...  4.22 us
    ppermute x3, waiting for transfers between devices, swap(): return lax.ppermute(value, 'fsdp', [(g, g ^ 1) for g in range(groups)])  2.93 us
  transfers between devices with their start and end apart: 42, of which 24 were waited for; matrix products, arithmetic and copies ran while one was open for 0% of the time, Pallas kernels for 3%

profile of v5, /device:TPU:62, one launch (start us, length us, event | category | flops | bytes accessed | tf_op | source)
XLA Modules:
  0.0 143.3 jit_solution(881214296247119655)
XLA Ops:
  2.5 2.1 %plan.1 = (s32[4,16]{1,0:T(4,128)S(1)}, bf16[2,96,256]{2,1,0:T(8,128)(2,1)S(1)}, bf16[2,96,256]{2,1,0:T(8,128)(2,1)S(1)}, bf16[2,96,256]{2,1,0:T(8,128)(2,1)S(1)...) custom-call(s32[16]{0:T(128)S(1)} %copy-done.1, ...), custom_call_target="tpu_custom_call" | custom-call | tf_op jit(solution)/shard_map/plan/pallas_call | solution.py:118
  6.7 4.4 %collective-permute-start.2 = (bf16[2,96,256]{2,1,0:T(8,128)(2,1)S(1)}, bf16[2,96,256]{2,1,0:T(8,128)(2,1)S(1)}, u32[]{:S(2)}, u32[]{:S(2)}) collective-permute-start(bf16[2,96,256]{2,1,0:T(8,128)(2,1)S(1)} %get-tuple-element.40), channel_id=1, source_target_pairs={{0,64},{16,80},{32,96},{48,112},{64,128},{80,144},{96,160},{112,17... | collective-permute-start | bytes 294920 | tf_op jit(solution)/shard_map/ppermute | solution.py:500
  12.1 5.8 %collective-permute-start.4 = (bf16[2,96,256]{2,1,0:T(8,128)(2,1)S(1)}, bf16[2,96,256]{2,1,0:T(8,128)(2,1)S(1)}, u32[]{:S(2)}, u32[]{:S(2)}) collective-permute-start(bf16[2,96,256]{2,1,0:T(8,128)(2,1)S(1)} %get-tuple-element.42), channel_id=1, source_target_pairs={{0,96},{16,112},{32,128},{48,144},{64,160},{80,176},{96,192},{112,... | collective-permute-start | bytes 294920 | tf_op jit(solution)/shard_map/ppermute | solution.py:500
  17.9 4.3 %collective-permute-start.6 = (bf16[2,96,256]{2,1,0:T(8,128)(2,1)S(1)}, bf16[2,96,256]{2,1,0:T(8,128)(2,1)S(1)}, u32[]{:S(2)}, u32[]{:S(2)}) collective-permute-start(bf16[2,96,256]{2,1,0:T(8,128)(2,1)S(1)} %get-tuple-element.44), channel_id=1, source_target_pairs={{0,128},{16,144},{32,160},{48,176},{64,192},{80,208},{96,224},{112... | collective-permute-start | bytes 294920 | tf_op jit(solution)/shard_map/ppermute | solution.py:500
  23.1 8.6 %collective-permute-done.5.refs_6_ = bf16[2,96,256]{2,1,0:T(8,128)(2,1)S(1)} collective-permute-done((bf16[2,96,256]{2,1,0:T(8,128)(2,1)S(1)}, bf16[2,96,256]{2,1,0:T(8,128)(2,1)S(1)}, u32[]{:S(2)}, u32[]{:S(2)}) %collective-permute-start.5) | collective-permute-done | bytes 98336 | tf_op jit(solution)/shard_map/ppermute | solution.py:500
  34.9 2.7 %collective-permute-start.11 = (bf16[768,256]{1,0:T(8,128)(2,1)S(1)}, bf16[768,256]{1,0:T(8,128)(2,1)S(1)}, u32[]{:S(2)}, u32[]{:S(2)}) collective-permute-start(bf16[768,256]{1,0:T(8,128)(2,1)S(1)} %bitcast.11), channel_id=1, source_target_pairs={{0,1},{1,2},{2,3},{3,0},{4,5},{5,6},{6,7},{7,4},{8,9},{9,10},{10,1... | collective-permute-start | bytes 1179656 | tf_op jit(solution)/shard_map/ppermute | solution.py:470
  37.6 2.1 %collective-permute-done.8.refs_2_ = bf16[768,256]{1,0:T(8,128)(2,1)S(1)} collective-permute-done((bf16[768,256]{1,0:T(8,128)(2,1)S(1)}, bf16[768,256]{1,0:T(8,128)(2,1)S(1)}, u32[]{:S(2)}, u32[]{:S(2)}) %collective-permute-start.8) | collective-permute-done | bytes 393248 | tf_op jit(solution)/shard_map/ppermute | solution.py:470
  42.8 4.0 %collective-permute-done.10.refs_4_ = bf16[768,256]{1,0:T(8,128)(2,1)S(1)} collective-permute-done((bf16[768,256]{1,0:T(8,128)(2,1)S(1)}, bf16[768,256]{1,0:T(8,128)(2,1)S(1)}, u32[]{:S(2)}, u32[]{:S(2)}) %collective-permute-start.10) | collective-permute-done | bytes 393248 | tf_op jit(solution)/shard_map/ppermute | solution.py:470
  48.1 3.4 %collective-permute-done.13.refs_7_ = bf16[768,256]{1,0:T(8,128)(2,1)S(1)} collective-permute-done((bf16[768,256]{1,0:T(8,128)(2,1)S(1)}, bf16[768,256]{1,0:T(8,128)(2,1)S(1)}, u32[]{:S(2)}, u32[]{:S(2)}) %collective-permute-start.13) | collective-permute-done | bytes 393248 | tf_op jit(solution)/shard_map/ppermute | solution.py:470
  56.0 2.5 %collective-permute-start.17 = (bf16[11,64,256]{2,1,0:T(8,128)(2,1)S(1)}, bf16[11,64,256]{2,1,0:T(8,128)(2,1)S(1)}, u32[]{:S(2)}, u32[]{:S(2)}) collective-permute-start(bf16[11,64,256]{2,1,0:T(8,128)(2,1)S(1)} %get-tuple-element.48.refs_1_), channel_id=1, source_target_pairs={{0,4},{1,5},{2,6},{3,7},{4,8},{5,9},{6,10},{7,11},{8,12},{9,13},{1... | collective-permute-start | bytes 1081352 | tf_op jit(solution)/shard_map/ppermute | solution.py:470
  58.5 2.2 %collective-permute-done.14.refs_2_ = bf16[11,64,256]{2,1,0:T(8,128)(2,1)S(1)} collective-permute-done((bf16[11,64,256]{2,1,0:T(8,128)(2,1)S(1)}, bf16[11,64,256]{2,1,0:T(8,128)(2,1)S(1)}, u32[]{:S(2)}, u32[]{:S(2)}) %collective-permute-start.14) | collective-permute-done | bytes 360480 | tf_op jit(solution)/shard_map/ppermute | solution.py:470
  62.7 3.3 %collective-permute-done.16.refs_4_ = bf16[11,64,256]{2,1,0:T(8,128)(2,1)S(1)} collective-permute-done((bf16[11,64,256]{2,1,0:T(8,128)(2,1)S(1)}, bf16[11,64,256]{2,1,0:T(8,128)(2,1)S(1)}, u32[]{:S(2)}, u32[]{:S(2)}) %collective-permute-start.16) | collective-permute-done | bytes 360480 | tf_op jit(solution)/shard_map/ppermute | solution.py:470
  66.0 2.4 %collective-permute-done.18.refs_6_ = bf16[11,64,256]{2,1,0:T(8,128)(2,1)S(1)} collective-permute-done((bf16[11,64,256]{2,1,0:T(8,128)(2,1)S(1)}, bf16[11,64,256]{2,1,0:T(8,128)(2,1)S(1)}, u32[]{:S(2)}, u32[]{:S(2)}) %collective-permute-start.18) | collective-permute-done | bytes 360480 | tf_op jit(solution)/shard_map/ppermute | solution.py:470
  68.4 2.4 %collective-permute-done.19.refs_7_ = bf16[11,64,256]{2,1,0:T(8,128)(2,1)S(1)} collective-permute-done((bf16[11,64,256]{2,1,0:T(8,128)(2,1)S(1)}, bf16[11,64,256]{2,1,0:T(8,128)(2,1)S(1)}, u32[]{:S(2)}, u32[]{:S(2)}) %collective-permute-start.19) | collective-permute-done | bytes 360480 | tf_op jit(solution)/shard_map/ppermute | solution.py:470
  71.3 2.0 %collective-permute-start.21 = (bf16[11,64,256]{2,1,0:T(8,128)(2,1)S(1)}, bf16[11,64,256]{2,1,0:T(8,128)(2,1)S(1)}, u32[]{:S(2)}, u32[]{:S(2)}) collective-permute-start(bf16[11,64,256]{2,1,0:T(8,128)(2,1)S(1)} %get-tuple-element.50.refs_1_), channel_id=1, source_target_pairs={{0,3},{1,0},{2,1},{3,2},{4,7},{5,4},{6,5},{7,6},{8,11},{9,8},{10,9... | collective-permute-start | bytes 1081352 | tf_op jit(solution)/shard_map/ppermute | solution.py:470
  73.3 3.2 %collective-permute-start.23 = (bf16[11,64,256]{2,1,0:T(8,128)(2,1)S(1)}, bf16[11,64,256]{2,1,0:T(8,128)(2,1)S(1)}, u32[]{:S(2)}, u32[]{:S(2)}) collective-permute-start(bf16[11,64,256]{2,1,0:T(8,128)(2,1)S(1)} %get-tuple-element.50.refs_1_), channel_id=1, source_target_pairs={{0,1},{1,2},{2,3},{3,0},{4,5},{5,6},{6,7},{7,4},{8,9},{9,10},{10,1... | collective-permute-start | bytes 1081352 | tf_op jit(solution)/shard_map/ppermute | solution.py:470
  76.5 2.2 %collective-permute-done.20.refs_2_ = bf16[11,64,256]{2,1,0:T(8,128)(2,1)S(1)} collective-permute-done((bf16[11,64,256]{2,1,0:T(8,128)(2,1)S(1)}, bf16[11,64,256]{2,1,0:T(8,128)(2,1)S(1)}, u32[]{:S(2)}, u32[]{:S(2)}) %collective-permute-start.20) | collective-permute-done | bytes 360480 | tf_op jit(solution)/shard_map/ppermute | solution.py:470
  80.7 3.1 %collective-permute-done.22.refs_4_ = bf16[11,64,256]{2,1,0:T(8,128)(2,1)S(1)} collective-permute-done((bf16[11,64,256]{2,1,0:T(8,128)(2,1)S(1)}, bf16[11,64,256]{2,1,0:T(8,128)(2,1)S(1)}, u32[]{:S(2)}, u32[]{:S(2)}) %collective-permute-start.22) | collective-permute-done | bytes 360480 | tf_op jit(solution)/shard_map/ppermute | solution.py:470
  83.9 2.6 %collective-permute-done.24.refs_6_ = bf16[11,64,256]{2,1,0:T(8,128)(2,1)S(1)} collective-permute-done((bf16[11,64,256]{2,1,0:T(8,128)(2,1)S(1)}, bf16[11,64,256]{2,1,0:T(8,128)(2,1)S(1)}, u32[]{:S(2)}, u32[]{:S(2)}) %collective-permute-start.24) | collective-permute-done | bytes 360480 | tf_op jit(solution)/shard_map/ppermute | solution.py:470
  86.4 2.2 %collective-permute-done.25.refs_7_ = bf16[11,64,256]{2,1,0:T(8,128)(2,1)S(1)} collective-permute-done((bf16[11,64,256]{2,1,0:T(8,128)(2,1)S(1)}, bf16[11,64,256]{2,1,0:T(8,128)(2,1)S(1)}, u32[]{:S(2)}, u32[]{:S(2)}) %collective-permute-start.25) | collective-permute-done | bytes 360480 | tf_op jit(solution)/shard_map/ppermute | solution.py:470
  88.6 4.2 %step.1 = (bf16[2,96,256]{2,1,0:T(8,128)(2,1)S(1)}, bf16[2,96,256]{2,1,0:T(8,128)(2,1)S(1)}, bf16[2,96,256]{2,1,0:T(8,128)(2,1)S(1)}, bf16[2,96,256]{2,1,0:T(8,1...) custom-call(s32[2]{0:T(128)S(1)} %broadcast_select_fusion.place_ref,, ...), custom_call_target="tpu_custom_call" | custom-call | flops 2415919104 | bytes 6291456 | tf_op jit(solution)/shard_map/step/pallas_call | solution.py:294
  93.2 2.0 %collective-permute-start.27 = (bf16[2,96,256]{2,1,0:T(8,128)(2,1)S(1)}, bf16[2,96,256]{2,1,0:T(8,128)(2,1)S(1)}, u32[]{:S(2)}, u32[]{:S(2)}) collective-permute-start(bf16[2,96,256]{2,1,0:T(8,128)(2,1)S(1)} %get-tuple-element.53.refs_7_), channel_id=1, source_target_pairs={{0,32},{16,48},{32,64},{48,80},{64,96},{80,112},{96,128},{112,144}... | collective-permute-start | bytes 294920 | tf_op jit(solution)/shard_map/ppermute | solution.py:500
  95.2 2.9 %collective-permute-start.29 = (bf16[2,96,256]{2,1,0:T(8,128)(2,1)S(1)}, bf16[2,96,256]{2,1,0:T(8,128)(2,1)S(1)}, u32[]{:S(2)}, u32[]{:S(2)}) collective-permute-start(bf16[2,96,256]{2,1,0:T(8,128)(2,1)S(1)} %get-tuple-element.55.refs_6_), channel_id=1, source_target_pairs={{0,64},{16,80},{32,96},{48,112},{64,128},{80,144},{96,160},{112,17... | collective-permute-start | bytes 294920 | tf_op jit(solution)/shard_map/ppermute | solution.py:500
  98.1 2.8 %collective-permute-start.30 = (bf16[2,96,256]{2,1,0:T(8,128)(2,1)S(1)}, bf16[2,96,256]{2,1,0:T(8,128)(2,1)S(1)}, u32[]{:S(2)}, u32[]{:S(2)}) collective-permute-start(bf16[2,96,256]{2,1,0:T(8,128)(2,1)S(1)} %get-tuple-element.56.refs_3_), channel_id=1, source_target_pairs={{0,160},{16,176},{32,192},{48,208},{64,224},{80,240},{96,0},{112,1... | collective-permute-start | bytes 294920 | tf_op jit(solution)/shard_map/ppermute | solution.py:500
  100.9 2.2 %collective-permute-start.31 = (bf16[2,96,256]{2,1,0:T(8,128)(2,1)S(1)}, bf16[2,96,256]{2,1,0:T(8,128)(2,1)S(1)}, u32[]{:S(2)}, u32[]{:S(2)}) collective-permute-start(bf16[2,96,256]{2,1,0:T(8,128)(2,1)S(1)} %get-tuple-element.57.refs_5_), channel_id=1, source_target_pairs={{0,96},{16,112},{32,128},{48,144},{64,160},{80,176},{96,192},{112,... | collective-permute-start | bytes 294920 | tf_op jit(solution)/shard_map/ppermute | solution.py:500
  103.1 3.0 %collective-permute-start.32 = (bf16[2,96,256]{2,1,0:T(8,128)(2,1)S(1)}, bf16[2,96,256]{2,1,0:T(8,128)(2,1)S(1)}, u32[]{:S(2)}, u32[]{:S(2)}) collective-permute-start(bf16[2,96,256]{2,1,0:T(8,128)(2,1)S(1)} %get-tuple-element.58.refs_4_), channel_id=1, source_target_pairs={{0,128},{16,144},{32,160},{48,176},{64,192},{80,208},{96,224},{112... | collective-permute-start | bytes 294920 | tf_op jit(solution)/shard_map/ppermute | solution.py:500
  107.1 2.9 %collective-permute-done.31.refs_6_ = bf16[2,96,256]{2,1,0:T(8,128)(2,1)S(1)} collective-permute-done((bf16[2,96,256]{2,1,0:T(8,128)(2,1)S(1)}, bf16[2,96,256]{2,1,0:T(8,128)(2,1)S(1)}, u32[]{:S(2)}, u32[]{:S(2)}) %collective-permute-start.31) | collective-permute-done | bytes 98336 | tf_op jit(solution)/shard_map/ppermute | solution.py:500
  110.0 2.7 %collective-permute-done.32.refs_7_ = bf16[2,96,256]{2,1,0:T(8,128)(2,1)S(1)} collective-permute-done((bf16[2,96,256]{2,1,0:T(8,128)(2,1)S(1)}, bf16[2,96,256]{2,1,0:T(8,128)(2,1)S(1)}, u32[]{:S(2)}, u32[]{:S(2)}) %collective-permute-start.32) | collective-permute-done | bytes 98336 | tf_op jit(solution)/shard_map/ppermute | solution.py:500
  120.0 2.9 %collective-permute-start.38 = (bf16[2,96,256]{2,1,0:T(8,128)(2,1)S(1)}, bf16[2,96,256]{2,1,0:T(8,128)(2,1)S(1)}, u32[]{:S(2)}, u32[]{:S(2)}) collective-permute-start(bf16[2,96,256]{2,1,0:T(8,128)(2,1)S(1)} %get-tuple-element.66), channel_id=1, source_target_pairs={{0,192},{16,208},{32,224},{48,240},{64,0},{80,16},{96,32},{112,48}... | collective-permute-start | bytes 294920 | tf_op jit(solution)/shard_map/ppermute | solution.py:500
  123.0 3.3 %collective-permute-start.39 = (bf16[2,96,256]{2,1,0:T(8,128)(2,1)S(1)}, bf16[2,96,256]{2,1,0:T(8,128)(2,1)S(1)}, u32[]{:S(2)}, u32[]{:S(2)}) collective-permute-start(bf16[2,96,256]{2,1,0:T(8,128)(2,1)S(1)} %get-tuple-element.67), channel_id=1, source_target_pairs={{0,96},{16,112},{32,128},{48,144},{64,160},{80,176},{96,192},{112,... | collective-permute-start | bytes 294920 | tf_op jit(solution)/shard_map/ppermute | solution.py:500
  128.0 3.0 %collective-permute-start.41 = (bf16[2,96,256]{2,1,0:T(8,128)(2,1)S(1)}, bf16[2,96,256]{2,1,0:T(8,128)(2,1)S(1)}, u32[]{:S(2)}, u32[]{:S(2)}) collective-permute-start(bf16[2,96,256]{2,1,0:T(8,128)(2,1)S(1)} %get-tuple-element.69), channel_id=1, source_target_pairs={{0,128},{16,144},{32,160},{48,176},{64,192},{80,208},{96,224},{112... | collective-permute-start | bytes 294920 | tf_op jit(solution)/shard_map/ppermute | solution.py:500
  135.0 6.6 %collective-permute-done.40.refs_6_ = bf16[2,96,256]{2,1,0:T(8,128)(2,1)S(1)} collective-permute-done((bf16[2,96,256]{2,1,0:T(8,128)(2,1)S(1)}, bf16[2,96,256]{2,1,0:T(8,128)(2,1)S(1)}, u32[]{:S(2)}, u32[]{:S(2)}) %collective-permute-start.40) | collective-permute-done | bytes 98336 | tf_op jit(solution)/shard_map/ppermute | solution.py:500
  (70 shorter events, 38.4 us)
Async XLA Ops:
  4.6 13.3 %collective-permute-start = (bf16[2,96,256]{2,1,0:T(8,128)(2,1)S(1)}, bf16[2,96,256]{2,1,0:T(8,128)(2,1)S(1)}, u32[]{:S(2)}, u32[]{:S(2)}) collective-permute-start(bf16[2,96,256]{2,1,0:T(8,128)(2,1)S(1)} %get-tuple-element.38), channel_id=1, source_target_pairs={{0,32},{16,48},{32,64},{48,80},{64,96},{80,112},{96,128},{112,144}... | collective-permute-start | bytes 294920 | tf_op jit(solution)/shard_map/ppermute | solution.py:500
  6.6 11.3 %collective-permute-start.1 = (bf16[2,96,256]{2,1,0:T(8,128)(2,1)S(1)}, bf16[2,96,256]{2,1,0:T(8,128)(2,1)S(1)}, u32[]{:S(2)}, u32[]{:S(2)}) collective-permute-start(bf16[2,96,256]{2,1,0:T(8,128)(2,1)S(1)} %get-tuple-element.39), channel_id=1, source_target_pairs={{0,224},{16,240},{32,0},{48,16},{64,32},{80,48},{96,64},{112,80},{... | collective-permute-start | bytes 294920 | tf_op jit(solution)/shard_map/ppermute | solution.py:500
  6.7 15.5 %collective-permute-start.2 = (bf16[2,96,256]{2,1,0:T(8,128)(2,1)S(1)}, bf16[2,96,256]{2,1,0:T(8,128)(2,1)S(1)}, u32[]{:S(2)}, u32[]{:S(2)}) collective-permute-start(bf16[2,96,256]{2,1,0:T(8,128)(2,1)S(1)} %get-tuple-element.40), channel_id=1, source_target_pairs={{0,64},{16,80},{32,96},{48,112},{64,128},{80,144},{96,160},{112,17... | collective-permute-start | bytes 294920 | tf_op jit(solution)/shard_map/ppermute | solution.py:500
  11.0 11.1 %collective-permute-start.3 = (bf16[2,96,256]{2,1,0:T(8,128)(2,1)S(1)}, bf16[2,96,256]{2,1,0:T(8,128)(2,1)S(1)}, u32[]{:S(2)}, u32[]{:S(2)}) collective-permute-start(bf16[2,96,256]{2,1,0:T(8,128)(2,1)S(1)} %get-tuple-element.41), channel_id=1, source_target_pairs={{0,192},{16,208},{32,224},{48,240},{64,0},{80,16},{96,32},{112,48}... | collective-permute-start | bytes 294920 | tf_op jit(solution)/shard_map/ppermute | solution.py:500
  12.1 11.0 %collective-permute-start.4 = (bf16[2,96,256]{2,1,0:T(8,128)(2,1)S(1)}, bf16[2,96,256]{2,1,0:T(8,128)(2,1)S(1)}, u32[]{:S(2)}, u32[]{:S(2)}) collective-permute-start(bf16[2,96,256]{2,1,0:T(8,128)(2,1)S(1)} %get-tuple-element.42), channel_id=1, source_target_pairs={{0,96},{16,112},{32,128},{48,144},{64,160},{80,176},{96,192},{112,... | collective-permute-start | bytes 294920 | tf_op jit(solution)/shard_map/ppermute | solution.py:500
  17.9 13.8 %collective-permute-start.5 = (bf16[2,96,256]{2,1,0:T(8,128)(2,1)S(1)}, bf16[2,96,256]{2,1,0:T(8,128)(2,1)S(1)}, u32[]{:S(2)}, u32[]{:S(2)}) collective-permute-start(bf16[2,96,256]{2,1,0:T(8,128)(2,1)S(1)} %get-tuple-element.43), channel_id=1, source_target_pairs={{0,160},{16,176},{32,192},{48,208},{64,224},{80,240},{96,0},{112,1... | collective-permute-start | bytes 294920 | tf_op jit(solution)/shard_map/ppermute | solution.py:500
  17.9 13.8 %collective-permute-start.6 = (bf16[2,96,256]{2,1,0:T(8,128)(2,1)S(1)}, bf16[2,96,256]{2,1,0:T(8,128)(2,1)S(1)}, u32[]{:S(2)}, u32[]{:S(2)}) collective-permute-start(bf16[2,96,256]{2,1,0:T(8,128)(2,1)S(1)} %get-tuple-element.44), channel_id=1, source_target_pairs={{0,128},{16,144},{32,160},{48,176},{64,192},{80,208},{96,224},{112... | collective-permute-start | bytes 294920 | tf_op jit(solution)/shard_map/ppermute | solution.py:500
  33.5 9.0 %collective-permute-start.9 = (bf16[768,256]{1,0:T(8,128)(2,1)S(1)}, bf16[768,256]{1,0:T(8,128)(2,1)S(1)}, u32[]{:S(2)}, u32[]{:S(2)}) collective-permute-start(bf16[768,256]{1,0:T(8,128)(2,1)S(1)} %bitcast.10), channel_id=1, source_target_pairs={{0,3},{1,0},{2,1},{3,2},{4,7},{5,4},{6,5},{7,6},{8,11},{9,8},{10,9... | collective-permute-start | bytes 1179656 | tf_op jit(solution)/shard_map/ppermute | solution.py:470
  34.4 12.4 %collective-permute-start.10 = (bf16[768,256]{1,0:T(8,128)(2,1)S(1)}, bf16[768,256]{1,0:T(8,128)(2,1)S(1)}, u32[]{:S(2)}, u32[]{:S(2)}) collective-permute-start(bf16[768,256]{1,0:T(8,128)(2,1)S(1)} %bitcast.7), channel_id=1, source_target_pairs={{0,3},{1,0},{2,1},{3,2},{4,7},{5,4},{6,5},{7,6},{8,11},{9,8},{10,9... | collective-permute-start | bytes 1179656 | tf_op jit(solution)/shard_map/ppermute | solution.py:470
  34.9 11.8 %collective-permute-start.11 = (bf16[768,256]{1,0:T(8,128)(2,1)S(1)}, bf16[768,256]{1,0:T(8,128)(2,1)S(1)}, u32[]{:S(2)}, u32[]{:S(2)}) collective-permute-start(bf16[768,256]{1,0:T(8,128)(2,1)S(1)} %bitcast.11), channel_id=1, source_target_pairs={{0,1},{1,2},{2,3},{3,0},{4,5},{5,6},{6,7},{7,4},{8,9},{9,10},{10,1... | collective-permute-start | bytes 1179656 | tf_op jit(solution)/shard_map/ppermute | solution.py:470
  42.5 9.0 %collective-permute-start.13 = (bf16[768,256]{1,0:T(8,128)(2,1)S(1)}, bf16[768,256]{1,0:T(8,128)(2,1)S(1)}, u32[]{:S(2)}, u32[]{:S(2)}) collective-permute-start(bf16[768,256]{1,0:T(8,128)(2,1)S(1)} %collective-permute-done.9.refs_3_), channel_id=1, source_target_pairs={{0,3},{1,0},{2,1},{3,2},{4,7},{5,4},{6,5},{7,6},{8,11},{9,8},{10,9... | collective-permute-start | bytes 1179656 | tf_op jit(solution)/shard_map/ppermute | solution.py:470
  53.5 8.7 %collective-permute-start.15 = (bf16[11,64,256]{2,1,0:T(8,128)(2,1)S(1)}, bf16[11,64,256]{2,1,0:T(8,128)(2,1)S(1)}, u32[]{:S(2)}, u32[]{:S(2)}) collective-permute-start(bf16[11,64,256]{2,1,0:T(8,128)(2,1)S(1)} %get-tuple-element.48.refs_1_), channel_id=1, source_target_pairs={{0,12},{1,13},{2,14},{3,15},{4,0},{5,1},{6,2},{7,3},{8,4},{9,5},{1... | collective-permute-start | bytes 1081352 | tf_op jit(solution)/shard_map/ppermute | solution.py:470
  55.3 10.7 %collective-permute-start.16 = (bf16[11,64,256]{2,1,0:T(8,128)(2,1)S(1)}, bf16[11,64,256]{2,1,0:T(8,128)(2,1)S(1)}, u32[]{:S(2)}, u32[]{:S(2)}) collective-permute-start(bf16[11,64,256]{2,1,0:T(8,128)(2,1)S(1)} %get-tuple-element.47.refs_0_), channel_id=1, source_target_pairs={{0,12},{1,13},{2,14},{3,15},{4,0},{5,1},{6,2},{7,3},{8,4},{9,5},{1... | collective-permute-start | bytes 1081352 | tf_op jit(solution)/shard_map/ppermute | solution.py:470
  56.0 10.0 %collective-permute-start.17 = (bf16[11,64,256]{2,1,0:T(8,128)(2,1)S(1)}, bf16[11,64,256]{2,1,0:T(8,128)(2,1)S(1)}, u32[]{:S(2)}, u32[]{:S(2)}) collective-permute-start(bf16[11,64,256]{2,1,0:T(8,128)(2,1)S(1)} %get-tuple-element.48.refs_1_), channel_id=1, source_target_pairs={{0,4},{1,5},{2,6},{3,7},{4,8},{5,9},{6,10},{7,11},{8,12},{9,13},{1... | collective-permute-start | bytes 1081352 | tf_op jit(solution)/shard_map/ppermute | solution.py:470
  71.3 8.7 %collective-permute-start.21 = (bf16[11,64,256]{2,1,0:T(8,128)(2,1)S(1)}, bf16[11,64,256]{2,1,0:T(8,128)(2,1)S(1)}, u32[]{:S(2)}, u32[]{:S(2)}) collective-permute-start(bf16[11,64,256]{2,1,0:T(8,128)(2,1)S(1)} %get-tuple-element.50.refs_1_), channel_id=1, source_target_pairs={{0,3},{1,0},{2,1},{3,2},{4,7},{5,4},{6,5},{7,6},{8,11},{9,8},{10,9... | collective-permute-start | bytes 1081352 | tf_op jit(solution)/shard_map/ppermute | solution.py:470
  73.3 10.6 %collective-permute-start.22 = (bf16[11,64,256]{2,1,0:T(8,128)(2,1)S(1)}, bf16[11,64,256]{2,1,0:T(8,128)(2,1)S(1)}, u32[]{:S(2)}, u32[]{:S(2)}) collective-permute-start(bf16[11,64,256]{2,1,0:T(8,128)(2,1)S(1)} %get-tuple-element.49.refs_0_), channel_id=1, source_target_pairs={{0,3},{1,0},{2,1},{3,2},{4,7},{5,4},{6,5},{7,6},{8,11},{9,8},{10,9... | collective-permute-start | bytes 1081352 | tf_op jit(solution)/shard_map/ppermute | solution.py:470
  73.3 10.5 %collective-permute-start.23 = (bf16[11,64,256]{2,1,0:T(8,128)(2,1)S(1)}, bf16[11,64,256]{2,1,0:T(8,128)(2,1)S(1)}, u32[]{:S(2)}, u32[]{:S(2)}) collective-permute-start(bf16[11,64,256]{2,1,0:T(8,128)(2,1)S(1)} %get-tuple-element.50.refs_1_), channel_id=1, source_target_pairs={{0,1},{1,2},{2,3},{3,0},{4,5},{5,6},{6,7},{7,4},{8,9},{9,10},{10,1... | collective-permute-start | bytes 1081352 | tf_op jit(solution)/shard_map/ppermute | solution.py:470
  80.0 8.6 %collective-permute-start.25 = (bf16[11,64,256]{2,1,0:T(8,128)(2,1)S(1)}, bf16[11,64,256]{2,1,0:T(8,128)(2,1)S(1)}, u32[]{:S(2)}, u32[]{:S(2)}) collective-permute-start(bf16[11,64,256]{2,1,0:T(8,128)(2,1)S(1)} %collective-permute-done.21.refs_3_), channel_id=1, source_target_pairs={{0,3},{1,0},{2,1},{3,2},{4,7},{5,4},{6,5},{7,6},{8,11},{9,8},{10,9... | collective-permute-start | bytes 1081352 | tf_op jit(solution)/shard_map/ppermute | solution.py:470
  93.2 10.0 %collective-permute-start.27 = (bf16[2,96,256]{2,1,0:T(8,128)(2,1)S(1)}, bf16[2,96,256]{2,1,0:T(8,128)(2,1)S(1)}, u32[]{:S(2)}, u32[]{:S(2)}) collective-permute-start(bf16[2,96,256]{2,1,0:T(8,128)(2,1)S(1)} %get-tuple-element.53.refs_7_), channel_id=1, source_target_pairs={{0,32},{16,48},{32,64},{48,80},{64,96},{80,112},{96,128},{112,144}... | collective-permute-start | bytes 294920 | tf_op jit(solution)/shard_map/ppermute | solution.py:500
  95.2 11.0 %collective-permute-start.28 = (bf16[2,96,256]{2,1,0:T(8,128)(2,1)S(1)}, bf16[2,96,256]{2,1,0:T(8,128)(2,1)S(1)}, u32[]{:S(2)}, u32[]{:S(2)}) collective-permute-start(bf16[2,96,256]{2,1,0:T(8,128)(2,1)S(1)} %get-tuple-element.54.refs_2_), channel_id=1, source_target_pairs={{0,192},{16,208},{32,224},{48,240},{64,0},{80,16},{96,32},{112,48}... | collective-permute-start | bytes 294920 | tf_op jit(solution)/shard_map/ppermute | solution.py:500
  95.2 11.6 %collective-permute-start.29 = (bf16[2,96,256]{2,1,0:T(8,128)(2,1)S(1)}, bf16[2,96,256]{2,1,0:T(8,128)(2,1)S(1)}, u32[]{:S(2)}, u32[]{:S(2)}) collective-permute-start(bf16[2,96,256]{2,1,0:T(8,128)(2,1)S(1)} %get-tuple-element.55.refs_6_), channel_id=1, source_target_pairs={{0,64},{16,80},{32,96},{48,112},{64,128},{80,144},{96,160},{112,17... | collective-permute-start | bytes 294920 | tf_op jit(solution)/shard_map/ppermute | solution.py:500
  98.1 9.0 %collective-permute-start.30 = (bf16[2,96,256]{2,1,0:T(8,128)(2,1)S(1)}, bf16[2,96,256]{2,1,0:T(8,128)(2,1)S(1)}, u32[]{:S(2)}, u32[]{:S(2)}) collective-permute-start(bf16[2,96,256]{2,1,0:T(8,128)(2,1)S(1)} %get-tuple-element.56.refs_3_), channel_id=1, source_target_pairs={{0,160},{16,176},{32,192},{48,208},{64,224},{80,240},{96,0},{112,1... | collective-permute-start | bytes 294920 | tf_op jit(solution)/shard_map/ppermute | solution.py:500
  100.9 9.1 %collective-permute-start.31 = (bf16[2,96,256]{2,1,0:T(8,128)(2,1)S(1)}, bf16[2,96,256]{2,1,0:T(8,128)(2,1)S(1)}, u32[]{:S(2)}, u32[]{:S(2)}) collective-permute-start(bf16[2,96,256]{2,1,0:T(8,128)(2,1)S(1)} %get-tuple-element.57.refs_5_), channel_id=1, source_target_pairs={{0,96},{16,112},{32,128},{48,144},{64,160},{80,176},{96,192},{112,... | collective-permute-start | bytes 294920 | tf_op jit(solution)/shard_map/ppermute | solution.py:500
  103.1 9.6 %collective-permute-start.32 = (bf16[2,96,256]{2,1,0:T(8,128)(2,1)S(1)}, bf16[2,96,256]{2,1,0:T(8,128)(2,1)S(1)}, u32[]{:S(2)}, u32[]{:S(2)}) collective-permute-start(bf16[2,96,256]{2,1,0:T(8,128)(2,1)S(1)} %get-tuple-element.58.refs_4_), channel_id=1, source_target_pairs={{0,128},{16,144},{32,160},{48,176},{64,192},{80,208},{96,224},{112... | collective-permute-start | bytes 294920 | tf_op jit(solution)/shard_map/ppermute | solution.py:500
  113.6 9.3 %collective-permute-start.33 = (bf16[8,96,256]{2,1,0:T(8,128)(2,1)S(1)}, bf16[8,96,256]{2,1,0:T(8,128)(2,1)S(1)}, u32[]{:S(2)}, u32[]{:S(2)}) collective-permute-start(bf16[8,96,256]{2,1,0:T(8,128)(2,1)S(1)} %get-tuple-element.59), channel_id=1, source_target_pairs={{0,16},{16,0},{32,48},{48,32},{64,80},{80,64},{96,112},{112,96},{1... | collective-permute-start | bytes 1179656 | tf_op jit(solution)/shard_map/ppermute | solution.py:519
  116.7 9.5 %collective-permute-start.35 = (bf16[2,96,256]{2,1,0:T(8,128)(2,1)S(1)}, bf16[2,96,256]{2,1,0:T(8,128)(2,1)S(1)}, u32[]{:S(2)}, u32[]{:S(2)}) collective-permute-start(bf16[2,96,256]{2,1,0:T(8,128)(2,1)S(1)} %get-tuple-element.63), channel_id=1, source_target_pairs={{0,32},{16,48},{32,64},{48,80},{64,96},{80,112},{96,128},{112,144}... | collective-permute-start | bytes 294920 | tf_op jit(solution)/shard_map/ppermute | solution.py:500
  118.5 9.5 %collective-permute-start.36 = (bf16[2,96,256]{2,1,0:T(8,128)(2,1)S(1)}, bf16[2,96,256]{2,1,0:T(8,128)(2,1)S(1)}, u32[]{:S(2)}, u32[]{:S(2)}) collective-permute-start(bf16[2,96,256]{2,1,0:T(8,128)(2,1)S(1)} %get-tuple-element.64), channel_id=1, source_target_pairs={{0,224},{16,240},{32,0},{48,16},{64,32},{80,48},{96,64},{112,80},{... | collective-permute-start | bytes 294920 | tf_op jit(solution)/shard_map/ppermute | solution.py:500
  118.8 15.4 %collective-permute-start.37 = (bf16[2,96,256]{2,1,0:T(8,128)(2,1)S(1)}, bf16[2,96,256]{2,1,0:T(8,128)(2,1)S(1)}, u32[]{:S(2)}, u32[]{:S(2)}) collective-permute-start(bf16[2,96,256]{2,1,0:T(8,128)(2,1)S(1)} %get-tuple-element.65), channel_id=1, source_target_pairs={{0,64},{16,80},{32,96},{48,112},{64,128},{80,144},{96,160},{112,17... | collective-permute-start | bytes 294920 | tf_op jit(solution)/shard_map/ppermute | solution.py:500
  120.0 14.2 %collective-permute-start.38 = (bf16[2,96,256]{2,1,0:T(8,128)(2,1)S(1)}, bf16[2,96,256]{2,1,0:T(8,128)(2,1)S(1)}, u32[]{:S(2)}, u32[]{:S(2)}) collective-permute-start(bf16[2,96,256]{2,1,0:T(8,128)(2,1)S(1)} %get-tuple-element.66), channel_id=1, source_target_pairs={{0,192},{16,208},{32,224},{48,240},{64,0},{80,16},{96,32},{112,48}... | collective-permute-start | bytes 294920 | tf_op jit(solution)/shard_map/ppermute | solution.py:500
  123.0 12.1 %collective-permute-start.39 = (bf16[2,96,256]{2,1,0:T(8,128)(2,1)S(1)}, bf16[2,96,256]{2,1,0:T(8,128)(2,1)S(1)}, u32[]{:S(2)}, u32[]{:S(2)}) collective-permute-start(bf16[2,96,256]{2,1,0:T(8,128)(2,1)S(1)} %get-tuple-element.67), channel_id=1, source_target_pairs={{0,96},{16,112},{32,128},{48,144},{64,160},{80,176},{96,192},{112,... | collective-permute-start | bytes 294920 | tf_op jit(solution)/shard_map/ppermute | solution.py:500
  126.2 15.4 %collective-permute-start.40 = (bf16[2,96,256]{2,1,0:T(8,128)(2,1)S(1)}, bf16[2,96,256]{2,1,0:T(8,128)(2,1)S(1)}, u32[]{:S(2)}, u32[]{:S(2)}) collective-permute-start(bf16[2,96,256]{2,1,0:T(8,128)(2,1)S(1)} %get-tuple-element.68), channel_id=1, source_target_pairs={{0,160},{16,176},{32,192},{48,208},{64,224},{80,240},{96,0},{112,1... | collective-permute-start | bytes 294920 | tf_op jit(solution)/shard_map/ppermute | solution.py:500
  128.0 13.6 %collective-permute-start.41 = (bf16[2,96,256]{2,1,0:T(8,128)(2,1)S(1)}, bf16[2,96,256]{2,1,0:T(8,128)(2,1)S(1)}, u32[]{:S(2)}, u32[]{:S(2)}) collective-permute-start(bf16[2,96,256]{2,1,0:T(8,128)(2,1)S(1)} %get-tuple-element.69), channel_id=1, source_target_pairs={{0,128},{16,144},{32,160},{48,176},{64,192},{80,208},{96,224},{112... | collective-permute-start | bytes 294920 | tf_op jit(solution)/shard_map/ppermute | solution.py:500
  (12 other events, 69.4 us)

commit v6 on v5

--- a/solution.py
+++ b/solution.py
@@ -54,62 +54,36 @@
 
 
 def plan_kernel(owner_ref, spot_ref, grads_ref, table_ref, *refs):
-    outs, empty_ref = refs[:-1], refs[-1]
+    outs, (empty_ref, held, sem) = refs[:-3], refs[-3:]
     count, planes = owner_ref.shape[0], len(outs)
-
-    def clear(g, _):
+    copy = pltpu.make_async_copy(grads_ref, held, sem)
+    copy.start()
+    for g in range(count):
         table_ref[1, g] = 0
         table_ref[2, g] = -1
         table_ref[3, g] = -1
-        return 0
-
-    lax.fori_loop(0, count, clear, 0)
-
-    def first(e, _):
+    for e in range(count):
         g = owner_ref[e]
         seen = table_ref[1, g]
         table_ref[1, g] = seen + 1
-
-        @pl.when(seen == 0)
-        def _():
-            table_ref[0, g] = e
-
-        @pl.when(seen > 0)
-        def _():
-            table_ref[2, g] = e
-
-        return 0
-
-    lax.fori_loop(0, count, first, 0)
-
-    def empties(g, n):
-        none = table_ref[1, g] == 0
-
-        @pl.when(none)
-        def _():
-            empty_ref[n] = g
-
-        return n + none.astype(jnp.int32)
-
-    lax.fori_loop(0, count, empties, 0)
-
-    def second(g, n):
+        table_ref[jnp.where(seen == 0, 0, 2), g] = e
+    n = jnp.int32(0)
+    for g in range(count):
+        empty_ref[n] = g
+        n = n + (table_ref[1, g] == 0).astype(jnp.int32)
+    n = jnp.int32(0)
+    for g in range(count):
         e = table_ref[2, g]
         two = e >= 0
-
-        @pl.when(two)
-        def _():
-            h = empty_ref[n]
-            table_ref[2, g] = h
-            table_ref[0, h] = e
-            table_ref[3, h] = g
-
-        return n + two.astype(jnp.int32)
-
-    lax.fori_loop(0, count, second, 0)
+        h = jnp.where(two, empty_ref[n], count)
+        table_ref[2, g] = jnp.where(two, h, -1)
+        table_ref[0, h] = e
+        table_ref[3, h] = g
+        n = n + two.astype(jnp.int32)
+    copy.wait()
     for away in range(planes):
         for other in range(2):
-            outs[away][other] = grads_ref[table_ref[0, group_at(spot_ref, away, other, planes)]]
+            outs[away][other] = held[table_ref[0, group_at(spot_ref, away, other, planes)]]
 
 
 def plan(owner, spot, grads):
@@ -117,10 +91,15 @@
     planes = count // 2
     return pl.pallas_call(
         plan_kernel,
-        out_shape=(shape_of(4, count, dtype=jnp.int32),) + (shape_of(2, rows, cols),) * planes,
-        in_specs=[SMEM, SMEM, VMEM],
+        out_shape=(shape_of(4, count + 1, dtype=jnp.int32),)
+        + (shape_of(2, rows, cols),) * planes,
+        in_specs=[SMEM, SMEM, ANY],
         out_specs=(SMEM,) + (VMEM,) * planes,
-        scratch_shapes=[pltpu.SMEM((count,), jnp.int32)],
+        scratch_shapes=[
+            pltpu.SMEM((count + 1,), jnp.int32),
+            pltpu.VMEM(grads.shape, grads.dtype),
+            pltpu.SemaphoreType.DMA,
+        ],
         compiler_params=params(8),
         name="plan",
     )(owner, spot, grads)
@@ -157,113 +136,140 @@
     return parts.astype(jnp.bfloat16)
 
 
-def gram_kernel(place_ref, *refs):
-    lists = in_lists(refs[: 2 * SIDE])
-    *outs, picked = refs[2 * SIDE :]
-    each = lists[0][0].shape[0] // BLOCK
+def gram_sums(place_ref, own, got, acc, picked, write):
+    each = own[0].shape[0] // BLOCK
     side = 2 * each
     turn = lax.rem(place_ref[0], SIDE) * PIECE
+    lists = (own, got)
 
     def block(s, i):
         start = (i % each) * BLOCK
         return lists[i // each][s][start : start + BLOCK, :]
 
-    for s in range(SIDE):
+    for s in range(len(own)):
         for i in range(side):
             start = pl.multiple_of((i % each) * BLOCK + turn, PIECE)
             picked[s, i * PIECE : (i + 1) * PIECE, :] = lists[i // each][s][pl.ds(start, PIECE), :]
     index = {pair: t for t, pair in enumerate(pairs_of(side * BLOCK))}
-    cut = outs[0].shape[0]
     for j in range(side):
         total = jnp.zeros(((side - j) * PIECE, BLOCK), jnp.float32)
-        for s in range(SIDE):
+        for s in range(len(own)):
             total = total + lax.dot_general(
                 picked[s, j * PIECE :, :],
                 block(s, j),
                 (((1,), (1,)), ((), ())),
                 preferred_element_type=jnp.float32,
             )
-        total = total.astype(jnp.bfloat16)
         for i in range(j, side):
             t = index[i, j]
-            outs[t // cut][t % cut] = total[(i - j) * PIECE : (i - j + 1) * PIECE, :]
+            value = total[(i - j) * PIECE : (i - j + 1) * PIECE, :]
+            write(t, value if acc is None else value + acc[t])
     total = jnp.zeros((1, BLOCK), jnp.float32)
-    for i in range(side):
-        values = block(0, i).astype(jnp.float32)
-        total = total + jnp.sum(values * values, axis=0, keepdims=True)
-    total = jnp.sum(total, axis=1, keepdims=True)
-    outs[1][outs[1].shape[0] - 1] = split(total, (PIECE, BLOCK))
+    for s in range(len(own)):
+        for i in range(side):
+            values = block(s, i).astype(jnp.float32)
+            total = total + jnp.sum(values * values, axis=0, keepdims=True)
+    return jnp.sum(total, axis=1, keepdims=True)
+
+
+def gram_first_kernel(place_ref, *refs):
+    own, got, (acc, square, picked) = refs[:6:2], (refs[1], refs[5], refs[3]), refs[6:]
+
+    def write(t, value):
+        acc[t] = value
+
+    total = gram_sums(place_ref, own, got, None, picked, write)
+    square[...] = jnp.broadcast_to(total, square.shape)
+
+
+def gram_last_kernel(place_ref, own, got, acc, square, first, second, picked):
+    cut = first.shape[0]
+
+    def write(t, value):
+        (first, second)[t // cut][t % cut] = value.astype(jnp.bfloat16)
+
+    total = gram_sums(place_ref, [own], [got], acc, picked, write)
+    second[second.shape[0] - 1] = split(total + square[0:1, :], (PIECE, BLOCK))
 
 
 def gram_quarter(place, lists):
-    rows = 2 * lists[0][0].shape[0]
+    own, got = lists
+    rows = 2 * own[0].shape[0]
     blocks = len(pairs_of(rows))
     cut = (blocks + 1) // 2
-    return pl.pallas_call(
-        gram_kernel,
+    acc, square = pl.pallas_call(
+        gram_first_kernel,
+        out_shape=(
+            shape_of(blocks, PIECE, BLOCK, dtype=jnp.float32),
+            shape_of(8, BLOCK, dtype=jnp.float32),
+        ),
+        in_specs=[SMEM] + [VMEM] * 6,
+        out_specs=(VMEM,) * 2,
+        scratch_shapes=[pltpu.VMEM((SIDE - 1, rows // SIDE, BLOCK), jnp.bfloat16)],
+        compiler_params=params(16),
+        cost_estimate=cost(3 * blocks * BLOCK**3 // 2, 4 * MIB),
+        name="gram_first",
+    )(place, own[0], got[0], own[1], got[3], own[3], got[1])
+    return pl.pallas_call(
+        gram_last_kernel,
         out_shape=(shape_of(cut, PIECE, BLOCK), shape_of(blocks + 1 - cut, PIECE, BLOCK)),
-        in_specs=[SMEM] + [VMEM] * (2 * SIDE),
+        in_specs=[SMEM] + [VMEM] * 4,
         out_specs=(VMEM,) * 2,
-        scratch_shapes=[pltpu.VMEM((SIDE, rows // SIDE, BLOCK), jnp.bfloat16)],
+        scratch_shapes=[pltpu.VMEM((1, rows // SIDE, BLOCK), jnp.bfloat16)],
         compiler_params=params(16),
-        cost_estimate=cost(2 * blocks * BLOCK**3, 4 * MIB),
-        name="gram",
-    )(place, *out_of_lists(lists))
-
-
-def add_kernel(*refs):
-    lists, outs = in_lists(refs[: 2 * SIDE]), refs[2 * SIDE :]
-    for ins, out in zip(lists, outs):
+        name="gram_last",
+    )(place, own[2], got[2], acc, square)
+
+
+def add_kernel(rows, *refs):
+    lists, (first, second, inverse_ref) = in_lists(refs[: 2 * SIDE]), refs[2 * SIDE :]
+    number = jnp.zeros((1, BLOCK), jnp.float32)
+    for piece in lists[1]:
+        last = piece.shape[0] - 1
+        number = number + jnp.sum(piece[last].astype(jnp.float32), axis=0, keepdims=True)
+    inverse = 1.0 / jnp.sqrt(number / rows + 1e-06)
+    scale = inverse * inverse
+    inverse_ref[...] = jnp.broadcast_to(inverse, inverse_ref.shape)
+    for ins, out in zip(lists, (first, second)):
         total = ins[0][...].astype(jnp.float32)
         for other in ins[1:]:
             total = total + other[...].astype(jnp.float32)
-        out[...] = total.astype(jnp.bfloat16)
-    last = outs[1].shape[0] - 1
-    number = jnp.zeros((1, BLOCK), jnp.float32)
-    for piece in lists[1]:
-        number = number + jnp.sum(piece[last].astype(jnp.float32), axis=0, keepdims=True)
-    outs[1][last] = split(number, (PIECE, BLOCK))
-
-
-def add(lists):
-    return pl.pallas_call(
-        add_kernel,
-        out_shape=tuple(shape_of(*pieces[0].shape) for pieces in lists),
+        out[...] = jnp.where(scale > 0, total * scale, 0.0).astype(jnp.bfloat16)
+
+
+def add(lists, rows):
+    return pl.pallas_call(
+        functools.partial(add_kernel, rows),
+        out_shape=(
+            shape_of(*lists[0][0].shape),
+            shape_of(*lists[1][0].shape),
+            shape_of(8, BLOCK, dtype=jnp.float32),
+        ),
         in_specs=[VMEM] * (2 * SIDE),
-        out_specs=(VMEM,) * 2,
+        out_specs=(VMEM,) * 3,
         compiler_params=params(12),
         name="add",
     )(*out_of_lists(lists))
 
 
-def step_kernel(pairs, factor, planes, place_ref, own_ref, got_ref, *refs):
+def step_kernel(pairs, factor, planes, place_ref, own_ref, got_ref, inverse_ref, *refs):
     early, late = in_lists(refs[: 2 * SIDE])
     outs, (gram, normed, left) = refs[2 * SIDE : -3], refs[-3:]
     half = own_ref.shape[0]
     blocks = early[0].shape[0]
-    total = jnp.zeros((1, BLOCK), jnp.float32)
-    for s in range(SIDE):
-        total = total + jnp.sum(
-            late[s][len(pairs) - blocks].astype(jnp.float32), axis=0, keepdims=True
-        )
-    inverse = 1.0 / jnp.sqrt(total / (2 * half) + 1e-06)
-    scale = inverse * inverse
     side = 2 * half // BLOCK
     for k, ref in enumerate((own_ref, got_ref)):
         for i in range(half // BLOCK):
-            values = ref[i * BLOCK : (i + 1) * BLOCK, :].astype(jnp.float32) * inverse
-            normed[k * half + i * BLOCK : k * half + (i + 1) * BLOCK, :] = values.astype(
-                jnp.bfloat16
-            )
+            values = ref[i * BLOCK : (i + 1) * BLOCK, :].astype(jnp.float32)
+            normed[k * half + i * BLOCK : k * half + (i + 1) * BLOCK, :] = (
+                values * inverse_ref[0:1, :]
+            ).astype(jnp.bfloat16)
     for t, (i, j) in enumerate(pairs):
         source, u = (early, t) if t < blocks else (late, t - blocks)
         for s in range(SIDE):
             p = lax.rem(place_ref[0] - s + SIDE, SIDE)
             rows = pl.ds(pl.multiple_of(i * BLOCK + p * PIECE, PIECE), PIECE)
-            values = source[s][u].astype(jnp.float32) * scale
-            gram[rows, j * BLOCK : (j + 1) * BLOCK] = jnp.where(scale > 0, values, 0.0).astype(
-                jnp.bfloat16
-            )
+            gram[rows, j * BLOCK : (j + 1) * BLOCK] = source[s][u]
     for i, j in pairs:
         if i != j:
             block = gram[i * BLOCK : (i + 1) * BLOCK, j * BLOCK : (j + 1) * BLOCK]
@@ -288,13 +294,13 @@
             outs[away + 1][k] = values[each:]
 
 
-def step(place, own, got, lists, factor, planes):
+def step(place, own, got, inverse, lists, factor, planes):
     half, cols = own.shape
     rows = 2 * half
     return pl.pallas_call(
         functools.partial(step_kernel, pairs_of(rows), factor, planes),
         out_shape=(shape_of(2, half // planes, cols),) * planes,
-        in_specs=[SMEM] + [VMEM] * (2 + 2 * SIDE),
+        in_specs=[SMEM] + [VMEM] * (3 + 2 * SIDE),
         out_specs=(VMEM,) * planes,
         scratch_shapes=[
             pltpu.VMEM((rows, rows), jnp.bfloat16),
@@ -304,7 +310,7 @@
         compiler_params=params(28),
         cost_estimate=cost(4 * rows * rows * cols, 6 * 1024 * 1024),
         name="step",
-    )(place, own, got, *out_of_lists(lists))
+    )(place, own, got, inverse, *out_of_lists(lists))
 
 
 def pick_kernel(planes, table_ref, spot_ref, *refs):
@@ -492,7 +498,7 @@
 def over_planes(blocks, sign):
     planes = len(blocks)
     got = list(blocks)
-    for away in nearest_first(planes)[1:]:
+    for away in farthest_first(planes)[1:]:
         moves = []
         for group in range(2 * planes):
             plane, core = divmod(group, 2)
@@ -501,16 +507,16 @@
     return got
 
 
-def nearest_first(planes):
-    return sorted(range(planes), key=lambda a: min(a, planes - a))
+def farthest_first(planes):
+    return sorted(range(planes), key=lambda a: -min(a, planes - a) if a else -planes)
 
 
 def in_turn(blocks):
-    return [blocks[away] for away in nearest_first(len(blocks))]
+    return [blocks[away] for away in farthest_first(len(blocks))]
 
 
 def in_place(refs):
-    order = nearest_first(len(refs))
+    order = farthest_first(len(refs))
     return [refs[order.index(away)] for away in range(len(refs))]
 
 
@@ -536,8 +542,8 @@
     got = swap(give)
     own, got = own.reshape(rows // 2, cols_dev), got.reshape(rows // 2, cols_dev)
     parts = gram_quarter(place, gather(own, got, 0))
-    parts = add(gather(*parts, 1))
-    done = step(place, own, got, gather(*parts, 0), factor, planes)
+    *parts, inverse = add(gather(*parts, 1), rows)
+    done = step(place, own, got, inverse, gather(*parts, 0), factor, planes)
     back = over_planes(done, -1)
     mine, give, rest = pick(table, spot, back)
     sends = merge(table, spot, mine, swap(give))

time: 143 us -> 141 us (0.986)
  the two profiles are of different devices: /device:TPU:62 before, /device:TPU:1 now
where the time goes in v6:
time: 141 us; the launch traced here: 140 us
  starting transfers between devices  68.4 us (49%)
  waiting for transfers between devices  54.4 us (39%)
  Pallas kernels  14.4 us (10%)
  local copies, waits for them, and re-layouts  1.88 us (1%)
    ppermute x21, starting transfers between devices, over_planes(): got[away] = lax.ppermute(blocks[away], 'fsdp', moves)  39.9 us
    ppermute x21, waiting for transfers between devices, over_planes(): got[away] = lax.ppermute(blocks[away], 'fsdp', moves)  28.1 us
    ppermute x18, waiting for transfers between devices, neighbour(): return lax.ppermute(value, ('fsdp', 'grp'), moves)  24.4 us
    ppermute x18, starting transfers between devices, neighbour(): return lax.ppermute(value, ('fsdp', 'grp'), moves)  23.4 us
    ppermute x3, starting transfers between devices, swap(): return lax.ppermute(value, 'fsdp', [(g, g ^ 1) for g in range(groups)])  5.04 us
    pallas_call x1, Pallas kernels, step(): pl.pallas_call(functools.partial(step_kernel, pairs_of(rows), factor, pla...  3.65 us
  transfers between devices with their start and end apart: 42, of which 25 were waited for; matrix products, arithmetic and copies ran while one was open for 0% of the time, Pallas kernels for 4%

profile of v6, /device:TPU:1, one launch (start us, length us, event | category | flops | bytes accessed | tf_op | source)
XLA Modules:
  0.0 140.3 jit_solution(16112125758156168008)
XLA Ops:
  4.1 7.8 %collective-permute-start = (bf16[2,96,256]{2,1,0:T(8,128)(2,1)S(1)}, bf16[2,96,256]{2,1,0:T(8,128)(2,1)S(1)}, u32[]{:S(2)}, u32[]{:S(2)}) collective-permute-start(bf16[2,96,256]{2,1,0:T(8,128)(2,1)S(1)} %get-tuple-element.41), channel_id=1, source_target_pairs={{0,128},{16,144},{32,160},{48,176},{64,192},{80,208},{96,224},{112... | collective-permute-start | bytes 294920 | tf_op jit(solution)/shard_map/ppermute | solution.py:506
  11.9 1.6 %collective-permute-start.1 = (bf16[2,96,256]{2,1,0:T(8,128)(2,1)S(1)}, bf16[2,96,256]{2,1,0:T(8,128)(2,1)S(1)}, u32[]{:S(2)}, u32[]{:S(2)}) collective-permute-start(bf16[2,96,256]{2,1,0:T(8,128)(2,1)S(1)} %get-tuple-element.42), channel_id=1, source_target_pairs={{0,96},{16,112},{32,128},{48,144},{64,160},{80,176},{96,192},{112,... | collective-permute-start | bytes 294920 | tf_op jit(solution)/shard_map/ppermute | solution.py:506
  13.5 2.8 %collective-permute-start.2 = (bf16[2,96,256]{2,1,0:T(8,128)(2,1)S(1)}, bf16[2,96,256]{2,1,0:T(8,128)(2,1)S(1)}, u32[]{:S(2)}, u32[]{:S(2)}) collective-permute-start(bf16[2,96,256]{2,1,0:T(8,128)(2,1)S(1)} %get-tuple-element.43), channel_id=1, source_target_pairs={{0,160},{16,176},{32,192},{48,208},{64,224},{80,240},{96,0},{112,1... | collective-permute-start | bytes 294920 | tf_op jit(solution)/shard_map/ppermute | solution.py:506
  17.6 2.4 %collective-permute-start.4 = (bf16[2,96,256]{2,1,0:T(8,128)(2,1)S(1)}, bf16[2,96,256]{2,1,0:T(8,128)(2,1)S(1)}, u32[]{:S(2)}, u32[]{:S(2)}) collective-permute-start(bf16[2,96,256]{2,1,0:T(8,128)(2,1)S(1)} %get-tuple-element.45), channel_id=1, source_target_pairs={{0,192},{16,208},{32,224},{48,240},{64,0},{80,16},{96,32},{112,48}... | collective-permute-start | bytes 294920 | tf_op jit(solution)/shard_map/ppermute | solution.py:506
  20.7 4.6 %collective-permute-done.1.refs_2_ = bf16[2,96,256]{2,1,0:T(8,128)(2,1)S(1)} collective-permute-done((bf16[2,96,256]{2,1,0:T(8,128)(2,1)S(1)}, bf16[2,96,256]{2,1,0:T(8,128)(2,1)S(1)}, u32[]{:S(2)}, u32[]{:S(2)}) %collective-permute-start.1) | collective-permute-done | bytes 98336 | tf_op jit(solution)/shard_map/ppermute | solution.py:506
  25.3 3.0 %collective-permute-done.4.refs_5_ = bf16[2,96,256]{2,1,0:T(8,128)(2,1)S(1)} collective-permute-done((bf16[2,96,256]{2,1,0:T(8,128)(2,1)S(1)}, bf16[2,96,256]{2,1,0:T(8,128)(2,1)S(1)}, u32[]{:S(2)}, u32[]{:S(2)}) %collective-permute-start.4) | collective-permute-done | bytes 98336 | tf_op jit(solution)/shard_map/ppermute | solution.py:506
  33.1 2.7 %collective-permute-start.10 = (bf16[768,256]{1,0:T(8,128)(2,1)S(1)}, bf16[768,256]{1,0:T(8,128)(2,1)S(1)}, u32[]{:S(2)}, u32[]{:S(2)}) collective-permute-start(bf16[768,256]{1,0:T(8,128)(2,1)S(1)} %bitcast.10), channel_id=1, source_target_pairs={{0,3},{1,0},{2,1},{3,2},{4,7},{5,4},{6,5},{7,6},{8,11},{9,8},{10,9... | collective-permute-start | bytes 1179656 | tf_op jit(solution)/shard_map/ppermute | solution.py:476
  37.3 2.6 %collective-permute-done.8.refs_2_ = bf16[768,256]{1,0:T(8,128)(2,1)S(1)} collective-permute-done((bf16[768,256]{1,0:T(8,128)(2,1)S(1)}, bf16[768,256]{1,0:T(8,128)(2,1)S(1)}, u32[]{:S(2)}, u32[]{:S(2)}) %collective-permute-start.8) | collective-permute-done | bytes 393248 | tf_op jit(solution)/shard_map/ppermute | solution.py:476
  40.5 3.1 %collective-permute-start.11 = (bf16[768,256]{1,0:T(8,128)(2,1)S(1)}, bf16[768,256]{1,0:T(8,128)(2,1)S(1)}, u32[]{:S(2)}, u32[]{:S(2)}) collective-permute-start(bf16[768,256]{1,0:T(8,128)(2,1)S(1)} %collective-permute-done.10.refs_3_), channel_id=1, source_target_pairs={{0,3},{1,0},{2,1},{3,2},{4,7},{5,4},{6,5},{7,6},{8,11},{9,8},{10,9... | collective-permute-start | bytes 1179656 | tf_op jit(solution)/shard_map/ppermute | solution.py:476
  46.2 2.5 %collective-permute-done.9.own = bf16[768,256]{1,0:T(8,128)(2,1)S(1)} collective-permute-done((bf16[768,256]{1,0:T(8,128)(2,1)S(1)}, bf16[768,256]{1,0:T(8,128)(2,1)S(1)}, u32[]{:S(2)}, u32[]{:S(2)}) %collective-permute-start.9) | collective-permute-done | bytes 393248 | tf_op jit(solution)/shard_map/ppermute | solution.py:476
  54.3 3.6 %collective-permute-done.14.refs_2_ = bf16[11,64,256]{2,1,0:T(8,128)(2,1)S(1)} collective-permute-done((bf16[11,64,256]{2,1,0:T(8,128)(2,1)S(1)}, bf16[11,64,256]{2,1,0:T(8,128)(2,1)S(1)}, u32[]{:S(2)}, u32[]{:S(2)}) %collective-permute-start.14) | collective-permute-done | bytes 360480 | tf_op jit(solution)/shard_map/ppermute | solution.py:476
  57.9 2.7 %collective-permute-start.19 = (bf16[11,64,256]{2,1,0:T(8,128)(2,1)S(1)}, bf16[11,64,256]{2,1,0:T(8,128)(2,1)S(1)}, u32[]{:S(2)}, u32[]{:S(2)}) collective-permute-start(bf16[11,64,256]{2,1,0:T(8,128)(2,1)S(1)} %collective-permute-done.15.refs_3_), channel_id=1, source_target_pairs={{0,12},{1,13},{2,14},{3,15},{4,0},{5,1},{6,2},{7,3},{8,4},{9,5},{1... | collective-permute-start | bytes 1081352 | tf_op jit(solution)/shard_map/ppermute | solution.py:476
  61.9 3.9 %collective-permute-done.18.refs_6_ = bf16[11,64,256]{2,1,0:T(8,128)(2,1)S(1)} collective-permute-done((bf16[11,64,256]{2,1,0:T(8,128)(2,1)S(1)}, bf16[11,64,256]{2,1,0:T(8,128)(2,1)S(1)}, u32[]{:S(2)}, u32[]{:S(2)}) %collective-permute-start.18) | collective-permute-done | bytes 360480 | tf_op jit(solution)/shard_map/ppermute | solution.py:476
  67.0 2.8 %collective-permute-start.21 = (bf16[11,64,256]{2,1,0:T(8,128)(2,1)S(1)}, bf16[11,64,256]{2,1,0:T(8,128)(2,1)S(1)}, u32[]{:S(2)}, u32[]{:S(2)}) collective-permute-start(bf16[11,64,256]{2,1,0:T(8,128)(2,1)S(1)} %get-tuple-element.56.refs_1_), channel_id=1, source_target_pairs={{0,3},{1,0},{2,1},{3,2},{4,7},{5,4},{6,5},{7,6},{8,11},{9,8},{10,9... | collective-permute-start | bytes 1081352 | tf_op jit(solution)/shard_map/ppermute | solution.py:476
  71.3 3.6 %collective-permute-done.20.refs_2_ = bf16[11,64,256]{2,1,0:T(8,128)(2,1)S(1)} collective-permute-done((bf16[11,64,256]{2,1,0:T(8,128)(2,1)S(1)}, bf16[11,64,256]{2,1,0:T(8,128)(2,1)S(1)}, u32[]{:S(2)}, u32[]{:S(2)}) %collective-permute-start.20) | collective-permute-done | bytes 360480 | tf_op jit(solution)/shard_map/ppermute | solution.py:476
  74.8 2.8 %collective-permute-start.25 = (bf16[11,64,256]{2,1,0:T(8,128)(2,1)S(1)}, bf16[11,64,256]{2,1,0:T(8,128)(2,1)S(1)}, u32[]{:S(2)}, u32[]{:S(2)}) collective-permute-start(bf16[11,64,256]{2,1,0:T(8,128)(2,1)S(1)} %collective-permute-done.21.refs_3_), channel_id=1, source_target_pairs={{0,3},{1,0},{2,1},{3,2},{4,7},{5,4},{6,5},{7,6},{8,11},{9,8},{10,9... | collective-permute-start | bytes 1081352 | tf_op jit(solution)/shard_map/ppermute | solution.py:476
  78.7 4.2 %collective-permute-done.24.refs_6_ = bf16[11,64,256]{2,1,0:T(8,128)(2,1)S(1)} collective-permute-done((bf16[11,64,256]{2,1,0:T(8,128)(2,1)S(1)}, bf16[11,64,256]{2,1,0:T(8,128)(2,1)S(1)}, u32[]{:S(2)}, u32[]{:S(2)}) %collective-permute-start.24) | collective-permute-done | bytes 360480 | tf_op jit(solution)/shard_map/ppermute | solution.py:476
  82.8 3.7 %step.1 = (bf16[2,96,256]{2,1,0:T(8,128)(2,1)S(1)}, bf16[2,96,256]{2,1,0:T(8,128)(2,1)S(1)}, bf16[2,96,256]{2,1,0:T(8,128)(2,1)S(1)}, bf16[2,96,256]{2,1,0:T(8,1...) custom-call(s32[2]{0:T(128)S(1)} %broadcast_select_fusion.place_ref,, ...), custom_call_target="tpu_custom_call" | custom-call | flops 2415919104 | bytes 6291456 | tf_op jit(solution)/shard_map/step/pallas_call | solution.py:300
  86.5 3.2 %collective-permute-start.26 = (bf16[2,96,256]{2,1,0:T(8,128)(2,1)S(1)}, bf16[2,96,256]{2,1,0:T(8,128)(2,1)S(1)}, u32[]{:S(2)}, u32[]{:S(2)}) collective-permute-start(bf16[2,96,256]{2,1,0:T(8,128)(2,1)S(1)} %get-tuple-element.58.refs_4_), channel_id=1, source_target_pairs={{0,128},{16,144},{32,160},{48,176},{64,192},{80,208},{96,224},{112... | collective-permute-start | bytes 294920 | tf_op jit(solution)/shard_map/ppermute | solution.py:506
  89.6 1.7 %collective-permute-start.27 = (bf16[2,96,256]{2,1,0:T(8,128)(2,1)S(1)}, bf16[2,96,256]{2,1,0:T(8,128)(2,1)S(1)}, u32[]{:S(2)}, u32[]{:S(2)}) collective-permute-start(bf16[2,96,256]{2,1,0:T(8,128)(2,1)S(1)} %get-tuple-element.59.refs_3_), channel_id=1, source_target_pairs={{0,160},{16,176},{32,192},{48,208},{64,224},{80,240},{96,0},{112,1... | collective-permute-start | bytes 294920 | tf_op jit(solution)/shard_map/ppermute | solution.py:506
  91.3 1.6 %collective-permute-start.28 = (bf16[2,96,256]{2,1,0:T(8,128)(2,1)S(1)}, bf16[2,96,256]{2,1,0:T(8,128)(2,1)S(1)}, u32[]{:S(2)}, u32[]{:S(2)}) collective-permute-start(bf16[2,96,256]{2,1,0:T(8,128)(2,1)S(1)} %get-tuple-element.60.refs_5_), channel_id=1, source_target_pairs={{0,96},{16,112},{32,128},{48,144},{64,160},{80,176},{96,192},{112,... | collective-permute-start | bytes 294920 | tf_op jit(solution)/shard_map/ppermute | solution.py:506
  92.9 2.9 %collective-permute-start.29 = (bf16[2,96,256]{2,1,0:T(8,128)(2,1)S(1)}, bf16[2,96,256]{2,1,0:T(8,128)(2,1)S(1)}, u32[]{:S(2)}, u32[]{:S(2)}) collective-permute-start(bf16[2,96,256]{2,1,0:T(8,128)(2,1)S(1)} %get-tuple-element.61.refs_2_), channel_id=1, source_target_pairs={{0,192},{16,208},{32,224},{48,240},{64,0},{80,16},{96,32},{112,48}... | collective-permute-start | bytes 294920 | tf_op jit(solution)/shard_map/ppermute | solution.py:506
  95.8 3.0 %collective-permute-start.31 = (bf16[2,96,256]{2,1,0:T(8,128)(2,1)S(1)}, bf16[2,96,256]{2,1,0:T(8,128)(2,1)S(1)}, u32[]{:S(2)}, u32[]{:S(2)}) collective-permute-start(bf16[2,96,256]{2,1,0:T(8,128)(2,1)S(1)} %get-tuple-element.63.refs_1_), channel_id=1, source_target_pairs={{0,224},{16,240},{32,0},{48,16},{64,32},{80,48},{96,64},{112,80},{... | collective-permute-start | bytes 294920 | tf_op jit(solution)/shard_map/ppermute | solution.py:506
  98.8 4.9 %collective-permute-done.29.refs_4_ = bf16[2,96,256]{2,1,0:T(8,128)(2,1)S(1)} collective-permute-done((bf16[2,96,256]{2,1,0:T(8,128)(2,1)S(1)}, bf16[2,96,256]{2,1,0:T(8,128)(2,1)S(1)}, u32[]{:S(2)}, u32[]{:S(2)}) %collective-permute-start.29) | collective-permute-done | bytes 98336 | tf_op jit(solution)/shard_map/ppermute | solution.py:506
  103.7 1.8 %collective-permute-done.30.refs_5_ = bf16[2,96,256]{2,1,0:T(8,128)(2,1)S(1)} collective-permute-done((bf16[2,96,256]{2,1,0:T(8,128)(2,1)S(1)}, bf16[2,96,256]{2,1,0:T(8,128)(2,1)S(1)}, u32[]{:S(2)}, u32[]{:S(2)}) %collective-permute-start.30) | collective-permute-done | bytes 98336 | tf_op jit(solution)/shard_map/ppermute | solution.py:506
  106.6 2.5 %collective-permute-done.32.refs_7_ = bf16[2,96,256]{2,1,0:T(8,128)(2,1)S(1)} collective-permute-done((bf16[2,96,256]{2,1,0:T(8,128)(2,1)S(1)}, bf16[2,96,256]{2,1,0:T(8,128)(2,1)S(1)}, u32[]{:S(2)}, u32[]{:S(2)}) %collective-permute-start.32) | collective-permute-done | bytes 98336 | tf_op jit(solution)/shard_map/ppermute | solution.py:506
  110.0 4.0 %collective-permute-start.34 = (bf16[8,2,96,256]{3,2,1,0:T(8,128)(2,1)S(1)}, bf16[8,2,96,256]{3,2,1,0:T(8,128)(2,1)S(1)}, u32[]{:S(2)}, u32[]{:S(2)}) collective-permute-start(bf16[8,2,96,256]{3,2,1,0:T(8,128)(2,1)S(1)} %get-tuple-element.67), channel_id=1, source_target_pairs={{0,16},{16,0},{32,48},{48,32},{64,80},{80,64},{96,112},{112,96},{1... | collective-permute-start | bytes 2359304 | tf_op jit(solution)/shard_map/ppermute | solution.py:525
  114.0 1.8 %collective-permute-done.34.got_ref = bf16[8,2,96,256]{3,2,1,0:T(8,128)(2,1)S(1)} collective-permute-done((bf16[8,2,96,256]{3,2,1,0:T(8,128)(2,1)S(1)}, bf16[8,2,96,256]{3,2,1,0:T(8,128)(2,1)S(1)}, u32[]{:S(2)}, u32[]{:S(2)}) %collective-permute-start.34) | collective-permute-done | bytes 786464 | tf_op jit(solution)/shard_map/ppermute | solution.py:525
  116.7 2.0 %collective-permute-start.35 = (bf16[2,96,256]{2,1,0:T(8,128)(2,1)S(1)}, bf16[2,96,256]{2,1,0:T(8,128)(2,1)S(1)}, u32[]{:S(2)}, u32[]{:S(2)}) collective-permute-start(bf16[2,96,256]{2,1,0:T(8,128)(2,1)S(1)} %get-tuple-element.69), channel_id=1, source_target_pairs={{0,128},{16,144},{32,160},{48,176},{64,192},{80,208},{96,224},{112... | collective-permute-start | bytes 294920 | tf_op jit(solution)/shard_map/ppermute | solution.py:506
  120.2 2.9 %collective-permute-start.37 = (bf16[2,96,256]{2,1,0:T(8,128)(2,1)S(1)}, bf16[2,96,256]{2,1,0:T(8,128)(2,1)S(1)}, u32[]{:S(2)}, u32[]{:S(2)}) collective-permute-start(bf16[2,96,256]{2,1,0:T(8,128)(2,1)S(1)} %get-tuple-element.71), channel_id=1, source_target_pairs={{0,160},{16,176},{32,192},{48,208},{64,224},{80,240},{96,0},{112,1... | collective-permute-start | bytes 294920 | tf_op jit(solution)/shard_map/ppermute | solution.py:506
  123.1 2.1 %collective-permute-start.38 = (bf16[2,96,256]{2,1,0:T(8,128)(2,1)S(1)}, bf16[2,96,256]{2,1,0:T(8,128)(2,1)S(1)}, u32[]{:S(2)}, u32[]{:S(2)}) collective-permute-start(bf16[2,96,256]{2,1,0:T(8,128)(2,1)S(1)} %get-tuple-element.72), channel_id=1, source_target_pairs={{0,64},{16,80},{32,96},{48,112},{64,128},{80,144},{96,160},{112,17... | collective-permute-start | bytes 294920 | tf_op jit(solution)/shard_map/ppermute | solution.py:506
  127.7 7.4 %collective-permute-done.36.refs_2_ = bf16[2,96,256]{2,1,0:T(8,128)(2,1)S(1)} collective-permute-done((bf16[2,96,256]{2,1,0:T(8,128)(2,1)S(1)}, bf16[2,96,256]{2,1,0:T(8,128)(2,1)S(1)}, u32[]{:S(2)}, u32[]{:S(2)}) %collective-permute-start.36) | collective-permute-done | bytes 98336 | tf_op jit(solution)/shard_map/ppermute | solution.py:506
  (71 shorter events, 37.2 us)
Async XLA Ops:
  4.1 15.9 %collective-permute-start = (bf16[2,96,256]{2,1,0:T(8,128)(2,1)S(1)}, bf16[2,96,256]{2,1,0:T(8,128)(2,1)S(1)}, u32[]{:S(2)}, u32[]{:S(2)}) collective-permute-start(bf16[2,96,256]{2,1,0:T(8,128)(2,1)S(1)} %get-tuple-element.41), channel_id=1, source_target_pairs={{0,128},{16,144},{32,160},{48,176},{64,192},{80,208},{96,224},{112... | collective-permute-start | bytes 294920 | tf_op jit(solution)/shard_map/ppermute | solution.py:506
  11.9 13.4 %collective-permute-start.1 = (bf16[2,96,256]{2,1,0:T(8,128)(2,1)S(1)}, bf16[2,96,256]{2,1,0:T(8,128)(2,1)S(1)}, u32[]{:S(2)}, u32[]{:S(2)}) collective-permute-start(bf16[2,96,256]{2,1,0:T(8,128)(2,1)S(1)} %get-tuple-element.42), channel_id=1, source_target_pairs={{0,96},{16,112},{32,128},{48,144},{64,160},{80,176},{96,192},{112,... | collective-permute-start | bytes 294920 | tf_op jit(solution)/shard_map/ppermute | solution.py:506
  13.5 11.8 %collective-permute-start.2 = (bf16[2,96,256]{2,1,0:T(8,128)(2,1)S(1)}, bf16[2,96,256]{2,1,0:T(8,128)(2,1)S(1)}, u32[]{:S(2)}, u32[]{:S(2)}) collective-permute-start(bf16[2,96,256]{2,1,0:T(8,128)(2,1)S(1)} %get-tuple-element.43), channel_id=1, source_target_pairs={{0,160},{16,176},{32,192},{48,208},{64,224},{80,240},{96,0},{112,1... | collective-permute-start | bytes 294920 | tf_op jit(solution)/shard_map/ppermute | solution.py:506
  16.4 9.0 %collective-permute-start.3 = (bf16[2,96,256]{2,1,0:T(8,128)(2,1)S(1)}, bf16[2,96,256]{2,1,0:T(8,128)(2,1)S(1)}, u32[]{:S(2)}, u32[]{:S(2)}) collective-permute-start(bf16[2,96,256]{2,1,0:T(8,128)(2,1)S(1)} %get-tuple-element.44), channel_id=1, source_target_pairs={{0,64},{16,80},{32,96},{48,112},{64,128},{80,144},{96,160},{112,17... | collective-permute-start | bytes 294920 | tf_op jit(solution)/shard_map/ppermute | solution.py:506
  17.6 10.8 %collective-permute-start.4 = (bf16[2,96,256]{2,1,0:T(8,128)(2,1)S(1)}, bf16[2,96,256]{2,1,0:T(8,128)(2,1)S(1)}, u32[]{:S(2)}, u32[]{:S(2)}) collective-permute-start(bf16[2,96,256]{2,1,0:T(8,128)(2,1)S(1)} %get-tuple-element.45), channel_id=1, source_target_pairs={{0,192},{16,208},{32,224},{48,240},{64,0},{80,16},{96,32},{112,48}... | collective-permute-start | bytes 294920 | tf_op jit(solution)/shard_map/ppermute | solution.py:506
  19.9 9.9 %collective-permute-start.5 = (bf16[2,96,256]{2,1,0:T(8,128)(2,1)S(1)}, bf16[2,96,256]{2,1,0:T(8,128)(2,1)S(1)}, u32[]{:S(2)}, u32[]{:S(2)}) collective-permute-start(bf16[2,96,256]{2,1,0:T(8,128)(2,1)S(1)} %get-tuple-element.46), channel_id=1, source_target_pairs={{0,32},{16,48},{32,64},{48,80},{64,96},{80,112},{96,128},{112,144}... | collective-permute-start | bytes 294920 | tf_op jit(solution)/shard_map/ppermute | solution.py:506
  31.8 8.1 %collective-permute-start.8 = (bf16[768,256]{1,0:T(8,128)(2,1)S(1)}, bf16[768,256]{1,0:T(8,128)(2,1)S(1)}, u32[]{:S(2)}, u32[]{:S(2)}) collective-permute-start(bf16[768,256]{1,0:T(8,128)(2,1)S(1)} %bitcast.6), channel_id=1, source_target_pairs={{0,1},{1,2},{2,3},{3,0},{4,5},{5,6},{6,7},{7,4},{8,9},{9,10},{10,1... | collective-permute-start | bytes 1179656 | tf_op jit(solution)/shard_map/ppermute | solution.py:476
  35.8 8.9 %collective-permute-start.12 = (bf16[768,256]{1,0:T(8,128)(2,1)S(1)}, bf16[768,256]{1,0:T(8,128)(2,1)S(1)}, u32[]{:S(2)}, u32[]{:S(2)}) collective-permute-start(bf16[768,256]{1,0:T(8,128)(2,1)S(1)} %bitcast.7), channel_id=1, source_target_pairs={{0,3},{1,0},{2,1},{3,2},{4,7},{5,4},{6,5},{7,6},{8,11},{9,8},{10,9... | collective-permute-start | bytes 1179656 | tf_op jit(solution)/shard_map/ppermute | solution.py:476
  36.3 8.5 %collective-permute-start.13 = (bf16[768,256]{1,0:T(8,128)(2,1)S(1)}, bf16[768,256]{1,0:T(8,128)(2,1)S(1)}, u32[]{:S(2)}, u32[]{:S(2)}) collective-permute-start(bf16[768,256]{1,0:T(8,128)(2,1)S(1)} %bitcast.11), channel_id=1, source_target_pairs={{0,1},{1,2},{2,3},{3,0},{4,5},{5,6},{6,7},{7,4},{8,9},{9,10},{10,1... | collective-permute-start | bytes 1179656 | tf_op jit(solution)/shard_map/ppermute | solution.py:476
  39.9 8.7 %collective-permute-start.9 = (bf16[768,256]{1,0:T(8,128)(2,1)S(1)}, bf16[768,256]{1,0:T(8,128)(2,1)S(1)}, u32[]{:S(2)}, u32[]{:S(2)}) collective-permute-start(bf16[768,256]{1,0:T(8,128)(2,1)S(1)} %collective-permute-done.8.refs_2_), channel_id=1, source_target_pairs={{0,1},{1,2},{2,3},{3,0},{4,5},{5,6},{6,7},{7,4},{8,9},{9,10},{10,1... | collective-permute-start | bytes 1179656 | tf_op jit(solution)/shard_map/ppermute | solution.py:476
  40.5 8.4 %collective-permute-start.11 = (bf16[768,256]{1,0:T(8,128)(2,1)S(1)}, bf16[768,256]{1,0:T(8,128)(2,1)S(1)}, u32[]{:S(2)}, u32[]{:S(2)}) collective-permute-start(bf16[768,256]{1,0:T(8,128)(2,1)S(1)} %collective-permute-done.10.refs_3_), channel_id=1, source_target_pairs={{0,3},{1,0},{2,1},{3,2},{4,7},{5,4},{6,5},{7,6},{8,11},{9,8},{10,9... | collective-permute-start | bytes 1179656 | tf_op jit(solution)/shard_map/ppermute | solution.py:476
  49.9 8.0 %collective-permute-start.14 = (bf16[11,64,256]{2,1,0:T(8,128)(2,1)S(1)}, bf16[11,64,256]{2,1,0:T(8,128)(2,1)S(1)}, u32[]{:S(2)}, u32[]{:S(2)}) collective-permute-start(bf16[11,64,256]{2,1,0:T(8,128)(2,1)S(1)} %get-tuple-element.52.refs_0_), channel_id=1, source_target_pairs={{0,4},{1,5},{2,6},{3,7},{4,8},{5,9},{6,10},{7,11},{8,12},{9,13},{1... | collective-permute-start | bytes 1081352 | tf_op jit(solution)/shard_map/ppermute | solution.py:476
  52.8 9.0 %collective-permute-start.16 = (bf16[11,64,256]{2,1,0:T(8,128)(2,1)S(1)}, bf16[11,64,256]{2,1,0:T(8,128)(2,1)S(1)}, u32[]{:S(2)}, u32[]{:S(2)}) collective-permute-start(bf16[11,64,256]{2,1,0:T(8,128)(2,1)S(1)} %get-tuple-element.52.refs_0_), channel_id=1, source_target_pairs={{0,12},{1,13},{2,14},{3,15},{4,0},{5,1},{6,2},{7,3},{8,4},{9,5},{1... | collective-permute-start | bytes 1081352 | tf_op jit(solution)/shard_map/ppermute | solution.py:476
  57.9 7.8 %collective-permute-start.18 = (bf16[11,64,256]{2,1,0:T(8,128)(2,1)S(1)}, bf16[11,64,256]{2,1,0:T(8,128)(2,1)S(1)}, u32[]{:S(2)}, u32[]{:S(2)}) collective-permute-start(bf16[11,64,256]{2,1,0:T(8,128)(2,1)S(1)} %collective-permute-done.14.refs_2_), channel_id=1, source_target_pairs={{0,4},{1,5},{2,6},{3,7},{4,8},{5,9},{6,10},{7,11},{8,12},{9,13},{1... | collective-permute-start | bytes 1081352 | tf_op jit(solution)/shard_map/ppermute | solution.py:476
  66.2 8.6 %collective-permute-start.20 = (bf16[11,64,256]{2,1,0:T(8,128)(2,1)S(1)}, bf16[11,64,256]{2,1,0:T(8,128)(2,1)S(1)}, u32[]{:S(2)}, u32[]{:S(2)}) collective-permute-start(bf16[11,64,256]{2,1,0:T(8,128)(2,1)S(1)} %get-tuple-element.55.refs_0_), channel_id=1, source_target_pairs={{0,1},{1,2},{2,3},{3,0},{4,5},{5,6},{6,7},{7,4},{8,9},{9,10},{10,1... | collective-permute-start | bytes 1081352 | tf_op jit(solution)/shard_map/ppermute | solution.py:476
  67.0 7.9 %collective-permute-start.21 = (bf16[11,64,256]{2,1,0:T(8,128)(2,1)S(1)}, bf16[11,64,256]{2,1,0:T(8,128)(2,1)S(1)}, u32[]{:S(2)}, u32[]{:S(2)}) collective-permute-start(bf16[11,64,256]{2,1,0:T(8,128)(2,1)S(1)} %get-tuple-element.56.refs_1_), channel_id=1, source_target_pairs={{0,3},{1,0},{2,1},{3,2},{4,7},{5,4},{6,5},{7,6},{8,11},{9,8},{10,9... | collective-permute-start | bytes 1081352 | tf_op jit(solution)/shard_map/ppermute | solution.py:476
  69.8 8.2 %collective-permute-start.22 = (bf16[11,64,256]{2,1,0:T(8,128)(2,1)S(1)}, bf16[11,64,256]{2,1,0:T(8,128)(2,1)S(1)}, u32[]{:S(2)}, u32[]{:S(2)}) collective-permute-start(bf16[11,64,256]{2,1,0:T(8,128)(2,1)S(1)} %get-tuple-element.55.refs_0_), channel_id=1, source_target_pairs={{0,3},{1,0},{2,1},{3,2},{4,7},{5,4},{6,5},{7,6},{8,11},{9,8},{10,9... | collective-permute-start | bytes 1081352 | tf_op jit(solution)/shard_map/ppermute | solution.py:476
  74.8 8.0 %collective-permute-start.24 = (bf16[11,64,256]{2,1,0:T(8,128)(2,1)S(1)}, bf16[11,64,256]{2,1,0:T(8,128)(2,1)S(1)}, u32[]{:S(2)}, u32[]{:S(2)}) collective-permute-start(bf16[11,64,256]{2,1,0:T(8,128)(2,1)S(1)} %collective-permute-done.20.refs_2_), channel_id=1, source_target_pairs={{0,1},{1,2},{2,3},{3,0},{4,5},{5,6},{6,7},{7,4},{8,9},{9,10},{10,1... | collective-permute-start | bytes 1081352 | tf_op jit(solution)/shard_map/ppermute | solution.py:476
  74.8 8.0 %collective-permute-start.25 = (bf16[11,64,256]{2,1,0:T(8,128)(2,1)S(1)}, bf16[11,64,256]{2,1,0:T(8,128)(2,1)S(1)}, u32[]{:S(2)}, u32[]{:S(2)}) collective-permute-start(bf16[11,64,256]{2,1,0:T(8,128)(2,1)S(1)} %collective-permute-done.21.refs_3_), channel_id=1, source_target_pairs={{0,3},{1,0},{2,1},{3,2},{4,7},{5,4},{6,5},{7,6},{8,11},{9,8},{10,9... | collective-permute-start | bytes 1081352 | tf_op jit(solution)/shard_map/ppermute | solution.py:476
  86.5 9.3 %collective-permute-start.26 = (bf16[2,96,256]{2,1,0:T(8,128)(2,1)S(1)}, bf16[2,96,256]{2,1,0:T(8,128)(2,1)S(1)}, u32[]{:S(2)}, u32[]{:S(2)}) collective-permute-start(bf16[2,96,256]{2,1,0:T(8,128)(2,1)S(1)} %get-tuple-element.58.refs_4_), channel_id=1, source_target_pairs={{0,128},{16,144},{32,160},{48,176},{64,192},{80,208},{96,224},{112... | collective-permute-start | bytes 294920 | tf_op jit(solution)/shard_map/ppermute | solution.py:506
  89.6 9.1 %collective-permute-start.27 = (bf16[2,96,256]{2,1,0:T(8,128)(2,1)S(1)}, bf16[2,96,256]{2,1,0:T(8,128)(2,1)S(1)}, u32[]{:S(2)}, u32[]{:S(2)}) collective-permute-start(bf16[2,96,256]{2,1,0:T(8,128)(2,1)S(1)} %get-tuple-element.59.refs_3_), channel_id=1, source_target_pairs={{0,160},{16,176},{32,192},{48,208},{64,224},{80,240},{96,0},{112,1... | collective-permute-start | bytes 294920 | tf_op jit(solution)/shard_map/ppermute | solution.py:506
  92.9 10.8 %collective-permute-start.29 = (bf16[2,96,256]{2,1,0:T(8,128)(2,1)S(1)}, bf16[2,96,256]{2,1,0:T(8,128)(2,1)S(1)}, u32[]{:S(2)}, u32[]{:S(2)}) collective-permute-start(bf16[2,96,256]{2,1,0:T(8,128)(2,1)S(1)} %get-tuple-element.61.refs_2_), channel_id=1, source_target_pairs={{0,192},{16,208},{32,224},{48,240},{64,0},{80,16},{96,32},{112,48}... | collective-permute-start | bytes 294920 | tf_op jit(solution)/shard_map/ppermute | solution.py:506
  95.8 9.7 %collective-permute-start.30 = (bf16[2,96,256]{2,1,0:T(8,128)(2,1)S(1)}, bf16[2,96,256]{2,1,0:T(8,128)(2,1)S(1)}, u32[]{:S(2)}, u32[]{:S(2)}) collective-permute-start(bf16[2,96,256]{2,1,0:T(8,128)(2,1)S(1)} %get-tuple-element.62.refs_6_), channel_id=1, source_target_pairs={{0,64},{16,80},{32,96},{48,112},{64,128},{80,144},{96,160},{112,17... | collective-permute-start | bytes 294920 | tf_op jit(solution)/shard_map/ppermute | solution.py:506
  95.8 10.8 %collective-permute-start.31 = (bf16[2,96,256]{2,1,0:T(8,128)(2,1)S(1)}, bf16[2,96,256]{2,1,0:T(8,128)(2,1)S(1)}, u32[]{:S(2)}, u32[]{:S(2)}) collective-permute-start(bf16[2,96,256]{2,1,0:T(8,128)(2,1)S(1)} %get-tuple-element.63.refs_1_), channel_id=1, source_target_pairs={{0,224},{16,240},{32,0},{48,16},{64,32},{80,48},{96,64},{112,80},{... | collective-permute-start | bytes 294920 | tf_op jit(solution)/shard_map/ppermute | solution.py:506
  98.8 10.4 %collective-permute-start.32 = (bf16[2,96,256]{2,1,0:T(8,128)(2,1)S(1)}, bf16[2,96,256]{2,1,0:T(8,128)(2,1)S(1)}, u32[]{:S(2)}, u32[]{:S(2)}) collective-permute-start(bf16[2,96,256]{2,1,0:T(8,128)(2,1)S(1)} %get-tuple-element.64.refs_7_), channel_id=1, source_target_pairs={{0,32},{16,48},{32,64},{48,80},{64,96},{80,112},{96,128},{112,144}... | collective-permute-start | bytes 294920 | tf_op jit(solution)/shard_map/ppermute | solution.py:506
  113.9 11.3 %collective-permute-start.33 = (bf16[8,96,256]{2,1,0:T(8,128)(2,1)S(1)}, bf16[8,96,256]{2,1,0:T(8,128)(2,1)S(1)}, u32[]{:S(2)}, u32[]{:S(2)}) collective-permute-start(bf16[8,96,256]{2,1,0:T(8,128)(2,1)S(1)} %get-tuple-element.65), channel_id=1, source_target_pairs={{0,16},{16,0},{32,48},{48,32},{64,80},{80,64},{96,112},{112,96},{1... | collective-permute-start | bytes 1179656 | tf_op jit(solution)/shard_map/ppermute | solution.py:525
  116.7 10.0 %collective-permute-start.35 = (bf16[2,96,256]{2,1,0:T(8,128)(2,1)S(1)}, bf16[2,96,256]{2,1,0:T(8,128)(2,1)S(1)}, u32[]{:S(2)}, u32[]{:S(2)}) collective-permute-start(bf16[2,96,256]{2,1,0:T(8,128)(2,1)S(1)} %get-tuple-element.69), channel_id=1, source_target_pairs={{0,128},{16,144},{32,160},{48,176},{64,192},{80,208},{96,224},{112... | collective-permute-start | bytes 294920 | tf_op jit(solution)/shard_map/ppermute | solution.py:506
  118.7 16.4 %collective-permute-start.36 = (bf16[2,96,256]{2,1,0:T(8,128)(2,1)S(1)}, bf16[2,96,256]{2,1,0:T(8,128)(2,1)S(1)}, u32[]{:S(2)}, u32[]{:S(2)}) collective-permute-start(bf16[2,96,256]{2,1,0:T(8,128)(2,1)S(1)} %get-tuple-element.70), channel_id=1, source_target_pairs={{0,96},{16,112},{32,128},{48,144},{64,160},{80,176},{96,192},{112,... | collective-permute-start | bytes 294920 | tf_op jit(solution)/shard_map/ppermute | solution.py:506
  120.2 18.1 %collective-permute-start.37 = (bf16[2,96,256]{2,1,0:T(8,128)(2,1)S(1)}, bf16[2,96,256]{2,1,0:T(8,128)(2,1)S(1)}, u32[]{:S(2)}, u32[]{:S(2)}) collective-permute-start(bf16[2,96,256]{2,1,0:T(8,128)(2,1)S(1)} %get-tuple-element.71), channel_id=1, source_target_pairs={{0,160},{16,176},{32,192},{48,208},{64,224},{80,240},{96,0},{112,1... | collective-permute-start | bytes 294920 | tf_op jit(solution)/shard_map/ppermute | solution.py:506
  123.1 15.1 %collective-permute-start.38 = (bf16[2,96,256]{2,1,0:T(8,128)(2,1)S(1)}, bf16[2,96,256]{2,1,0:T(8,128)(2,1)S(1)}, u32[]{:S(2)}, u32[]{:S(2)}) collective-permute-start(bf16[2,96,256]{2,1,0:T(8,128)(2,1)S(1)} %get-tuple-element.72), channel_id=1, source_target_pairs={{0,64},{16,80},{32,96},{48,112},{64,128},{80,144},{96,160},{112,17... | collective-permute-start | bytes 294920 | tf_op jit(solution)/shard_map/ppermute | solution.py:506
  125.2 13.0 %collective-permute-start.39 = (bf16[2,96,256]{2,1,0:T(8,128)(2,1)S(1)}, bf16[2,96,256]{2,1,0:T(8,128)(2,1)S(1)}, u32[]{:S(2)}, u32[]{:S(2)}) collective-permute-start(bf16[2,96,256]{2,1,0:T(8,128)(2,1)S(1)} %get-tuple-element.73), channel_id=1, source_target_pairs={{0,192},{16,208},{32,224},{48,240},{64,0},{80,16},{96,32},{112,48}... | collective-permute-start | bytes 294920 | tf_op jit(solution)/shard_map/ppermute | solution.py:506
  126.7 11.6 %collective-permute-start.40 = (bf16[2,96,256]{2,1,0:T(8,128)(2,1)S(1)}, bf16[2,96,256]{2,1,0:T(8,128)(2,1)S(1)}, u32[]{:S(2)}, u32[]{:S(2)}) collective-permute-start(bf16[2,96,256]{2,1,0:T(8,128)(2,1)S(1)} %get-tuple-element.74), channel_id=1, source_target_pairs={{0,32},{16,48},{32,64},{48,80},{64,96},{80,112},{96,128},{112,144}... | collective-permute-start | bytes 294920 | tf_op jit(solution)/shard_map/ppermute | solution.py:506
  (12 other events, 63.4 us)

commit v7 on v6

--- a/solution.py
+++ b/solution.py
@@ -31,8 +31,16 @@
     return pl.CostEstimate(flops=flops, bytes_accessed=size, transcendentals=0)
 
 
-def part(at, size):
-    return pl.ds(pl.multiple_of(lax.rem(at, SIDE) * size, size), size)
+def spot_here():
+    me = lax.axis_index("fsdp")
+    return lax.div(me, 2), lax.rem(me, 2)
+
+
+def place_here():
+    at = lax.axis_index("grp")
+    x, y = lax.rem(at, SIDE), lax.div(at, SIDE)
+    _, core = spot_here()
+    return jnp.where(core == 0, x, y), jnp.where(core == 0, y, x)
 
 
 def pairs_of(rows):
@@ -48,12 +56,12 @@
         copy.wait()
 
 
-def group_at(spot_ref, away, other, planes):
-    core = spot_ref[1]
-    return 2 * lax.rem(spot_ref[0] + away, planes) + (1 - core if other else core)
-
-
-def plan_kernel(owner_ref, spot_ref, grads_ref, table_ref, *refs):
+def group_at(away, other, planes):
+    plane, core = spot_here()
+    return 2 * lax.rem(plane + away, planes) + (1 - core if other else core)
+
+
+def plan_kernel(owner_ref, grads_ref, table_ref, *refs):
     outs, (empty_ref, held, sem) = refs[:-3], refs[-3:]
     count, planes = owner_ref.shape[0], len(outs)
     copy = pltpu.make_async_copy(grads_ref, held, sem)
@@ -83,17 +91,17 @@
     copy.wait()
     for away in range(planes):
         for other in range(2):
-            outs[away][other] = held[table_ref[0, group_at(spot_ref, away, other, planes)]]
-
-
-def plan(owner, spot, grads):
+            outs[away][other] = held[table_ref[0, group_at(away, other, planes)]]
+
+
+def plan(owner, grads):
     count, rows, cols = grads.shape
     planes = count // 2
     return pl.pallas_call(
         plan_kernel,
         out_shape=(shape_of(4, count + 1, dtype=jnp.int32),)
         + (shape_of(2, rows, cols),) * planes,
-        in_specs=[SMEM, SMEM, ANY],
+        in_specs=[SMEM, ANY],
         out_specs=(SMEM,) + (VMEM,) * planes,
         scratch_shapes=[
             pltpu.SMEM((count + 1,), jnp.int32),
@@ -102,7 +110,7 @@
         ],
         compiler_params=params(8),
         name="plan",
-    )(owner, spot, grads)
+    )(owner, grads)
 
 
 def sort_kernel(*refs):
@@ -136,10 +144,10 @@
     return parts.astype(jnp.bfloat16)
 
 
-def gram_sums(place_ref, own, got, acc, picked, write):
+def gram_sums(own, got, acc, picked, write):
     each = own[0].shape[0] // BLOCK
     side = 2 * each
-    turn = lax.rem(place_ref[0], SIDE) * PIECE
+    turn = place_here()[0] * PIECE
     lists = (own, got)
 
     def block(s, i):
@@ -172,27 +180,27 @@
     return jnp.sum(total, axis=1, keepdims=True)
 
 
-def gram_first_kernel(place_ref, *refs):
+def gram_first_kernel(*refs):
     own, got, (acc, square, picked) = refs[:6:2], (refs[1], refs[5], refs[3]), refs[6:]
 
     def write(t, value):
         acc[t] = value
 
-    total = gram_sums(place_ref, own, got, None, picked, write)
+    total = gram_sums(own, got, None, picked, write)
     square[...] = jnp.broadcast_to(total, square.shape)
 
 
-def gram_last_kernel(place_ref, own, got, acc, square, first, second, picked):
+def gram_last_kernel(own, got, acc, square, first, second, picked):
     cut = first.shape[0]
 
     def write(t, value):
         (first, second)[t // cut][t % cut] = value.astype(jnp.bfloat16)
 
-    total = gram_sums(place_ref, [own], [got], acc, picked, write)
+    total = gram_sums([own], [got], acc, picked, write)
     second[second.shape[0] - 1] = split(total + square[0:1, :], (PIECE, BLOCK))
 
 
-def gram_quarter(place, lists):
+def gram_quarter(lists):
     own, got = lists
     rows = 2 * own[0].shape[0]
     blocks = len(pairs_of(rows))
@@ -203,22 +211,22 @@
             shape_of(blocks, PIECE, BLOCK, dtype=jnp.float32),
             shape_of(8, BLOCK, dtype=jnp.float32),
         ),
-        in_specs=[SMEM] + [VMEM] * 6,
+        in_specs=[VMEM] * 6,
         out_specs=(VMEM,) * 2,
         scratch_shapes=[pltpu.VMEM((SIDE - 1, rows // SIDE, BLOCK), jnp.bfloat16)],
         compiler_params=params(16),
         cost_estimate=cost(3 * blocks * BLOCK**3 // 2, 4 * MIB),
         name="gram_first",
-    )(place, own[0], got[0], own[1], got[3], own[3], got[1])
+    )(own[0], got[0], own[1], got[3], own[3], got[1])
     return pl.pallas_call(
         gram_last_kernel,
         out_shape=(shape_of(cut, PIECE, BLOCK), shape_of(blocks + 1 - cut, PIECE, BLOCK)),
-        in_specs=[SMEM] + [VMEM] * 4,
+        in_specs=[VMEM] * 4,
         out_specs=(VMEM,) * 2,
         scratch_shapes=[pltpu.VMEM((1, rows // SIDE, BLOCK), jnp.bfloat16)],
         compiler_params=params(16),
         name="gram_last",
-    )(place, own[2], got[2], acc, square)
+    )(own[2], got[2], acc, square)
 
 
 def add_kernel(rows, *refs):
@@ -252,12 +260,13 @@
     )(*out_of_lists(lists))
 
 
-def step_kernel(pairs, factor, planes, place_ref, own_ref, got_ref, inverse_ref, *refs):
+def step_kernel(pairs, factor, planes, own_ref, got_ref, inverse_ref, *refs):
     early, late = in_lists(refs[: 2 * SIDE])
     outs, (gram, normed, left) = refs[2 * SIDE : -3], refs[-3:]
     half = own_ref.shape[0]
     blocks = early[0].shape[0]
     side = 2 * half // BLOCK
+    first, _ = place_here()
     for k, ref in enumerate((own_ref, got_ref)):
         for i in range(half // BLOCK):
             values = ref[i * BLOCK : (i + 1) * BLOCK, :].astype(jnp.float32)
@@ -267,7 +276,7 @@
     for t, (i, j) in enumerate(pairs):
         source, u = (early, t) if t < blocks else (late, t - blocks)
         for s in range(SIDE):
-            p = lax.rem(place_ref[0] - s + SIDE, SIDE)
+            p = lax.rem(first - s + SIDE, SIDE)
             rows = pl.ds(pl.multiple_of(i * BLOCK + p * PIECE, PIECE), PIECE)
             gram[rows, j * BLOCK : (j + 1) * BLOCK] = source[s][u]
     for i, j in pairs:
@@ -294,13 +303,13 @@
             outs[away + 1][k] = values[each:]
 
 
-def step(place, own, got, inverse, lists, factor, planes):
+def step(own, got, inverse, lists, factor, planes):
     half, cols = own.shape
     rows = 2 * half
     return pl.pallas_call(
         functools.partial(step_kernel, pairs_of(rows), factor, planes),
         out_shape=(shape_of(2, half // planes, cols),) * planes,
-        in_specs=[SMEM] + [VMEM] * (3 + 2 * SIDE),
+        in_specs=[VMEM] * (3 + 2 * SIDE),
         out_specs=(VMEM,) * planes,
         scratch_shapes=[
             pltpu.VMEM((rows, rows), jnp.bfloat16),
@@ -310,15 +319,15 @@
         compiler_params=params(28),
         cost_estimate=cost(4 * rows * rows * cols, 6 * 1024 * 1024),
         name="step",
-    )(place, own, got, inverse, *out_of_lists(lists))
-
-
-def pick_kernel(planes, table_ref, spot_ref, *refs):
-    ins, (mine_ref, give_ref, rest_ref) = in_place(refs[:planes]), refs[planes:]
+    )(own, got, inverse, *out_of_lists(lists))
+
+
+def pick_kernel(planes, table_ref, *refs):
+    ins, (mine_ref, give_ref) = in_place(refs[:planes]), refs[planes:]
     for up, ref in enumerate(ins):
-        owner = table_ref[3, group_at(spot_ref, up, 0, planes)]
-        away = lax.rem(lax.div(jnp.maximum(owner, 0), 2) - spot_ref[0] + planes, planes)
-        here = lax.rem(jnp.maximum(owner, 0), 2) == spot_ref[1]
+        owner = table_ref[3, group_at(up, 0, planes)]
+        away = lax.rem(lax.div(jnp.maximum(owner, 0), 2) - spot_here()[0] + planes, planes)
+        here = lax.rem(jnp.maximum(owner, 0), 2) == spot_here()[1]
 
         @pl.when(jnp.logical_and(owner >= 0, here))
         def _():
@@ -328,26 +337,24 @@
         def _():
             give_ref[away] = ref[...]
 
-        rest_ref[up] = ref[1]
-
-
-def pick(table, spot, back):
+
+def pick(table, back):
     planes = len(back)
     block = back[0].shape
     return pl.pallas_call(
         functools.partial(pick_kernel, planes),
-        out_shape=(shape_of(planes, *block),) * 2 + (shape_of(planes, *block[1:]),),
-        in_specs=[SMEM] * 2 + [VMEM] * planes,
-        out_specs=(VMEM,) * 3,
+        out_shape=(shape_of(planes, *block),) * 2,
+        in_specs=[SMEM] + [VMEM] * planes,
+        out_specs=(VMEM,) * 2,
         compiler_params=params(8),
         name="pick",
-    )(table, spot, *in_turn(back))
-
-
-def merge_kernel(planes, table_ref, spot_ref, mine_ref, got_ref, *outs):
+    )(table, *in_turn(back))
+
+
+def merge_kernel(planes, table_ref, mine_ref, got_ref, *outs):
     for away, out in enumerate(outs):
-        helper = table_ref[2, group_at(spot_ref, away, 0, planes)]
-        here = lax.rem(jnp.maximum(helper, 0), 2) == spot_ref[1]
+        helper = table_ref[2, group_at(away, 0, planes)]
+        here = lax.rem(jnp.maximum(helper, 0), 2) == spot_here()[1]
 
         @pl.when(helper < 0)
         def _():
@@ -363,58 +370,58 @@
             out[1] = got_ref[away, 0]
 
 
-def merge(table, spot, mine, got):
+def merge(table, mine, got):
     planes = mine.shape[0]
     return pl.pallas_call(
         functools.partial(merge_kernel, planes),
         out_shape=(shape_of(*mine.shape[1:]),) * planes,
-        in_specs=[SMEM] * 2 + [VMEM] * 2,
+        in_specs=[SMEM] + [VMEM] * 2,
         out_specs=(VMEM,) * planes,
         compiler_params=params(8),
         name="merge",
-    )(table, spot, mine, got)
-
-
-def update_kernel(planes, table_ref, spot_ref, *refs):
-    ins, (rest_ref, out_ref, sems) = in_place(refs[:planes]), refs[planes:]
+    )(table, mine, got)
+
+
+def update_kernel(planes, table_ref, *refs):
+    own_ref, rest_ref, out_ref, sems = refs
     moves = []
     for away in range(planes):
-        e = table_ref[0, group_at(spot_ref, away, 0, planes)]
-        moves.append((ins[away].at[0], out_ref.at[e]))
-        e = table_ref[0, group_at(spot_ref, away, 1, planes)]
+        e = table_ref[0, group_at(away, 0, planes)]
+        moves.append((own_ref.at[away], out_ref.at[e]))
+        e = table_ref[0, group_at(away, 1, planes)]
         moves.append((rest_ref.at[away], out_ref.at[e]))
     move_all(moves, sems)
 
 
-def update_of(table, spot, back, rest):
+def update_of(table, own, rest):
     planes, rows, cols = rest.shape
     return pl.pallas_call(
         functools.partial(update_kernel, planes),
         out_shape=shape_of(2 * planes, rows, cols),
-        in_specs=[SMEM] * 2 + [VMEM] * (planes + 1),
+        in_specs=[SMEM] + [VMEM] * 2,
         out_specs=ANY,
         scratch_shapes=[pltpu.SemaphoreType.DMA((2 * planes,))],
         compiler_params=params(8),
         name="update",
-    )(table, spot, *in_turn(back), rest)
-
-
-def slot_moves(spot_ref, ins, out_ref, slot):
+    )(table, own, rest)
+
+
+def slot_moves(ins, out_ref, slot):
     planes = len(ins)
     moves = []
     for away, ref in enumerate(ins):
         for k in range(2):
             rows = ref.shape[1]
-            start = group_at(spot_ref, planes - away, k, planes) * rows
+            start = group_at(planes - away, k, planes) * rows
             to = out_ref.at[slot, pl.ds(pl.multiple_of(start, rows), rows)]
             moves.append((ref.at[k], to))
     return moves
 
 
-def first_kernel(planes, table_ref, spot_ref, *refs):
+def first_kernel(planes, table_ref, *refs):
     ins, (out_ref, zero, sems) = refs[:planes], refs[planes:]
-    moves = slot_moves(spot_ref, ins, out_ref, 0)
-    owns = table_ref[1, group_at(spot_ref, 0, 0, planes)] > 0
+    moves = slot_moves(ins, out_ref, 0)
+    owns = table_ref[1, group_at(0, 0, planes)] > 0
 
     @pl.when(owns)
     def _():
@@ -426,18 +433,18 @@
         move_all([(zero, b) for _, b in moves], sems)
 
 
-def second_kernel(planes, spot_ref, *refs):
+def second_kernel(planes, *refs):
     ins, (_, out_ref, sems) = in_place(refs[:planes]), refs[planes:]
-    move_all(slot_moves(spot_ref, ins, out_ref, 1), sems)
-
-
-def first_slot(table, spot, done):
+    move_all(slot_moves(ins, out_ref, 1), sems)
+
+
+def first_slot(table, done):
     planes = len(done)
     _, rows, cols = done[0].shape
     return pl.pallas_call(
         functools.partial(first_kernel, planes),
         out_shape=shape_of(MOST, 2 * planes * rows, cols),
-        in_specs=[SMEM] * 2 + [VMEM] * planes,
+        in_specs=[SMEM] + [VMEM] * planes,
         out_specs=ANY,
         scratch_shapes=[
             pltpu.VMEM((rows, cols), jnp.bfloat16),
@@ -445,21 +452,21 @@
         ],
         compiler_params=params(8),
         name="first_slot",
-    )(table, spot, *done)
-
-
-def second_slot(spot, came, owned):
+    )(table, *done)
+
+
+def second_slot(came, owned):
     planes = len(came)
     return pl.pallas_call(
         functools.partial(second_kernel, planes),
         out_shape=shape_of(*owned.shape),
-        in_specs=[SMEM] + [VMEM] * planes + [ANY],
+        in_specs=[VMEM] * planes + [ANY],
         out_specs=ANY,
         scratch_shapes=[pltpu.SemaphoreType.DMA((2 * planes,))],
-        input_output_aliases={planes + 1: 0},
+        input_output_aliases={planes: 0},
         compiler_params=params(8),
         name="second_slot",
-    )(spot, *in_turn(came), owned)
+    )(*in_turn(came), owned)
 
 
 def neighbour(value, order, amount):
@@ -532,24 +539,20 @@
     rows = rows_dev * groups
     cols = cols_dev * lax.axis_size("grp")
     factor = 0.2 * math.sqrt(max(rows, cols))
-    at = lax.axis_index("grp")
-    me = lax.axis_index("fsdp")
-    along = jnp.stack([lax.rem(at, SIDE), lax.div(at, SIDE)]).astype(jnp.int32)
-    place = jnp.where(lax.rem(me, 2) == 0, along, along[::-1])
-    spot = jnp.stack([lax.div(me, 2), lax.rem(me, 2)]).astype(jnp.int32)
-    table, *sends = plan(owner, spot, grads)
+    table, *sends = plan(owner, grads)
     own, give = sort(over_planes(sends, 1))
     got = swap(give)
     own, got = own.reshape(rows // 2, cols_dev), got.reshape(rows // 2, cols_dev)
-    parts = gram_quarter(place, gather(own, got, 0))
+    parts = gram_quarter(gather(own, got, 0))
     *parts, inverse = add(gather(*parts, 1), rows)
-    done = step(place, own, got, inverse, gather(*parts, 0), factor, planes)
+    done = step(own, got, inverse, gather(*parts, 0), factor, planes)
     back = over_planes(done, -1)
-    mine, give, rest = pick(table, spot, back)
-    sends = merge(table, spot, mine, swap(give))
+    mine, give = pick(table, back)
+    sends = merge(table, mine, swap(give))
     came = over_planes(sends, 1)
-    update = update_of(table, spot, back, swap(rest))
-    owned = second_slot(spot, came, first_slot(table, spot, done))
+    own, rest = sort(back)
+    update = update_of(table, own, swap(rest))
+    owned = second_slot(came, first_slot(table, done))
     return (update, owned)
 
 

time: 141 us -> 139 us (0.986)
  Pallas kernels: 14.4 us -> 12.3 us
where the time goes in v7:
time: 139 us
  starting transfers between devices  68.3 us (49%)
  waiting for transfers between devices  55.2 us (40%)
  Pallas kernels  12.3 us (9%)
  local copies, waits for them, and re-layouts  1.78 us (1%)
    ppermute x21, starting transfers between devices, over_planes(): got[away] = lax.ppermute(blocks[away], 'fsdp', moves)  39.9 us
    ppermute x21, waiting for transfers between devices, over_planes(): got[away] = lax.ppermute(blocks[away], 'fsdp', moves)  28.1 us
    ppermute x18, waiting for transfers between devices, neighbour(): return lax.ppermute(value, ('fsdp', 'grp'), moves)  25.2 us
    ppermute x18, starting transfers between devices, neighbour(): return lax.ppermute(value, ('fsdp', 'grp'), moves)  23.4 us
    ppermute x3, starting transfers between devices, swap(): return lax.ppermute(value, 'fsdp', [(g, g ^ 1) for g in range(groups)])  5 us
    pallas_call x1, Pallas kernels, step(): pl.pallas_call(functools.partial(step_kernel, pairs_of(rows), factor, pla...  3.14 us
  transfers between devices with their start and end apart: 42, of which 25 were waited for; matrix products, arithmetic and copies ran while one was open for 0% of the time, Pallas kernels for 4%

profile of v7, /device:TPU:1, one launch (start us, length us, event | category | flops | bytes accessed | tf_op | source)
XLA Modules:
  0.0 138.6 jit_solution(6473643303986551110)
XLA Ops:
  4.0 7.8 %collective-permute-start = (bf16[2,96,256]{2,1,0:T(8,128)(2,1)S(1)}, bf16[2,96,256]{2,1,0:T(8,128)(2,1)S(1)}, u32[]{:S(2)}, u32[]{:S(2)}) collective-permute-start(bf16[2,96,256]{2,1,0:T(8,128)(2,1)S(1)} %get-tuple-element.42), channel_id=1, source_target_pairs={{0,128},{16,144},{32,160},{48,176},{64,192},{80,208},{96,224},{112... | collective-permute-start | bytes 294920 | tf_op jit(solution)/shard_map/ppermute | solution.py:513
  11.8 1.6 %collective-permute-start.1 = (bf16[2,96,256]{2,1,0:T(8,128)(2,1)S(1)}, bf16[2,96,256]{2,1,0:T(8,128)(2,1)S(1)}, u32[]{:S(2)}, u32[]{:S(2)}) collective-permute-start(bf16[2,96,256]{2,1,0:T(8,128)(2,1)S(1)} %get-tuple-element.43), channel_id=1, source_target_pairs={{0,96},{16,112},{32,128},{48,144},{64,160},{80,176},{96,192},{112,... | collective-permute-start | bytes 294920 | tf_op jit(solution)/shard_map/ppermute | solution.py:513
  13.5 2.8 %collective-permute-start.2 = (bf16[2,96,256]{2,1,0:T(8,128)(2,1)S(1)}, bf16[2,96,256]{2,1,0:T(8,128)(2,1)S(1)}, u32[]{:S(2)}, u32[]{:S(2)}) collective-permute-start(bf16[2,96,256]{2,1,0:T(8,128)(2,1)S(1)} %get-tuple-element.44), channel_id=1, source_target_pairs={{0,160},{16,176},{32,192},{48,208},{64,224},{80,240},{96,0},{112,1... | collective-permute-start | bytes 294920 | tf_op jit(solution)/shard_map/ppermute | solution.py:513
  17.5 2.4 %collective-permute-start.4 = (bf16[2,96,256]{2,1,0:T(8,128)(2,1)S(1)}, bf16[2,96,256]{2,1,0:T(8,128)(2,1)S(1)}, u32[]{:S(2)}, u32[]{:S(2)}) collective-permute-start(bf16[2,96,256]{2,1,0:T(8,128)(2,1)S(1)} %get-tuple-element.46), channel_id=1, source_target_pairs={{0,192},{16,208},{32,224},{48,240},{64,0},{80,16},{96,32},{112,48}... | collective-permute-start | bytes 294920 | tf_op jit(solution)/shard_map/ppermute | solution.py:513
  20.6 4.6 %collective-permute-done.1.refs_2_ = bf16[2,96,256]{2,1,0:T(8,128)(2,1)S(1)} collective-permute-done((bf16[2,96,256]{2,1,0:T(8,128)(2,1)S(1)}, bf16[2,96,256]{2,1,0:T(8,128)(2,1)S(1)}, u32[]{:S(2)}, u32[]{:S(2)}) %collective-permute-start.1) | collective-permute-done | bytes 98336 | tf_op jit(solution)/shard_map/ppermute | solution.py:513
  25.3 3.0 %collective-permute-done.4.refs_5_ = bf16[2,96,256]{2,1,0:T(8,128)(2,1)S(1)} collective-permute-done((bf16[2,96,256]{2,1,0:T(8,128)(2,1)S(1)}, bf16[2,96,256]{2,1,0:T(8,128)(2,1)S(1)}, u32[]{:S(2)}, u32[]{:S(2)}) %collective-permute-start.4) | collective-permute-done | bytes 98336 | tf_op jit(solution)/shard_map/ppermute | solution.py:513
  33.0 2.7 %collective-permute-start.10 = (bf16[768,256]{1,0:T(8,128)(2,1)S(1)}, bf16[768,256]{1,0:T(8,128)(2,1)S(1)}, u32[]{:S(2)}, u32[]{:S(2)}) collective-permute-start(bf16[768,256]{1,0:T(8,128)(2,1)S(1)} %bitcast.6), channel_id=1, source_target_pairs={{0,3},{1,0},{2,1},{3,2},{4,7},{5,4},{6,5},{7,6},{8,11},{9,8},{10,9... | collective-permute-start | bytes 1179656 | tf_op jit(solution)/shard_map/ppermute | solution.py:483
  37.2 2.6 %collective-permute-done.8.refs_2_ = bf16[768,256]{1,0:T(8,128)(2,1)S(1)} collective-permute-done((bf16[768,256]{1,0:T(8,128)(2,1)S(1)}, bf16[768,256]{1,0:T(8,128)(2,1)S(1)}, u32[]{:S(2)}, u32[]{:S(2)}) %collective-permute-start.8) | collective-permute-done | bytes 393248 | tf_op jit(solution)/shard_map/ppermute | solution.py:483
  40.4 3.1 %collective-permute-start.11 = (bf16[768,256]{1,0:T(8,128)(2,1)S(1)}, bf16[768,256]{1,0:T(8,128)(2,1)S(1)}, u32[]{:S(2)}, u32[]{:S(2)}) collective-permute-start(bf16[768,256]{1,0:T(8,128)(2,1)S(1)} %collective-permute-done.10.refs_3_), channel_id=1, source_target_pairs={{0,3},{1,0},{2,1},{3,2},{4,7},{5,4},{6,5},{7,6},{8,11},{9,8},{10,9... | collective-permute-start | bytes 1179656 | tf_op jit(solution)/shard_map/ppermute | solution.py:483
  45.5 3.0 %collective-permute-done.9.own = bf16[768,256]{1,0:T(8,128)(2,1)S(1)} collective-permute-done((bf16[768,256]{1,0:T(8,128)(2,1)S(1)}, bf16[768,256]{1,0:T(8,128)(2,1)S(1)}, u32[]{:S(2)}, u32[]{:S(2)}) %collective-permute-start.9) | collective-permute-done | bytes 393248 | tf_op jit(solution)/shard_map/ppermute | solution.py:483
  53.7 3.6 %collective-permute-done.14.refs_2_ = bf16[11,64,256]{2,1,0:T(8,128)(2,1)S(1)} collective-permute-done((bf16[11,64,256]{2,1,0:T(8,128)(2,1)S(1)}, bf16[11,64,256]{2,1,0:T(8,128)(2,1)S(1)}, u32[]{:S(2)}, u32[]{:S(2)}) %collective-permute-start.14) | collective-permute-done | bytes 360480 | tf_op jit(solution)/shard_map/ppermute | solution.py:483
  57.3 2.7 %collective-permute-start.19 = (bf16[11,64,256]{2,1,0:T(8,128)(2,1)S(1)}, bf16[11,64,256]{2,1,0:T(8,128)(2,1)S(1)}, u32[]{:S(2)}, u32[]{:S(2)}) collective-permute-start(bf16[11,64,256]{2,1,0:T(8,128)(2,1)S(1)} %collective-permute-done.15.refs_3_), channel_id=1, source_target_pairs={{0,12},{1,13},{2,14},{3,15},{4,0},{5,1},{6,2},{7,3},{8,4},{9,5},{1... | collective-permute-start | bytes 1081352 | tf_op jit(solution)/shard_map/ppermute | solution.py:483
  61.2 3.9 %collective-permute-done.18.refs_6_ = bf16[11,64,256]{2,1,0:T(8,128)(2,1)S(1)} collective-permute-done((bf16[11,64,256]{2,1,0:T(8,128)(2,1)S(1)}, bf16[11,64,256]{2,1,0:T(8,128)(2,1)S(1)}, u32[]{:S(2)}, u32[]{:S(2)}) %collective-permute-start.18) | collective-permute-done | bytes 360480 | tf_op jit(solution)/shard_map/ppermute | solution.py:483
  66.3 2.8 %collective-permute-start.21 = (bf16[11,64,256]{2,1,0:T(8,128)(2,1)S(1)}, bf16[11,64,256]{2,1,0:T(8,128)(2,1)S(1)}, u32[]{:S(2)}, u32[]{:S(2)}) collective-permute-start(bf16[11,64,256]{2,1,0:T(8,128)(2,1)S(1)} %get-tuple-element.57.refs_1_), channel_id=1, source_target_pairs={{0,3},{1,0},{2,1},{3,2},{4,7},{5,4},{6,5},{7,6},{8,11},{9,8},{10,9... | collective-permute-start | bytes 1081352 | tf_op jit(solution)/shard_map/ppermute | solution.py:483
  70.6 3.6 %collective-permute-done.20.refs_2_ = bf16[11,64,256]{2,1,0:T(8,128)(2,1)S(1)} collective-permute-done((bf16[11,64,256]{2,1,0:T(8,128)(2,1)S(1)}, bf16[11,64,256]{2,1,0:T(8,128)(2,1)S(1)}, u32[]{:S(2)}, u32[]{:S(2)}) %collective-permute-start.20) | collective-permute-done | bytes 360480 | tf_op jit(solution)/shard_map/ppermute | solution.py:483
  74.2 2.8 %collective-permute-start.25 = (bf16[11,64,256]{2,1,0:T(8,128)(2,1)S(1)}, bf16[11,64,256]{2,1,0:T(8,128)(2,1)S(1)}, u32[]{:S(2)}, u32[]{:S(2)}) collective-permute-start(bf16[11,64,256]{2,1,0:T(8,128)(2,1)S(1)} %collective-permute-done.21.refs_3_), channel_id=1, source_target_pairs={{0,3},{1,0},{2,1},{3,2},{4,7},{5,4},{6,5},{7,6},{8,11},{9,8},{10,9... | collective-permute-start | bytes 1081352 | tf_op jit(solution)/shard_map/ppermute | solution.py:483
  78.0 4.2 %collective-permute-done.24.refs_6_ = bf16[11,64,256]{2,1,0:T(8,128)(2,1)S(1)} collective-permute-done((bf16[11,64,256]{2,1,0:T(8,128)(2,1)S(1)}, bf16[11,64,256]{2,1,0:T(8,128)(2,1)S(1)}, u32[]{:S(2)}, u32[]{:S(2)}) %collective-permute-start.24) | collective-permute-done | bytes 360480 | tf_op jit(solution)/shard_map/ppermute | solution.py:483
  82.2 3.1 %step.1 = (bf16[2,96,256]{2,1,0:T(8,128)(2,1)S(1)}, bf16[2,96,256]{2,1,0:T(8,128)(2,1)S(1)}, bf16[2,96,256]{2,1,0:T(8,128)(2,1)S(1)}, bf16[2,96,256]{2,1,0:T(8,1...) custom-call(bf16[768,256]{1,0:T(8,128)(2,1)S(1)} %bitcast.5, ...), custom_call_target="tpu_custom_call" | custom-call | flops 2415919104 | bytes 6291456 | tf_op jit(solution)/shard_map/step/pallas_call | solution.py:309
  85.3 3.2 %collective-permute-start.26 = (bf16[2,96,256]{2,1,0:T(8,128)(2,1)S(1)}, bf16[2,96,256]{2,1,0:T(8,128)(2,1)S(1)}, u32[]{:S(2)}, u32[]{:S(2)}) collective-permute-start(bf16[2,96,256]{2,1,0:T(8,128)(2,1)S(1)} %get-tuple-element.59.refs_4_), channel_id=1, source_target_pairs={{0,128},{16,144},{32,160},{48,176},{64,192},{80,208},{96,224},{112... | collective-permute-start | bytes 294920 | tf_op jit(solution)/shard_map/ppermute | solution.py:513
  88.5 1.7 %collective-permute-start.27 = (bf16[2,96,256]{2,1,0:T(8,128)(2,1)S(1)}, bf16[2,96,256]{2,1,0:T(8,128)(2,1)S(1)}, u32[]{:S(2)}, u32[]{:S(2)}) collective-permute-start(bf16[2,96,256]{2,1,0:T(8,128)(2,1)S(1)} %get-tuple-element.60.refs_3_), channel_id=1, source_target_pairs={{0,160},{16,176},{32,192},{48,208},{64,224},{80,240},{96,0},{112,1... | collective-permute-start | bytes 294920 | tf_op jit(solution)/shard_map/ppermute | solution.py:513
  91.8 2.9 %collective-permute-start.29 = (bf16[2,96,256]{2,1,0:T(8,128)(2,1)S(1)}, bf16[2,96,256]{2,1,0:T(8,128)(2,1)S(1)}, u32[]{:S(2)}, u32[]{:S(2)}) collective-permute-start(bf16[2,96,256]{2,1,0:T(8,128)(2,1)S(1)} %get-tuple-element.62.refs_2_), channel_id=1, source_target_pairs={{0,192},{16,208},{32,224},{48,240},{64,0},{80,16},{96,32},{112,48}... | collective-permute-start | bytes 294920 | tf_op jit(solution)/shard_map/ppermute | solution.py:513
  94.7 3.0 %collective-permute-start.31 = (bf16[2,96,256]{2,1,0:T(8,128)(2,1)S(1)}, bf16[2,96,256]{2,1,0:T(8,128)(2,1)S(1)}, u32[]{:S(2)}, u32[]{:S(2)}) collective-permute-start(bf16[2,96,256]{2,1,0:T(8,128)(2,1)S(1)} %get-tuple-element.64.refs_1_), channel_id=1, source_target_pairs={{0,224},{16,240},{32,0},{48,16},{64,32},{80,48},{96,64},{112,80},{... | collective-permute-start | bytes 294920 | tf_op jit(solution)/shard_map/ppermute | solution.py:513
  97.7 4.9 %collective-permute-done.29.refs_4_ = bf16[2,96,256]{2,1,0:T(8,128)(2,1)S(1)} collective-permute-done((bf16[2,96,256]{2,1,0:T(8,128)(2,1)S(1)}, bf16[2,96,256]{2,1,0:T(8,128)(2,1)S(1)}, u32[]{:S(2)}, u32[]{:S(2)}) %collective-permute-start.29) | collective-permute-done | bytes 98336 | tf_op jit(solution)/shard_map/ppermute | solution.py:513
  102.6 1.9 %collective-permute-done.30.refs_5_ = bf16[2,96,256]{2,1,0:T(8,128)(2,1)S(1)} collective-permute-done((bf16[2,96,256]{2,1,0:T(8,128)(2,1)S(1)}, bf16[2,96,256]{2,1,0:T(8,128)(2,1)S(1)}, u32[]{:S(2)}, u32[]{:S(2)}) %collective-permute-start.30) | collective-permute-done | bytes 98336 | tf_op jit(solution)/shard_map/ppermute | solution.py:513
  105.4 2.6 %collective-permute-done.32.refs_7_ = bf16[2,96,256]{2,1,0:T(8,128)(2,1)S(1)} collective-permute-done((bf16[2,96,256]{2,1,0:T(8,128)(2,1)S(1)}, bf16[2,96,256]{2,1,0:T(8,128)(2,1)S(1)}, u32[]{:S(2)}, u32[]{:S(2)}) %collective-permute-start.32) | collective-permute-done | bytes 98336 | tf_op jit(solution)/shard_map/ppermute | solution.py:513
  108.8 3.9 %collective-permute-start.34 = (bf16[8,2,96,256]{3,2,1,0:T(8,128)(2,1)S(1)}, bf16[8,2,96,256]{3,2,1,0:T(8,128)(2,1)S(1)}, u32[]{:S(2)}, u32[]{:S(2)}) collective-permute-start(bf16[8,2,96,256]{3,2,1,0:T(8,128)(2,1)S(1)} %get-tuple-element.69), channel_id=1, source_target_pairs={{0,16},{16,0},{32,48},{48,32},{64,80},{80,64},{96,112},{112,96},{1... | collective-permute-start | bytes 2359304 | tf_op jit(solution)/shard_map/ppermute | solution.py:532
  112.9 1.7 %collective-permute-done.34.got_ref = bf16[8,2,96,256]{3,2,1,0:T(8,128)(2,1)S(1)} collective-permute-done((bf16[8,2,96,256]{3,2,1,0:T(8,128)(2,1)S(1)}, bf16[8,2,96,256]{3,2,1,0:T(8,128)(2,1)S(1)}, u32[]{:S(2)}, u32[]{:S(2)}) %collective-permute-start.34) | collective-permute-done | bytes 786464 | tf_op jit(solution)/shard_map/ppermute | solution.py:532
  115.5 2.0 %collective-permute-start.35 = (bf16[2,96,256]{2,1,0:T(8,128)(2,1)S(1)}, bf16[2,96,256]{2,1,0:T(8,128)(2,1)S(1)}, u32[]{:S(2)}, u32[]{:S(2)}) collective-permute-start(bf16[2,96,256]{2,1,0:T(8,128)(2,1)S(1)} %get-tuple-element.71), channel_id=1, source_target_pairs={{0,128},{16,144},{32,160},{48,176},{64,192},{80,208},{96,224},{112... | collective-permute-start | bytes 294920 | tf_op jit(solution)/shard_map/ppermute | solution.py:513
  119.0 3.0 %collective-permute-start.37 = (bf16[2,96,256]{2,1,0:T(8,128)(2,1)S(1)}, bf16[2,96,256]{2,1,0:T(8,128)(2,1)S(1)}, u32[]{:S(2)}, u32[]{:S(2)}) collective-permute-start(bf16[2,96,256]{2,1,0:T(8,128)(2,1)S(1)} %get-tuple-element.73), channel_id=1, source_target_pairs={{0,160},{16,176},{32,192},{48,208},{64,224},{80,240},{96,0},{112,1... | collective-permute-start | bytes 294920 | tf_op jit(solution)/shard_map/ppermute | solution.py:513
  121.9 2.1 %collective-permute-start.38 = (bf16[2,96,256]{2,1,0:T(8,128)(2,1)S(1)}, bf16[2,96,256]{2,1,0:T(8,128)(2,1)S(1)}, u32[]{:S(2)}, u32[]{:S(2)}) collective-permute-start(bf16[2,96,256]{2,1,0:T(8,128)(2,1)S(1)} %get-tuple-element.74), channel_id=1, source_target_pairs={{0,64},{16,80},{32,96},{48,112},{64,128},{80,144},{96,160},{112,17... | collective-permute-start | bytes 294920 | tf_op jit(solution)/shard_map/ppermute | solution.py:513
  126.5 7.4 %collective-permute-done.36.refs_2_ = bf16[2,96,256]{2,1,0:T(8,128)(2,1)S(1)} collective-permute-done((bf16[2,96,256]{2,1,0:T(8,128)(2,1)S(1)}, bf16[2,96,256]{2,1,0:T(8,128)(2,1)S(1)}, u32[]{:S(2)}, u32[]{:S(2)}) %collective-permute-start.36) | collective-permute-done | bytes 98336 | tf_op jit(solution)/shard_map/ppermute | solution.py:513
  133.9 1.7 %first_slot.1.refs_8_ = bf16[2,1536,256]{2,1,0:T(8,128)(2,1)} custom-call(s32[4,17]{1,0:T(4,128)S(1)} %get-tuple-element.40.table_ref, bf16[2,96,256]{2,1,0:T(8,128)(2,1)S(1)} %get-tuple-element.58.refs_0_, bf16[2,96,256]{2,1,0:T(8,128)(2,1)S(1)} %get-tuple-element.64.refs_1_, bf16[2,96,256]{2,1,0:T(8,128)(2,1)S(1)} %get-tuple-element.62.refs_2_, ...), custom_call_target="tpu_custom_call" | custom-call | tf_op jit(solution)/shard_map/first_slot/pallas_call | solution.py:444
  (68 shorter events, 35.3 us)
Async XLA Ops:
  4.0 15.9 %collective-permute-start = (bf16[2,96,256]{2,1,0:T(8,128)(2,1)S(1)}, bf16[2,96,256]{2,1,0:T(8,128)(2,1)S(1)}, u32[]{:S(2)}, u32[]{:S(2)}) collective-permute-start(bf16[2,96,256]{2,1,0:T(8,128)(2,1)S(1)} %get-tuple-element.42), channel_id=1, source_target_pairs={{0,128},{16,144},{32,160},{48,176},{64,192},{80,208},{96,224},{112... | collective-permute-start | bytes 294920 | tf_op jit(solution)/shard_map/ppermute | solution.py:513
  11.8 13.4 %collective-permute-start.1 = (bf16[2,96,256]{2,1,0:T(8,128)(2,1)S(1)}, bf16[2,96,256]{2,1,0:T(8,128)(2,1)S(1)}, u32[]{:S(2)}, u32[]{:S(2)}) collective-permute-start(bf16[2,96,256]{2,1,0:T(8,128)(2,1)S(1)} %get-tuple-element.43), channel_id=1, source_target_pairs={{0,96},{16,112},{32,128},{48,144},{64,160},{80,176},{96,192},{112,... | collective-permute-start | bytes 294920 | tf_op jit(solution)/shard_map/ppermute | solution.py:513
  13.5 11.8 %collective-permute-start.2 = (bf16[2,96,256]{2,1,0:T(8,128)(2,1)S(1)}, bf16[2,96,256]{2,1,0:T(8,128)(2,1)S(1)}, u32[]{:S(2)}, u32[]{:S(2)}) collective-permute-start(bf16[2,96,256]{2,1,0:T(8,128)(2,1)S(1)} %get-tuple-element.44), channel_id=1, source_target_pairs={{0,160},{16,176},{32,192},{48,208},{64,224},{80,240},{96,0},{112,1... | collective-permute-start | bytes 294920 | tf_op jit(solution)/shard_map/ppermute | solution.py:513
  16.3 9.0 %collective-permute-start.3 = (bf16[2,96,256]{2,1,0:T(8,128)(2,1)S(1)}, bf16[2,96,256]{2,1,0:T(8,128)(2,1)S(1)}, u32[]{:S(2)}, u32[]{:S(2)}) collective-permute-start(bf16[2,96,256]{2,1,0:T(8,128)(2,1)S(1)} %get-tuple-element.45), channel_id=1, source_target_pairs={{0,64},{16,80},{32,96},{48,112},{64,128},{80,144},{96,160},{112,17... | collective-permute-start | bytes 294920 | tf_op jit(solution)/shard_map/ppermute | solution.py:513
  17.5 10.8 %collective-permute-start.4 = (bf16[2,96,256]{2,1,0:T(8,128)(2,1)S(1)}, bf16[2,96,256]{2,1,0:T(8,128)(2,1)S(1)}, u32[]{:S(2)}, u32[]{:S(2)}) collective-permute-start(bf16[2,96,256]{2,1,0:T(8,128)(2,1)S(1)} %get-tuple-element.46), channel_id=1, source_target_pairs={{0,192},{16,208},{32,224},{48,240},{64,0},{80,16},{96,32},{112,48}... | collective-permute-start | bytes 294920 | tf_op jit(solution)/shard_map/ppermute | solution.py:513
  19.9 9.9 %collective-permute-start.5 = (bf16[2,96,256]{2,1,0:T(8,128)(2,1)S(1)}, bf16[2,96,256]{2,1,0:T(8,128)(2,1)S(1)}, u32[]{:S(2)}, u32[]{:S(2)}) collective-permute-start(bf16[2,96,256]{2,1,0:T(8,128)(2,1)S(1)} %get-tuple-element.47), channel_id=1, source_target_pairs={{0,32},{16,48},{32,64},{48,80},{64,96},{80,112},{96,128},{112,144}... | collective-permute-start | bytes 294920 | tf_op jit(solution)/shard_map/ppermute | solution.py:513
  31.7 8.1 %collective-permute-start.8 = (bf16[768,256]{1,0:T(8,128)(2,1)S(1)}, bf16[768,256]{1,0:T(8,128)(2,1)S(1)}, u32[]{:S(2)}, u32[]{:S(2)}) collective-permute-start(bf16[768,256]{1,0:T(8,128)(2,1)S(1)} %bitcast.2), channel_id=1, source_target_pairs={{0,1},{1,2},{2,3},{3,0},{4,5},{5,6},{6,7},{7,4},{8,9},{9,10},{10,1... | collective-permute-start | bytes 1179656 | tf_op jit(solution)/shard_map/ppermute | solution.py:483
  35.7 8.9 %collective-permute-start.12 = (bf16[768,256]{1,0:T(8,128)(2,1)S(1)}, bf16[768,256]{1,0:T(8,128)(2,1)S(1)}, u32[]{:S(2)}, u32[]{:S(2)}) collective-permute-start(bf16[768,256]{1,0:T(8,128)(2,1)S(1)} %bitcast.3), channel_id=1, source_target_pairs={{0,3},{1,0},{2,1},{3,2},{4,7},{5,4},{6,5},{7,6},{8,11},{9,8},{10,9... | collective-permute-start | bytes 1179656 | tf_op jit(solution)/shard_map/ppermute | solution.py:483
  36.2 8.5 %collective-permute-start.13 = (bf16[768,256]{1,0:T(8,128)(2,1)S(1)}, bf16[768,256]{1,0:T(8,128)(2,1)S(1)}, u32[]{:S(2)}, u32[]{:S(2)}) collective-permute-start(bf16[768,256]{1,0:T(8,128)(2,1)S(1)} %bitcast.7), channel_id=1, source_target_pairs={{0,1},{1,2},{2,3},{3,0},{4,5},{5,6},{6,7},{7,4},{8,9},{9,10},{10,1... | collective-permute-start | bytes 1179656 | tf_op jit(solution)/shard_map/ppermute | solution.py:483
  39.8 8.7 %collective-permute-start.9 = (bf16[768,256]{1,0:T(8,128)(2,1)S(1)}, bf16[768,256]{1,0:T(8,128)(2,1)S(1)}, u32[]{:S(2)}, u32[]{:S(2)}) collective-permute-start(bf16[768,256]{1,0:T(8,128)(2,1)S(1)} %collective-permute-done.8.refs_2_), channel_id=1, source_target_pairs={{0,1},{1,2},{2,3},{3,0},{4,5},{5,6},{6,7},{7,4},{8,9},{9,10},{10,1... | collective-permute-start | bytes 1179656 | tf_op jit(solution)/shard_map/ppermute | solution.py:483
  40.4 8.4 %collective-permute-start.11 = (bf16[768,256]{1,0:T(8,128)(2,1)S(1)}, bf16[768,256]{1,0:T(8,128)(2,1)S(1)}, u32[]{:S(2)}, u32[]{:S(2)}) collective-permute-start(bf16[768,256]{1,0:T(8,128)(2,1)S(1)} %collective-permute-done.10.refs_3_), channel_id=1, source_target_pairs={{0,3},{1,0},{2,1},{3,2},{4,7},{5,4},{6,5},{7,6},{8,11},{9,8},{10,9... | collective-permute-start | bytes 1179656 | tf_op jit(solution)/shard_map/ppermute | solution.py:483
  49.3 8.0 %collective-permute-start.14 = (bf16[11,64,256]{2,1,0:T(8,128)(2,1)S(1)}, bf16[11,64,256]{2,1,0:T(8,128)(2,1)S(1)}, u32[]{:S(2)}, u32[]{:S(2)}) collective-permute-start(bf16[11,64,256]{2,1,0:T(8,128)(2,1)S(1)} %get-tuple-element.53.refs_0_), channel_id=1, source_target_pairs={{0,4},{1,5},{2,6},{3,7},{4,8},{5,9},{6,10},{7,11},{8,12},{9,13},{1... | collective-permute-start | bytes 1081352 | tf_op jit(solution)/shard_map/ppermute | solution.py:483
  52.2 9.0 %collective-permute-start.16 = (bf16[11,64,256]{2,1,0:T(8,128)(2,1)S(1)}, bf16[11,64,256]{2,1,0:T(8,128)(2,1)S(1)}, u32[]{:S(2)}, u32[]{:S(2)}) collective-permute-start(bf16[11,64,256]{2,1,0:T(8,128)(2,1)S(1)} %get-tuple-element.53.refs_0_), channel_id=1, source_target_pairs={{0,12},{1,13},{2,14},{3,15},{4,0},{5,1},{6,2},{7,3},{8,4},{9,5},{1... | collective-permute-start | bytes 1081352 | tf_op jit(solution)/shard_map/ppermute | solution.py:483
  57.3 7.8 %collective-permute-start.18 = (bf16[11,64,256]{2,1,0:T(8,128)(2,1)S(1)}, bf16[11,64,256]{2,1,0:T(8,128)(2,1)S(1)}, u32[]{:S(2)}, u32[]{:S(2)}) collective-permute-start(bf16[11,64,256]{2,1,0:T(8,128)(2,1)S(1)} %collective-permute-done.14.refs_2_), channel_id=1, source_target_pairs={{0,4},{1,5},{2,6},{3,7},{4,8},{5,9},{6,10},{7,11},{8,12},{9,13},{1... | collective-permute-start | bytes 1081352 | tf_op jit(solution)/shard_map/ppermute | solution.py:483
  65.6 8.6 %collective-permute-start.20 = (bf16[11,64,256]{2,1,0:T(8,128)(2,1)S(1)}, bf16[11,64,256]{2,1,0:T(8,128)(2,1)S(1)}, u32[]{:S(2)}, u32[]{:S(2)}) collective-permute-start(bf16[11,64,256]{2,1,0:T(8,128)(2,1)S(1)} %get-tuple-element.56.refs_0_), channel_id=1, source_target_pairs={{0,1},{1,2},{2,3},{3,0},{4,5},{5,6},{6,7},{7,4},{8,9},{9,10},{10,1... | collective-permute-start | bytes 1081352 | tf_op jit(solution)/shard_map/ppermute | solution.py:483
  66.3 7.9 %collective-permute-start.21 = (bf16[11,64,256]{2,1,0:T(8,128)(2,1)S(1)}, bf16[11,64,256]{2,1,0:T(8,128)(2,1)S(1)}, u32[]{:S(2)}, u32[]{:S(2)}) collective-permute-start(bf16[11,64,256]{2,1,0:T(8,128)(2,1)S(1)} %get-tuple-element.57.refs_1_), channel_id=1, source_target_pairs={{0,3},{1,0},{2,1},{3,2},{4,7},{5,4},{6,5},{7,6},{8,11},{9,8},{10,9... | collective-permute-start | bytes 1081352 | tf_op jit(solution)/shard_map/ppermute | solution.py:483
  69.2 8.2 %collective-permute-start.22 = (bf16[11,64,256]{2,1,0:T(8,128)(2,1)S(1)}, bf16[11,64,256]{2,1,0:T(8,128)(2,1)S(1)}, u32[]{:S(2)}, u32[]{:S(2)}) collective-permute-start(bf16[11,64,256]{2,1,0:T(8,128)(2,1)S(1)} %get-tuple-element.56.refs_0_), channel_id=1, source_target_pairs={{0,3},{1,0},{2,1},{3,2},{4,7},{5,4},{6,5},{7,6},{8,11},{9,8},{10,9... | collective-permute-start | bytes 1081352 | tf_op jit(solution)/shard_map/ppermute | solution.py:483
  74.2 8.0 %collective-permute-start.24 = (bf16[11,64,256]{2,1,0:T(8,128)(2,1)S(1)}, bf16[11,64,256]{2,1,0:T(8,128)(2,1)S(1)}, u32[]{:S(2)}, u32[]{:S(2)}) collective-permute-start(bf16[11,64,256]{2,1,0:T(8,128)(2,1)S(1)} %collective-permute-done.20.refs_2_), channel_id=1, source_target_pairs={{0,1},{1,2},{2,3},{3,0},{4,5},{5,6},{6,7},{7,4},{8,9},{9,10},{10,1... | collective-permute-start | bytes 1081352 | tf_op jit(solution)/shard_map/ppermute | solution.py:483
  74.2 8.0 %collective-permute-start.25 = (bf16[11,64,256]{2,1,0:T(8,128)(2,1)S(1)}, bf16[11,64,256]{2,1,0:T(8,128)(2,1)S(1)}, u32[]{:S(2)}, u32[]{:S(2)}) collective-permute-start(bf16[11,64,256]{2,1,0:T(8,128)(2,1)S(1)} %collective-permute-done.21.refs_3_), channel_id=1, source_target_pairs={{0,3},{1,0},{2,1},{3,2},{4,7},{5,4},{6,5},{7,6},{8,11},{9,8},{10,9... | collective-permute-start | bytes 1081352 | tf_op jit(solution)/shard_map/ppermute | solution.py:483
  85.3 9.3 %collective-permute-start.26 = (bf16[2,96,256]{2,1,0:T(8,128)(2,1)S(1)}, bf16[2,96,256]{2,1,0:T(8,128)(2,1)S(1)}, u32[]{:S(2)}, u32[]{:S(2)}) collective-permute-start(bf16[2,96,256]{2,1,0:T(8,128)(2,1)S(1)} %get-tuple-element.59.refs_4_), channel_id=1, source_target_pairs={{0,128},{16,144},{32,160},{48,176},{64,192},{80,208},{96,224},{112... | collective-permute-start | bytes 294920 | tf_op jit(solution)/shard_map/ppermute | solution.py:513
  88.5 9.1 %collective-permute-start.27 = (bf16[2,96,256]{2,1,0:T(8,128)(2,1)S(1)}, bf16[2,96,256]{2,1,0:T(8,128)(2,1)S(1)}, u32[]{:S(2)}, u32[]{:S(2)}) collective-permute-start(bf16[2,96,256]{2,1,0:T(8,128)(2,1)S(1)} %get-tuple-element.60.refs_3_), channel_id=1, source_target_pairs={{0,160},{16,176},{32,192},{48,208},{64,224},{80,240},{96,0},{112,1... | collective-permute-start | bytes 294920 | tf_op jit(solution)/shard_map/ppermute | solution.py:513
  91.8 10.8 %collective-permute-start.29 = (bf16[2,96,256]{2,1,0:T(8,128)(2,1)S(1)}, bf16[2,96,256]{2,1,0:T(8,128)(2,1)S(1)}, u32[]{:S(2)}, u32[]{:S(2)}) collective-permute-start(bf16[2,96,256]{2,1,0:T(8,128)(2,1)S(1)} %get-tuple-element.62.refs_2_), channel_id=1, source_target_pairs={{0,192},{16,208},{32,224},{48,240},{64,0},{80,16},{96,32},{112,48}... | collective-permute-start | bytes 294920 | tf_op jit(solution)/shard_map/ppermute | solution.py:513
  94.6 9.9 %collective-permute-start.30 = (bf16[2,96,256]{2,1,0:T(8,128)(2,1)S(1)}, bf16[2,96,256]{2,1,0:T(8,128)(2,1)S(1)}, u32[]{:S(2)}, u32[]{:S(2)}) collective-permute-start(bf16[2,96,256]{2,1,0:T(8,128)(2,1)S(1)} %get-tuple-element.63.refs_6_), channel_id=1, source_target_pairs={{0,64},{16,80},{32,96},{48,112},{64,128},{80,144},{96,160},{112,17... | collective-permute-start | bytes 294920 | tf_op jit(solution)/shard_map/ppermute | solution.py:513
  94.7 10.8 %collective-permute-start.31 = (bf16[2,96,256]{2,1,0:T(8,128)(2,1)S(1)}, bf16[2,96,256]{2,1,0:T(8,128)(2,1)S(1)}, u32[]{:S(2)}, u32[]{:S(2)}) collective-permute-start(bf16[2,96,256]{2,1,0:T(8,128)(2,1)S(1)} %get-tuple-element.64.refs_1_), channel_id=1, source_target_pairs={{0,224},{16,240},{32,0},{48,16},{64,32},{80,48},{96,64},{112,80},{... | collective-permute-start | bytes 294920 | tf_op jit(solution)/shard_map/ppermute | solution.py:513
  97.6 10.4 %collective-permute-start.32 = (bf16[2,96,256]{2,1,0:T(8,128)(2,1)S(1)}, bf16[2,96,256]{2,1,0:T(8,128)(2,1)S(1)}, u32[]{:S(2)}, u32[]{:S(2)}) collective-permute-start(bf16[2,96,256]{2,1,0:T(8,128)(2,1)S(1)} %get-tuple-element.65.refs_7_), channel_id=1, source_target_pairs={{0,32},{16,48},{32,64},{48,80},{64,96},{80,112},{96,128},{112,144}... | collective-permute-start | bytes 294920 | tf_op jit(solution)/shard_map/ppermute | solution.py:513
  112.8 11.2 %collective-permute-start.33 = (bf16[8,96,256]{2,1,0:T(8,128)(2,1)S(1)}, bf16[8,96,256]{2,1,0:T(8,128)(2,1)S(1)}, u32[]{:S(2)}, u32[]{:S(2)}) collective-permute-start(bf16[8,96,256]{2,1,0:T(8,128)(2,1)S(1)} %get-tuple-element.67), channel_id=1, source_target_pairs={{0,16},{16,0},{32,48},{48,32},{64,80},{80,64},{96,112},{112,96},{1... | collective-permute-start | bytes 1179656 | tf_op jit(solution)/shard_map/ppermute | solution.py:532
  115.5 10.0 %collective-permute-start.35 = (bf16[2,96,256]{2,1,0:T(8,128)(2,1)S(1)}, bf16[2,96,256]{2,1,0:T(8,128)(2,1)S(1)}, u32[]{:S(2)}, u32[]{:S(2)}) collective-permute-start(bf16[2,96,256]{2,1,0:T(8,128)(2,1)S(1)} %get-tuple-element.71), channel_id=1, source_target_pairs={{0,128},{16,144},{32,160},{48,176},{64,192},{80,208},{96,224},{112... | collective-permute-start | bytes 294920 | tf_op jit(solution)/shard_map/ppermute | solution.py:513
  117.5 16.5 %collective-permute-start.36 = (bf16[2,96,256]{2,1,0:T(8,128)(2,1)S(1)}, bf16[2,96,256]{2,1,0:T(8,128)(2,1)S(1)}, u32[]{:S(2)}, u32[]{:S(2)}) collective-permute-start(bf16[2,96,256]{2,1,0:T(8,128)(2,1)S(1)} %get-tuple-element.72), channel_id=1, source_target_pairs={{0,96},{16,112},{32,128},{48,144},{64,160},{80,176},{96,192},{112,... | collective-permute-start | bytes 294920 | tf_op jit(solution)/shard_map/ppermute | solution.py:513
  119.0 18.2 %collective-permute-start.37 = (bf16[2,96,256]{2,1,0:T(8,128)(2,1)S(1)}, bf16[2,96,256]{2,1,0:T(8,128)(2,1)S(1)}, u32[]{:S(2)}, u32[]{:S(2)}) collective-permute-start(bf16[2,96,256]{2,1,0:T(8,128)(2,1)S(1)} %get-tuple-element.73), channel_id=1, source_target_pairs={{0,160},{16,176},{32,192},{48,208},{64,224},{80,240},{96,0},{112,1... | collective-permute-start | bytes 294920 | tf_op jit(solution)/shard_map/ppermute | solution.py:513
  121.9 15.3 %collective-permute-start.38 = (bf16[2,96,256]{2,1,0:T(8,128)(2,1)S(1)}, bf16[2,96,256]{2,1,0:T(8,128)(2,1)S(1)}, u32[]{:S(2)}, u32[]{:S(2)}) collective-permute-start(bf16[2,96,256]{2,1,0:T(8,128)(2,1)S(1)} %get-tuple-element.74), channel_id=1, source_target_pairs={{0,64},{16,80},{32,96},{48,112},{64,128},{80,144},{96,160},{112,17... | collective-permute-start | bytes 294920 | tf_op jit(solution)/shard_map/ppermute | solution.py:513
  124.0 13.2 %collective-permute-start.39 = (bf16[2,96,256]{2,1,0:T(8,128)(2,1)S(1)}, bf16[2,96,256]{2,1,0:T(8,128)(2,1)S(1)}, u32[]{:S(2)}, u32[]{:S(2)}) collective-permute-start(bf16[2,96,256]{2,1,0:T(8,128)(2,1)S(1)} %get-tuple-element.75), channel_id=1, source_target_pairs={{0,192},{16,208},{32,224},{48,240},{64,0},{80,16},{96,32},{112,48}... | collective-permute-start | bytes 294920 | tf_op jit(solution)/shard_map/ppermute | solution.py:513
  125.5 11.7 %collective-permute-start.40 = (bf16[2,96,256]{2,1,0:T(8,128)(2,1)S(1)}, bf16[2,96,256]{2,1,0:T(8,128)(2,1)S(1)}, u32[]{:S(2)}, u32[]{:S(2)}) collective-permute-start(bf16[2,96,256]{2,1,0:T(8,128)(2,1)S(1)} %get-tuple-element.76), channel_id=1, source_target_pairs={{0,32},{16,48},{32,64},{48,80},{64,96},{80,112},{96,128},{112,144}... | collective-permute-start | bytes 294920 | tf_op jit(solution)/shard_map/ppermute | solution.py:513
  (12 other events, 63.4 us)

commit v8 on v7

--- a/solution.py
+++ b/solution.py
@@ -61,7 +61,7 @@
     return 2 * lax.rem(plane + away, planes) + (1 - core if other else core)
 
 
-def plan_kernel(owner_ref, grads_ref, table_ref, *refs):
+def plan_kernel(owner_ref, grads_ref, table_ref, marks_ref, *refs):
     outs, (empty_ref, held, sem) = refs[:-3], refs[-3:]
     count, planes = owner_ref.shape[0], len(outs)
     copy = pltpu.make_async_copy(grads_ref, held, sem)
@@ -88,6 +88,20 @@
         table_ref[0, h] = e
         table_ref[3, h] = g
         n = n + two.astype(jnp.int32)
+    plane, core = spot_here()
+    for away in range(planes):
+        group = group_at(away, 0, planes)
+        helper = table_ref[2, group]
+        here = jnp.where(lax.rem(jnp.maximum(helper, 0), 2) == core, 0, 1)
+        mark = jnp.where(helper < 0, -1, here)
+        marks_ref[away : away + 1, :] = jnp.full((1, marks_ref.shape[1]), mark, jnp.int32)
+        owner = table_ref[3, group]
+        there = jnp.maximum(owner, 0)
+        up = lax.rem(lax.div(there, 2) - plane + planes, planes)
+        mark = 2 * up + jnp.where(lax.rem(there, 2) == core, 0, 1)
+        mark = jnp.where(owner < 0, -1, mark)
+        row = planes + away
+        marks_ref[row : row + 1, :] = jnp.full((1, marks_ref.shape[1]), mark, jnp.int32)
     copy.wait()
     for away in range(planes):
         for other in range(2):
@@ -99,10 +113,13 @@
     planes = count // 2
     return pl.pallas_call(
         plan_kernel,
-        out_shape=(shape_of(4, count + 1, dtype=jnp.int32),)
+        out_shape=(
+            shape_of(4, count + 1, dtype=jnp.int32),
+            shape_of(2 * planes, 128, dtype=jnp.int32),
+        )
         + (shape_of(2, rows, cols),) * planes,
         in_specs=[SMEM, ANY],
-        out_specs=(SMEM,) + (VMEM,) * planes,
+        out_specs=(SMEM,) + (VMEM,) * (planes + 1),
         scratch_shapes=[
             pltpu.SMEM((count + 1,), jnp.int32),
             pltpu.VMEM(grads.shape, grads.dtype),
@@ -322,64 +339,63 @@
     )(own, got, inverse, *out_of_lists(lists))
 
 
-def pick_kernel(planes, table_ref, *refs):
+def pick_kernel(planes, marks_ref, *refs):
     ins, (mine_ref, give_ref) = in_place(refs[:planes]), refs[planes:]
     for up, ref in enumerate(ins):
-        owner = table_ref[3, group_at(up, 0, planes)]
-        away = lax.rem(lax.div(jnp.maximum(owner, 0), 2) - spot_here()[0] + planes, planes)
-        here = lax.rem(jnp.maximum(owner, 0), 2) == spot_here()[1]
-
-        @pl.when(jnp.logical_and(owner >= 0, here))
+        mark = marks_ref[planes + up, 0]
+        away = lax.div(jnp.maximum(mark, 0), 2)
+        other = lax.rem(jnp.maximum(mark, 0), 2)
+
+        @pl.when(jnp.logical_and(mark >= 0, other == 0))
         def _():
             mine_ref[away] = ref[...]
 
-        @pl.when(jnp.logical_and(owner >= 0, jnp.logical_not(here)))
+        @pl.when(jnp.logical_and(mark >= 0, other == 1))
         def _():
             give_ref[away] = ref[...]
 
 
-def pick(table, back):
+def pick(marks, back):
     planes = len(back)
     block = back[0].shape
     return pl.pallas_call(
         functools.partial(pick_kernel, planes),
         out_shape=(shape_of(planes, *block),) * 2,
-        in_specs=[SMEM] + [VMEM] * planes,
+        in_specs=[VMEM] * (planes + 1),
         out_specs=(VMEM,) * 2,
         compiler_params=params(8),
         name="pick",
-    )(table, *in_turn(back))
-
-
-def merge_kernel(planes, table_ref, mine_ref, got_ref, *outs):
+    )(marks, *in_turn(back))
+
+
+def merge_kernel(marks_ref, mine_ref, got_ref, *outs):
     for away, out in enumerate(outs):
-        helper = table_ref[2, group_at(away, 0, planes)]
-        here = lax.rem(jnp.maximum(helper, 0), 2) == spot_here()[1]
-
-        @pl.when(helper < 0)
+        mark = marks_ref[away, 0]
+
+        @pl.when(mark < 0)
         def _():
             out[...] = jnp.zeros(out.shape, out.dtype)
 
-        @pl.when(jnp.logical_and(helper >= 0, here))
+        @pl.when(mark == 0)
         def _():
             out[...] = mine_ref[away]
 
-        @pl.when(jnp.logical_and(helper >= 0, jnp.logical_not(here)))
+        @pl.when(mark > 0)
         def _():
             out[0] = got_ref[away, 1]
             out[1] = got_ref[away, 0]
 
 
-def merge(table, mine, got):
+def merge(marks, mine, got):
     planes = mine.shape[0]
     return pl.pallas_call(
-        functools.partial(merge_kernel, planes),
+        merge_kernel,
         out_shape=(shape_of(*mine.shape[1:]),) * planes,
-        in_specs=[SMEM] + [VMEM] * 2,
+        in_specs=[VMEM] * 3,
         out_specs=(VMEM,) * planes,
         compiler_params=params(8),
         name="merge",
-    )(table, mine, got)
+    )(marks, mine, got)
 
 
 def update_kernel(planes, table_ref, *refs):
@@ -539,7 +555,7 @@
     rows = rows_dev * groups
     cols = cols_dev * lax.axis_size("grp")
     factor = 0.2 * math.sqrt(max(rows, cols))
-    table, *sends = plan(owner, grads)
+    table, marks, *sends = plan(owner, grads)
     own, give = sort(over_planes(sends, 1))
     got = swap(give)
     own, got = own.reshape(rows // 2, cols_dev), got.reshape(rows // 2, cols_dev)
@@ -547,8 +563,8 @@
     *parts, inverse = add(gather(*parts, 1), rows)
     done = step(own, got, inverse, gather(*parts, 0), factor, planes)
     back = over_planes(done, -1)
-    mine, give = pick(table, back)
-    sends = merge(table, mine, swap(give))
+    mine, give = pick(marks, back)
+    sends = merge(marks, mine, swap(give))
     came = over_planes(sends, 1)
     own, rest = sort(back)
     update = update_of(table, own, swap(rest))

time: 139 us -> 138 us (level)
  transfers between devices with their start and end apart: 42 -> 42, of which waited for: 25 -> 25; matrix products, arithmetic and copies ran while one was open for 0% -> 0% of each run, Pallas kernels for 4% -> 3%
where the time goes in v8:
time: 138 us
  starting transfers between devices  67.9 us (49%)
  waiting for transfers between devices  55.6 us (40%)
  Pallas kernels  11.6 us (8%)
  local copies, waits for them, and re-layouts  1.78 us (1%)
    ppermute x21, starting transfers between devices, over_planes(): got[away] = lax.ppermute(blocks[away], 'fsdp', moves)  39.9 us
    ppermute x21, waiting for transfers between devices, over_planes(): got[away] = lax.ppermute(blocks[away], 'fsdp', moves)  28.5 us
    ppermute x18, waiting for transfers between devices, neighbour(): return lax.ppermute(value, ('fsdp', 'grp'), moves)  25.2 us
    ppermute x18, starting transfers between devices, neighbour(): return lax.ppermute(value, ('fsdp', 'grp'), moves)  23.4 us
    ppermute x3, starting transfers between devices, swap(): return lax.ppermute(value, 'fsdp', [(g, g ^ 1) for g in range(groups)])  4.57 us
    pallas_call x1, Pallas kernels, step(): pl.pallas_call(functools.partial(step_kernel, pairs_of(rows), factor, pla...  3.13 us
  transfers between devices with their start and end apart: 42, of which 25 were waited for; matrix products, arithmetic and copies ran while one was open for 0% of the time, Pallas kernels for 3%

profile of v8, /device:TPU:1, one launch (start us, length us, event | category | flops | bytes accessed | tf_op | source)
XLA Modules:
  0.0 137.8 jit_solution(481060094639368921)
XLA Ops:
  2.4 1.7 %plan.1 = (s32[4,17]{1,0:T(4,128)S(1)}, s32[16,128]{1,0:T(8,128)S(1)}, bf16[2,96,256]{2,1,0:T(8,128)(2,1)S(1)}, bf16[2,96,256]{2,1,0:T(8,128)(2,1)S(1)}, bf16[2,...) custom-call(s32[16]{0:T(128)S(1)} %copy-done.1, ...), custom_call_target="tpu_custom_call" | custom-call | tf_op jit(solution)/shard_map/plan/pallas_call | solution.py:114
  4.1 7.8 %collective-permute-start = (bf16[2,96,256]{2,1,0:T(8,128)(2,1)S(1)}, bf16[2,96,256]{2,1,0:T(8,128)(2,1)S(1)}, u32[]{:S(2)}, u32[]{:S(2)}) collective-permute-start(bf16[2,96,256]{2,1,0:T(8,128)(2,1)S(1)} %get-tuple-element.43), channel_id=1, source_target_pairs={{0,128},{16,144},{32,160},{48,176},{64,192},{80,208},{96,224},{112... | collective-permute-start | bytes 294920 | tf_op jit(solution)/shard_map/ppermute | solution.py:529
  11.9 1.6 %collective-permute-start.1 = (bf16[2,96,256]{2,1,0:T(8,128)(2,1)S(1)}, bf16[2,96,256]{2,1,0:T(8,128)(2,1)S(1)}, u32[]{:S(2)}, u32[]{:S(2)}) collective-permute-start(bf16[2,96,256]{2,1,0:T(8,128)(2,1)S(1)} %get-tuple-element.44), channel_id=1, source_target_pairs={{0,96},{16,112},{32,128},{48,144},{64,160},{80,176},{96,192},{112,... | collective-permute-start | bytes 294920 | tf_op jit(solution)/shard_map/ppermute | solution.py:529
  13.6 2.8 %collective-permute-start.2 = (bf16[2,96,256]{2,1,0:T(8,128)(2,1)S(1)}, bf16[2,96,256]{2,1,0:T(8,128)(2,1)S(1)}, u32[]{:S(2)}, u32[]{:S(2)}) collective-permute-start(bf16[2,96,256]{2,1,0:T(8,128)(2,1)S(1)} %get-tuple-element.45), channel_id=1, source_target_pairs={{0,160},{16,176},{32,192},{48,208},{64,224},{80,240},{96,0},{112,1... | collective-permute-start | bytes 294920 | tf_op jit(solution)/shard_map/ppermute | solution.py:529
  17.6 2.4 %collective-permute-start.4 = (bf16[2,96,256]{2,1,0:T(8,128)(2,1)S(1)}, bf16[2,96,256]{2,1,0:T(8,128)(2,1)S(1)}, u32[]{:S(2)}, u32[]{:S(2)}) collective-permute-start(bf16[2,96,256]{2,1,0:T(8,128)(2,1)S(1)} %get-tuple-element.47), channel_id=1, source_target_pairs={{0,192},{16,208},{32,224},{48,240},{64,0},{80,16},{96,32},{112,48}... | collective-permute-start | bytes 294920 | tf_op jit(solution)/shard_map/ppermute | solution.py:529
  20.7 4.6 %collective-permute-done.1.refs_2_ = bf16[2,96,256]{2,1,0:T(8,128)(2,1)S(1)} collective-permute-done((bf16[2,96,256]{2,1,0:T(8,128)(2,1)S(1)}, bf16[2,96,256]{2,1,0:T(8,128)(2,1)S(1)}, u32[]{:S(2)}, u32[]{:S(2)}) %collective-permute-start.1) | collective-permute-done | bytes 98336 | tf_op jit(solution)/shard_map/ppermute | solution.py:529
  25.4 3.0 %collective-permute-done.4.refs_5_ = bf16[2,96,256]{2,1,0:T(8,128)(2,1)S(1)} collective-permute-done((bf16[2,96,256]{2,1,0:T(8,128)(2,1)S(1)}, bf16[2,96,256]{2,1,0:T(8,128)(2,1)S(1)}, u32[]{:S(2)}, u32[]{:S(2)}) %collective-permute-start.4) | collective-permute-done | bytes 98336 | tf_op jit(solution)/shard_map/ppermute | solution.py:529
  33.1 2.7 %collective-permute-start.10 = (bf16[768,256]{1,0:T(8,128)(2,1)S(1)}, bf16[768,256]{1,0:T(8,128)(2,1)S(1)}, u32[]{:S(2)}, u32[]{:S(2)}) collective-permute-start(bf16[768,256]{1,0:T(8,128)(2,1)S(1)} %bitcast.6), channel_id=1, source_target_pairs={{0,3},{1,0},{2,1},{3,2},{4,7},{5,4},{6,5},{7,6},{8,11},{9,8},{10,9... | collective-permute-start | bytes 1179656 | tf_op jit(solution)/shard_map/ppermute | solution.py:499
  37.3 2.6 %collective-permute-done.8.refs_2_ = bf16[768,256]{1,0:T(8,128)(2,1)S(1)} collective-permute-done((bf16[768,256]{1,0:T(8,128)(2,1)S(1)}, bf16[768,256]{1,0:T(8,128)(2,1)S(1)}, u32[]{:S(2)}, u32[]{:S(2)}) %collective-permute-start.8) | collective-permute-done | bytes 393248 | tf_op jit(solution)/shard_map/ppermute | solution.py:499
  40.6 3.1 %collective-permute-start.11 = (bf16[768,256]{1,0:T(8,128)(2,1)S(1)}, bf16[768,256]{1,0:T(8,128)(2,1)S(1)}, u32[]{:S(2)}, u32[]{:S(2)}) collective-permute-start(bf16[768,256]{1,0:T(8,128)(2,1)S(1)} %collective-permute-done.10.refs_3_), channel_id=1, source_target_pairs={{0,3},{1,0},{2,1},{3,2},{4,7},{5,4},{6,5},{7,6},{8,11},{9,8},{10,9... | collective-permute-start | bytes 1179656 | tf_op jit(solution)/shard_map/ppermute | solution.py:499
  45.6 3.0 %collective-permute-done.9.own = bf16[768,256]{1,0:T(8,128)(2,1)S(1)} collective-permute-done((bf16[768,256]{1,0:T(8,128)(2,1)S(1)}, bf16[768,256]{1,0:T(8,128)(2,1)S(1)}, u32[]{:S(2)}, u32[]{:S(2)}) %collective-permute-start.9) | collective-permute-done | bytes 393248 | tf_op jit(solution)/shard_map/ppermute | solution.py:499
  53.8 3.6 %collective-permute-done.14.refs_2_ = bf16[11,64,256]{2,1,0:T(8,128)(2,1)S(1)} collective-permute-done((bf16[11,64,256]{2,1,0:T(8,128)(2,1)S(1)}, bf16[11,64,256]{2,1,0:T(8,128)(2,1)S(1)}, u32[]{:S(2)}, u32[]{:S(2)}) %collective-permute-start.14) | collective-permute-done | bytes 360480 | tf_op jit(solution)/shard_map/ppermute | solution.py:499
  57.4 2.7 %collective-permute-start.19 = (bf16[11,64,256]{2,1,0:T(8,128)(2,1)S(1)}, bf16[11,64,256]{2,1,0:T(8,128)(2,1)S(1)}, u32[]{:S(2)}, u32[]{:S(2)}) collective-permute-start(bf16[11,64,256]{2,1,0:T(8,128)(2,1)S(1)} %collective-permute-done.15.refs_3_), channel_id=1, source_target_pairs={{0,12},{1,13},{2,14},{3,15},{4,0},{5,1},{6,2},{7,3},{8,4},{9,5},{1... | collective-permute-start | bytes 1081352 | tf_op jit(solution)/shard_map/ppermute | solution.py:499
  61.4 3.9 %collective-permute-done.18.refs_6_ = bf16[11,64,256]{2,1,0:T(8,128)(2,1)S(1)} collective-permute-done((bf16[11,64,256]{2,1,0:T(8,128)(2,1)S(1)}, bf16[11,64,256]{2,1,0:T(8,128)(2,1)S(1)}, u32[]{:S(2)}, u32[]{:S(2)}) %collective-permute-start.18) | collective-permute-done | bytes 360480 | tf_op jit(solution)/shard_map/ppermute | solution.py:499
  66.4 2.8 %collective-permute-start.21 = (bf16[11,64,256]{2,1,0:T(8,128)(2,1)S(1)}, bf16[11,64,256]{2,1,0:T(8,128)(2,1)S(1)}, u32[]{:S(2)}, u32[]{:S(2)}) collective-permute-start(bf16[11,64,256]{2,1,0:T(8,128)(2,1)S(1)} %get-tuple-element.58.refs_1_), channel_id=1, source_target_pairs={{0,3},{1,0},{2,1},{3,2},{4,7},{5,4},{6,5},{7,6},{8,11},{9,8},{10,9... | collective-permute-start | bytes 1081352 | tf_op jit(solution)/shard_map/ppermute | solution.py:499
  70.7 3.6 %collective-permute-done.20.refs_2_ = bf16[11,64,256]{2,1,0:T(8,128)(2,1)S(1)} collective-permute-done((bf16[11,64,256]{2,1,0:T(8,128)(2,1)S(1)}, bf16[11,64,256]{2,1,0:T(8,128)(2,1)S(1)}, u32[]{:S(2)}, u32[]{:S(2)}) %collective-permute-start.20) | collective-permute-done | bytes 360480 | tf_op jit(solution)/shard_map/ppermute | solution.py:499
  74.3 2.8 %collective-permute-start.25 = (bf16[11,64,256]{2,1,0:T(8,128)(2,1)S(1)}, bf16[11,64,256]{2,1,0:T(8,128)(2,1)S(1)}, u32[]{:S(2)}, u32[]{:S(2)}) collective-permute-start(bf16[11,64,256]{2,1,0:T(8,128)(2,1)S(1)} %collective-permute-done.21.refs_3_), channel_id=1, source_target_pairs={{0,3},{1,0},{2,1},{3,2},{4,7},{5,4},{6,5},{7,6},{8,11},{9,8},{10,9... | collective-permute-start | bytes 1081352 | tf_op jit(solution)/shard_map/ppermute | solution.py:499
  78.1 4.2 %collective-permute-done.24.refs_6_ = bf16[11,64,256]{2,1,0:T(8,128)(2,1)S(1)} collective-permute-done((bf16[11,64,256]{2,1,0:T(8,128)(2,1)S(1)}, bf16[11,64,256]{2,1,0:T(8,128)(2,1)S(1)}, u32[]{:S(2)}, u32[]{:S(2)}) %collective-permute-start.24) | collective-permute-done | bytes 360480 | tf_op jit(solution)/shard_map/ppermute | solution.py:499
  82.3 3.1 %step.1 = (bf16[2,96,256]{2,1,0:T(8,128)(2,1)S(1)}, bf16[2,96,256]{2,1,0:T(8,128)(2,1)S(1)}, bf16[2,96,256]{2,1,0:T(8,128)(2,1)S(1)}, bf16[2,96,256]{2,1,0:T(8,1...) custom-call(bf16[768,256]{1,0:T(8,128)(2,1)S(1)} %bitcast.5, ...), custom_call_target="tpu_custom_call" | custom-call | flops 2415919104 | bytes 6291456 | tf_op jit(solution)/shard_map/step/pallas_call | solution.py:326
  85.4 3.2 %collective-permute-start.26 = (bf16[2,96,256]{2,1,0:T(8,128)(2,1)S(1)}, bf16[2,96,256]{2,1,0:T(8,128)(2,1)S(1)}, u32[]{:S(2)}, u32[]{:S(2)}) collective-permute-start(bf16[2,96,256]{2,1,0:T(8,128)(2,1)S(1)} %get-tuple-element.60.refs_4_), channel_id=1, source_target_pairs={{0,128},{16,144},{32,160},{48,176},{64,192},{80,208},{96,224},{112... | collective-permute-start | bytes 294920 | tf_op jit(solution)/shard_map/ppermute | solution.py:529
  88.6 1.7 %collective-permute-start.27 = (bf16[2,96,256]{2,1,0:T(8,128)(2,1)S(1)}, bf16[2,96,256]{2,1,0:T(8,128)(2,1)S(1)}, u32[]{:S(2)}, u32[]{:S(2)}) collective-permute-start(bf16[2,96,256]{2,1,0:T(8,128)(2,1)S(1)} %get-tuple-element.61.refs_3_), channel_id=1, source_target_pairs={{0,160},{16,176},{32,192},{48,208},{64,224},{80,240},{96,0},{112,1... | collective-permute-start | bytes 294920 | tf_op jit(solution)/shard_map/ppermute | solution.py:529
  91.9 2.9 %collective-permute-start.29 = (bf16[2,96,256]{2,1,0:T(8,128)(2,1)S(1)}, bf16[2,96,256]{2,1,0:T(8,128)(2,1)S(1)}, u32[]{:S(2)}, u32[]{:S(2)}) collective-permute-start(bf16[2,96,256]{2,1,0:T(8,128)(2,1)S(1)} %get-tuple-element.63.refs_2_), channel_id=1, source_target_pairs={{0,192},{16,208},{32,224},{48,240},{64,0},{80,16},{96,32},{112,48}... | collective-permute-start | bytes 294920 | tf_op jit(solution)/shard_map/ppermute | solution.py:529
  94.8 3.0 %collective-permute-start.31 = (bf16[2,96,256]{2,1,0:T(8,128)(2,1)S(1)}, bf16[2,96,256]{2,1,0:T(8,128)(2,1)S(1)}, u32[]{:S(2)}, u32[]{:S(2)}) collective-permute-start(bf16[2,96,256]{2,1,0:T(8,128)(2,1)S(1)} %get-tuple-element.65.refs_1_), channel_id=1, source_target_pairs={{0,224},{16,240},{32,0},{48,16},{64,32},{80,48},{96,64},{112,80},{... | collective-permute-start | bytes 294920 | tf_op jit(solution)/shard_map/ppermute | solution.py:529
  97.8 4.9 %collective-permute-done.29.refs_4_ = bf16[2,96,256]{2,1,0:T(8,128)(2,1)S(1)} collective-permute-done((bf16[2,96,256]{2,1,0:T(8,128)(2,1)S(1)}, bf16[2,96,256]{2,1,0:T(8,128)(2,1)S(1)}, u32[]{:S(2)}, u32[]{:S(2)}) %collective-permute-start.29) | collective-permute-done | bytes 98336 | tf_op jit(solution)/shard_map/ppermute | solution.py:529
  102.6 2.1 %collective-permute-done.30.refs_5_ = bf16[2,96,256]{2,1,0:T(8,128)(2,1)S(1)} collective-permute-done((bf16[2,96,256]{2,1,0:T(8,128)(2,1)S(1)}, bf16[2,96,256]{2,1,0:T(8,128)(2,1)S(1)}, u32[]{:S(2)}, u32[]{:S(2)}) %collective-permute-start.30) | collective-permute-done | bytes 98336 | tf_op jit(solution)/shard_map/ppermute | solution.py:529
  105.6 3.0 %collective-permute-done.32.refs_7_ = bf16[2,96,256]{2,1,0:T(8,128)(2,1)S(1)} collective-permute-done((bf16[2,96,256]{2,1,0:T(8,128)(2,1)S(1)}, bf16[2,96,256]{2,1,0:T(8,128)(2,1)S(1)}, u32[]{:S(2)}, u32[]{:S(2)}) %collective-permute-start.32) | collective-permute-done | bytes 98336 | tf_op jit(solution)/shard_map/ppermute | solution.py:529
  109.0 3.5 %collective-permute-start.34 = (bf16[8,2,96,256]{3,2,1,0:T(8,128)(2,1)S(1)}, bf16[8,2,96,256]{3,2,1,0:T(8,128)(2,1)S(1)}, u32[]{:S(2)}, u32[]{:S(2)}) collective-permute-start(bf16[8,2,96,256]{3,2,1,0:T(8,128)(2,1)S(1)} %get-tuple-element.71), channel_id=1, source_target_pairs={{0,16},{16,0},{32,48},{48,32},{64,80},{80,64},{96,112},{112,96},{1... | collective-permute-start | bytes 2359304 | tf_op jit(solution)/shard_map/ppermute | solution.py:548
  112.7 1.7 %collective-permute-done.34.got_ref = bf16[8,2,96,256]{3,2,1,0:T(8,128)(2,1)S(1)} collective-permute-done((bf16[8,2,96,256]{3,2,1,0:T(8,128)(2,1)S(1)}, bf16[8,2,96,256]{3,2,1,0:T(8,128)(2,1)S(1)}, u32[]{:S(2)}, u32[]{:S(2)}) %collective-permute-start.34) | collective-permute-done | bytes 786464 | tf_op jit(solution)/shard_map/ppermute | solution.py:548
  114.8 2.0 %collective-permute-start.35 = (bf16[2,96,256]{2,1,0:T(8,128)(2,1)S(1)}, bf16[2,96,256]{2,1,0:T(8,128)(2,1)S(1)}, u32[]{:S(2)}, u32[]{:S(2)}) collective-permute-start(bf16[2,96,256]{2,1,0:T(8,128)(2,1)S(1)} %get-tuple-element.73), channel_id=1, source_target_pairs={{0,128},{16,144},{32,160},{48,176},{64,192},{80,208},{96,224},{112... | collective-permute-start | bytes 294920 | tf_op jit(solution)/shard_map/ppermute | solution.py:529
  118.3 2.9 %collective-permute-start.37 = (bf16[2,96,256]{2,1,0:T(8,128)(2,1)S(1)}, bf16[2,96,256]{2,1,0:T(8,128)(2,1)S(1)}, u32[]{:S(2)}, u32[]{:S(2)}) collective-permute-start(bf16[2,96,256]{2,1,0:T(8,128)(2,1)S(1)} %get-tuple-element.75), channel_id=1, source_target_pairs={{0,160},{16,176},{32,192},{48,208},{64,224},{80,240},{96,0},{112,1... | collective-permute-start | bytes 294920 | tf_op jit(solution)/shard_map/ppermute | solution.py:529
  121.3 2.1 %collective-permute-start.38 = (bf16[2,96,256]{2,1,0:T(8,128)(2,1)S(1)}, bf16[2,96,256]{2,1,0:T(8,128)(2,1)S(1)}, u32[]{:S(2)}, u32[]{:S(2)}) collective-permute-start(bf16[2,96,256]{2,1,0:T(8,128)(2,1)S(1)} %get-tuple-element.76), channel_id=1, source_target_pairs={{0,64},{16,80},{32,96},{48,112},{64,128},{80,144},{96,160},{112,17... | collective-permute-start | bytes 294920 | tf_op jit(solution)/shard_map/ppermute | solution.py:529
  125.8 7.4 %collective-permute-done.36.refs_2_ = bf16[2,96,256]{2,1,0:T(8,128)(2,1)S(1)} collective-permute-done((bf16[2,96,256]{2,1,0:T(8,128)(2,1)S(1)}, bf16[2,96,256]{2,1,0:T(8,128)(2,1)S(1)}, u32[]{:S(2)}, u32[]{:S(2)}) %collective-permute-start.36) | collective-permute-done | bytes 98336 | tf_op jit(solution)/shard_map/ppermute | solution.py:529
  (68 shorter events, 34.5 us)
Async XLA Ops:
  4.1 15.9 %collective-permute-start = (bf16[2,96,256]{2,1,0:T(8,128)(2,1)S(1)}, bf16[2,96,256]{2,1,0:T(8,128)(2,1)S(1)}, u32[]{:S(2)}, u32[]{:S(2)}) collective-permute-start(bf16[2,96,256]{2,1,0:T(8,128)(2,1)S(1)} %get-tuple-element.43), channel_id=1, source_target_pairs={{0,128},{16,144},{32,160},{48,176},{64,192},{80,208},{96,224},{112... | collective-permute-start | bytes 294920 | tf_op jit(solution)/shard_map/ppermute | solution.py:529
  11.9 13.4 %collective-permute-start.1 = (bf16[2,96,256]{2,1,0:T(8,128)(2,1)S(1)}, bf16[2,96,256]{2,1,0:T(8,128)(2,1)S(1)}, u32[]{:S(2)}, u32[]{:S(2)}) collective-permute-start(bf16[2,96,256]{2,1,0:T(8,128)(2,1)S(1)} %get-tuple-element.44), channel_id=1, source_target_pairs={{0,96},{16,112},{32,128},{48,144},{64,160},{80,176},{96,192},{112,... | collective-permute-start | bytes 294920 | tf_op jit(solution)/shard_map/ppermute | solution.py:529
  13.6 11.8 %collective-permute-start.2 = (bf16[2,96,256]{2,1,0:T(8,128)(2,1)S(1)}, bf16[2,96,256]{2,1,0:T(8,128)(2,1)S(1)}, u32[]{:S(2)}, u32[]{:S(2)}) collective-permute-start(bf16[2,96,256]{2,1,0:T(8,128)(2,1)S(1)} %get-tuple-element.45), channel_id=1, source_target_pairs={{0,160},{16,176},{32,192},{48,208},{64,224},{80,240},{96,0},{112,1... | collective-permute-start | bytes 294920 | tf_op jit(solution)/shard_map/ppermute | solution.py:529
  16.4 9.0 %collective-permute-start.3 = (bf16[2,96,256]{2,1,0:T(8,128)(2,1)S(1)}, bf16[2,96,256]{2,1,0:T(8,128)(2,1)S(1)}, u32[]{:S(2)}, u32[]{:S(2)}) collective-permute-start(bf16[2,96,256]{2,1,0:T(8,128)(2,1)S(1)} %get-tuple-element.46), channel_id=1, source_target_pairs={{0,64},{16,80},{32,96},{48,112},{64,128},{80,144},{96,160},{112,17... | collective-permute-start | bytes 294920 | tf_op jit(solution)/shard_map/ppermute | solution.py:529
  17.6 10.8 %collective-permute-start.4 = (bf16[2,96,256]{2,1,0:T(8,128)(2,1)S(1)}, bf16[2,96,256]{2,1,0:T(8,128)(2,1)S(1)}, u32[]{:S(2)}, u32[]{:S(2)}) collective-permute-start(bf16[2,96,256]{2,1,0:T(8,128)(2,1)S(1)} %get-tuple-element.47), channel_id=1, source_target_pairs={{0,192},{16,208},{32,224},{48,240},{64,0},{80,16},{96,32},{112,48}... | collective-permute-start | bytes 294920 | tf_op jit(solution)/shard_map/ppermute | solution.py:529
  20.0 9.9 %collective-permute-start.5 = (bf16[2,96,256]{2,1,0:T(8,128)(2,1)S(1)}, bf16[2,96,256]{2,1,0:T(8,128)(2,1)S(1)}, u32[]{:S(2)}, u32[]{:S(2)}) collective-permute-start(bf16[2,96,256]{2,1,0:T(8,128)(2,1)S(1)} %get-tuple-element.48), channel_id=1, source_target_pairs={{0,32},{16,48},{32,64},{48,80},{64,96},{80,112},{96,128},{112,144}... | collective-permute-start | bytes 294920 | tf_op jit(solution)/shard_map/ppermute | solution.py:529
  31.8 8.1 %collective-permute-start.8 = (bf16[768,256]{1,0:T(8,128)(2,1)S(1)}, bf16[768,256]{1,0:T(8,128)(2,1)S(1)}, u32[]{:S(2)}, u32[]{:S(2)}) collective-permute-start(bf16[768,256]{1,0:T(8,128)(2,1)S(1)} %bitcast.2), channel_id=1, source_target_pairs={{0,1},{1,2},{2,3},{3,0},{4,5},{5,6},{6,7},{7,4},{8,9},{9,10},{10,1... | collective-permute-start | bytes 1179656 | tf_op jit(solution)/shard_map/ppermute | solution.py:499
  35.8 8.9 %collective-permute-start.12 = (bf16[768,256]{1,0:T(8,128)(2,1)S(1)}, bf16[768,256]{1,0:T(8,128)(2,1)S(1)}, u32[]{:S(2)}, u32[]{:S(2)}) collective-permute-start(bf16[768,256]{1,0:T(8,128)(2,1)S(1)} %bitcast.3), channel_id=1, source_target_pairs={{0,3},{1,0},{2,1},{3,2},{4,7},{5,4},{6,5},{7,6},{8,11},{9,8},{10,9... | collective-permute-start | bytes 1179656 | tf_op jit(solution)/shard_map/ppermute | solution.py:499
  36.3 8.5 %collective-permute-start.13 = (bf16[768,256]{1,0:T(8,128)(2,1)S(1)}, bf16[768,256]{1,0:T(8,128)(2,1)S(1)}, u32[]{:S(2)}, u32[]{:S(2)}) collective-permute-start(bf16[768,256]{1,0:T(8,128)(2,1)S(1)} %bitcast.7), channel_id=1, source_target_pairs={{0,1},{1,2},{2,3},{3,0},{4,5},{5,6},{6,7},{7,4},{8,9},{9,10},{10,1... | collective-permute-start | bytes 1179656 | tf_op jit(solution)/shard_map/ppermute | solution.py:499
  39.9 8.7 %collective-permute-start.9 = (bf16[768,256]{1,0:T(8,128)(2,1)S(1)}, bf16[768,256]{1,0:T(8,128)(2,1)S(1)}, u32[]{:S(2)}, u32[]{:S(2)}) collective-permute-start(bf16[768,256]{1,0:T(8,128)(2,1)S(1)} %collective-permute-done.8.refs_2_), channel_id=1, source_target_pairs={{0,1},{1,2},{2,3},{3,0},{4,5},{5,6},{6,7},{7,4},{8,9},{9,10},{10,1... | collective-permute-start | bytes 1179656 | tf_op jit(solution)/shard_map/ppermute | solution.py:499
  40.6 8.4 %collective-permute-start.11 = (bf16[768,256]{1,0:T(8,128)(2,1)S(1)}, bf16[768,256]{1,0:T(8,128)(2,1)S(1)}, u32[]{:S(2)}, u32[]{:S(2)}) collective-permute-start(bf16[768,256]{1,0:T(8,128)(2,1)S(1)} %collective-permute-done.10.refs_3_), channel_id=1, source_target_pairs={{0,3},{1,0},{2,1},{3,2},{4,7},{5,4},{6,5},{7,6},{8,11},{9,8},{10,9... | collective-permute-start | bytes 1179656 | tf_op jit(solution)/shard_map/ppermute | solution.py:499
  49.4 8.0 %collective-permute-start.14 = (bf16[11,64,256]{2,1,0:T(8,128)(2,1)S(1)}, bf16[11,64,256]{2,1,0:T(8,128)(2,1)S(1)}, u32[]{:S(2)}, u32[]{:S(2)}) collective-permute-start(bf16[11,64,256]{2,1,0:T(8,128)(2,1)S(1)} %get-tuple-element.54.refs_0_), channel_id=1, source_target_pairs={{0,4},{1,5},{2,6},{3,7},{4,8},{5,9},{6,10},{7,11},{8,12},{9,13},{1... | collective-permute-start | bytes 1081352 | tf_op jit(solution)/shard_map/ppermute | solution.py:499
  52.3 9.0 %collective-permute-start.16 = (bf16[11,64,256]{2,1,0:T(8,128)(2,1)S(1)}, bf16[11,64,256]{2,1,0:T(8,128)(2,1)S(1)}, u32[]{:S(2)}, u32[]{:S(2)}) collective-permute-start(bf16[11,64,256]{2,1,0:T(8,128)(2,1)S(1)} %get-tuple-element.54.refs_0_), channel_id=1, source_target_pairs={{0,12},{1,13},{2,14},{3,15},{4,0},{5,1},{6,2},{7,3},{8,4},{9,5},{1... | collective-permute-start | bytes 1081352 | tf_op jit(solution)/shard_map/ppermute | solution.py:499
  57.4 7.8 %collective-permute-start.18 = (bf16[11,64,256]{2,1,0:T(8,128)(2,1)S(1)}, bf16[11,64,256]{2,1,0:T(8,128)(2,1)S(1)}, u32[]{:S(2)}, u32[]{:S(2)}) collective-permute-start(bf16[11,64,256]{2,1,0:T(8,128)(2,1)S(1)} %collective-permute-done.14.refs_2_), channel_id=1, source_target_pairs={{0,4},{1,5},{2,6},{3,7},{4,8},{5,9},{6,10},{7,11},{8,12},{9,13},{1... | collective-permute-start | bytes 1081352 | tf_op jit(solution)/shard_map/ppermute | solution.py:499
  65.7 8.6 %collective-permute-start.20 = (bf16[11,64,256]{2,1,0:T(8,128)(2,1)S(1)}, bf16[11,64,256]{2,1,0:T(8,128)(2,1)S(1)}, u32[]{:S(2)}, u32[]{:S(2)}) collective-permute-start(bf16[11,64,256]{2,1,0:T(8,128)(2,1)S(1)} %get-tuple-element.57.refs_0_), channel_id=1, source_target_pairs={{0,1},{1,2},{2,3},{3,0},{4,5},{5,6},{6,7},{7,4},{8,9},{9,10},{10,1... | collective-permute-start | bytes 1081352 | tf_op jit(solution)/shard_map/ppermute | solution.py:499
  66.4 7.9 %collective-permute-start.21 = (bf16[11,64,256]{2,1,0:T(8,128)(2,1)S(1)}, bf16[11,64,256]{2,1,0:T(8,128)(2,1)S(1)}, u32[]{:S(2)}, u32[]{:S(2)}) collective-permute-start(bf16[11,64,256]{2,1,0:T(8,128)(2,1)S(1)} %get-tuple-element.58.refs_1_), channel_id=1, source_target_pairs={{0,3},{1,0},{2,1},{3,2},{4,7},{5,4},{6,5},{7,6},{8,11},{9,8},{10,9... | collective-permute-start | bytes 1081352 | tf_op jit(solution)/shard_map/ppermute | solution.py:499
  69.3 8.2 %collective-permute-start.22 = (bf16[11,64,256]{2,1,0:T(8,128)(2,1)S(1)}, bf16[11,64,256]{2,1,0:T(8,128)(2,1)S(1)}, u32[]{:S(2)}, u32[]{:S(2)}) collective-permute-start(bf16[11,64,256]{2,1,0:T(8,128)(2,1)S(1)} %get-tuple-element.57.refs_0_), channel_id=1, source_target_pairs={{0,3},{1,0},{2,1},{3,2},{4,7},{5,4},{6,5},{7,6},{8,11},{9,8},{10,9... | collective-permute-start | bytes 1081352 | tf_op jit(solution)/shard_map/ppermute | solution.py:499
  74.3 8.0 %collective-permute-start.24 = (bf16[11,64,256]{2,1,0:T(8,128)(2,1)S(1)}, bf16[11,64,256]{2,1,0:T(8,128)(2,1)S(1)}, u32[]{:S(2)}, u32[]{:S(2)}) collective-permute-start(bf16[11,64,256]{2,1,0:T(8,128)(2,1)S(1)} %collective-permute-done.20.refs_2_), channel_id=1, source_target_pairs={{0,1},{1,2},{2,3},{3,0},{4,5},{5,6},{6,7},{7,4},{8,9},{9,10},{10,1... | collective-permute-start | bytes 1081352 | tf_op jit(solution)/shard_map/ppermute | solution.py:499
  74.3 8.0 %collective-permute-start.25 = (bf16[11,64,256]{2,1,0:T(8,128)(2,1)S(1)}, bf16[11,64,256]{2,1,0:T(8,128)(2,1)S(1)}, u32[]{:S(2)}, u32[]{:S(2)}) collective-permute-start(bf16[11,64,256]{2,1,0:T(8,128)(2,1)S(1)} %collective-permute-done.21.refs_3_), channel_id=1, source_target_pairs={{0,3},{1,0},{2,1},{3,2},{4,7},{5,4},{6,5},{7,6},{8,11},{9,8},{10,9... | collective-permute-start | bytes 1081352 | tf_op jit(solution)/shard_map/ppermute | solution.py:499
  85.4 9.3 %collective-permute-start.26 = (bf16[2,96,256]{2,1,0:T(8,128)(2,1)S(1)}, bf16[2,96,256]{2,1,0:T(8,128)(2,1)S(1)}, u32[]{:S(2)}, u32[]{:S(2)}) collective-permute-start(bf16[2,96,256]{2,1,0:T(8,128)(2,1)S(1)} %get-tuple-element.60.refs_4_), channel_id=1, source_target_pairs={{0,128},{16,144},{32,160},{48,176},{64,192},{80,208},{96,224},{112... | collective-permute-start | bytes 294920 | tf_op jit(solution)/shard_map/ppermute | solution.py:529
  88.6 9.2 %collective-permute-start.27 = (bf16[2,96,256]{2,1,0:T(8,128)(2,1)S(1)}, bf16[2,96,256]{2,1,0:T(8,128)(2,1)S(1)}, u32[]{:S(2)}, u32[]{:S(2)}) collective-permute-start(bf16[2,96,256]{2,1,0:T(8,128)(2,1)S(1)} %get-tuple-element.61.refs_3_), channel_id=1, source_target_pairs={{0,160},{16,176},{32,192},{48,208},{64,224},{80,240},{96,0},{112,1... | collective-permute-start | bytes 294920 | tf_op jit(solution)/shard_map/ppermute | solution.py:529
  91.9 10.8 %collective-permute-start.29 = (bf16[2,96,256]{2,1,0:T(8,128)(2,1)S(1)}, bf16[2,96,256]{2,1,0:T(8,128)(2,1)S(1)}, u32[]{:S(2)}, u32[]{:S(2)}) collective-permute-start(bf16[2,96,256]{2,1,0:T(8,128)(2,1)S(1)} %get-tuple-element.63.refs_2_), channel_id=1, source_target_pairs={{0,192},{16,208},{32,224},{48,240},{64,0},{80,16},{96,32},{112,48}... | collective-permute-start | bytes 294920 | tf_op jit(solution)/shard_map/ppermute | solution.py:529
  94.7 10.0 %collective-permute-start.30 = (bf16[2,96,256]{2,1,0:T(8,128)(2,1)S(1)}, bf16[2,96,256]{2,1,0:T(8,128)(2,1)S(1)}, u32[]{:S(2)}, u32[]{:S(2)}) collective-permute-start(bf16[2,96,256]{2,1,0:T(8,128)(2,1)S(1)} %get-tuple-element.64.refs_6_), channel_id=1, source_target_pairs={{0,64},{16,80},{32,96},{48,112},{64,128},{80,144},{96,160},{112,17... | collective-permute-start | bytes 294920 | tf_op jit(solution)/shard_map/ppermute | solution.py:529
  94.8 10.8 %collective-permute-start.31 = (bf16[2,96,256]{2,1,0:T(8,128)(2,1)S(1)}, bf16[2,96,256]{2,1,0:T(8,128)(2,1)S(1)}, u32[]{:S(2)}, u32[]{:S(2)}) collective-permute-start(bf16[2,96,256]{2,1,0:T(8,128)(2,1)S(1)} %get-tuple-element.65.refs_1_), channel_id=1, source_target_pairs={{0,224},{16,240},{32,0},{48,16},{64,32},{80,48},{96,64},{112,80},{... | collective-permute-start | bytes 294920 | tf_op jit(solution)/shard_map/ppermute | solution.py:529
  97.7 10.8 %collective-permute-start.32 = (bf16[2,96,256]{2,1,0:T(8,128)(2,1)S(1)}, bf16[2,96,256]{2,1,0:T(8,128)(2,1)S(1)}, u32[]{:S(2)}, u32[]{:S(2)}) collective-permute-start(bf16[2,96,256]{2,1,0:T(8,128)(2,1)S(1)} %get-tuple-element.66.refs_7_), channel_id=1, source_target_pairs={{0,32},{16,48},{32,64},{48,80},{64,96},{80,112},{96,128},{112,144}... | collective-permute-start | bytes 294920 | tf_op jit(solution)/shard_map/ppermute | solution.py:529
  112.5 10.8 %collective-permute-start.33 = (bf16[8,96,256]{2,1,0:T(8,128)(2,1)S(1)}, bf16[8,96,256]{2,1,0:T(8,128)(2,1)S(1)}, u32[]{:S(2)}, u32[]{:S(2)}) collective-permute-start(bf16[8,96,256]{2,1,0:T(8,128)(2,1)S(1)} %get-tuple-element.68), channel_id=1, source_target_pairs={{0,16},{16,0},{32,48},{48,32},{64,80},{80,64},{96,112},{112,96},{1... | collective-permute-start | bytes 1179656 | tf_op jit(solution)/shard_map/ppermute | solution.py:548
  114.8 10.0 %collective-permute-start.35 = (bf16[2,96,256]{2,1,0:T(8,128)(2,1)S(1)}, bf16[2,96,256]{2,1,0:T(8,128)(2,1)S(1)}, u32[]{:S(2)}, u32[]{:S(2)}) collective-permute-start(bf16[2,96,256]{2,1,0:T(8,128)(2,1)S(1)} %get-tuple-element.73), channel_id=1, source_target_pairs={{0,128},{16,144},{32,160},{48,176},{64,192},{80,208},{96,224},{112... | collective-permute-start | bytes 294920 | tf_op jit(solution)/shard_map/ppermute | solution.py:529
  116.8 16.4 %collective-permute-start.36 = (bf16[2,96,256]{2,1,0:T(8,128)(2,1)S(1)}, bf16[2,96,256]{2,1,0:T(8,128)(2,1)S(1)}, u32[]{:S(2)}, u32[]{:S(2)}) collective-permute-start(bf16[2,96,256]{2,1,0:T(8,128)(2,1)S(1)} %get-tuple-element.74), channel_id=1, source_target_pairs={{0,96},{16,112},{32,128},{48,144},{64,160},{80,176},{96,192},{112,... | collective-permute-start | bytes 294920 | tf_op jit(solution)/shard_map/ppermute | solution.py:529
  118.3 18.1 %collective-permute-start.37 = (bf16[2,96,256]{2,1,0:T(8,128)(2,1)S(1)}, bf16[2,96,256]{2,1,0:T(8,128)(2,1)S(1)}, u32[]{:S(2)}, u32[]{:S(2)}) collective-permute-start(bf16[2,96,256]{2,1,0:T(8,128)(2,1)S(1)} %get-tuple-element.75), channel_id=1, source_target_pairs={{0,160},{16,176},{32,192},{48,208},{64,224},{80,240},{96,0},{112,1... | collective-permute-start | bytes 294920 | tf_op jit(solution)/shard_map/ppermute | solution.py:529
  121.3 15.1 %collective-permute-start.38 = (bf16[2,96,256]{2,1,0:T(8,128)(2,1)S(1)}, bf16[2,96,256]{2,1,0:T(8,128)(2,1)S(1)}, u32[]{:S(2)}, u32[]{:S(2)}) collective-permute-start(bf16[2,96,256]{2,1,0:T(8,128)(2,1)S(1)} %get-tuple-element.76), channel_id=1, source_target_pairs={{0,64},{16,80},{32,96},{48,112},{64,128},{80,144},{96,160},{112,17... | collective-permute-start | bytes 294920 | tf_op jit(solution)/shard_map/ppermute | solution.py:529
  123.4 13.0 %collective-permute-start.39 = (bf16[2,96,256]{2,1,0:T(8,128)(2,1)S(1)}, bf16[2,96,256]{2,1,0:T(8,128)(2,1)S(1)}, u32[]{:S(2)}, u32[]{:S(2)}) collective-permute-start(bf16[2,96,256]{2,1,0:T(8,128)(2,1)S(1)} %get-tuple-element.77), channel_id=1, source_target_pairs={{0,192},{16,208},{32,224},{48,240},{64,0},{80,16},{96,32},{112,48}... | collective-permute-start | bytes 294920 | tf_op jit(solution)/shard_map/ppermute | solution.py:529
  124.8 11.6 %collective-permute-start.40 = (bf16[2,96,256]{2,1,0:T(8,128)(2,1)S(1)}, bf16[2,96,256]{2,1,0:T(8,128)(2,1)S(1)}, u32[]{:S(2)}, u32[]{:S(2)}) collective-permute-start(bf16[2,96,256]{2,1,0:T(8,128)(2,1)S(1)} %get-tuple-element.78), channel_id=1, source_target_pairs={{0,32},{16,48},{32,64},{48,80},{64,96},{80,112},{96,128},{112,144}... | collective-permute-start | bytes 294920 | tf_op jit(solution)/shard_map/ppermute | solution.py:529
  (12 other events, 63.0 us)

commit v9 on v8

--- a/solution.py
+++ b/solution.py
@@ -450,7 +450,7 @@
 
 
 def second_kernel(planes, *refs):
-    ins, (_, out_ref, sems) = in_place(refs[:planes]), refs[planes:]
+    ins, (_, out_ref, sems) = in_place(refs[:planes], 1), refs[planes:]
     move_all(slot_moves(ins, out_ref, 1), sems)
 
 
@@ -482,7 +482,7 @@
         input_output_aliases={planes: 0},
         compiler_params=params(8),
         name="second_slot",
-    )(*in_turn(came), owned)
+    )(*in_turn(came, 1), owned)
 
 
 def neighbour(value, order, amount):
@@ -521,7 +521,7 @@
 def over_planes(blocks, sign):
     planes = len(blocks)
     got = list(blocks)
-    for away in farthest_first(planes)[1:]:
+    for away in range(1, planes):
         moves = []
         for group in range(2 * planes):
             plane, core = divmod(group, 2)
@@ -530,16 +530,16 @@
     return got
 
 
-def farthest_first(planes):
-    return sorted(range(planes), key=lambda a: -min(a, planes - a) if a else -planes)
-
-
-def in_turn(blocks):
-    return [blocks[away] for away in farthest_first(len(blocks))]
-
-
-def in_place(refs):
-    order = farthest_first(len(refs))
+def by_distance(planes, sign=-1):
+    return [0] + sorted(range(1, planes), key=lambda a: sign * min(a, planes - a))
+
+
+def in_turn(blocks, sign=-1):
+    return [blocks[away] for away in by_distance(len(blocks), sign)]
+
+
+def in_place(refs, sign=-1):
+    order = by_distance(len(refs), sign)
     return [refs[order.index(away)] for away in range(len(refs))]
 
 

time: 138 us -> 138 us (level)
  the two profiles are of different devices: /device:TPU:1 before, /device:TPU:38 now
where the time goes in v9:
time: 138 us
  starting transfers between devices  71.4 us (52%)
  waiting for transfers between devices  52.5 us (38%)
  Pallas kernels  11.6 us (8%)
  local copies, waits for them, and re-layouts  1.78 us (1%)
    ppermute x21, starting transfers between devices, over_planes(): got[away] = lax.ppermute(blocks[away], 'fsdp', moves)  48.2 us
    ppermute x18, waiting for transfers between devices, neighbour(): return lax.ppermute(value, ('fsdp', 'grp'), moves)  30.5 us
    ppermute x18, starting transfers between devices, neighbour(): return lax.ppermute(value, ('fsdp', 'grp'), moves)  22.3 us
    ppermute x21, waiting for transfers between devices, over_planes(): got[away] = lax.ppermute(blocks[away], 'fsdp', moves)  19.2 us
    pallas_call x1, Pallas kernels, step(): pl.pallas_call(functools.partial(step_kernel, pairs_of(rows), factor, pla...  3.13 us
    ppermute x3, waiting for transfers between devices, swap(): return lax.ppermute(value, 'fsdp', [(g, g ^ 1) for g in range(groups)])  2.79 us
  transfers between devices with their start and end apart: 42, of which 25 were waited for; matrix products, arithmetic and copies ran while one was open for 0% of the time, Pallas kernels for 3%

profile of v9, /device:TPU:38, one launch (start us, length us, event | category | flops | bytes accessed | tf_op | source)
XLA Modules:
  0.0 138.2 jit_solution(10001416543508741412)
XLA Ops:
  4.1 6.4 %collective-permute-start = (bf16[2,96,256]{2,1,0:T(8,128)(2,1)S(1)}, bf16[2,96,256]{2,1,0:T(8,128)(2,1)S(1)}, u32[]{:S(2)}, u32[]{:S(2)}) collective-permute-start(bf16[2,96,256]{2,1,0:T(8,128)(2,1)S(1)} %get-tuple-element.43), channel_id=1, source_target_pairs={{0,128},{16,144},{32,160},{48,176},{64,192},{80,208},{96,224},{112... | collective-permute-start | bytes 294920 | tf_op jit(solution)/shard_map/ppermute | solution.py:529
  10.5 5.0 %collective-permute-start.2 = (bf16[2,96,256]{2,1,0:T(8,128)(2,1)S(1)}, bf16[2,96,256]{2,1,0:T(8,128)(2,1)S(1)}, u32[]{:S(2)}, u32[]{:S(2)}) collective-permute-start(bf16[2,96,256]{2,1,0:T(8,128)(2,1)S(1)} %get-tuple-element.45), channel_id=1, source_target_pairs={{0,160},{16,176},{32,192},{48,208},{64,224},{80,240},{96,0},{112,1... | collective-permute-start | bytes 294920 | tf_op jit(solution)/shard_map/ppermute | solution.py:529
  15.8 3.9 %collective-permute-start.4 = (bf16[2,96,256]{2,1,0:T(8,128)(2,1)S(1)}, bf16[2,96,256]{2,1,0:T(8,128)(2,1)S(1)}, u32[]{:S(2)}, u32[]{:S(2)}) collective-permute-start(bf16[2,96,256]{2,1,0:T(8,128)(2,1)S(1)} %get-tuple-element.47), channel_id=1, source_target_pairs={{0,192},{16,208},{32,224},{48,240},{64,0},{80,16},{96,32},{112,48}... | collective-permute-start | bytes 294920 | tf_op jit(solution)/shard_map/ppermute | solution.py:529
  19.6 4.9 %collective-permute-start.6 = (bf16[2,96,256]{2,1,0:T(8,128)(2,1)S(1)}, bf16[2,96,256]{2,1,0:T(8,128)(2,1)S(1)}, u32[]{:S(2)}, u32[]{:S(2)}) collective-permute-start(bf16[2,96,256]{2,1,0:T(8,128)(2,1)S(1)} %get-tuple-element.49), channel_id=1, source_target_pairs={{0,224},{16,240},{32,0},{48,16},{64,32},{80,48},{96,64},{112,80},{... | collective-permute-start | bytes 294920 | tf_op jit(solution)/shard_map/ppermute | solution.py:529
  24.6 2.4 %collective-permute-done.3.refs_4_ = bf16[2,96,256]{2,1,0:T(8,128)(2,1)S(1)} collective-permute-done((bf16[2,96,256]{2,1,0:T(8,128)(2,1)S(1)}, bf16[2,96,256]{2,1,0:T(8,128)(2,1)S(1)}, u32[]{:S(2)}, u32[]{:S(2)}) %collective-permute-start.3) | collective-permute-done | bytes 98336 | tf_op jit(solution)/shard_map/ppermute | solution.py:529
  32.0 2.7 %collective-permute-start.13 = (bf16[768,256]{1,0:T(8,128)(2,1)S(1)}, bf16[768,256]{1,0:T(8,128)(2,1)S(1)}, u32[]{:S(2)}, u32[]{:S(2)}) collective-permute-start(bf16[768,256]{1,0:T(8,128)(2,1)S(1)} %bitcast.7), channel_id=1, source_target_pairs={{0,1},{1,2},{2,3},{3,0},{4,5},{5,6},{6,7},{7,4},{8,9},{9,10},{10,1... | collective-permute-start | bytes 1179656 | tf_op jit(solution)/shard_map/ppermute | solution.py:499
  34.7 2.1 %collective-permute-done.8.refs_2_ = bf16[768,256]{1,0:T(8,128)(2,1)S(1)} collective-permute-done((bf16[768,256]{1,0:T(8,128)(2,1)S(1)}, bf16[768,256]{1,0:T(8,128)(2,1)S(1)}, u32[]{:S(2)}, u32[]{:S(2)}) %collective-permute-start.8) | collective-permute-done | bytes 393248 | tf_op jit(solution)/shard_map/ppermute | solution.py:499
  39.6 4.2 %collective-permute-done.12.refs_4_ = bf16[768,256]{1,0:T(8,128)(2,1)S(1)} collective-permute-done((bf16[768,256]{1,0:T(8,128)(2,1)S(1)}, bf16[768,256]{1,0:T(8,128)(2,1)S(1)}, u32[]{:S(2)}, u32[]{:S(2)}) %collective-permute-start.12) | collective-permute-done | bytes 393248 | tf_op jit(solution)/shard_map/ppermute | solution.py:499
  45.2 3.4 %collective-permute-done.11.got = bf16[768,256]{1,0:T(8,128)(2,1)S(1)} collective-permute-done((bf16[768,256]{1,0:T(8,128)(2,1)S(1)}, bf16[768,256]{1,0:T(8,128)(2,1)S(1)}, u32[]{:S(2)}, u32[]{:S(2)}) %collective-permute-start.11) | collective-permute-done | bytes 393248 | tf_op jit(solution)/shard_map/ppermute | solution.py:499
  49.0 1.8 %collective-permute-start.14 = (bf16[11,64,256]{2,1,0:T(8,128)(2,1)S(1)}, bf16[11,64,256]{2,1,0:T(8,128)(2,1)S(1)}, u32[]{:S(2)}, u32[]{:S(2)}) collective-permute-start(bf16[11,64,256]{2,1,0:T(8,128)(2,1)S(1)} %get-tuple-element.54.refs_0_), channel_id=1, source_target_pairs={{0,4},{1,5},{2,6},{3,7},{4,8},{5,9},{6,10},{7,11},{8,12},{9,13},{1... | collective-permute-start | bytes 1081352 | tf_op jit(solution)/shard_map/ppermute | solution.py:499
  52.5 1.8 %collective-permute-start.16 = (bf16[11,64,256]{2,1,0:T(8,128)(2,1)S(1)}, bf16[11,64,256]{2,1,0:T(8,128)(2,1)S(1)}, u32[]{:S(2)}, u32[]{:S(2)}) collective-permute-start(bf16[11,64,256]{2,1,0:T(8,128)(2,1)S(1)} %get-tuple-element.54.refs_0_), channel_id=1, source_target_pairs={{0,12},{1,13},{2,14},{3,15},{4,0},{5,1},{6,2},{7,3},{8,4},{9,5},{1... | collective-permute-start | bytes 1081352 | tf_op jit(solution)/shard_map/ppermute | solution.py:499
  54.5 3.4 %collective-permute-done.14.refs_2_ = bf16[11,64,256]{2,1,0:T(8,128)(2,1)S(1)} collective-permute-done((bf16[11,64,256]{2,1,0:T(8,128)(2,1)S(1)}, bf16[11,64,256]{2,1,0:T(8,128)(2,1)S(1)}, u32[]{:S(2)}, u32[]{:S(2)}) %collective-permute-start.14) | collective-permute-done | bytes 360480 | tf_op jit(solution)/shard_map/ppermute | solution.py:499
  58.3 2.9 %collective-permute-start.19 = (bf16[11,64,256]{2,1,0:T(8,128)(2,1)S(1)}, bf16[11,64,256]{2,1,0:T(8,128)(2,1)S(1)}, u32[]{:S(2)}, u32[]{:S(2)}) collective-permute-start(bf16[11,64,256]{2,1,0:T(8,128)(2,1)S(1)} %collective-permute-done.15.refs_3_), channel_id=1, source_target_pairs={{0,12},{1,13},{2,14},{3,15},{4,0},{5,1},{6,2},{7,3},{8,4},{9,5},{1... | collective-permute-start | bytes 1081352 | tf_op jit(solution)/shard_map/ppermute | solution.py:499
  63.0 3.9 %collective-permute-done.18.refs_6_ = bf16[11,64,256]{2,1,0:T(8,128)(2,1)S(1)} collective-permute-done((bf16[11,64,256]{2,1,0:T(8,128)(2,1)S(1)}, bf16[11,64,256]{2,1,0:T(8,128)(2,1)S(1)}, u32[]{:S(2)}, u32[]{:S(2)}) %collective-permute-start.18) | collective-permute-done | bytes 360480 | tf_op jit(solution)/shard_map/ppermute | solution.py:499
  67.4 2.0 %collective-permute-start.21 = (bf16[11,64,256]{2,1,0:T(8,128)(2,1)S(1)}, bf16[11,64,256]{2,1,0:T(8,128)(2,1)S(1)}, u32[]{:S(2)}, u32[]{:S(2)}) collective-permute-start(bf16[11,64,256]{2,1,0:T(8,128)(2,1)S(1)} %get-tuple-element.58.refs_1_), channel_id=1, source_target_pairs={{0,3},{1,0},{2,1},{3,2},{4,7},{5,4},{6,5},{7,6},{8,11},{9,8},{10,9... | collective-permute-start | bytes 1081352 | tf_op jit(solution)/shard_map/ppermute | solution.py:499
  69.4 3.2 %collective-permute-start.23 = (bf16[11,64,256]{2,1,0:T(8,128)(2,1)S(1)}, bf16[11,64,256]{2,1,0:T(8,128)(2,1)S(1)}, u32[]{:S(2)}, u32[]{:S(2)}) collective-permute-start(bf16[11,64,256]{2,1,0:T(8,128)(2,1)S(1)} %get-tuple-element.58.refs_1_), channel_id=1, source_target_pairs={{0,1},{1,2},{2,3},{3,0},{4,5},{5,6},{6,7},{7,4},{8,9},{9,10},{10,1... | collective-permute-start | bytes 1081352 | tf_op jit(solution)/shard_map/ppermute | solution.py:499
  72.6 2.2 %collective-permute-done.20.refs_2_ = bf16[11,64,256]{2,1,0:T(8,128)(2,1)S(1)} collective-permute-done((bf16[11,64,256]{2,1,0:T(8,128)(2,1)S(1)}, bf16[11,64,256]{2,1,0:T(8,128)(2,1)S(1)}, u32[]{:S(2)}, u32[]{:S(2)}) %collective-permute-start.20) | collective-permute-done | bytes 360480 | tf_op jit(solution)/shard_map/ppermute | solution.py:499
  76.8 3.1 %collective-permute-done.22.refs_4_ = bf16[11,64,256]{2,1,0:T(8,128)(2,1)S(1)} collective-permute-done((bf16[11,64,256]{2,1,0:T(8,128)(2,1)S(1)}, bf16[11,64,256]{2,1,0:T(8,128)(2,1)S(1)}, u32[]{:S(2)}, u32[]{:S(2)}) %collective-permute-start.22) | collective-permute-done | bytes 360480 | tf_op jit(solution)/shard_map/ppermute | solution.py:499
  80.0 2.6 %collective-permute-done.24.refs_6_ = bf16[11,64,256]{2,1,0:T(8,128)(2,1)S(1)} collective-permute-done((bf16[11,64,256]{2,1,0:T(8,128)(2,1)S(1)}, bf16[11,64,256]{2,1,0:T(8,128)(2,1)S(1)}, u32[]{:S(2)}, u32[]{:S(2)}) %collective-permute-start.24) | collective-permute-done | bytes 360480 | tf_op jit(solution)/shard_map/ppermute | solution.py:499
  82.5 2.2 %collective-permute-done.25.refs_7_ = bf16[11,64,256]{2,1,0:T(8,128)(2,1)S(1)} collective-permute-done((bf16[11,64,256]{2,1,0:T(8,128)(2,1)S(1)}, bf16[11,64,256]{2,1,0:T(8,128)(2,1)S(1)}, u32[]{:S(2)}, u32[]{:S(2)}) %collective-permute-start.25) | collective-permute-done | bytes 360480 | tf_op jit(solution)/shard_map/ppermute | solution.py:499
  84.7 3.1 %step.1 = (bf16[2,96,256]{2,1,0:T(8,128)(2,1)S(1)}, bf16[2,96,256]{2,1,0:T(8,128)(2,1)S(1)}, bf16[2,96,256]{2,1,0:T(8,128)(2,1)S(1)}, bf16[2,96,256]{2,1,0:T(8,1...) custom-call(bf16[768,256]{1,0:T(8,128)(2,1)S(1)} %bitcast.5, ...), custom_call_target="tpu_custom_call" | custom-call | flops 2415919104 | bytes 6291456 | tf_op jit(solution)/shard_map/step/pallas_call | solution.py:326
  87.9 4.3 %collective-permute-start.26 = (bf16[2,96,256]{2,1,0:T(8,128)(2,1)S(1)}, bf16[2,96,256]{2,1,0:T(8,128)(2,1)S(1)}, u32[]{:S(2)}, u32[]{:S(2)}) collective-permute-start(bf16[2,96,256]{2,1,0:T(8,128)(2,1)S(1)} %get-tuple-element.60.refs_4_), channel_id=1, source_target_pairs={{0,128},{16,144},{32,160},{48,176},{64,192},{80,208},{96,224},{112... | collective-permute-start | bytes 294920 | tf_op jit(solution)/shard_map/ppermute | solution.py:529
  92.2 1.9 %collective-permute-start.27 = (bf16[2,96,256]{2,1,0:T(8,128)(2,1)S(1)}, bf16[2,96,256]{2,1,0:T(8,128)(2,1)S(1)}, u32[]{:S(2)}, u32[]{:S(2)}) collective-permute-start(bf16[2,96,256]{2,1,0:T(8,128)(2,1)S(1)} %get-tuple-element.61.refs_3_), channel_id=1, source_target_pairs={{0,160},{16,176},{32,192},{48,208},{64,224},{80,240},{96,0},{112,1... | collective-permute-start | bytes 294920 | tf_op jit(solution)/shard_map/ppermute | solution.py:529
  94.1 3.1 %collective-permute-start.28 = (bf16[2,96,256]{2,1,0:T(8,128)(2,1)S(1)}, bf16[2,96,256]{2,1,0:T(8,128)(2,1)S(1)}, u32[]{:S(2)}, u32[]{:S(2)}) collective-permute-start(bf16[2,96,256]{2,1,0:T(8,128)(2,1)S(1)} %get-tuple-element.62.refs_5_), channel_id=1, source_target_pairs={{0,96},{16,112},{32,128},{48,144},{64,160},{80,176},{96,192},{112,... | collective-permute-start | bytes 294920 | tf_op jit(solution)/shard_map/ppermute | solution.py:529
  100.8 3.1 %collective-permute-done.27.refs_2_ = bf16[2,96,256]{2,1,0:T(8,128)(2,1)S(1)} collective-permute-done((bf16[2,96,256]{2,1,0:T(8,128)(2,1)S(1)}, bf16[2,96,256]{2,1,0:T(8,128)(2,1)S(1)}, u32[]{:S(2)}, u32[]{:S(2)}) %collective-permute-start.27) | collective-permute-done | bytes 98336 | tf_op jit(solution)/shard_map/ppermute | solution.py:529
  105.2 2.7 %collective-permute-done.30.refs_5_ = bf16[2,96,256]{2,1,0:T(8,128)(2,1)S(1)} collective-permute-done((bf16[2,96,256]{2,1,0:T(8,128)(2,1)S(1)}, bf16[2,96,256]{2,1,0:T(8,128)(2,1)S(1)}, u32[]{:S(2)}, u32[]{:S(2)}) %collective-permute-start.30) | collective-permute-done | bytes 98336 | tf_op jit(solution)/shard_map/ppermute | solution.py:529
  112.1 2.0 %collective-permute-start.36 = (bf16[2,96,256]{2,1,0:T(8,128)(2,1)S(1)}, bf16[2,96,256]{2,1,0:T(8,128)(2,1)S(1)}, u32[]{:S(2)}, u32[]{:S(2)}) collective-permute-start(bf16[2,96,256]{2,1,0:T(8,128)(2,1)S(1)} %get-tuple-element.74), channel_id=1, source_target_pairs={{0,224},{16,240},{32,0},{48,16},{64,32},{80,48},{96,64},{112,80},{... | collective-permute-start | bytes 294920 | tf_op jit(solution)/shard_map/ppermute | solution.py:529
  115.5 2.7 %collective-permute-start.38 = (bf16[2,96,256]{2,1,0:T(8,128)(2,1)S(1)}, bf16[2,96,256]{2,1,0:T(8,128)(2,1)S(1)}, u32[]{:S(2)}, u32[]{:S(2)}) collective-permute-start(bf16[2,96,256]{2,1,0:T(8,128)(2,1)S(1)} %get-tuple-element.76), channel_id=1, source_target_pairs={{0,192},{16,208},{32,224},{48,240},{64,0},{80,16},{96,32},{112,48}... | collective-permute-start | bytes 294920 | tf_op jit(solution)/shard_map/ppermute | solution.py:529
  118.2 3.8 %collective-permute-start.39 = (bf16[2,96,256]{2,1,0:T(8,128)(2,1)S(1)}, bf16[2,96,256]{2,1,0:T(8,128)(2,1)S(1)}, u32[]{:S(2)}, u32[]{:S(2)}) collective-permute-start(bf16[2,96,256]{2,1,0:T(8,128)(2,1)S(1)} %get-tuple-element.77), channel_id=1, source_target_pairs={{0,96},{16,112},{32,128},{48,144},{64,160},{80,176},{96,192},{112,... | collective-permute-start | bytes 294920 | tf_op jit(solution)/shard_map/ppermute | solution.py:529
  123.3 3.2 %collective-permute-start.41 = (bf16[2,96,256]{2,1,0:T(8,128)(2,1)S(1)}, bf16[2,96,256]{2,1,0:T(8,128)(2,1)S(1)}, u32[]{:S(2)}, u32[]{:S(2)}) collective-permute-start(bf16[2,96,256]{2,1,0:T(8,128)(2,1)S(1)} %get-tuple-element.79), channel_id=1, source_target_pairs={{0,128},{16,144},{32,160},{48,176},{64,192},{80,208},{96,224},{112... | collective-permute-start | bytes 294920 | tf_op jit(solution)/shard_map/ppermute | solution.py:529
  129.7 2.9 %collective-permute-done.39.refs_5_ = bf16[2,96,256]{2,1,0:T(8,128)(2,1)S(1)} collective-permute-done((bf16[2,96,256]{2,1,0:T(8,128)(2,1)S(1)}, bf16[2,96,256]{2,1,0:T(8,128)(2,1)S(1)}, u32[]{:S(2)}, u32[]{:S(2)}) %collective-permute-start.39) | collective-permute-done | bytes 98336 | tf_op jit(solution)/shard_map/ppermute | solution.py:529
  132.7 4.3 %collective-permute-done.40.refs_6_ = bf16[2,96,256]{2,1,0:T(8,128)(2,1)S(1)} collective-permute-done((bf16[2,96,256]{2,1,0:T(8,128)(2,1)S(1)}, bf16[2,96,256]{2,1,0:T(8,128)(2,1)S(1)}, u32[]{:S(2)}, u32[]{:S(2)}) %collective-permute-start.40) | collective-permute-done | bytes 98336 | tf_op jit(solution)/shard_map/ppermute | solution.py:529
  (68 shorter events, 35.9 us)
Async XLA Ops:
  4.1 15.6 %collective-permute-start = (bf16[2,96,256]{2,1,0:T(8,128)(2,1)S(1)}, bf16[2,96,256]{2,1,0:T(8,128)(2,1)S(1)}, u32[]{:S(2)}, u32[]{:S(2)}) collective-permute-start(bf16[2,96,256]{2,1,0:T(8,128)(2,1)S(1)} %get-tuple-element.43), channel_id=1, source_target_pairs={{0,128},{16,144},{32,160},{48,176},{64,192},{80,208},{96,224},{112... | collective-permute-start | bytes 294920 | tf_op jit(solution)/shard_map/ppermute | solution.py:529
  10.5 9.2 %collective-permute-start.1 = (bf16[2,96,256]{2,1,0:T(8,128)(2,1)S(1)}, bf16[2,96,256]{2,1,0:T(8,128)(2,1)S(1)}, u32[]{:S(2)}, u32[]{:S(2)}) collective-permute-start(bf16[2,96,256]{2,1,0:T(8,128)(2,1)S(1)} %get-tuple-element.44), channel_id=1, source_target_pairs={{0,96},{16,112},{32,128},{48,144},{64,160},{80,176},{96,192},{112,... | collective-permute-start | bytes 294920 | tf_op jit(solution)/shard_map/ppermute | solution.py:529
  10.5 14.1 %collective-permute-start.2 = (bf16[2,96,256]{2,1,0:T(8,128)(2,1)S(1)}, bf16[2,96,256]{2,1,0:T(8,128)(2,1)S(1)}, u32[]{:S(2)}, u32[]{:S(2)}) collective-permute-start(bf16[2,96,256]{2,1,0:T(8,128)(2,1)S(1)} %get-tuple-element.45), channel_id=1, source_target_pairs={{0,160},{16,176},{32,192},{48,208},{64,224},{80,240},{96,0},{112,1... | collective-permute-start | bytes 294920 | tf_op jit(solution)/shard_map/ppermute | solution.py:529
  15.5 11.4 %collective-permute-start.3 = (bf16[2,96,256]{2,1,0:T(8,128)(2,1)S(1)}, bf16[2,96,256]{2,1,0:T(8,128)(2,1)S(1)}, u32[]{:S(2)}, u32[]{:S(2)}) collective-permute-start(bf16[2,96,256]{2,1,0:T(8,128)(2,1)S(1)} %get-tuple-element.46), channel_id=1, source_target_pairs={{0,64},{16,80},{32,96},{48,112},{64,128},{80,144},{96,160},{112,17... | collective-permute-start | bytes 294920 | tf_op jit(solution)/shard_map/ppermute | solution.py:529
  15.8 11.2 %collective-permute-start.4 = (bf16[2,96,256]{2,1,0:T(8,128)(2,1)S(1)}, bf16[2,96,256]{2,1,0:T(8,128)(2,1)S(1)}, u32[]{:S(2)}, u32[]{:S(2)}) collective-permute-start(bf16[2,96,256]{2,1,0:T(8,128)(2,1)S(1)} %get-tuple-element.47), channel_id=1, source_target_pairs={{0,192},{16,208},{32,224},{48,240},{64,0},{80,16},{96,32},{112,48}... | collective-permute-start | bytes 294920 | tf_op jit(solution)/shard_map/ppermute | solution.py:529
  19.6 8.5 %collective-permute-start.5 = (bf16[2,96,256]{2,1,0:T(8,128)(2,1)S(1)}, bf16[2,96,256]{2,1,0:T(8,128)(2,1)S(1)}, u32[]{:S(2)}, u32[]{:S(2)}) collective-permute-start(bf16[2,96,256]{2,1,0:T(8,128)(2,1)S(1)} %get-tuple-element.48), channel_id=1, source_target_pairs={{0,32},{16,48},{32,64},{48,80},{64,96},{80,112},{96,128},{112,144}... | collective-permute-start | bytes 294920 | tf_op jit(solution)/shard_map/ppermute | solution.py:529
  19.6 9.1 %collective-permute-start.6 = (bf16[2,96,256]{2,1,0:T(8,128)(2,1)S(1)}, bf16[2,96,256]{2,1,0:T(8,128)(2,1)S(1)}, u32[]{:S(2)}, u32[]{:S(2)}) collective-permute-start(bf16[2,96,256]{2,1,0:T(8,128)(2,1)S(1)} %get-tuple-element.49), channel_id=1, source_target_pairs={{0,224},{16,240},{32,0},{48,16},{64,32},{80,48},{96,64},{112,80},{... | collective-permute-start | bytes 294920 | tf_op jit(solution)/shard_map/ppermute | solution.py:529
  30.7 9.0 %collective-permute-start.10 = (bf16[768,256]{1,0:T(8,128)(2,1)S(1)}, bf16[768,256]{1,0:T(8,128)(2,1)S(1)}, u32[]{:S(2)}, u32[]{:S(2)}) collective-permute-start(bf16[768,256]{1,0:T(8,128)(2,1)S(1)} %bitcast.6), channel_id=1, source_target_pairs={{0,3},{1,0},{2,1},{3,2},{4,7},{5,4},{6,5},{7,6},{8,11},{9,8},{10,9... | collective-permute-start | bytes 1179656 | tf_op jit(solution)/shard_map/ppermute | solution.py:499
  31.5 12.4 %collective-permute-start.12 = (bf16[768,256]{1,0:T(8,128)(2,1)S(1)}, bf16[768,256]{1,0:T(8,128)(2,1)S(1)}, u32[]{:S(2)}, u32[]{:S(2)}) collective-permute-start(bf16[768,256]{1,0:T(8,128)(2,1)S(1)} %bitcast.3), channel_id=1, source_target_pairs={{0,3},{1,0},{2,1},{3,2},{4,7},{5,4},{6,5},{7,6},{8,11},{9,8},{10,9... | collective-permute-start | bytes 1179656 | tf_op jit(solution)/shard_map/ppermute | solution.py:499
  32.0 11.8 %collective-permute-start.13 = (bf16[768,256]{1,0:T(8,128)(2,1)S(1)}, bf16[768,256]{1,0:T(8,128)(2,1)S(1)}, u32[]{:S(2)}, u32[]{:S(2)}) collective-permute-start(bf16[768,256]{1,0:T(8,128)(2,1)S(1)} %bitcast.7), channel_id=1, source_target_pairs={{0,1},{1,2},{2,3},{3,0},{4,5},{5,6},{6,7},{7,4},{8,9},{9,10},{10,1... | collective-permute-start | bytes 1179656 | tf_op jit(solution)/shard_map/ppermute | solution.py:499
  39.6 9.0 %collective-permute-start.11 = (bf16[768,256]{1,0:T(8,128)(2,1)S(1)}, bf16[768,256]{1,0:T(8,128)(2,1)S(1)}, u32[]{:S(2)}, u32[]{:S(2)}) collective-permute-start(bf16[768,256]{1,0:T(8,128)(2,1)S(1)} %collective-permute-done.10.refs_3_), channel_id=1, source_target_pairs={{0,3},{1,0},{2,1},{3,2},{4,7},{5,4},{6,5},{7,6},{8,11},{9,8},{10,9... | collective-permute-start | bytes 1179656 | tf_op jit(solution)/shard_map/ppermute | solution.py:499
  49.0 8.9 %collective-permute-start.14 = (bf16[11,64,256]{2,1,0:T(8,128)(2,1)S(1)}, bf16[11,64,256]{2,1,0:T(8,128)(2,1)S(1)}, u32[]{:S(2)}, u32[]{:S(2)}) collective-permute-start(bf16[11,64,256]{2,1,0:T(8,128)(2,1)S(1)} %get-tuple-element.54.refs_0_), channel_id=1, source_target_pairs={{0,4},{1,5},{2,6},{3,7},{4,8},{5,9},{6,10},{7,11},{8,12},{9,13},{1... | collective-permute-start | bytes 1081352 | tf_op jit(solution)/shard_map/ppermute | solution.py:499
  52.5 9.6 %collective-permute-start.16 = (bf16[11,64,256]{2,1,0:T(8,128)(2,1)S(1)}, bf16[11,64,256]{2,1,0:T(8,128)(2,1)S(1)}, u32[]{:S(2)}, u32[]{:S(2)}) collective-permute-start(bf16[11,64,256]{2,1,0:T(8,128)(2,1)S(1)} %get-tuple-element.54.refs_0_), channel_id=1, source_target_pairs={{0,12},{1,13},{2,14},{3,15},{4,0},{5,1},{6,2},{7,3},{8,4},{9,5},{1... | collective-permute-start | bytes 1081352 | tf_op jit(solution)/shard_map/ppermute | solution.py:499
  54.3 8.6 %collective-permute-start.17 = (bf16[11,64,256]{2,1,0:T(8,128)(2,1)S(1)}, bf16[11,64,256]{2,1,0:T(8,128)(2,1)S(1)}, u32[]{:S(2)}, u32[]{:S(2)}) collective-permute-start(bf16[11,64,256]{2,1,0:T(8,128)(2,1)S(1)} %get-tuple-element.55.refs_1_), channel_id=1, source_target_pairs={{0,4},{1,5},{2,6},{3,7},{4,8},{5,9},{6,10},{7,11},{8,12},{9,13},{1... | collective-permute-start | bytes 1081352 | tf_op jit(solution)/shard_map/ppermute | solution.py:499
  57.9 8.9 %collective-permute-start.18 = (bf16[11,64,256]{2,1,0:T(8,128)(2,1)S(1)}, bf16[11,64,256]{2,1,0:T(8,128)(2,1)S(1)}, u32[]{:S(2)}, u32[]{:S(2)}) collective-permute-start(bf16[11,64,256]{2,1,0:T(8,128)(2,1)S(1)} %collective-permute-done.14.refs_2_), channel_id=1, source_target_pairs={{0,4},{1,5},{2,6},{3,7},{4,8},{5,9},{6,10},{7,11},{8,12},{9,13},{1... | collective-permute-start | bytes 1081352 | tf_op jit(solution)/shard_map/ppermute | solution.py:499
  58.3 8.5 %collective-permute-start.19 = (bf16[11,64,256]{2,1,0:T(8,128)(2,1)S(1)}, bf16[11,64,256]{2,1,0:T(8,128)(2,1)S(1)}, u32[]{:S(2)}, u32[]{:S(2)}) collective-permute-start(bf16[11,64,256]{2,1,0:T(8,128)(2,1)S(1)} %collective-permute-done.15.refs_3_), channel_id=1, source_target_pairs={{0,12},{1,13},{2,14},{3,15},{4,0},{5,1},{6,2},{7,3},{8,4},{9,5},{1... | collective-permute-start | bytes 1081352 | tf_op jit(solution)/shard_map/ppermute | solution.py:499
  67.4 8.7 %collective-permute-start.21 = (bf16[11,64,256]{2,1,0:T(8,128)(2,1)S(1)}, bf16[11,64,256]{2,1,0:T(8,128)(2,1)S(1)}, u32[]{:S(2)}, u32[]{:S(2)}) collective-permute-start(bf16[11,64,256]{2,1,0:T(8,128)(2,1)S(1)} %get-tuple-element.58.refs_1_), channel_id=1, source_target_pairs={{0,3},{1,0},{2,1},{3,2},{4,7},{5,4},{6,5},{7,6},{8,11},{9,8},{10,9... | collective-permute-start | bytes 1081352 | tf_op jit(solution)/shard_map/ppermute | solution.py:499
  69.4 10.6 %collective-permute-start.22 = (bf16[11,64,256]{2,1,0:T(8,128)(2,1)S(1)}, bf16[11,64,256]{2,1,0:T(8,128)(2,1)S(1)}, u32[]{:S(2)}, u32[]{:S(2)}) collective-permute-start(bf16[11,64,256]{2,1,0:T(8,128)(2,1)S(1)} %get-tuple-element.57.refs_0_), channel_id=1, source_target_pairs={{0,3},{1,0},{2,1},{3,2},{4,7},{5,4},{6,5},{7,6},{8,11},{9,8},{10,9... | collective-permute-start | bytes 1081352 | tf_op jit(solution)/shard_map/ppermute | solution.py:499
  69.4 10.5 %collective-permute-start.23 = (bf16[11,64,256]{2,1,0:T(8,128)(2,1)S(1)}, bf16[11,64,256]{2,1,0:T(8,128)(2,1)S(1)}, u32[]{:S(2)}, u32[]{:S(2)}) collective-permute-start(bf16[11,64,256]{2,1,0:T(8,128)(2,1)S(1)} %get-tuple-element.58.refs_1_), channel_id=1, source_target_pairs={{0,1},{1,2},{2,3},{3,0},{4,5},{5,6},{6,7},{7,4},{8,9},{9,10},{10,1... | collective-permute-start | bytes 1081352 | tf_op jit(solution)/shard_map/ppermute | solution.py:499
  76.1 8.6 %collective-permute-start.25 = (bf16[11,64,256]{2,1,0:T(8,128)(2,1)S(1)}, bf16[11,64,256]{2,1,0:T(8,128)(2,1)S(1)}, u32[]{:S(2)}, u32[]{:S(2)}) collective-permute-start(bf16[11,64,256]{2,1,0:T(8,128)(2,1)S(1)} %collective-permute-done.21.refs_3_), channel_id=1, source_target_pairs={{0,3},{1,0},{2,1},{3,2},{4,7},{5,4},{6,5},{7,6},{8,11},{9,8},{10,9... | collective-permute-start | bytes 1081352 | tf_op jit(solution)/shard_map/ppermute | solution.py:499
  87.9 12.3 %collective-permute-start.26 = (bf16[2,96,256]{2,1,0:T(8,128)(2,1)S(1)}, bf16[2,96,256]{2,1,0:T(8,128)(2,1)S(1)}, u32[]{:S(2)}, u32[]{:S(2)}) collective-permute-start(bf16[2,96,256]{2,1,0:T(8,128)(2,1)S(1)} %get-tuple-element.60.refs_4_), channel_id=1, source_target_pairs={{0,128},{16,144},{32,160},{48,176},{64,192},{80,208},{96,224},{112... | collective-permute-start | bytes 294920 | tf_op jit(solution)/shard_map/ppermute | solution.py:529
  92.2 11.7 %collective-permute-start.27 = (bf16[2,96,256]{2,1,0:T(8,128)(2,1)S(1)}, bf16[2,96,256]{2,1,0:T(8,128)(2,1)S(1)}, u32[]{:S(2)}, u32[]{:S(2)}) collective-permute-start(bf16[2,96,256]{2,1,0:T(8,128)(2,1)S(1)} %get-tuple-element.61.refs_3_), channel_id=1, source_target_pairs={{0,160},{16,176},{32,192},{48,208},{64,224},{80,240},{96,0},{112,1... | collective-permute-start | bytes 294920 | tf_op jit(solution)/shard_map/ppermute | solution.py:529
  94.1 11.1 %collective-permute-start.28 = (bf16[2,96,256]{2,1,0:T(8,128)(2,1)S(1)}, bf16[2,96,256]{2,1,0:T(8,128)(2,1)S(1)}, u32[]{:S(2)}, u32[]{:S(2)}) collective-permute-start(bf16[2,96,256]{2,1,0:T(8,128)(2,1)S(1)} %get-tuple-element.62.refs_5_), channel_id=1, source_target_pairs={{0,96},{16,112},{32,128},{48,144},{64,160},{80,176},{96,192},{112,... | collective-permute-start | bytes 294920 | tf_op jit(solution)/shard_map/ppermute | solution.py:529
  98.6 9.3 %collective-permute-start.30 = (bf16[2,96,256]{2,1,0:T(8,128)(2,1)S(1)}, bf16[2,96,256]{2,1,0:T(8,128)(2,1)S(1)}, u32[]{:S(2)}, u32[]{:S(2)}) collective-permute-start(bf16[2,96,256]{2,1,0:T(8,128)(2,1)S(1)} %get-tuple-element.64.refs_6_), channel_id=1, source_target_pairs={{0,64},{16,80},{32,96},{48,112},{64,128},{80,144},{96,160},{112,17... | collective-permute-start | bytes 294920 | tf_op jit(solution)/shard_map/ppermute | solution.py:529
  109.4 8.9 %collective-permute-start.33 = (bf16[8,96,256]{2,1,0:T(8,128)(2,1)S(1)}, bf16[8,96,256]{2,1,0:T(8,128)(2,1)S(1)}, u32[]{:S(2)}, u32[]{:S(2)}) collective-permute-start(bf16[8,96,256]{2,1,0:T(8,128)(2,1)S(1)} %get-tuple-element.68), channel_id=1, source_target_pairs={{0,16},{16,0},{32,48},{48,32},{64,80},{80,64},{96,112},{112,96},{1... | collective-permute-start | bytes 1179656 | tf_op jit(solution)/shard_map/ppermute | solution.py:548
  112.0 10.1 %collective-permute-start.35 = (bf16[2,96,256]{2,1,0:T(8,128)(2,1)S(1)}, bf16[2,96,256]{2,1,0:T(8,128)(2,1)S(1)}, u32[]{:S(2)}, u32[]{:S(2)}) collective-permute-start(bf16[2,96,256]{2,1,0:T(8,128)(2,1)S(1)} %get-tuple-element.73), channel_id=1, source_target_pairs={{0,32},{16,48},{32,64},{48,80},{64,96},{80,112},{96,128},{112,144}... | collective-permute-start | bytes 294920 | tf_op jit(solution)/shard_map/ppermute | solution.py:529
  112.1 11.2 %collective-permute-start.36 = (bf16[2,96,256]{2,1,0:T(8,128)(2,1)S(1)}, bf16[2,96,256]{2,1,0:T(8,128)(2,1)S(1)}, u32[]{:S(2)}, u32[]{:S(2)}) collective-permute-start(bf16[2,96,256]{2,1,0:T(8,128)(2,1)S(1)} %get-tuple-element.74), channel_id=1, source_target_pairs={{0,224},{16,240},{32,0},{48,16},{64,32},{80,48},{96,64},{112,80},{... | collective-permute-start | bytes 294920 | tf_op jit(solution)/shard_map/ppermute | solution.py:529
  114.1 15.6 %collective-permute-start.37 = (bf16[2,96,256]{2,1,0:T(8,128)(2,1)S(1)}, bf16[2,96,256]{2,1,0:T(8,128)(2,1)S(1)}, u32[]{:S(2)}, u32[]{:S(2)}) collective-permute-start(bf16[2,96,256]{2,1,0:T(8,128)(2,1)S(1)} %get-tuple-element.75), channel_id=1, source_target_pairs={{0,64},{16,80},{32,96},{48,112},{64,128},{80,144},{96,160},{112,17... | collective-permute-start | bytes 294920 | tf_op jit(solution)/shard_map/ppermute | solution.py:529
  115.5 14.2 %collective-permute-start.38 = (bf16[2,96,256]{2,1,0:T(8,128)(2,1)S(1)}, bf16[2,96,256]{2,1,0:T(8,128)(2,1)S(1)}, u32[]{:S(2)}, u32[]{:S(2)}) collective-permute-start(bf16[2,96,256]{2,1,0:T(8,128)(2,1)S(1)} %get-tuple-element.76), channel_id=1, source_target_pairs={{0,192},{16,208},{32,224},{48,240},{64,0},{80,16},{96,32},{112,48}... | collective-permute-start | bytes 294920 | tf_op jit(solution)/shard_map/ppermute | solution.py:529
  118.2 14.4 %collective-permute-start.39 = (bf16[2,96,256]{2,1,0:T(8,128)(2,1)S(1)}, bf16[2,96,256]{2,1,0:T(8,128)(2,1)S(1)}, u32[]{:S(2)}, u32[]{:S(2)}) collective-permute-start(bf16[2,96,256]{2,1,0:T(8,128)(2,1)S(1)} %get-tuple-element.77), channel_id=1, source_target_pairs={{0,96},{16,112},{32,128},{48,144},{64,160},{80,176},{96,192},{112,... | collective-permute-start | bytes 294920 | tf_op jit(solution)/shard_map/ppermute | solution.py:529
  122.0 14.9 %collective-permute-start.40 = (bf16[2,96,256]{2,1,0:T(8,128)(2,1)S(1)}, bf16[2,96,256]{2,1,0:T(8,128)(2,1)S(1)}, u32[]{:S(2)}, u32[]{:S(2)}) collective-permute-start(bf16[2,96,256]{2,1,0:T(8,128)(2,1)S(1)} %get-tuple-element.78), channel_id=1, source_target_pairs={{0,160},{16,176},{32,192},{48,208},{64,224},{80,240},{96,0},{112,1... | collective-permute-start | bytes 294920 | tf_op jit(solution)/shard_map/ppermute | solution.py:529
  123.3 13.7 %collective-permute-start.41 = (bf16[2,96,256]{2,1,0:T(8,128)(2,1)S(1)}, bf16[2,96,256]{2,1,0:T(8,128)(2,1)S(1)}, u32[]{:S(2)}, u32[]{:S(2)}) collective-permute-start(bf16[2,96,256]{2,1,0:T(8,128)(2,1)S(1)} %get-tuple-element.79), channel_id=1, source_target_pairs={{0,128},{16,144},{32,160},{48,176},{64,192},{80,208},{96,224},{112... | collective-permute-start | bytes 294920 | tf_op jit(solution)/shard_map/ppermute | solution.py:529
  (12 other events, 65.4 us)
